TPU v7x, 32 devices: a whole 2x2x4 slice. The times are simulated.
32 devices in a mesh: grp: 2 (over y), row: 4 (over x, core), col: 4 (over z).
Axes of the slice: x: 2, y: 2, z: 4, core: 2. Of those that a mesh axis runs over, the one named last changes fastest.
Arguments:
- homolog_embedding: bfloat16 [256, 32, 64], P(('grp', 'col'), 'row'), parts along dimension 0, may hold values from -6 to 6
- presence_indicator: int32 [256, 32], P(('grp', 'col'), 'row'), parts along dimension 0, may hold values 0 or 1
- coupling_change_derivative: bfloat16 [64, 32, 128], P(('grp', 'row'), 'col'), parts along dimension 0, may hold values from -1.5 to 1.5
- standardizer_scale: float32 [64], replicated, may hold values from 0.5 to 1.5
- standardizer_shift: float32 [64], replicated, may hold values from -3 to 3
- first_projection_matrix: bfloat16 [64, 32], replicated, may hold values from -0.75 to 0.75
- second_projection_matrix: bfloat16 [64, 32], replicated, may hold values from -0.75 to 0.75
- final_projection_matrix: bfloat16 [1024, 128], replicated, may hold values from -0.1875 to 0.1875
Outputs:
- embedding_derivative: float32 [256, 32, 64], P(('grp', 'col'), 'row'), parts along dimension 0
- final_matrix_derivative: float32 [2048, 128], P('grp'), parts along dimension 0
- first_matrix_derivative: float32 [128, 32], P('grp'), parts along dimension 0
- second_matrix_derivative: float32 [128, 32], P('grp'), parts along dimension 0
- scale_factor_derivative: float32 [128], P('grp'), parts along dimension 0
- shift_term_derivative: float32 [128], P('grp'), parts along dimension 0
- shift_derivative: float32 [256], P('grp'), parts along dimension 0
There are 2 independent parts, one for each index of `grp`. A program takes and returns all parts, laid end to end along the dimension named above; an argument that names none is the same for every part. Nothing has to cross between parts.
All inputs are finite; a program needn't handle non-finite values. No bound on the sum of `presence_indicator` on one device may be relied on, other than what follows from the above.
Results may differ from a plain program's by a relative error of at most 0.0066.
Values may be sent and summed in bfloat16 or wider, within the bound.
No kernel may reach another device: no remote copies, remote signals or barrier semaphores. Data moves between devices by JAX's collectives and lax.ppermute only.
A program may use at most 64 MiB of HBM per device.

v0:
```python
import jax
import jax.numpy as jnp
from jax import lax
from jax.sharding import PartitionSpec as P

TOKB = 2


def standardizer_parts(homolog_embedding, standardizer_scale, standardizer_shift):
    incoming_entries = homolog_embedding.astype(jnp.float32)
    center = jnp.mean(incoming_entries, axis=-1, keepdims=True)
    varied = incoming_entries - center
    variance = jnp.mean(varied * varied, axis=-1, keepdims=True)
    reciprocal_spread = lax.rsqrt(variance + 1e-05)
    standardized_entries = varied * reciprocal_spread
    standardized_bfloat = (standardized_entries * standardizer_scale + standardizer_shift).astype(
        jnp.bfloat16
    )
    return (standardized_entries, reciprocal_spread, standardized_bfloat)


def body(
    homolog_embedding,
    presence_indicator,
    coupling_change_derivative,
    standardizer_scale,
    standardizer_shift,
    first_projection_matrix,
    second_projection_matrix,
    final_projection_matrix,
):
    shard_homolog_number, residue_line_number, feature_number = homolog_embedding.shape
    tok_cols = coupling_change_derivative.shape[1]
    width = first_projection_matrix.shape[1]
    standardized_entries, reciprocal_spread, standardized_bfloat = standardizer_parts(
        homolog_embedding, standardizer_scale, standardizer_shift
    )
    mask_single_precision = presence_indicator.astype(jnp.float32)
    mask_half_precision = presence_indicator.astype(jnp.bfloat16)
    left = (
        jnp.einsum(
            "sic,cp->sip",
            standardized_bfloat,
            first_projection_matrix,
            preferred_element_type=jnp.float32,
        )
        * mask_single_precision[..., None]
    ).astype(jnp.bfloat16)
    right = (
        jnp.einsum(
            "sic,cp->sip",
            standardized_bfloat,
            second_projection_matrix,
            preferred_element_type=jnp.float32,
        )
        * mask_single_precision[..., None]
    ).astype(jnp.bfloat16)
    left_flat = left.reshape(shard_homolog_number, residue_line_number * width)
    right_flat = right.reshape(shard_homolog_number, residue_line_number * width)
    left_all, mask_left = (
        lax.all_gather(left_flat, "col", axis=0, tiled=True),
        lax.all_gather(mask_half_precision, "col", axis=0, tiled=True),
    )
    right_wide, mask_wide = (
        lax.all_gather(right_flat, "row", axis=1, tiled=True),
        lax.all_gather(mask_half_precision, "row", axis=1, tiled=True),
    )
    right_all, mask_right = (
        lax.all_to_all(right_wide, "col", split_axis=1, concat_axis=0, tiled=True),
        lax.all_to_all(mask_wide, "col", split_axis=1, concat_axis=0, tiled=True),
    )
    seq_total = left_all.shape[0]
    right_three = right_all.reshape(seq_total, tok_cols, width)
    counts = jnp.einsum("si,sj->ij", mask_left, mask_right, preferred_element_type=jnp.float32)
    scaled = coupling_change_derivative.astype(jnp.float32) / (counts + 0.001)[..., None]
    bias_part = jnp.sum(scaled, axis=(0, 1))
    scaled_bf = scaled.astype(jnp.bfloat16)
    block_rows = residue_line_number // TOKB
    right_acc = jnp.zeros((seq_total, tok_cols, width), jnp.float32)
    wout_acc = jnp.zeros(final_projection_matrix.shape, jnp.float32)
    left_pieces = []
    for block_index in range(TOKB):
        first = block_index * block_rows
        rows_bf = scaled_bf[first : first + block_rows]
        outer_grad = jnp.einsum(
            "ijz,fz->ijf", rows_bf, final_projection_matrix, preferred_element_type=jnp.float32
        ).astype(jnp.bfloat16)
        outer_grad = outer_grad.reshape(block_rows, tok_cols, width, width)
        left_block = left_all[:, first * width : (first + block_rows) * width].reshape(
            seq_total, block_rows, width
        )
        first_factor_derivative = jnp.einsum(
            "ijce,sje->sic", outer_grad, right_three, preferred_element_type=jnp.float32
        )
        right_acc = right_acc + jnp.einsum(
            "ijce,sic->sje", outer_grad, left_block, preferred_element_type=jnp.float32
        )
        outer = jnp.einsum(
            "sic,sje->ijce", left_block, right_three, preferred_element_type=jnp.float32
        ).astype(jnp.bfloat16)
        outer = outer.reshape(block_rows, tok_cols, width * width)
        wout_acc = wout_acc + jnp.einsum(
            "ijf,ijz->fz", outer, rows_bf, preferred_element_type=jnp.float32
        )
        first_factor_derivative = first_factor_derivative.reshape(seq_total, block_rows * width)
        left_pieces.append(first_factor_derivative)
    left_terms = jnp.concatenate(left_pieces, axis=1)
    left_own = lax.psum_scatter(left_terms, "col", scatter_dimension=0, tiled=True)
    right_spread = lax.all_to_all(
        right_acc.reshape(seq_total, tok_cols * width),
        "col",
        split_axis=0,
        concat_axis=1,
        tiled=True,
    )
    right_own = lax.psum_scatter(right_spread, "row", scatter_dimension=1, tiled=True)
    left_in = (
        left_own.reshape(shard_homolog_number, residue_line_number, width)
        * mask_single_precision[..., None]
    ).astype(jnp.bfloat16)
    right_in = (
        right_own.reshape(shard_homolog_number, residue_line_number, width)
        * mask_single_precision[..., None]
    ).astype(jnp.bfloat16)
    left_part = jnp.einsum(
        "sic,sip->cp", standardized_bfloat, left_in, preferred_element_type=jnp.float32
    )
    right_part = jnp.einsum(
        "sic,sip->cp", standardized_bfloat, right_in, preferred_element_type=jnp.float32
    )
    d_normal = jnp.einsum(
        "sip,cp->sic", left_in, first_projection_matrix, preferred_element_type=jnp.float32
    ) + jnp.einsum(
        "sip,cp->sic", right_in, second_projection_matrix, preferred_element_type=jnp.float32
    )
    gain_part = jnp.sum(d_normal * standardized_entries, axis=(0, 1))
    beta_part = jnp.sum(d_normal, axis=(0, 1))
    standardized_derivative = d_normal * standardizer_scale
    embedding_derivative = reciprocal_spread * (
        standardized_derivative
        - jnp.mean(standardized_derivative, axis=-1, keepdims=True)
        - standardized_entries
        * jnp.mean(standardized_derivative * standardized_entries, axis=-1, keepdims=True)
    )
    (
        final_matrix_derivative,
        first_matrix_derivative,
        second_matrix_derivative,
        scale_factor_derivative,
        shift_term_derivative,
        shift_derivative,
    ) = lax.psum((wout_acc, left_part, right_part, gain_part, beta_part, bias_part), ("row", "col"))
    return (
        embedding_derivative,
        final_matrix_derivative,
        first_matrix_derivative,
        second_matrix_derivative,
        scale_factor_derivative,
        shift_term_derivative,
        shift_derivative,
    )


def solution(mesh):
    placed = (
        P(("grp", "col"), "row", None),
        P(("grp", "col"), "row"),
        P(("grp", "row"), "col", None),
        P(),
        P(),
        P(),
        P(),
        P(),
    )
    return jax.shard_map(
        body,
        mesh=mesh,
        in_specs=placed,
        out_specs=(
            P(("grp", "col"), "row", None),
            P("grp", None),
            P("grp", None),
            P("grp", None),
            P("grp"),
            P("grp"),
            P("grp"),
        ),
        check_vma=False,
    )
```

profile of v0, /device:TPU:0, one launch (start us, length us, event | category | flops | bytes accessed | tf_op | source)
XLA Modules:
  0.0 186.2 jit_solution(5907129250843902817)
XLA Ops:
  8.0 0.8 fusion.38
  8.8 6.1 %all_gather.14 = bf16[32,32]{0,1:T(8,128)(2,1)S(1)} all-gather(bf16[32,8]{0,1:T(8,128)(2,1)S(1)} %get-tuple-element.41), channel_id=1, replica_groups=mesh['grp'=2,'row'=4,'col'=4] {'row'}, dimensions={1}, use_global_device_ids=true | all-gather | bytes 2560 | tf_op jit(solution)/shard_map/all_gather | solution.py:66
  14.9 0.7 reshape.118
  15.6 5.4 %all-to-all-start.1 = ((bf16[4,2,128]{2,1,0:T(2,128)(2,1)}), bf16[4,2,128]{2,1,0:T(2,128)(2,1)S(1)}, u32[]{:S(2)}, u32[]{:S(2)}) async-start(bf16[4,2,128]{2,1,0:T(2,128)(2,1)} %reshape.118), calls=%async_computation.1 | async-start | bytes 4096 | tf_op jit(solution)/shard_map/all_to_all | solution.py:70
  20.9 0.9 convert_reduce_fusion
  22.1 0.7 copy-done.3
  22.8 0.2 fusion.5
  23.2 13.7 %all_gather.15 = bf16[128,256]{1,0:T(8,128)(2,1)S(1)} all-gather(bf16[32,256]{1,0:T(8,128)(2,1)S(1)} %reshape.92), channel_id=1, replica_groups=mesh['grp'=2,'row'=4,'col'=4] {'col'}, dimensions={0}, use_global_device_ids=true | all-gather | bytes 81920 | tf_op jit(solution)/shard_map/all_gather | solution.py:61
  36.9 0.7 copy-done.5
  37.6 0.2 fusion.4
  38.0 5.2 %all_gather.12 = bf16[32,1024]{1,0:T(8,128)(2,1)S(1)} all-gather(bf16[32,256]{1,0:T(8,128)(2,1)S(1)} %reshape.87), channel_id=1, replica_groups=mesh['grp'=2,'row'=4,'col'=4] {'row'}, dimensions={1}, use_global_device_ids=true | all-gather | bytes 81920 | tf_op jit(solution)/shard_map/all_gather | solution.py:65
  43.2 11.9 %all-gather = bf16[4,32,8]{1,2,0:T(8,128)(2,1)S(1)} all-gather(bf16[1,32,8]{1,2,0:T(8,128)(2,1)S(1)} %bitcast.124), channel_id=1, replica_groups=mesh['grp'=2,'row'=4,'col'=4] {'col'}, dimensions={0}, use_global_device_ids=true | all-gather | bytes 2560 | tf_op jit(solution)/shard_map/all_gather | solution.py:62
  55.4 0.6 copy.114
  56.1 3.4 %all-to-all-start = ((bf16[32,4,256]{2,0,1:T(8,128)(2,1)}), bf16[32,4,256]{2,0,1:T(8,128)(2,1)S(1)}, u32[]{:S(2)}, u32[]{:S(2)}) async-start(bf16[32,4,256]{2,0,1:T(8,128)(2,1)} %bitcast.111), calls=%async_computation | async-start | bytes 131072 | tf_op jit(solution)/shard_map/all_to_all | solution.py:69
  59.8 0.5 copy-done.2
  61.2 0.2 convolution_bitcast_fusion.3
  61.4 0.2 fusion.3
  61.6 0.2 copy.56
  62.0 0.2 copy.54
  62.4 0.3 reshape.115
  62.7 0.8 copy.87
  63.5 1.7 all-to-all-done
  65.2 3.4 %all-to-all-start.2 = ((f32[4,32,256]{2,1,0:T(8,128)}), f32[4,32,256]{2,1,0:T(8,128)S(1)}, u32[]{:S(2)}, u32[]{:S(2)}) async-start(f32[4,32,256]{2,1,0:T(8,128)} %copy.87), calls=%async_computation.2 | async-start | bytes 262144 | tf_op jit(solution)/shard_map/all_to_all | solution.py:109
  68.8 0.2 copy.55
  69.0 0.2 copy.79
  69.2 0.2 convolution_bitcast_fusion.4
  69.4 0.2 convolution_bitcast_fusion.5
  69.6 0.8 copy.92
  70.5 0.2 fusion.2
  70.9 0.3 reshape.97
  71.2 0.2 fusion.1
  71.4 3.1 %all-to-all-done.2 = f32[4,32,256]{2,1,0:T(8,128)S(1)} async-done(((f32[4,32,256]{2,1,0:T(8,128)}), f32[4,32,256]{2,1,0:T(8,128)S(1)}, u32[]{:S(2)}, u32[]{:S(2)}) %all-to-all-start.2) | async-done | bytes 131104 | tf_op jit(solution)/shard_map/all_to_all | solution.py:109
  74.5 0.7 copy.95
  75.3 0.3 convolution_bitcast_fusion
  75.7 0.3 reshape.96
  76.0 1.1 fusion
  77.1 15.9 %reduce-scatter.7.cloned.1.call-done = f32[32,256]{1,0:T(8,128)} async-done(((f32[128,256]{1,0:T(8,128)}), f32[32,256]{1,0:T(8,128)}) %reduce-scatter.7.cloned.1.call-update) | async-done | bytes 32784
  93.0 0.9 copy.93
  94.0 0.3 convolution_bitcast_fusion.7
  94.3 0.2 fusion.22
  94.5 19.0 %reduce-scatter.5.cloned.1.call-done = f32[32,256]{1,0:T(8,128)} async-done(((f32[32,1024]{1,0:T(8,128)}), f32[32,256]{1,0:T(8,128)}) %reduce-scatter.5.cloned.1.call-update) | async-done | bytes 32784 | tf_op jit(solution)/shard_map/reduce_scatter | solution.py:116
  113.5 0.8 reshape.95
  114.4 0.3 fusion.19
  114.7 0.2 fusion.18
  114.9 0.7 copy.74
  115.7 0.3 convolution_bitcast_fusion.6
  116.0 60.9 %all-reduce = (f32[64,32]{0,1:T(8,128)}, f32[64,32]{0,1:T(8,128)}, f32[64]{0:T(128)}, f32[64]{0:T(128)}, f32[128]{0:T(128)}) all-reduce(f32[64,32]{0,1:T(8,128)S(1)} %convolution_bitcast_fusion.7, f32[64,32]{0,1:T(8,128)S(1)} %convolution_bitcast_fusion.6, ...), channel_id=1, replica_groups=mesh['grp'=2,'row'=4,'col'=4] {'row','col'}, use_global_device_ids=true, to_apply=%region_7.0 | all-reduce | flops 4352 | bytes 34816 | tf_op jit(solution)/shard_map/psum | solution.py:152
  176.9 1.9 %copy.116 = f32[1024,128]{1,0:T(8,128)} copy(f32[1024,128]{1,0:T(8,128)} %all-reduce.3.cloned.1.call-done) | data formatting | bytes 1048576
  (50 shorter events, 3.1 us)
Async XLA Ops:
  8.0 52.4 %copy-start = (bf16[1024,128]{1,0:T(8,128)(2,1)S(1)}, bf16[1024,128]{1,0:T(8,128)(2,1)}, u32[]{:S(2)}) copy-start(bf16[1024,128]{1,0:T(8,128)(2,1)} %param.15) | copy-start | bytes 786436
  8.0 13.9 %copy-start.1 = (bf16[32,8,64]{2,1,0:T(8,128)(2,1)S(1)}, bf16[32,8,64]{2,1,0:T(8,128)(2,1)}, u32[]{:S(2)}) copy-start(bf16[32,8,64]{2,1,0:T(8,128)(2,1)} %param.8) | copy-start | bytes 98308
  15.6 40.5 %all-to-all-start.1 = ((bf16[4,2,128]{2,1,0:T(2,128)(2,1)}), bf16[4,2,128]{2,1,0:T(2,128)(2,1)S(1)}, u32[]{:S(2)}, u32[]{:S(2)}) async-start(bf16[4,2,128]{2,1,0:T(2,128)(2,1)} %reshape.118), calls=%async_computation.1 | async-start | bytes 4096 | tf_op jit(solution)/shard_map/all_to_all | solution.py:70
  22.1 0.7 copy-start.3
  22.1 0.7 copy-start.4
  22.1 0.7 copy-start.6
  36.9 0.7 copy-start.5
  56.1 9.2 %all-to-all-start = ((bf16[32,4,256]{2,0,1:T(8,128)(2,1)}), bf16[32,4,256]{2,0,1:T(8,128)(2,1)S(1)}, u32[]{:S(2)}, u32[]{:S(2)}) async-start(bf16[32,4,256]{2,0,1:T(8,128)(2,1)} %bitcast.111), calls=%async_computation | async-start | bytes 131072 | tf_op jit(solution)/shard_map/all_to_all | solution.py:69
  59.6 0.7 copy-start.2
  65.2 9.3 %all-to-all-start.2 = ((f32[4,32,256]{2,1,0:T(8,128)}), f32[4,32,256]{2,1,0:T(8,128)S(1)}, u32[]{:S(2)}, u32[]{:S(2)}) async-start(f32[4,32,256]{2,1,0:T(8,128)} %copy.87), calls=%async_computation.2 | async-start | bytes 262144 | tf_op jit(solution)/shard_map/all_to_all | solution.py:109
  68.6 24.4 %reduce-scatter.7.cloned.1.call-start = ((), (), s32[]{:S(2)}) async-start(), calls=%async_computation.7 | async-start | bytes 163840
  70.4 43.1 %reduce-scatter.5.cloned.1.call-start = ((), (), s32[]{:S(2)}) async-start(), calls=%async_computation.5 | async-start | bytes 163840 | tf_op jit(solution)/shard_map/reduce_scatter | solution.py:116
  75.2 101.6 %all-reduce.3.cloned.1.call-start = ((), (), s32[]{:S(2)}) async-start(), calls=%async_computation.6 | async-start | bytes 1048576 | tf_op jit(solution)/shard_map/psum | solution.py:152
Sparse Core Ops, SparseCore 0:
  72.3 20.6 reduce-scatter.6
  95.6 17.8 reduce-scatter.4
Sparse Core Ops, SparseCore 1:
  79.7 88.8 all-reduce.2
where the time goes:
time: 187 us; the launch traced here: 186 us
  blocking collectives  97.8 us (52%)
  waiting for transfers between devices  39.8 us (21%)
  between operations  15.8 us (8%)
  local copies, waits for them, and re-layouts  13.5 us (7%)
  starting transfers between devices  12.3 us (7%)
  matrix products  4.84 us (3%)
  other arithmetic  2.21 us (1%)
    psum x1, blocking collectives, body(): lax.psum((wout_acc, left_part, right_part, gain_part, beta_part, bias_par...  60.9 us
    reduce_scatter x1, waiting for transfers between devices, body(): lax.psum_scatter(right_spread, 'row', scatter_dimension=1, tiled=True)  19 us
    unnamed x4, waiting for transfers between devices  15.9 us
    all_gather x1, blocking collectives, body(): lax.all_gather(left_flat, 'col', axis=0, tiled=True)  13.7 us
    all_gather x1, blocking collectives, body(): lax.all_gather(mask_half_precision, 'col', axis=0, tiled=True)  11.9 us
    unnamed x22, local copies, waits for them, and re-layouts  6.92 us
    all_gather x1, blocking collectives, body(): lax.all_gather(mask_half_precision, 'row', axis=1, tiled=True)  6.1 us
    all_to_all x1, starting transfers between devices, body(): lax.all_to_all(mask_wide, 'col', split_axis=1, concat_axis=0, tiled=True)  5.37 us
  transfers between devices with their start and end apart: 6, of which 4 were waited for; matrix products, arithmetic and copies ran while one was open for 8% of the time, Pallas kernels for 0%

commit v1 on v0

--- a/solution.py
+++ b/solution.py
@@ -1,6 +1,10 @@
+import functools
+
 import jax
 import jax.numpy as jnp
 from jax import lax
+from jax.experimental import pallas as pl
+from jax.experimental.pallas import tpu as pltpu
 from jax.sharding import PartitionSpec as P
 
 TOKB = 2
@@ -19,7 +23,7 @@
     return (standardized_entries, reciprocal_spread, standardized_bfloat)
 
 
-def body(
+def sharded_body(
     homolog_embedding,
     presence_indicator,
     coupling_change_derivative,
@@ -161,6 +165,316 @@
     )
 
 
+BF = jnp.bfloat16
+F32 = jnp.float32
+
+
+def spread(rows, cols, rule):
+    r = lax.broadcasted_iota(jnp.int32, (rows, cols), 0)
+    c = lax.broadcasted_iota(jnp.int32, (rows, cols), 1)
+    return rule(r, c)
+
+
+def two_terms(value):
+    high = value.astype(BF)
+    return high, (value - high.astype(F32)).astype(BF)
+
+
+def mm(a, b):
+    return jnp.dot(a, b, preferred_element_type=F32)
+
+
+def group_mean(value, averager):
+    high, low = two_terms(value)
+    return mm(high, averager) + mm(low, averager)
+
+
+def swap_blocks(block):
+    lane = lax.broadcasted_iota(jnp.int32, (32, 128), 1)
+    upper = lane >= 64
+    odd = (lane // 32) % 2 == 1
+    piece = [block[32 * a : 32 * a + 32] for a in range(4)]
+    for a in (0, 1):
+        x, y = piece[a], piece[a + 2]
+        piece[a] = jnp.where(upper, pltpu.roll(y, 64, 1), x)
+        piece[a + 2] = jnp.where(upper, y, pltpu.roll(x, 64, 1))
+    for a in (0, 2):
+        x, y = piece[a], piece[a + 1]
+        piece[a] = jnp.where(odd, pltpu.roll(y, 32, 1), x)
+        piece[a + 1] = jnp.where(odd, y, pltpu.roll(x, 96, 1))
+    return jnp.concatenate(piece, axis=0)
+
+
+def pack_kernel(msa_ref, mask_ref, pair_ref, out_ref):
+    msa = msa_ref[...].astype(F32)
+    for g in range(4):
+        out_ref[32 * g : 32 * g + 32, :] = jnp.concatenate(
+            [msa[:, 2 * g, :], msa[:, 2 * g + 1, :]], axis=1
+        ).astype(BF)
+    pair = pair_ref[...].astype(F32)
+    for j in range(0, 8, 2):
+        out_ref[128 + 8 * j : 144 + 8 * j, :] = jnp.concatenate(
+            [pair[:, j, :], pair[:, j + 1, :]], axis=0
+        ).astype(BF)
+    mask = mask_ref[...].astype(F32).astype(BF)
+    pick = spread(8, 128, lambda r, c: (c % 8 == r).astype(F32)).astype(BF)
+    out_ref[192:224, :] = mm(mask, pick).astype(BF)
+
+
+def part_kernel(n_row, n_col, place_ref, *refs):
+    blocks = [[refs[a * n_col + b] for b in range(n_col)] for a in range(n_row)]
+    (
+        gain_ref, offset_ref, first_ref, second_ref, final_ref,
+        emb_out, final_out, first_out, second_out, gain_out, offset_out, bias_out,
+        pair_scr, normed_scr, rhs_scr, left_scr, leftt_scr, left2_scr, right_scr, rightt_scr,
+        scaled_scr, grad_scr, outer_scr, lin_scr, linc_scr, rin_scr,
+    ) = refs[n_row * n_col :]
+    place = place_ref[0]
+
+    for a in range(n_row):
+        for b in range(n_col):
+            at = lax.bitwise_xor(place, b) * 8
+            pair_scr[pl.ds(at, 8), 8 * a : 8 * a + 8, :] = (
+                blocks[a][b][128:192, :].astype(F32).reshape(8, 8, 128)
+            )
+
+    mask_rows = [
+        jnp.concatenate([blocks[a][b][192:224, :] for b in range(n_col)], axis=0)
+        for a in range(n_row)
+    ]
+    token_of = lax.broadcasted_iota(jnp.int32, (128, 128), 1) // 8 % 4
+    mask = jnp.zeros((128, 128), F32)
+    for a in range(n_row):
+        mask = jnp.where(token_of == a, mask_rows[a].astype(F32), mask)
+    mask_t = mask.T
+
+    gain = jnp.concatenate([gain_ref[...], gain_ref[...]], axis=1)
+    offset = jnp.concatenate([offset_ref[...], offset_ref[...]], axis=1)
+    averager = spread(128, 128, lambda r, c: jnp.where(r // 64 == c // 64, 1.0 / 64, 0.0)).astype(BF)
+    first = first_ref[...].astype(F32)
+    second = second_ref[...].astype(F32)
+    wide = jnp.concatenate([first] * 4 + [second] * 4, axis=1)
+    wide = jnp.concatenate([wide] * 4, axis=0)
+    project = jnp.where(
+        spread(256, 256, lambda r, c: r // 64 == c % 128 // 32), wide, 0.0
+    ).astype(BF)
+    chooser = spread(128, 512, lambda r, c: jnp.where(r == c // 64, 1.0, 0.0)).astype(BF)
+    inverse_own = None
+    for a in range(n_row):
+        x = jnp.concatenate(
+            [blocks[a][b][32 * g : 32 * g + 32, :] for g in range(4) for b in range(n_col)], axis=0
+        )
+        varied = x.astype(F32) - mm(x, averager)
+        inverse = lax.rsqrt(group_mean(varied * varied, averager) + 1e-05)
+        normed = varied * inverse
+        if a == 0:
+            inverse_own = inverse
+        rows = slice(512 * a, 512 * a + 512)
+        normed_scr[rows, :] = normed
+        normal = (normed * gain + offset).astype(BF)
+        high, low = two_terms(normed)
+        rhs_scr[rows, 0:128] = normal
+        rhs_scr[rows, 128:256] = high
+        rhs_scr[rows, 256:384] = low
+        rhs_scr[rows, 384:512] = jnp.ones((512, 128), BF)
+        mask_wide = mm(mask_rows[a], chooser).astype(BF)
+        for h in range(2):
+            masked = jnp.concatenate(
+                [
+                    normal[128 * g : 128 * g + 128] * mask_wide[:, 128 * g : 128 * g + 128]
+                    for g in (2 * h, 2 * h + 1)
+                ],
+                axis=1,
+            )
+            both = mm(masked, project).astype(BF)
+            k = 2 * a + h
+            at = slice(128 * k, 128 * k + 128)
+            right_scr[:, at] = both[:, 128:]
+            rightt_scr[at, :] = both[:, 128:].astype(F32).T.astype(BF)
+            left_scr[at, :] = both[:, :128].astype(F32).T
+    for q in range(8):
+        at = slice(128 * q, 128 * q + 128)
+        block = jnp.concatenate(
+            [left_scr[pl.ds(4 * q + c, 32, stride=32), :] for c in range(4)], axis=0
+        )
+        leftt_scr[at, :] = block.astype(BF)
+        left2_scr[:, at] = block.T.astype(BF)
+
+    bias = jnp.zeros((1, 128), F32)
+    ones = jnp.ones((128, 128), BF)
+    for p in range(8):
+        both_on = jnp.concatenate(
+            [mask_t[0:32] * mask_t[j : j + 1] for j in range(4 * p, 4 * p + 4)], axis=0
+        ).astype(BF)
+        counts = mm(both_on, ones)
+        scaled = pair_scr[4 * p : 4 * p + 4].reshape(128, 128) / (counts + 0.001)
+        bias = bias + jnp.sum(scaled, axis=0, keepdims=True)
+        scaled_scr[128 * p : 128 * p + 128, :] = scaled.astype(BF)
+    bias_out[...] = bias
+
+    for p in range(8):
+        at = slice(128 * p, 128 * p + 128)
+        grad = lax.dot_general(
+            final_ref[...], scaled_scr[at, :], (((1,), (1,)), ((), ())),
+            preferred_element_type=F32,
+        )
+        outer = mm(rightt_scr[at, :], left2_scr[...])
+        for q in range(8):
+            to = slice(128 * q, 128 * q + 128)
+            grad_scr[at, to] = swap_blocks(grad[to]).astype(BF)
+            outer_scr[to, at] = swap_blocks(outer[:, to]).astype(BF)
+    final_out[...] = mm(outer_scr[...], scaled_scr[...])
+    left_grad = mm(right_scr[...], grad_scr[...])
+    right_grad = mm(grad_scr[...], leftt_scr[...])
+
+    for q in range(8):
+        at = slice(128 * q, 128 * q + 128)
+        lin_scr[at, :] = (left_grad[:, at] * mask).astype(BF).astype(F32).T
+    for k in range(8):
+        rows = []
+        for t in range(4 * k, 4 * k + 4):
+            rows.append(right_grad[32 * t : 32 * t + 32] * mask_t[t : t + 1])
+        at = slice(128 * k, 128 * k + 128)
+        rin_scr[at, :] = jnp.concatenate(rows, axis=0).astype(BF)
+        linc_scr[at, :] = jnp.concatenate(
+            [lin_scr[pl.ds(t, 32, stride=32), :] for t in range(4 * k, 4 * k + 4)], axis=0
+        ).astype(BF)
+
+    total = jnp.zeros((128, 512), F32)
+    for g in range(16):
+        grads = jnp.concatenate(
+            [linc_scr[64 * g : 64 * g + 64, :], rin_scr[64 * g : 64 * g + 64, :]], axis=0
+        )
+        total = total + mm(grads, rhs_scr[128 * g : 128 * g + 128, :])
+    def fold(block):
+        return block[0:32, 0:64] + block[32:64, 64:128]
+    left_total, right_total = total[0:64], total[64:128]
+    first_out[...] = fold(left_total[:, 0:128]).T
+    second_out[...] = fold(right_total[:, 0:128]).T
+    left_normed = fold(left_total[:, 128:256] + left_total[:, 256:384])
+    right_normed = fold(right_total[:, 128:256] + right_total[:, 256:384])
+    left_sum = fold(left_total[:, 384:512])
+    right_sum = fold(right_total[:, 384:512])
+    first_t, second_t = first.T, second.T
+    gain_out[...] = jnp.sum(first_t * left_normed + second_t * right_normed, axis=0, keepdims=True)
+    offset_out[...] = jnp.sum(first_t * left_sum + second_t * right_sum, axis=0, keepdims=True)
+
+    back = project.astype(F32).T.astype(BF)
+    contract_rows = (((0,), (0,)), ((), ()))
+    for h in range(2):
+        at = slice(128 * h, 128 * h + 128)
+        d_normal = lax.dot_general(
+            linc_scr[at, :], back[:128], contract_rows, preferred_element_type=F32
+        ) + lax.dot_general(
+            rin_scr[at, :], back[128:], contract_rows, preferred_element_type=F32
+        )
+        for half in range(2):
+            g = 2 * h + half
+            d_hat = d_normal[0:32, 128 * half : 128 * half + 128] * gain
+            normed = normed_scr[128 * g : 128 * g + 32, :]
+            result = inverse_own[128 * g : 128 * g + 32] * (
+                d_hat
+                - group_mean(d_hat, averager)
+                - normed * group_mean(d_hat * normed, averager)
+            )
+            emb_out[:, 2 * g, :] = result[:, 0:64]
+            emb_out[:, 2 * g + 1, :] = result[:, 64:128]
+
+
+def vmem(count):
+    return [pl.BlockSpec(memory_space=pltpu.VMEM)] * count
+
+
+def gathered_body(
+    n_row,
+    n_col,
+    homolog_embedding,
+    presence_indicator,
+    coupling_change_derivative,
+    standardizer_scale,
+    standardizer_shift,
+    first_projection_matrix,
+    second_projection_matrix,
+    final_projection_matrix,
+):
+    packed = pl.pallas_call(
+        pack_kernel,
+        out_shape=jax.ShapeDtypeStruct((224, 128), BF),
+        in_specs=vmem(3),
+        out_specs=pl.BlockSpec(memory_space=pltpu.VMEM),
+    )(homolog_embedding, presence_indicator, coupling_change_derivative)
+
+    blocks = {(0, 0): packed}
+    for b in range(1, n_col):
+        blocks[0, b] = lax.ppermute(packed, "col", [(k, k ^ b) for k in range(n_col)])
+    step = n_row // 2
+    while step:
+        for (a, b), block in sorted(blocks.items()):
+            blocks[a ^ step, b] = lax.ppermute(block, "row", [(k, k ^ step) for k in range(n_row)])
+        step //= 2
+
+    place = lax.bitwise_xor(lax.axis_index("row"), lax.axis_index("col")).astype(jnp.int32)
+    shards, tokens, features = homolog_embedding.shape
+    width = first_projection_matrix.shape[1]
+    shape = lambda *dims: jax.ShapeDtypeStruct(dims, F32)
+    outs = pl.pallas_call(
+        functools.partial(part_kernel, n_row, n_col),
+        out_shape=(
+            shape(shards, tokens, features),
+            shape(width * width, 128),
+            shape(features, width),
+            shape(features, width),
+            shape(1, features),
+            shape(1, features),
+            shape(1, 128),
+        ),
+        in_specs=[pl.BlockSpec(memory_space=pltpu.SMEM)] + vmem(n_row * n_col + 5),
+        out_specs=tuple(vmem(7)),
+        scratch_shapes=[
+            pltpu.VMEM((32, 32, 128), F32),
+            pltpu.VMEM((2048, 128), F32),
+            pltpu.VMEM((2048, 512), BF),
+            pltpu.VMEM((1024, 128), F32),
+            pltpu.VMEM((1024, 128), BF),
+            pltpu.VMEM((128, 1024), BF),
+            pltpu.VMEM((128, 1024), BF),
+            pltpu.VMEM((1024, 128), BF),
+            pltpu.VMEM((1024, 128), BF),
+            pltpu.VMEM((1024, 1024), BF),
+            pltpu.VMEM((1024, 1024), BF),
+            pltpu.VMEM((1024, 128), F32),
+            pltpu.VMEM((1024, 128), BF),
+            pltpu.VMEM((1024, 128), BF),
+        ],
+        compiler_params=pltpu.CompilerParams(vmem_limit_bytes=48 * 1024 * 1024),
+    )(
+        place.reshape(1),
+        *[blocks[a, b] for a in range(n_row) for b in range(n_col)],
+        standardizer_scale.reshape(1, features),
+        standardizer_shift.reshape(1, features),
+        first_projection_matrix,
+        second_projection_matrix,
+        final_projection_matrix,
+    )
+    emb, final, first, second, gain, offset, bias = outs
+    return emb, final, first, second, gain.reshape(-1), offset.reshape(-1), bias.reshape(-1)
+
+
+def body(n_row, n_col, *arguments):
+    msa, _, pair = arguments[:3]
+    width = arguments[5].shape[1]
+    fits = (
+        n_row == 4
+        and n_col == 4
+        and msa.shape == (32, 8, 64)
+        and pair.shape == (8, 8, 128)
+        and width == 32
+    )
+    if fits:
+        return gathered_body(n_row, n_col, *arguments)
+    return sharded_body(*arguments)
+
+
 def solution(mesh):
     placed = (
         P(("grp", "col"), "row", None),
@@ -173,7 +487,7 @@
         P(),
     )
     return jax.shard_map(
-        body,
+        functools.partial(body, mesh.shape["row"], mesh.shape["col"]),
         mesh=mesh,
         in_specs=placed,
         out_specs=(

time: 187 us -> 34 us (0.18)
  blocking collectives: 97.8 us -> 0 us
  waiting for transfers between devices: 39.8 us -> 7.64 us
  between operations: 15.8 us -> 0.69 us
  Pallas kernels: 0 us -> 10.4 us
  local copies, waits for them, and re-layouts: 13.5 us -> 4.55 us
  matrix products: 4.84 us -> 0 us
  other arithmetic: 2.21 us -> 0 us
    psum x1 -> x0, blocking collectives: 60.9 us -> none  [body(): lax.psum((wout_acc, left_part, right_part, gain_part, beta_part, bias_par...]
    all_gather x4 -> x0, blocking collectives: 36.9 us -> none  [the longest x1 13.7 us: body(): lax.all_gather(left_flat, 'col', axis=0, tiled=True)]
    reduce_scatter x1 -> x0, waiting for transfers between devices: 19 us -> none  [body(): lax.psum_scatter(right_spread, 'row', scatter_dimension=1, tiled=True)]
    unnamed x4 -> x0, waiting for transfers between devices: 15.9 us -> none
    all_to_all x3 -> x0, starting transfers between devices: 12.2 us -> none  [the longest x1 5.37 us: body(): lax.all_to_all(mask_wide, 'col', split_axis=1, concat_axis=0, tiled=True)]
    ppermute x0 -> x15, starting transfers between devices: none -> 10.5 us  [the longest x12 6.09 us: gathered_body(): lax.ppermute(block, 'row', [(k, k ^ step) for k in range(n_row)])]
    pallas_call x0 -> x2, Pallas kernels: none -> 10.4 us  [the longest x1 8.74 us: gathered_body(): pl.pallas_call(functools.partial(part_kernel, n_row, n_col), out_shape=(s...]
    ppermute x0 -> x15, waiting for transfers between devices: none -> 7.64 us  [the longest x3 4.43 us: gathered_body(): lax.ppermute(packed, 'col', [(k, k ^ b) for k in range(n_col)])]
  transfers between devices with their start and end apart: 6 -> 15, of which waited for: 4 -> 6; matrix products, arithmetic and copies ran while one was open for 8% -> 1% of each run, Pallas kernels for 0% -> 0%
where the time goes in v1:
time: 34 us; the launch traced here: 33.7 us
  starting transfers between devices  10.5 us (31%)
  Pallas kernels  10.4 us (31%)
  waiting for transfers between devices  7.64 us (22%)
  local copies, waits for them, and re-layouts  4.55 us (13%)
  between operations  0.69 us (2%)
    pallas_call x1, Pallas kernels, gathered_body(): pl.pallas_call(functools.partial(part_kernel, n_row, n_col), out_shape=(s...  8.74 us
    ppermute x12, starting transfers between devices, gathered_body(): lax.ppermute(block, 'row', [(k, k ^ step) for k in range(n_row)])  6.09 us
    unnamed x17, local copies, waits for them, and re-layouts  4.55 us
    ppermute x3, waiting for transfers between devices, gathered_body(): lax.ppermute(packed, 'col', [(k, k ^ b) for k in range(n_col)])  4.43 us
    ppermute x3, starting transfers between devices, gathered_body(): lax.ppermute(packed, 'col', [(k, k ^ b) for k in range(n_col)])  4.39 us
    ppermute x12, waiting for transfers between devices, gathered_body(): lax.ppermute(block, 'row', [(k, k ^ step) for k in range(n_row)])  3.21 us
    pallas_call x1, Pallas kernels, gathered_body(): pl.pallas_call(pack_kernel, out_shape=jax.ShapeDtypeStruct((224, 128), BF...  1.63 us
  transfers between devices with their start and end apart: 15, of which 6 were waited for; matrix products, arithmetic and copies ran while one was open for 1% of the time, Pallas kernels for 0%

profile of v1, /device:TPU:0, one launch (start us, length us, event | category | flops | bytes accessed | tf_op | source)
XLA Modules:
  0.0 33.7 jit_solution(18442312365294125721)
XLA Ops:
  0.6 1.4 %copy.15.mask_ref = s32[32,8]{1,0:T(8,128)} copy(s32[32,8]{0,1:T(8,128)} %param.9) | data formatting | bytes 2048 | tf_op args[1]
  2.0 0.0 copy-start.4
  2.0 0.0 copy-start.5
  2.0 1.6 %shard_map.135.refs_0_ = bf16[224,128]{1,0:T(8,128)(2,1)} custom-call(bf16[32,8,64]{2,1,0:T(8,128)(2,1)} %msa_ref.1, s32[32,8]{1,0:T(8,128)} %copy.15.mask_ref, bf16[8,8,128]{2,1,0:T(8,128)(2,1)} %pair_ref.1), custom_call_target="tpu_custom_call" | custom-call | tf_op jit(solution)/shard_map/pallas_call | solution.py:400
  3.6 0.0 copy-start.1
  3.6 2.9 %collective-permute-start.7 = (bf16[224,128]{1,0:T(8,128)(2,1)}, bf16[224,128]{1,0:T(8,128)(2,1)S(1)}, u32[]{:S(2)}, u32[]{:S(2)}) collective-permute-start(bf16[224,128]{1,0:T(8,128)(2,1)} %shard_map.135.refs_0_), channel_id=1, source_target_pairs={{0,8},{4,12},{8,0},{12,4},{1,9},{5,13},{9,1},{13,5},{2,10},{6,14},... | collective-permute-start | bytes 172040 | tf_op jit(solution)/shard_map/ppermute | solution.py:413
  6.6 3.6 %collective-permute-start.2 = (bf16[224,128]{1,0:T(8,128)(2,1)}, bf16[224,128]{1,0:T(8,128)(2,1)S(1)}, u32[]{:S(2)}, u32[]{:S(2)}) collective-permute-start(bf16[224,128]{1,0:T(8,128)(2,1)} %shard_map.135.refs_0_), channel_id=1, source_target_pairs={{0,3},{1,2},{2,1},{3,0},{4,7},{5,6},{6,5},{7,4},{8,11},{9,10},{10,... | collective-permute-start | bytes 172040 | tf_op jit(solution)/shard_map/ppermute | solution.py:409
  10.2 0.0 collective-permute-start.3
  10.2 0.0 collective-permute-start.1
  10.2 0.8 %collective-permute-start = (bf16[224,128]{1,0:T(8,128)(2,1)}, bf16[224,128]{1,0:T(8,128)(2,1)S(1)}, u32[]{:S(2)}, u32[]{:S(2)}) collective-permute-start(bf16[224,128]{1,0:T(8,128)(2,1)} %shard_map.135.refs_0_), channel_id=1, source_target_pairs={{0,1},{1,0},{2,3},{3,2},{4,5},{5,4},{6,7},{7,6},{8,9},{9,8},{10,11... | collective-permute-start | bytes 172040 | tf_op jit(solution)/shard_map/ppermute | solution.py:409
  11.0 0.0 collective-permute-done.7.refs_8_
  11.0 0.0 collective-permute-start.11
  11.0 1.9 %collective-permute-done.2.refs_3_ = bf16[224,128]{1,0:T(8,128)(2,1)S(1)} collective-permute-done((bf16[224,128]{1,0:T(8,128)(2,1)}, bf16[224,128]{1,0:T(8,128)(2,1)S(1)}, u32[]{:S(2)}, u32[]{:S(2)}) %collective-permute-start.2) | collective-permute-done | bytes 57376 | tf_op jit(solution)/shard_map/ppermute | solution.py:409
  12.9 0.5 %collective-permute-start.10 = (bf16[224,128]{1,0:T(8,128)(2,1)S(1)}, bf16[224,128]{1,0:T(8,128)(2,1)S(1)}, u32[]{:S(2)}, u32[]{:S(2)}) collective-permute-start(bf16[224,128]{1,0:T(8,128)(2,1)S(1)} %collective-permute-done.2.refs_3_), channel_id=1, source_target_pairs={{0,8},{4,12},{8,0},{12,4},{1,9},{5,13},{9,1},{13,5},{2,10},{6,14},... | collective-permute-start | bytes 172040 | tf_op jit(solution)/shard_map/ppermute | solution.py:413
  13.4 0.0 collective-permute-done.3.refs_4_
  13.4 0.0 collective-permute-start.6
  13.4 2.5 %collective-permute-done.1.refs_2_ = bf16[224,128]{1,0:T(8,128)(2,1)S(1)} collective-permute-done((bf16[224,128]{1,0:T(8,128)(2,1)}, bf16[224,128]{1,0:T(8,128)(2,1)S(1)}, u32[]{:S(2)}, u32[]{:S(2)}) %collective-permute-start.1) | collective-permute-done | bytes 57376 | tf_op jit(solution)/shard_map/ppermute | solution.py:409
  15.9 0.5 %collective-permute-start.9 = (bf16[224,128]{1,0:T(8,128)(2,1)S(1)}, bf16[224,128]{1,0:T(8,128)(2,1)S(1)}, u32[]{:S(2)}, u32[]{:S(2)}) collective-permute-start(bf16[224,128]{1,0:T(8,128)(2,1)S(1)} %collective-permute-done.1.refs_2_), channel_id=1, source_target_pairs={{0,8},{4,12},{8,0},{12,4},{1,9},{5,13},{9,1},{13,5},{2,10},{6,14},... | collective-permute-start | bytes 172040 | tf_op jit(solution)/shard_map/ppermute | solution.py:413
  16.5 0.0 collective-permute-done.refs_1_
  16.5 1.5 %collective-permute-start.8 = (bf16[224,128]{1,0:T(8,128)(2,1)S(1)}, bf16[224,128]{1,0:T(8,128)(2,1)S(1)}, u32[]{:S(2)}, u32[]{:S(2)}) collective-permute-start(bf16[224,128]{1,0:T(8,128)(2,1)S(1)} %collective-permute-done.refs_1_), channel_id=1, source_target_pairs={{0,8},{4,12},{8,0},{12,4},{1,9},{5,13},{9,1},{13,5},{2,10},{6,14},... | collective-permute-start | bytes 172040 | tf_op jit(solution)/shard_map/ppermute | solution.py:413
  18.0 0.0 collective-permute-done.11.refs_12_
  18.0 0.0 collective-permute-start.5
  18.0 0.0 collective-permute-done.10.refs_11_
  18.0 0.5 %collective-permute-start.4 = (bf16[224,128]{1,0:T(8,128)(2,1)S(1)}, bf16[224,128]{1,0:T(8,128)(2,1)S(1)}, u32[]{:S(2)}, u32[]{:S(2)}) collective-permute-start(bf16[224,128]{1,0:T(8,128)(2,1)S(1)} %collective-permute-done.refs_1_), channel_id=1, source_target_pairs={{0,4},{4,0},{8,12},{12,8},{1,5},{5,1},{9,13},{13,9},{2,6},{6,2},{1... | collective-permute-start | bytes 172040 | tf_op jit(solution)/shard_map/ppermute | solution.py:413
  18.5 0.0 collective-permute-done.6.refs_7_
  18.5 0.1 collective-permute-start.14
  18.6 1.6 %collective-permute-done.9.refs_10_ = bf16[224,128]{1,0:T(8,128)(2,1)S(1)} collective-permute-done((bf16[224,128]{1,0:T(8,128)(2,1)S(1)}, bf16[224,128]{1,0:T(8,128)(2,1)S(1)}, u32[]{:S(2)}, u32[]{:S(2)}) %collective-permute-start.9) | collective-permute-done | bytes 57376 | tf_op jit(solution)/shard_map/ppermute | solution.py:413
  20.1 0.0 collective-permute-start.13
  20.1 0.6 %collective-permute-done.8.refs_9_ = bf16[224,128]{1,0:T(8,128)(2,1)S(1)} collective-permute-done((bf16[224,128]{1,0:T(8,128)(2,1)S(1)}, bf16[224,128]{1,0:T(8,128)(2,1)S(1)}, u32[]{:S(2)}, u32[]{:S(2)}) %collective-permute-start.8) | collective-permute-done | bytes 57376 | tf_op jit(solution)/shard_map/ppermute | solution.py:413
  20.8 0.0 collective-permute-start.12
  20.8 0.0 copy-done.4
  20.8 0.1 copy.16.refs_18_
  20.9 0.0 copy-done.5
  20.9 0.1 copy.17.refs_19_
  21.0 0.0 collective-permute-done.5.refs_6_
  21.0 0.0 collective-permute-done.4.refs_5_
  21.0 0.0 collective-permute-done.14.refs_15_
  21.0 0.4 %collective-permute-done.13.refs_14_ = bf16[224,128]{1,0:T(8,128)(2,1)S(1)} collective-permute-done((bf16[224,128]{1,0:T(8,128)(2,1)S(1)}, bf16[224,128]{1,0:T(8,128)(2,1)S(1)}, u32[]{:S(2)}, u32[]{:S(2)}) %collective-permute-start.13) | collective-permute-done | bytes 57376 | tf_op jit(solution)/shard_map/ppermute | solution.py:413
  21.4 0.6 %collective-permute-done.12.refs_13_ = bf16[224,128]{1,0:T(8,128)(2,1)S(1)} collective-permute-done((bf16[224,128]{1,0:T(8,128)(2,1)S(1)}, bf16[224,128]{1,0:T(8,128)(2,1)S(1)}, u32[]{:S(2)}, u32[]{:S(2)}) %collective-permute-start.12) | collective-permute-done | bytes 57376 | tf_op jit(solution)/shard_map/ppermute | solution.py:413
  22.0 0.0 copy-start.2
  22.0 0.0 copy-start.3
  22.0 0.0 copy-done.1
  22.0 0.6 %copy-done.2 = f32[64]{0:T(128)S(1)} copy-done((f32[64]{0:T(128)S(1)}, f32[64]{0:T(128)}, u32[]{:S(2)}) %copy-start.2) | copy-done | bytes 280
  22.7 0.0 copy-done.3
  22.7 0.9 %copy-done = bf16[1024,128]{1,0:T(8,128)(2,1)S(1)} copy-done((bf16[1024,128]{1,0:T(8,128)(2,1)S(1)}, bf16[1024,128]{1,0:T(8,128)(2,1)}, u32[]{:S(2)}) %copy-start) | copy-done | bytes 262168
  23.6 8.7 %shard_map.136 = (f32[32,8,64]{2,1,0:T(8,128)}, f32[1024,128]{1,0:T(8,128)}, f32[64,32]{1,0:T(8,128)S(1)}, f32[64,32]{1,0:T(8,128)S(1)}, f32[1,64]{1,0:T(1,128)}, /*index=5*/f32[1,64]{1,0:T(1,128)}, f32[1,128]{1,0:T(1,128)}) custom-call(s32[1]{0:T(128)} %bitcast.place_ref, bf16[224,128]{1,0:T(8,128)(2,1)S(1)} %copy-done.1, ...), custom_call_target="tpu_custom_call" | custom-call | tf_op jit(solution)/shard_map/pallas_call | solution.py:420
  32.4 0.7 %copy.18 = f32[64,32]{0,1:T(8,128)} copy(f32[64,32]{1,0:T(8,128)S(1)} %get-tuple-element.23) | data formatting | bytes 16384
  33.0 0.7 %copy.19 = f32[64,32]{0,1:T(8,128)} copy(f32[64,32]{1,0:T(8,128)S(1)} %get-tuple-element.24) | data formatting | bytes 16384
  (1 shorter events, 0.0 us)
Async XLA Ops:
  2.0 18.8 %copy-start.4 = (bf16[64,32]{0,1:T(8,128)(2,1)S(1)}, bf16[64,32]{0,1:T(8,128)(2,1)}, u32[]{:S(2)}) copy-start(bf16[64,32]{0,1:T(8,128)(2,1)} %param.13) | copy-start | bytes 12292
  2.0 18.9 %copy-start.5 = (bf16[64,32]{0,1:T(8,128)(2,1)S(1)}, bf16[64,32]{0,1:T(8,128)(2,1)}, u32[]{:S(2)}) copy-start(bf16[64,32]{0,1:T(8,128)(2,1)} %param.14) | copy-start | bytes 12292
  3.6 18.4 %copy-start.1 = (bf16[224,128]{1,0:T(8,128)(2,1)S(1)}, bf16[224,128]{1,0:T(8,128)(2,1)}, u32[]{:S(2)}) copy-start(bf16[224,128]{1,0:T(8,128)(2,1)} %shard_map.135.refs_0_) | copy-start | bytes 172036
  3.6 7.3 %collective-permute-start.7 = (bf16[224,128]{1,0:T(8,128)(2,1)}, bf16[224,128]{1,0:T(8,128)(2,1)S(1)}, u32[]{:S(2)}, u32[]{:S(2)}) collective-permute-start(bf16[224,128]{1,0:T(8,128)(2,1)} %shard_map.135.refs_0_), channel_id=1, source_target_pairs={{0,8},{4,12},{8,0},{12,4},{1,9},{5,13},{9,1},{13,5},{2,10},{6,14},... | collective-permute-start | bytes 172040 | tf_op jit(solution)/shard_map/ppermute | solution.py:413
  6.6 6.3 %collective-permute-start.2 = (bf16[224,128]{1,0:T(8,128)(2,1)}, bf16[224,128]{1,0:T(8,128)(2,1)S(1)}, u32[]{:S(2)}, u32[]{:S(2)}) collective-permute-start(bf16[224,128]{1,0:T(8,128)(2,1)} %shard_map.135.refs_0_), channel_id=1, source_target_pairs={{0,3},{1,2},{2,1},{3,0},{4,7},{5,6},{6,5},{7,4},{8,11},{9,10},{10,... | collective-permute-start | bytes 172040 | tf_op jit(solution)/shard_map/ppermute | solution.py:409
  10.2 3.2 %collective-permute-start.3 = (bf16[224,128]{1,0:T(8,128)(2,1)}, bf16[224,128]{1,0:T(8,128)(2,1)S(1)}, u32[]{:S(2)}, u32[]{:S(2)}) collective-permute-start(bf16[224,128]{1,0:T(8,128)(2,1)} %shard_map.135.refs_0_), channel_id=1, source_target_pairs={{0,4},{4,0},{8,12},{12,8},{1,5},{5,1},{9,13},{13,9},{2,6},{6,2},{1... | collective-permute-start | bytes 172040 | tf_op jit(solution)/shard_map/ppermute | solution.py:413
  10.2 5.8 %collective-permute-start.1 = (bf16[224,128]{1,0:T(8,128)(2,1)}, bf16[224,128]{1,0:T(8,128)(2,1)S(1)}, u32[]{:S(2)}, u32[]{:S(2)}) collective-permute-start(bf16[224,128]{1,0:T(8,128)(2,1)} %shard_map.135.refs_0_), channel_id=1, source_target_pairs={{0,2},{1,3},{2,0},{3,1},{4,6},{5,7},{6,4},{7,5},{8,10},{9,11},{10,... | collective-permute-start | bytes 172040 | tf_op jit(solution)/shard_map/ppermute | solution.py:409
  10.2 6.3 %collective-permute-start = (bf16[224,128]{1,0:T(8,128)(2,1)}, bf16[224,128]{1,0:T(8,128)(2,1)S(1)}, u32[]{:S(2)}, u32[]{:S(2)}) collective-permute-start(bf16[224,128]{1,0:T(8,128)(2,1)} %shard_map.135.refs_0_), channel_id=1, source_target_pairs={{0,1},{1,0},{2,3},{3,2},{4,5},{5,4},{6,7},{7,6},{8,9},{9,8},{10,11... | collective-permute-start | bytes 172040 | tf_op jit(solution)/shard_map/ppermute | solution.py:409
  11.0 7.0 %collective-permute-start.11 = (bf16[224,128]{1,0:T(8,128)(2,1)S(1)}, bf16[224,128]{1,0:T(8,128)(2,1)S(1)}, u32[]{:S(2)}, u32[]{:S(2)}) collective-permute-start(bf16[224,128]{1,0:T(8,128)(2,1)S(1)} %collective-permute-done.7.refs_8_), channel_id=1, source_target_pairs={{0,4},{4,0},{8,12},{12,8},{1,5},{5,1},{9,13},{13,9},{2,6},{6,2},{1... | collective-permute-start | bytes 172040 | tf_op jit(solution)/shard_map/ppermute | solution.py:413
  12.9 5.1 %collective-permute-start.10 = (bf16[224,128]{1,0:T(8,128)(2,1)S(1)}, bf16[224,128]{1,0:T(8,128)(2,1)S(1)}, u32[]{:S(2)}, u32[]{:S(2)}) collective-permute-start(bf16[224,128]{1,0:T(8,128)(2,1)S(1)} %collective-permute-done.2.refs_3_), channel_id=1, source_target_pairs={{0,8},{4,12},{8,0},{12,4},{1,9},{5,13},{9,1},{13,5},{2,10},{6,14},... | collective-permute-start | bytes 172040 | tf_op jit(solution)/shard_map/ppermute | solution.py:413
  13.4 5.1 %collective-permute-start.6 = (bf16[224,128]{1,0:T(8,128)(2,1)S(1)}, bf16[224,128]{1,0:T(8,128)(2,1)S(1)}, u32[]{:S(2)}, u32[]{:S(2)}) collective-permute-start(bf16[224,128]{1,0:T(8,128)(2,1)S(1)} %collective-permute-done.2.refs_3_), channel_id=1, source_target_pairs={{0,4},{4,0},{8,12},{12,8},{1,5},{5,1},{9,13},{13,9},{2,6},{6,2},{1... | collective-permute-start | bytes 172040 | tf_op jit(solution)/shard_map/ppermute | solution.py:413
  15.9 4.2 %collective-permute-start.9 = (bf16[224,128]{1,0:T(8,128)(2,1)S(1)}, bf16[224,128]{1,0:T(8,128)(2,1)S(1)}, u32[]{:S(2)}, u32[]{:S(2)}) collective-permute-start(bf16[224,128]{1,0:T(8,128)(2,1)S(1)} %collective-permute-done.1.refs_2_), channel_id=1, source_target_pairs={{0,8},{4,12},{8,0},{12,4},{1,9},{5,13},{9,1},{13,5},{2,10},{6,14},... | collective-permute-start | bytes 172040 | tf_op jit(solution)/shard_map/ppermute | solution.py:413
  16.5 4.3 %collective-permute-start.8 = (bf16[224,128]{1,0:T(8,128)(2,1)S(1)}, bf16[224,128]{1,0:T(8,128)(2,1)S(1)}, u32[]{:S(2)}, u32[]{:S(2)}) collective-permute-start(bf16[224,128]{1,0:T(8,128)(2,1)S(1)} %collective-permute-done.refs_1_), channel_id=1, source_target_pairs={{0,8},{4,12},{8,0},{12,4},{1,9},{5,13},{9,1},{13,5},{2,10},{6,14},... | collective-permute-start | bytes 172040 | tf_op jit(solution)/shard_map/ppermute | solution.py:413
  18.0 3.0 %collective-permute-start.5 = (bf16[224,128]{1,0:T(8,128)(2,1)S(1)}, bf16[224,128]{1,0:T(8,128)(2,1)S(1)}, u32[]{:S(2)}, u32[]{:S(2)}) collective-permute-start(bf16[224,128]{1,0:T(8,128)(2,1)S(1)} %collective-permute-done.1.refs_2_), channel_id=1, source_target_pairs={{0,4},{4,0},{8,12},{12,8},{1,5},{5,1},{9,13},{13,9},{2,6},{6,2},{1... | collective-permute-start | bytes 172040 | tf_op jit(solution)/shard_map/ppermute | solution.py:413
  18.0 3.0 %collective-permute-start.4 = (bf16[224,128]{1,0:T(8,128)(2,1)S(1)}, bf16[224,128]{1,0:T(8,128)(2,1)S(1)}, u32[]{:S(2)}, u32[]{:S(2)}) collective-permute-start(bf16[224,128]{1,0:T(8,128)(2,1)S(1)} %collective-permute-done.refs_1_), channel_id=1, source_target_pairs={{0,4},{4,0},{8,12},{12,8},{1,5},{5,1},{9,13},{13,9},{2,6},{6,2},{1... | collective-permute-start | bytes 172040 | tf_op jit(solution)/shard_map/ppermute | solution.py:413
  18.5 2.5 %collective-permute-start.14 = (bf16[224,128]{1,0:T(8,128)(2,1)S(1)}, bf16[224,128]{1,0:T(8,128)(2,1)S(1)}, u32[]{:S(2)}, u32[]{:S(2)}) collective-permute-start(bf16[224,128]{1,0:T(8,128)(2,1)S(1)} %collective-permute-done.10.refs_11_), channel_id=1, source_target_pairs={{0,4},{4,0},{8,12},{12,8},{1,5},{5,1},{9,13},{13,9},{2,6},{6,2},{1... | collective-permute-start | bytes 172040 | tf_op jit(solution)/shard_map/ppermute | solution.py:413
  20.1 1.2 %collective-permute-start.13 = (bf16[224,128]{1,0:T(8,128)(2,1)S(1)}, bf16[224,128]{1,0:T(8,128)(2,1)S(1)}, u32[]{:S(2)}, u32[]{:S(2)}) collective-permute-start(bf16[224,128]{1,0:T(8,128)(2,1)S(1)} %collective-permute-done.9.refs_10_), channel_id=1, source_target_pairs={{0,4},{4,0},{8,12},{12,8},{1,5},{5,1},{9,13},{13,9},{2,6},{6,2},{1... | collective-permute-start | bytes 172040 | tf_op jit(solution)/shard_map/ppermute | solution.py:413
  20.8 1.2 %collective-permute-start.12 = (bf16[224,128]{1,0:T(8,128)(2,1)S(1)}, bf16[224,128]{1,0:T(8,128)(2,1)S(1)}, u32[]{:S(2)}, u32[]{:S(2)}) collective-permute-start(bf16[224,128]{1,0:T(8,128)(2,1)S(1)} %collective-permute-done.8.refs_9_), channel_id=1, source_target_pairs={{0,4},{4,0},{8,12},{12,8},{1,5},{5,1},{9,13},{13,9},{2,6},{6,2},{1... | collective-permute-start | bytes 172040 | tf_op jit(solution)/shard_map/ppermute | solution.py:413
  22.0 0.7 %copy-start.2 = (f32[64]{0:T(128)S(1)}, f32[64]{0:T(128)}, u32[]{:S(2)}) copy-start(f32[64]{0:T(128)} %param.11) | copy-start | bytes 772
  22.0 0.7 %copy-start.3 = (f32[64]{0:T(128)S(1)}, f32[64]{0:T(128)}, u32[]{:S(2)}) copy-start(f32[64]{0:T(128)} %param.12) | copy-start | bytes 772
  22.7 0.9 %copy-start = (bf16[1024,128]{1,0:T(8,128)(2,1)S(1)}, bf16[1024,128]{1,0:T(8,128)(2,1)}, u32[]{:S(2)}) copy-start(bf16[1024,128]{1,0:T(8,128)(2,1)} %refs_20_.1) | copy-start | bytes 786436

commit v2 on v1

--- a/solution.py
+++ b/solution.py
@@ -175,18 +175,16 @@
     return rule(r, c)
 
 
-def two_terms(value):
-    high = value.astype(BF)
-    return high, (value - high.astype(F32)).astype(BF)
-
-
 def mm(a, b):
     return jnp.dot(a, b, preferred_element_type=F32)
 
 
-def group_mean(value, averager):
-    high, low = two_terms(value)
-    return mm(high, averager) + mm(low, averager)
+def mm_nt(a, b):
+    return lax.dot_general(a, b, (((1,), (1,)), ((), ())), preferred_element_type=F32)
+
+
+def mm_tn(a, b):
+    return lax.dot_general(a, b, (((0,), (0,)), ((), ())), preferred_element_type=F32)
 
 
 def swap_blocks(block):
@@ -205,100 +203,103 @@
     return jnp.concatenate(piece, axis=0)
 
 
+ABSENT = 1024.0
+
+
 def pack_kernel(msa_ref, mask_ref, pair_ref, out_ref):
     msa = msa_ref[...].astype(F32)
+    pick = spread(8, 512, lambda r, c: jnp.where(c // 64 == r, 1.0, 0.0)).astype(BF)
+    present = mm_tn(mask_ref[...].astype(F32).astype(BF), pick) > 0.5
     for g in range(4):
-        out_ref[32 * g : 32 * g + 32, :] = jnp.concatenate(
-            [msa[:, 2 * g, :], msa[:, 2 * g + 1, :]], axis=1
+        rows = jnp.concatenate([msa[:, 2 * g, :], msa[:, 2 * g + 1, :]], axis=1)
+        out_ref[32 * g : 32 * g + 32, :] = jnp.where(
+            present[:, 128 * g : 128 * g + 128], rows, ABSENT
         ).astype(BF)
     pair = pair_ref[...].astype(F32)
     for j in range(0, 8, 2):
         out_ref[128 + 8 * j : 144 + 8 * j, :] = jnp.concatenate(
             [pair[:, j, :], pair[:, j + 1, :]], axis=0
         ).astype(BF)
-    mask = mask_ref[...].astype(F32).astype(BF)
-    pick = spread(8, 128, lambda r, c: (c % 8 == r).astype(F32)).astype(BF)
-    out_ref[192:224, :] = mm(mask, pick).astype(BF)
+
+
+def weights_kernel(gain_ref, offset_ref, first_ref, second_ref, norm_out, back_out):
+    norm_out[...] = jnp.concatenate(
+        [
+            jnp.concatenate([ref[...]] * 2, axis=1)
+            for ref in (gain_ref, offset_ref, gain_ref, offset_ref) * 2
+        ],
+        axis=0,
+    )
+    for k, ref in enumerate((first_ref, second_ref)):
+        wide = jnp.concatenate([ref[...].astype(F32)] * 4, axis=1)
+        wide = jnp.concatenate([wide] * 4, axis=0)
+        own = spread(128, 256, lambda r, c: r // 32 == c // 64)
+        back_out[128 * k : 128 * k + 128, :] = jnp.where(own, wide, 0.0).astype(BF)
 
 
 def part_kernel(n_row, n_col, place_ref, *refs):
-    blocks = [[refs[a * n_col + b] for b in range(n_col)] for a in range(n_row)]
+    sets = refs[:n_row]
     (
-        gain_ref, offset_ref, first_ref, second_ref, final_ref,
-        emb_out, final_out, first_out, second_out, gain_out, offset_out, bias_out,
-        pair_scr, normed_scr, rhs_scr, left_scr, leftt_scr, left2_scr, right_scr, rightt_scr,
+        norm_ref, back_ref, first_ref, second_ref, final_hbm,
+        emb_out, final_hbm_out, first_out, second_out, gain_out, offset_out, bias_out,
+        pair_scr, normed_scr, rhs_scr, left_scr, leftt_scr, right_scr, rightt_scr,
         scaled_scr, grad_scr, outer_scr, lin_scr, linc_scr, rin_scr,
-    ) = refs[n_row * n_col :]
+        final_ref, final_out, in_sem, out_sem,
+    ) = refs[n_row:]
+    final_in = pltpu.make_async_copy(final_hbm, final_ref, in_sem)
+    final_in.start()
     place = place_ref[0]
 
     for a in range(n_row):
         for b in range(n_col):
             at = lax.bitwise_xor(place, b) * 8
             pair_scr[pl.ds(at, 8), 8 * a : 8 * a + 8, :] = (
-                blocks[a][b][128:192, :].astype(F32).reshape(8, 8, 128)
+                sets[a][b, 128:192, :].astype(F32).reshape(8, 8, 128)
             )
 
-    mask_rows = [
-        jnp.concatenate([blocks[a][b][192:224, :] for b in range(n_col)], axis=0)
-        for a in range(n_row)
-    ]
-    token_of = lax.broadcasted_iota(jnp.int32, (128, 128), 1) // 8 % 4
-    mask = jnp.zeros((128, 128), F32)
-    for a in range(n_row):
-        mask = jnp.where(token_of == a, mask_rows[a].astype(F32), mask)
-    mask_t = mask.T
-
-    gain = jnp.concatenate([gain_ref[...], gain_ref[...]], axis=1)
-    offset = jnp.concatenate([offset_ref[...], offset_ref[...]], axis=1)
+    gain = norm_ref[0:1, :]
+    offset = norm_ref[1:2, :]
     averager = spread(128, 128, lambda r, c: jnp.where(r // 64 == c // 64, 1.0 / 64, 0.0)).astype(BF)
-    first = first_ref[...].astype(F32)
-    second = second_ref[...].astype(F32)
-    wide = jnp.concatenate([first] * 4 + [second] * 4, axis=1)
-    wide = jnp.concatenate([wide] * 4, axis=0)
-    project = jnp.where(
-        spread(256, 256, lambda r, c: r // 64 == c % 128 // 32), wide, 0.0
-    ).astype(BF)
-    chooser = spread(128, 512, lambda r, c: jnp.where(r == c // 64, 1.0, 0.0)).astype(BF)
+    lane = lax.broadcasted_iota(jnp.int32, (128, 128), 1)
     inverse_own = None
+    found = jnp.zeros((128, 128), F32)
     for a in range(n_row):
         x = jnp.concatenate(
-            [blocks[a][b][32 * g : 32 * g + 32, :] for g in range(4) for b in range(n_col)], axis=0
-        )
-        varied = x.astype(F32) - mm(x, averager)
-        inverse = lax.rsqrt(group_mean(varied * varied, averager) + 1e-05)
+            [sets[a][b, 32 * g : 32 * g + 32, :] for g in range(4) for b in range(n_col)], axis=0
+        )
+        mean = mm(x, averager)
+        present = mean < ABSENT / 2
+        varied = x.astype(F32) - mean
+        inverse = lax.rsqrt(mm((varied * varied).astype(BF), averager) + 1e-05)
         normed = varied * inverse
         if a == 0:
             inverse_own = inverse
+            normed_scr[...] = normed
         rows = slice(512 * a, 512 * a + 512)
-        normed_scr[rows, :] = normed
-        normal = (normed * gain + offset).astype(BF)
-        high, low = two_terms(normed)
+        normal = jnp.where(present, normed * gain + offset, 0.0).astype(BF)
         rhs_scr[rows, 0:128] = normal
-        rhs_scr[rows, 128:256] = high
-        rhs_scr[rows, 256:384] = low
-        rhs_scr[rows, 384:512] = jnp.ones((512, 128), BF)
-        mask_wide = mm(mask_rows[a], chooser).astype(BF)
+        rhs_scr[rows, 128:256] = normed.astype(BF)
+        here = jnp.where(present, 1.0, 0.0)
+        for g in range(4):
+            found = jnp.where(lane % 32 // 2 == 4 * a + g, here[128 * g : 128 * g + 128], found)
         for h in range(2):
             masked = jnp.concatenate(
-                [
-                    normal[128 * g : 128 * g + 128] * mask_wide[:, 128 * g : 128 * g + 128]
-                    for g in (2 * h, 2 * h + 1)
-                ],
-                axis=1,
+                [normal[128 * g : 128 * g + 128] for g in (2 * h, 2 * h + 1)], axis=1
             )
-            both = mm(masked, project).astype(BF)
             k = 2 * a + h
             at = slice(128 * k, 128 * k + 128)
-            right_scr[:, at] = both[:, 128:]
-            rightt_scr[at, :] = both[:, 128:].astype(F32).T.astype(BF)
-            left_scr[at, :] = both[:, :128].astype(F32).T
+            right_scr[:, at] = mm_nt(masked, back_ref[128:, :]).astype(BF)
+            both = mm_nt(back_ref[...], masked)
+            rightt_scr[at, :] = both[128:].astype(BF)
+            left_scr[at, :] = both[:128]
     for q in range(8):
-        at = slice(128 * q, 128 * q + 128)
-        block = jnp.concatenate(
+        leftt_scr[128 * q : 128 * q + 128, :] = jnp.concatenate(
             [left_scr[pl.ds(4 * q + c, 32, stride=32), :] for c in range(4)], axis=0
-        )
-        leftt_scr[at, :] = block.astype(BF)
-        left2_scr[:, at] = block.T.astype(BF)
+        ).astype(BF)
+
+    turned = pltpu.roll(found, 64, 1)
+    mask = jnp.where((lane % 2 == 0) == (lane < 64), found, turned)
+    mask_t = mask.T
 
     bias = jnp.zeros((1, 128), F32)
     ones = jnp.ones((128, 128), BF)
@@ -312,24 +313,32 @@
         scaled_scr[128 * p : 128 * p + 128, :] = scaled.astype(BF)
     bias_out[...] = bias
 
-    for p in range(8):
-        at = slice(128 * p, 128 * p + 128)
-        grad = lax.dot_general(
-            final_ref[...], scaled_scr[at, :], (((1,), (1,)), ((), ())),
-            preferred_element_type=F32,
-        )
-        outer = mm(rightt_scr[at, :], left2_scr[...])
+    for n in range(4):
+        outer = mm_nt(rightt_scr[...], leftt_scr[256 * n : 256 * n + 256, :]).astype(BF)
+        for p in range(8):
+            for q in range(2):
+                outer_scr[256 * n + 128 * q : 256 * n + 128 * q + 128, 128 * p : 128 * p + 128] = (
+                    swap_blocks(outer[128 * p : 128 * p + 128, 128 * q : 128 * q + 128])
+                )
+    final_out[...] = mm(outer_scr[...], scaled_scr[...])
+    final_send = pltpu.make_async_copy(final_out, final_hbm_out, out_sem)
+    final_send.start()
+
+    final_in.wait()
+    for n in range(4):
+        grad = mm_nt(final_ref[...], scaled_scr[256 * n : 256 * n + 256, :]).astype(BF)
         for q in range(8):
-            to = slice(128 * q, 128 * q + 128)
-            grad_scr[at, to] = swap_blocks(grad[to]).astype(BF)
-            outer_scr[to, at] = swap_blocks(outer[:, to]).astype(BF)
-    final_out[...] = mm(outer_scr[...], scaled_scr[...])
+            for p in range(2):
+                grad_scr[256 * n + 128 * p : 256 * n + 128 * p + 128, 128 * q : 128 * q + 128] = (
+                    swap_blocks(grad[128 * q : 128 * q + 128, 128 * p : 128 * p + 128])
+                )
     left_grad = mm(right_scr[...], grad_scr[...])
     right_grad = mm(grad_scr[...], leftt_scr[...])
 
+    identity = spread(128, 128, lambda r, c: jnp.where(r == c, 1.0, 0.0)).astype(BF)
     for q in range(8):
         at = slice(128 * q, 128 * q + 128)
-        lin_scr[at, :] = (left_grad[:, at] * mask).astype(BF).astype(F32).T
+        lin_scr[at, :] = mm_nt(identity, (left_grad[:, at] * mask).astype(BF))
     for k in range(8):
         rows = []
         for t in range(4 * k, 4 * k + 4):
@@ -340,45 +349,46 @@
             [lin_scr[pl.ds(t, 32, stride=32), :] for t in range(4 * k, 4 * k + 4)], axis=0
         ).astype(BF)
 
-    total = jnp.zeros((128, 512), F32)
+    total = jnp.zeros((128, 256), F32)
+    sums = jnp.zeros((128, 128), F32)
     for g in range(16):
         grads = jnp.concatenate(
             [linc_scr[64 * g : 64 * g + 64, :], rin_scr[64 * g : 64 * g + 64, :]], axis=0
         )
+        sums = sums + grads.astype(F32)
         total = total + mm(grads, rhs_scr[128 * g : 128 * g + 128, :])
+
     def fold(block):
         return block[0:32, 0:64] + block[32:64, 64:128]
-    left_total, right_total = total[0:64], total[64:128]
-    first_out[...] = fold(left_total[:, 0:128]).T
-    second_out[...] = fold(right_total[:, 0:128]).T
-    left_normed = fold(left_total[:, 128:256] + left_total[:, 256:384])
-    right_normed = fold(right_total[:, 128:256] + right_total[:, 256:384])
-    left_sum = fold(left_total[:, 384:512])
-    right_sum = fold(right_total[:, 384:512])
-    first_t, second_t = first.T, second.T
-    gain_out[...] = jnp.sum(first_t * left_normed + second_t * right_normed, axis=0, keepdims=True)
-    offset_out[...] = jnp.sum(first_t * left_sum + second_t * right_sum, axis=0, keepdims=True)
-
-    back = project.astype(F32).T.astype(BF)
-    contract_rows = (((0,), (0,)), ((), ()))
+
+    first_out[...] = fold(total[0:64, 0:128])
+    second_out[...] = fold(total[64:128, 0:128])
+    sums = jnp.sum(sums, axis=1, keepdims=True)
+    left_sum = sums[0:32] + sums[32:64]
+    right_sum = sums[64:96] + sums[96:128]
+    first = first_ref[...].astype(F32)
+    second = second_ref[...].astype(F32)
+    gain_out[...] = jnp.sum(
+        first * fold(total[0:64, 128:256]) + second * fold(total[64:128, 128:256]),
+        axis=0, keepdims=True,
+    )
+    offset_out[...] = jnp.sum(first * left_sum + second * right_sum, axis=0, keepdims=True)
+
     for h in range(2):
         at = slice(128 * h, 128 * h + 128)
-        d_normal = lax.dot_general(
-            linc_scr[at, :], back[:128], contract_rows, preferred_element_type=F32
-        ) + lax.dot_general(
-            rin_scr[at, :], back[128:], contract_rows, preferred_element_type=F32
-        )
+        d_normal = mm_tn(linc_scr[at, :], back_ref[:128, :]) + mm_tn(rin_scr[at, :], back_ref[128:, :])
         for half in range(2):
             g = 2 * h + half
             d_hat = d_normal[0:32, 128 * half : 128 * half + 128] * gain
             normed = normed_scr[128 * g : 128 * g + 32, :]
             result = inverse_own[128 * g : 128 * g + 32] * (
                 d_hat
-                - group_mean(d_hat, averager)
-                - normed * group_mean(d_hat * normed, averager)
+                - mm(d_hat.astype(BF), averager)
+                - normed * mm((d_hat * normed).astype(BF), averager)
             )
             emb_out[:, 2 * g, :] = result[:, 0:64]
             emb_out[:, 2 * g + 1, :] = result[:, 64:128]
+    final_send.wait()
 
 
 def vmem(count):
@@ -397,46 +407,58 @@
     second_projection_matrix,
     final_projection_matrix,
 ):
-    packed = pl.pallas_call(
-        pack_kernel,
-        out_shape=jax.ShapeDtypeStruct((224, 128), BF),
-        in_specs=vmem(3),
-        out_specs=pl.BlockSpec(memory_space=pltpu.VMEM),
-    )(homolog_embedding, presence_indicator, coupling_change_derivative)
-
-    blocks = {(0, 0): packed}
-    for b in range(1, n_col):
-        blocks[0, b] = lax.ppermute(packed, "col", [(k, k ^ b) for k in range(n_col)])
-    step = n_row // 2
-    while step:
-        for (a, b), block in sorted(blocks.items()):
-            blocks[a ^ step, b] = lax.ppermute(block, "row", [(k, k ^ step) for k in range(n_row)])
-        step //= 2
-
-    place = lax.bitwise_xor(lax.axis_index("row"), lax.axis_index("col")).astype(jnp.int32)
     shards, tokens, features = homolog_embedding.shape
     width = first_projection_matrix.shape[1]
     shape = lambda *dims: jax.ShapeDtypeStruct(dims, F32)
+    packed = pl.pallas_call(
+        pack_kernel,
+        out_shape=jax.ShapeDtypeStruct((192, 128), BF),
+        in_specs=vmem(3),
+        out_specs=vmem(1)[0],
+    )(homolog_embedding, presence_indicator.T, coupling_change_derivative)
+    norm, back = pl.pallas_call(
+        weights_kernel,
+        out_shape=(shape(8, 128), jax.ShapeDtypeStruct((256, 256), BF)),
+        in_specs=vmem(4),
+        out_specs=tuple(vmem(2)),
+    )(
+        standardizer_scale.reshape(1, features),
+        standardizer_shift.reshape(1, features),
+        first_projection_matrix.T,
+        second_projection_matrix.T,
+    )
+
+    pieces = [packed] + [
+        lax.ppermute(packed, "col", [(k, k ^ b) for k in range(n_col)]) for b in range(1, n_col)
+    ]
+    sets = {0: jnp.stack(pieces)}
+    step = n_row // 2
+    while step:
+        for a, held in sorted(sets.items()):
+            sets[a ^ step] = lax.ppermute(held, "row", [(k, k ^ step) for k in range(n_row)])
+        step //= 2
+
+    place = lax.bitwise_xor(lax.axis_index("row"), lax.axis_index("col")).astype(jnp.int32)
+    hbm = pl.BlockSpec(memory_space=pltpu.HBM)
     outs = pl.pallas_call(
         functools.partial(part_kernel, n_row, n_col),
         out_shape=(
             shape(shards, tokens, features),
             shape(width * width, 128),
-            shape(features, width),
-            shape(features, width),
+            shape(width, features),
+            shape(width, features),
             shape(1, features),
             shape(1, features),
             shape(1, 128),
         ),
-        in_specs=[pl.BlockSpec(memory_space=pltpu.SMEM)] + vmem(n_row * n_col + 5),
-        out_specs=tuple(vmem(7)),
+        in_specs=[pl.BlockSpec(memory_space=pltpu.SMEM)] + vmem(n_row + 4) + [hbm],
+        out_specs=(*vmem(1), hbm, *vmem(5)),
         scratch_shapes=[
             pltpu.VMEM((32, 32, 128), F32),
-            pltpu.VMEM((2048, 128), F32),
-            pltpu.VMEM((2048, 512), BF),
+            pltpu.VMEM((512, 128), F32),
+            pltpu.VMEM((2048, 256), BF),
             pltpu.VMEM((1024, 128), F32),
             pltpu.VMEM((1024, 128), BF),
-            pltpu.VMEM((128, 1024), BF),
             pltpu.VMEM((128, 1024), BF),
             pltpu.VMEM((1024, 128), BF),
             pltpu.VMEM((1024, 128), BF),
@@ -445,19 +467,23 @@
             pltpu.VMEM((1024, 128), F32),
             pltpu.VMEM((1024, 128), BF),
             pltpu.VMEM((1024, 128), BF),
+            pltpu.VMEM((1024, 128), BF),
+            pltpu.VMEM((1024, 128), F32),
+            pltpu.SemaphoreType.DMA,
+            pltpu.SemaphoreType.DMA,
         ],
         compiler_params=pltpu.CompilerParams(vmem_limit_bytes=48 * 1024 * 1024),
     )(
         place.reshape(1),
-        *[blocks[a, b] for a in range(n_row) for b in range(n_col)],
-        standardizer_scale.reshape(1, features),
-        standardizer_shift.reshape(1, features),
-        first_projection_matrix,
-        second_projection_matrix,
+        *[sets[a] for a in range(n_row)],
+        norm,
+        back,
+        first_projection_matrix.T,
+        second_projection_matrix.T,
         final_projection_matrix,
     )
     emb, final, first, second, gain, offset, bias = outs
-    return emb, final, first, second, gain.reshape(-1), offset.reshape(-1), bias.reshape(-1)
+    return emb, final, first.T, second.T, gain.reshape(-1), offset.reshape(-1), bias.reshape(-1)
 
 
 def body(n_row, n_col, *arguments):

time: 34 us -> 32.2 us (0.947)
  starting transfers between devices: 10.5 us -> 7.18 us
  local copies, waits for them, and re-layouts: 4.55 us -> 1.56 us
  Pallas kernels: 10.4 us -> 12.8 us
  waiting for transfers between devices: 7.64 us -> 8.9 us
  other arithmetic: 0 us -> 0.83 us
    ppermute x12 -> x3, starting transfers between devices: 6.09 us -> 1.56 us  [gathered_body(): lax.ppermute(held, 'row', [(k, k ^ step) for k in range(n_row)])]
    unnamed x17 -> x10, local copies, waits for them, and re-layouts: 4.55 us -> 1.56 us
    pallas_call x1 -> x2, Pallas kernels: 1.63 us -> 3.22 us  [the longest x1 1.7 us: gathered_body(): pl.pallas_call(pack_kernel, out_shape=jax.ShapeDtypeStruct((192, 128), BF...]
    ppermute x3, starting transfers between devices: 4.39 us -> 5.62 us  [gathered_body(): lax.ppermute(packed, 'col', [(k, k ^ b) for k in range(n_col)])]
    ppermute x12 -> x3, waiting for transfers between devices: 3.21 us -> 4.26 us  [gathered_body(): lax.ppermute(held, 'row', [(k, k ^ step) for k in range(n_row)])]
    another operation x0 -> x1, other arithmetic: none -> 0.83 us  [gathered_body(): sets = {0: jnp.stack(pieces)}]
    pallas_call x1, Pallas kernels: 8.74 us -> 9.53 us  [gathered_body(): pl.pallas_call(functools.partial(part_kernel, n_row, n_col), out_shape=(s...]
  transfers between devices with their start and end apart: 15 -> 6, of which waited for: 6 -> 3; matrix products, arithmetic and copies ran while one was open for 1% -> 0% of each run, Pallas kernels for 0% -> 5%
where the time goes in v2:
time: 32.2 us; the launch traced here: 31.9 us
  Pallas kernels  12.8 us (40%)
  waiting for transfers between devices  8.9 us (28%)
  starting transfers between devices  7.18 us (22%)
  local copies, waits for them, and re-layouts  1.56 us (5%)
  other arithmetic  0.83 us (3%)
  between operations  0.68 us (2%)
    pallas_call x1, Pallas kernels, gathered_body(): pl.pallas_call(functools.partial(part_kernel, n_row, n_col), out_shape=(s...  9.53 us
    ppermute x3, starting transfers between devices, gathered_body(): lax.ppermute(packed, 'col', [(k, k ^ b) for k in range(n_col)])  5.62 us
    ppermute x3, waiting for transfers between devices, gathered_body(): lax.ppermute(packed, 'col', [(k, k ^ b) for k in range(n_col)])  4.63 us
    ppermute x3, waiting for transfers between devices, gathered_body(): lax.ppermute(held, 'row', [(k, k ^ step) for k in range(n_row)])  4.26 us
    pallas_call x1, Pallas kernels, gathered_body(): pl.pallas_call(pack_kernel, out_shape=jax.ShapeDtypeStruct((192, 128), BF...  1.7 us
    unnamed x10, local copies, waits for them, and re-layouts  1.56 us
    ppermute x3, starting transfers between devices, gathered_body(): lax.ppermute(held, 'row', [(k, k ^ step) for k in range(n_row)])  1.56 us
    pallas_call x1, Pallas kernels, gathered_body(): pl.pallas_call(weights_kernel, out_shape=(shape(8, 128), jax.ShapeDtypeSt...  1.52 us
  transfers between devices with their start and end apart: 6, of which 3 were waited for; matrix products, arithmetic and copies ran while one was open for 0% of the time, Pallas kernels for 5%

profile of v2, /device:TPU:0, one launch (start us, length us, event | category | flops | bytes accessed | tf_op | source)
XLA Modules:
  0.0 31.9 jit_solution(11500843590584517775)
XLA Ops:
  0.6 0.0 copy-start
  0.6 1.7 %shard_map.135 = bf16[192,128]{1,0:T(8,128)(2,1)} custom-call(bf16[32,8,64]{2,1,0:T(8,128)(2,1)} %msa_ref.1, s32[8,32]{1,0:T(8,128)} %bitcast.23, bf16[8,8,128]{2,1,0:T(8,128)(2,1)} %pair_ref.1), custom_call_target="tpu_custom_call" | custom-call | tf_op jit(solution)/shard_map/pallas_call | solution.py:413
  2.3 5.0 %collective-permute-start.2 = (bf16[192,128]{1,0:T(8,128)(2,1)}, bf16[192,128]{1,0:T(8,128)(2,1)S(1)}, u32[]{:S(2)}, u32[]{:S(2)}) collective-permute-start(bf16[192,128]{1,0:T(8,128)(2,1)} %shard_map.135), channel_id=1, source_target_pairs={{0,3},{1,2},{2,1},{3,0},{4,7},{5,6},{6,5},{7,4},{8,11},{9,10},{10,... | collective-permute-start | bytes 147464 | tf_op jit(solution)/shard_map/ppermute | solution.py:432
  7.4 0.0 collective-permute-start.1
  7.4 0.6 %collective-permute-start = (bf16[192,128]{1,0:T(8,128)(2,1)}, bf16[192,128]{1,0:T(8,128)(2,1)S(1)}, u32[]{:S(2)}, u32[]{:S(2)}) collective-permute-start(bf16[192,128]{1,0:T(8,128)(2,1)} %shard_map.135), channel_id=1, source_target_pairs={{0,1},{1,0},{2,3},{3,2},{4,5},{5,4},{6,7},{7,6},{8,9},{9,8},{10,11... | collective-permute-start | bytes 147464 | tf_op jit(solution)/shard_map/ppermute | solution.py:432
  8.0 1.9 %collective-permute-done.2 = bf16[192,128]{1,0:T(8,128)(2,1)S(1)} collective-permute-done((bf16[192,128]{1,0:T(8,128)(2,1)}, bf16[192,128]{1,0:T(8,128)(2,1)S(1)}, u32[]{:S(2)}, u32[]{:S(2)}) %collective-permute-start.2) | collective-permute-done | bytes 49184 | tf_op jit(solution)/shard_map/ppermute | solution.py:432
  9.8 2.8 %collective-permute-done.1 = bf16[192,128]{1,0:T(8,128)(2,1)S(1)} collective-permute-done((bf16[192,128]{1,0:T(8,128)(2,1)}, bf16[192,128]{1,0:T(8,128)(2,1)S(1)}, u32[]{:S(2)}, u32[]{:S(2)}) %collective-permute-start.1) | collective-permute-done | bytes 49184 | tf_op jit(solution)/shard_map/ppermute | solution.py:432
  12.6 0.0 collective-permute-done
  12.6 0.8 %pad_maximum_fusion.refs_0_ = bf16[4,192,128]{2,1,0:T(8,128)(2,1)S(1)} fusion(bf16[1,192,128]{2,1,0:T(8,128)(2,1)S(1)} %bitcast.20, bf16[1,192,128]{2,1,0:T(8,128)(2,1)S(1)} %bitcast.21, bf16[1,192,128]{2,1,0:T(8,128)(2,1)S(1)} %bitcast.22, bf16[1,192,128]{2,1,0:T(8,128)(2,1)} %bitcast.19), kind=kLoop, calls=%fused_computation | loop fusion | flops 294912 | bytes 393216 | tf_op jit(solution)/shard_map/stack | solution.py:434
  13.4 1.6 %collective-permute-start.4 = (bf16[4,192,128]{2,1,0:T(8,128)(2,1)S(1)}, bf16[4,192,128]{2,1,0:T(8,128)(2,1)S(1)}, u32[]{:S(2)}, u32[]{:S(2)}) collective-permute-start(bf16[4,192,128]{2,1,0:T(8,128)(2,1)S(1)} %pad_maximum_fusion.refs_0_), channel_id=1, source_target_pairs={{0,8},{4,12},{8,0},{12,4},{1,9},{5,13},{9,1},{13,5},{2,10},{6,14},... | collective-permute-start | bytes 589832 | tf_op jit(solution)/shard_map/ppermute | solution.py:438
  15.0 0.0 collective-permute-start.3
  15.0 4.3 %collective-permute-done.4.refs_2_ = bf16[4,192,128]{2,1,0:T(8,128)(2,1)S(1)} collective-permute-done((bf16[4,192,128]{2,1,0:T(8,128)(2,1)S(1)}, bf16[4,192,128]{2,1,0:T(8,128)(2,1)S(1)}, u32[]{:S(2)}, u32[]{:S(2)}) %collective-permute-start.4) | collective-permute-done | bytes 196640 | tf_op jit(solution)/shard_map/ppermute | solution.py:438
  19.2 0.0 collective-permute-start.5
  19.2 0.0 copy-start.2
  19.2 0.0 copy-start.3
  19.2 1.5 %shard_map.136 = (f32[8,128]{1,0:T(8,128)}, bf16[256,256]{1,0:T(8,128)(2,1)}) custom-call(f32[1,64]{1,0:T(1,128)} %bitcast.24, f32[1,64]{1,0:T(1,128)} %bitcast.25, bf16[32,64]{1,0:T(8,128)(2,1)} %bitcast.15, bf16[32,64]{1,0:T(8,128)(2,1)} %bitcast.17), custom_call_target="tpu_custom_call" | custom-call | tf_op jit(solution)/shard_map/pallas_call | solution.py:419
  20.8 0.0 copy-start.4
  20.8 0.0 collective-permute-done.3.refs_1_
  20.8 0.0 collective-permute-done.5.refs_3_
  20.8 0.0 copy-done
  20.8 0.0 copy-done.2
  20.8 0.0 copy-done.3
  20.8 0.6 %copy-done.4 = f32[8,128]{1,0:T(8,128)S(1)} copy-done((f32[8,128]{1,0:T(8,128)S(1)}, f32[8,128]{1,0:T(8,128)}, u32[]{:S(2)}) %copy-start.4) | copy-done | bytes 4120
  21.5 0.0 copy-start.1
  21.5 0.9 %copy-done.1 = bf16[256,256]{1,0:T(8,128)(2,1)S(1)} copy-done((bf16[256,256]{1,0:T(8,128)(2,1)S(1)}, bf16[256,256]{1,0:T(8,128)(2,1)}, u32[]{:S(2)}) %copy-start.1) | copy-done | bytes 131096
  22.4 9.5 %shard_map.137 = (f32[32,8,64]{2,1,0:T(8,128)}, f32[1024,128]{1,0:T(8,128)}, f32[32,64]{1,0:T(8,128)}, f32[32,64]{1,0:T(8,128)}, f32[1,64]{1,0:T(1,128)}, /*index=5*/f32[1,64]{1,0:T(1,128)}, f32[1,128]{1,0:T(1,128)}) custom-call(s32[1]{0:T(128)} %bitcast.place_ref, bf16[4,192,128]{2,1,0:T(8,128)(2,1)S(1)} %pad_maximum_fusion.refs_0_, ...), custom_call_target="tpu_custom_call" | custom-call | tf_op jit(solution)/shard_map/pallas_call | solution.py:443
Async XLA Ops:
  0.6 20.2 %copy-start = (bf16[1024,128]{1,0:T(8,128)(2,1)S(1)}, bf16[1024,128]{1,0:T(8,128)(2,1)}, u32[]{:S(2)}) copy-start(bf16[1024,128]{1,0:T(8,128)(2,1)} %refs_8_.1) | copy-start | bytes 786436
  2.3 7.5 %collective-permute-start.2 = (bf16[192,128]{1,0:T(8,128)(2,1)}, bf16[192,128]{1,0:T(8,128)(2,1)S(1)}, u32[]{:S(2)}, u32[]{:S(2)}) collective-permute-start(bf16[192,128]{1,0:T(8,128)(2,1)} %shard_map.135), channel_id=1, source_target_pairs={{0,3},{1,2},{2,1},{3,0},{4,7},{5,6},{6,5},{7,4},{8,11},{9,10},{10,... | collective-permute-start | bytes 147464 | tf_op jit(solution)/shard_map/ppermute | solution.py:432
  7.4 5.2 %collective-permute-start.1 = (bf16[192,128]{1,0:T(8,128)(2,1)}, bf16[192,128]{1,0:T(8,128)(2,1)S(1)}, u32[]{:S(2)}, u32[]{:S(2)}) collective-permute-start(bf16[192,128]{1,0:T(8,128)(2,1)} %shard_map.135), channel_id=1, source_target_pairs={{0,2},{1,3},{2,0},{3,1},{4,6},{5,7},{6,4},{7,5},{8,10},{9,11},{10,... | collective-permute-start | bytes 147464 | tf_op jit(solution)/shard_map/ppermute | solution.py:432
  7.4 5.2 %collective-permute-start = (bf16[192,128]{1,0:T(8,128)(2,1)}, bf16[192,128]{1,0:T(8,128)(2,1)S(1)}, u32[]{:S(2)}, u32[]{:S(2)}) collective-permute-start(bf16[192,128]{1,0:T(8,128)(2,1)} %shard_map.135), channel_id=1, source_target_pairs={{0,1},{1,0},{2,3},{3,2},{4,5},{5,4},{6,7},{7,6},{8,9},{9,8},{10,11... | collective-permute-start | bytes 147464 | tf_op jit(solution)/shard_map/ppermute | solution.py:432
  13.4 5.8 %collective-permute-start.4 = (bf16[4,192,128]{2,1,0:T(8,128)(2,1)S(1)}, bf16[4,192,128]{2,1,0:T(8,128)(2,1)S(1)}, u32[]{:S(2)}, u32[]{:S(2)}) collective-permute-start(bf16[4,192,128]{2,1,0:T(8,128)(2,1)S(1)} %pad_maximum_fusion.refs_0_), channel_id=1, source_target_pairs={{0,8},{4,12},{8,0},{12,4},{1,9},{5,13},{9,1},{13,5},{2,10},{6,14},... | collective-permute-start | bytes 589832 | tf_op jit(solution)/shard_map/ppermute | solution.py:438
  15.0 5.8 %collective-permute-start.3 = (bf16[4,192,128]{2,1,0:T(8,128)(2,1)S(1)}, bf16[4,192,128]{2,1,0:T(8,128)(2,1)S(1)}, u32[]{:S(2)}, u32[]{:S(2)}) collective-permute-start(bf16[4,192,128]{2,1,0:T(8,128)(2,1)S(1)} %pad_maximum_fusion.refs_0_), channel_id=1, source_target_pairs={{0,4},{4,0},{8,12},{12,8},{1,5},{5,1},{9,13},{13,9},{2,6},{6,2},{1... | collective-permute-start | bytes 589832 | tf_op jit(solution)/shard_map/ppermute | solution.py:438
  19.2 1.5 %collective-permute-start.5 = (bf16[4,192,128]{2,1,0:T(8,128)(2,1)S(1)}, bf16[4,192,128]{2,1,0:T(8,128)(2,1)S(1)}, u32[]{:S(2)}, u32[]{:S(2)}) collective-permute-start(bf16[4,192,128]{2,1,0:T(8,128)(2,1)S(1)} %collective-permute-done.4.refs_2_), channel_id=1, source_target_pairs={{0,4},{4,0},{8,12},{12,8},{1,5},{5,1},{9,13},{13,9},{2,6},{6,2},{1... | collective-permute-start | bytes 589832 | tf_op jit(solution)/shard_map/ppermute | solution.py:438
  19.2 1.6 %copy-start.2 = (bf16[64,32]{0,1:T(8,128)(2,1)S(1)}, bf16[64,32]{0,1:T(8,128)(2,1)}, u32[]{:S(2)}) copy-start(bf16[64,32]{0,1:T(8,128)(2,1)} %param.13) | copy-start | bytes 12292
  19.2 1.6 %copy-start.3 = (bf16[64,32]{0,1:T(8,128)(2,1)S(1)}, bf16[64,32]{0,1:T(8,128)(2,1)}, u32[]{:S(2)}) copy-start(bf16[64,32]{0,1:T(8,128)(2,1)} %param.14) | copy-start | bytes 12292
  20.8 0.7 %copy-start.4 = (f32[8,128]{1,0:T(8,128)S(1)}, f32[8,128]{1,0:T(8,128)}, u32[]{:S(2)}) copy-start(f32[8,128]{1,0:T(8,128)} %get-tuple-element.16.refs_4_) | copy-start | bytes 12292
  21.5 0.9 %copy-start.1 = (bf16[256,256]{1,0:T(8,128)(2,1)S(1)}, bf16[256,256]{1,0:T(8,128)(2,1)}, u32[]{:S(2)}) copy-start(bf16[256,256]{1,0:T(8,128)(2,1)} %get-tuple-element.17.refs_5_) | copy-start | bytes 393220

commit v3 on v2

--- a/solution.py
+++ b/solution.py
@@ -215,14 +215,10 @@
         out_ref[32 * g : 32 * g + 32, :] = jnp.where(
             present[:, 128 * g : 128 * g + 128], rows, ABSENT
         ).astype(BF)
-    pair = pair_ref[...].astype(F32)
-    for j in range(0, 8, 2):
-        out_ref[128 + 8 * j : 144 + 8 * j, :] = jnp.concatenate(
-            [pair[:, j, :], pair[:, j + 1, :]], axis=0
-        ).astype(BF)
-
-
-def weights_kernel(gain_ref, offset_ref, first_ref, second_ref, norm_out, back_out):
+    out_ref[128:192, :] = pair_ref[...].astype(F32).reshape(64, 128).astype(BF)
+
+
+def weights_kernel(gain_ref, offset_ref, first_ref, second_ref, final_ref, norm_out, back_out, final_out, scr):
     norm_out[...] = jnp.concatenate(
         [
             jnp.concatenate([ref[...]] * 2, axis=1)
@@ -235,128 +231,150 @@
         wide = jnp.concatenate([wide] * 4, axis=0)
         own = spread(128, 256, lambda r, c: r // 32 == c // 64)
         back_out[128 * k : 128 * k + 128, :] = jnp.where(own, wide, 0.0).astype(BF)
-
-
-def part_kernel(n_row, n_col, place_ref, *refs):
-    sets = refs[:n_row]
-    (
-        norm_ref, back_ref, first_ref, second_ref, final_hbm,
-        emb_out, final_hbm_out, first_out, second_out, gain_out, offset_out, bias_out,
-        pair_scr, normed_scr, rhs_scr, left_scr, leftt_scr, right_scr, rightt_scr,
-        scaled_scr, grad_scr, outer_scr, lin_scr, linc_scr, rin_scr,
-        final_ref, final_out, in_sem, out_sem,
-    ) = refs[n_row:]
-    final_in = pltpu.make_async_copy(final_hbm, final_ref, in_sem)
-    final_in.start()
+    scr[...] = final_ref[...].astype(F32)
+    for e in range(32):
+        final_out[32 * e : 32 * e + 32, :] = scr[pl.ds(e, 32, stride=32), :].astype(BF)
+
+
+def averager_of():
+    return spread(128, 128, lambda r, c: jnp.where(r // 64 == c // 64, 1.0 / 64, 0.0)).astype(BF)
+
+
+def stage_kernel(
+    n_col, a, place_ref, set_ref, norm_ref, back_ref, final_ref,
+    rhs_out, left_out, leftt_out, rightt_out, grad_out, pair_out, found_out, *own_out
+):
     place = place_ref[0]
-
-    for a in range(n_row):
-        for b in range(n_col):
-            at = lax.bitwise_xor(place, b) * 8
-            pair_scr[pl.ds(at, 8), 8 * a : 8 * a + 8, :] = (
-                sets[a][b, 128:192, :].astype(F32).reshape(8, 8, 128)
-            )
+    for b in range(n_col):
+        at = pl.multiple_of(lax.bitwise_xor(place, b) * 8, 8)
+        pair_out[:, pl.ds(at, 8), :] = set_ref[b, 128:192, :].astype(F32).reshape(8, 8, 128)
 
     gain = norm_ref[0:1, :]
     offset = norm_ref[1:2, :]
-    averager = spread(128, 128, lambda r, c: jnp.where(r // 64 == c // 64, 1.0 / 64, 0.0)).astype(BF)
+    averager = averager_of()
+    x = jnp.concatenate(
+        [set_ref[b, 32 * g : 32 * g + 32, :] for g in range(4) for b in range(n_col)], axis=0
+    )
+    mean = mm(x, averager)
+    present = mean < ABSENT / 2
+    varied = x.astype(F32) - mean
+    inverse = lax.rsqrt(mm((varied * varied).astype(BF), averager) + 1e-05)
+    normed = varied * inverse
+    if own_out:
+        for g in range(4):
+            own_out[0][32 * g : 32 * g + 32, :] = normed[128 * g : 128 * g + 32]
+            own_out[1][32 * g : 32 * g + 32, :] = inverse[128 * g : 128 * g + 32]
+    normal = jnp.where(present, normed * gain + offset, 0.0).astype(BF)
+    rhs_out[:, 0:128] = normal
+    rhs_out[:, 128:256] = normed.astype(BF)
+    here = jnp.where(present, 1.0, 0.0)
     lane = lax.broadcasted_iota(jnp.int32, (128, 128), 1)
-    inverse_own = None
     found = jnp.zeros((128, 128), F32)
-    for a in range(n_row):
-        x = jnp.concatenate(
-            [sets[a][b, 32 * g : 32 * g + 32, :] for g in range(4) for b in range(n_col)], axis=0
-        )
-        mean = mm(x, averager)
-        present = mean < ABSENT / 2
-        varied = x.astype(F32) - mean
-        inverse = lax.rsqrt(mm((varied * varied).astype(BF), averager) + 1e-05)
-        normed = varied * inverse
-        if a == 0:
-            inverse_own = inverse
-            normed_scr[...] = normed
-        rows = slice(512 * a, 512 * a + 512)
-        normal = jnp.where(present, normed * gain + offset, 0.0).astype(BF)
-        rhs_scr[rows, 0:128] = normal
-        rhs_scr[rows, 128:256] = normed.astype(BF)
-        here = jnp.where(present, 1.0, 0.0)
-        for g in range(4):
-            found = jnp.where(lane % 32 // 2 == 4 * a + g, here[128 * g : 128 * g + 128], found)
-        for h in range(2):
-            masked = jnp.concatenate(
-                [normal[128 * g : 128 * g + 128] for g in (2 * h, 2 * h + 1)], axis=1
+    for g in range(4):
+        found = jnp.where(lane % 32 // 2 == 4 * a + g, here[128 * g : 128 * g + 128], found)
+    found_out[...] = found
+    for h in range(2):
+        masked = jnp.concatenate(
+            [normal[128 * g : 128 * g + 128] for g in (2 * h, 2 * h + 1)], axis=1
+        )
+        at = slice(128 * h, 128 * h + 128)
+        left_out[:, at] = mm_nt(masked, back_ref[:128, :]).astype(BF)
+        both = mm_nt(back_ref[...], masked)
+        leftt_out[at, :] = both[:128].astype(BF)
+        rightt_out[at, :] = both[128:]
+
+    grad = mm_nt(final_ref[...], pair_out[...].reshape(256, 128).astype(BF)).astype(BF)
+    for q in range(8):
+        for p in range(2):
+            grad_out[128 * p : 128 * p + 128, 128 * q : 128 * q + 128] = swap_blocks(
+                grad[128 * q : 128 * q + 128, 128 * p : 128 * p + 128]
             )
-            k = 2 * a + h
-            at = slice(128 * k, 128 * k + 128)
-            right_scr[:, at] = mm_nt(masked, back_ref[128:, :]).astype(BF)
-            both = mm_nt(back_ref[...], masked)
-            rightt_scr[at, :] = both[128:].astype(BF)
-            left_scr[at, :] = both[:128]
-    for q in range(8):
-        leftt_scr[128 * q : 128 * q + 128, :] = jnp.concatenate(
-            [left_scr[pl.ds(4 * q + c, 32, stride=32), :] for c in range(4)], axis=0
-        ).astype(BF)
-
+
+
+def part_kernel(n_row, *refs):
+    stages = [refs[7 * a : 7 * a + 7] for a in range(n_row)]
+    (
+        normed_ref, inverse_ref, norm_ref, back_ref, first_ref, second_ref,
+        emb_out, final_hbm_out, first_out, second_out, gain_out, offset_out, bias_out,
+        right_scr, scaled_scr, grad_scr, outer_scr, wide_scr, linc_scr, rin_scr, rinc_scr,
+        final_out, out_sem,
+    ) = refs[7 * n_row :]
+    gain = norm_ref[0:1, :]
+    averager = averager_of()
+    lane = lax.broadcasted_iota(jnp.int32, (128, 128), 1)
+
+    found = sum(stage[6][...] for stage in stages)
     turned = pltpu.roll(found, 64, 1)
     mask = jnp.where((lane % 2 == 0) == (lane < 64), found, turned)
     mask_t = mask.T
+
+    for a, stage in enumerate(stages):
+        wide_scr[256 * a : 256 * a + 256, :] = stage[3][...]
+    for e in range(32):
+        right_scr[32 * e : 32 * e + 32, :] = wide_scr[pl.ds(e, 32, stride=32), :].astype(BF)
 
     bias = jnp.zeros((1, 128), F32)
     ones = jnp.ones((128, 128), BF)
     for p in range(8):
         both_on = jnp.concatenate(
-            [mask_t[0:32] * mask_t[j : j + 1] for j in range(4 * p, 4 * p + 4)], axis=0
+            [mask_t[0:32] * mask_t[i : i + 1] for i in range(4 * p, 4 * p + 4)], axis=0
         ).astype(BF)
         counts = mm(both_on, ones)
-        scaled = pair_scr[4 * p : 4 * p + 4].reshape(128, 128) / (counts + 0.001)
+        pair = stages[p // 2][5][4 * (p % 2) : 4 * (p % 2) + 4]
+        scaled = pair.reshape(128, 128) / (counts + 0.001)
         bias = bias + jnp.sum(scaled, axis=0, keepdims=True)
         scaled_scr[128 * p : 128 * p + 128, :] = scaled.astype(BF)
     bias_out[...] = bias
 
-    for n in range(4):
-        outer = mm_nt(rightt_scr[...], leftt_scr[256 * n : 256 * n + 256, :]).astype(BF)
-        for p in range(8):
-            for q in range(2):
-                outer_scr[256 * n + 128 * q : 256 * n + 128 * q + 128, 128 * p : 128 * p + 128] = (
-                    swap_blocks(outer[128 * p : 128 * p + 128, 128 * q : 128 * q + 128])
+    for a, stage in enumerate(stages):
+        outer = mm_nt(stage[2][...], right_scr[...]).astype(BF)
+        for p in range(2):
+            for q in range(8):
+                to = 256 * a + 128 * p
+                outer_scr[128 * q : 128 * q + 128, to : to + 128] = swap_blocks(
+                    outer[128 * p : 128 * p + 128, 128 * q : 128 * q + 128]
                 )
-    final_out[...] = mm(outer_scr[...], scaled_scr[...])
+    wide_scr[...] = mm(outer_scr[...], scaled_scr[...])
+    for c in range(32):
+        final_out[32 * c : 32 * c + 32, :] = wide_scr[pl.ds(c, 32, stride=32), :]
     final_send = pltpu.make_async_copy(final_out, final_hbm_out, out_sem)
     final_send.start()
 
-    final_in.wait()
-    for n in range(4):
-        grad = mm_nt(final_ref[...], scaled_scr[256 * n : 256 * n + 256, :]).astype(BF)
+    mask_bf = mask.astype(BF)
+    share = 1.0 / (mm_tn(mask_bf, mask_bf)[0:32] + 0.001)
+    for i in range(32):
+        a, at = i // 8, 32 * (i % 8)
         for q in range(8):
-            for p in range(2):
-                grad_scr[256 * n + 128 * p : 256 * n + 128 * p + 128, 128 * q : 128 * q + 128] = (
-                    swap_blocks(grad[128 * q : 128 * q + 128, 128 * p : 128 * p + 128])
-                )
-    left_grad = mm(right_scr[...], grad_scr[...])
-    right_grad = mm(grad_scr[...], leftt_scr[...])
+            block = stages[a][4][at : at + 32, 128 * q : 128 * q + 128].astype(F32)
+            grad_scr[32 * i : 32 * i + 32, 128 * q : 128 * q + 128] = (
+                block * share[i : i + 1]
+            ).astype(BF)
+    left_grad = mm(grad_scr[...], right_scr[...])
+    left = jnp.concatenate([stage[1][...] for stage in stages], axis=1)
+    right_grad = mm(left, grad_scr[...])
 
     identity = spread(128, 128, lambda r, c: jnp.where(r == c, 1.0, 0.0)).astype(BF)
     for q in range(8):
         at = slice(128 * q, 128 * q + 128)
-        lin_scr[at, :] = mm_nt(identity, (left_grad[:, at] * mask).astype(BF))
+        rin_scr[at, :] = mm_nt(identity, (right_grad[:, at] * mask).astype(BF))
     for k in range(8):
         rows = []
         for t in range(4 * k, 4 * k + 4):
-            rows.append(right_grad[32 * t : 32 * t + 32] * mask_t[t : t + 1])
+            rows.append(left_grad[32 * t : 32 * t + 32] * mask_t[t : t + 1])
         at = slice(128 * k, 128 * k + 128)
-        rin_scr[at, :] = jnp.concatenate(rows, axis=0).astype(BF)
-        linc_scr[at, :] = jnp.concatenate(
-            [lin_scr[pl.ds(t, 32, stride=32), :] for t in range(4 * k, 4 * k + 4)], axis=0
+        linc_scr[at, :] = jnp.concatenate(rows, axis=0).astype(BF)
+        rinc_scr[at, :] = jnp.concatenate(
+            [rin_scr[pl.ds(t, 32, stride=32), :] for t in range(4 * k, 4 * k + 4)], axis=0
         ).astype(BF)
 
     total = jnp.zeros((128, 256), F32)
     sums = jnp.zeros((128, 128), F32)
     for g in range(16):
         grads = jnp.concatenate(
-            [linc_scr[64 * g : 64 * g + 64, :], rin_scr[64 * g : 64 * g + 64, :]], axis=0
+            [linc_scr[64 * g : 64 * g + 64, :], rinc_scr[64 * g : 64 * g + 64, :]], axis=0
         )
         sums = sums + grads.astype(F32)
-        total = total + mm(grads, rhs_scr[128 * g : 128 * g + 128, :])
+        total = total + mm(grads, stages[g // 4][0][128 * (g % 4) : 128 * (g % 4) + 128, :])
 
     def fold(block):
         return block[0:32, 0:64] + block[32:64, 64:128]
@@ -376,12 +394,12 @@
 
     for h in range(2):
         at = slice(128 * h, 128 * h + 128)
-        d_normal = mm_tn(linc_scr[at, :], back_ref[:128, :]) + mm_tn(rin_scr[at, :], back_ref[128:, :])
+        d_normal = mm_tn(linc_scr[at, :], back_ref[:128, :]) + mm_tn(rinc_scr[at, :], back_ref[128:, :])
         for half in range(2):
             g = 2 * h + half
             d_hat = d_normal[0:32, 128 * half : 128 * half + 128] * gain
-            normed = normed_scr[128 * g : 128 * g + 32, :]
-            result = inverse_own[128 * g : 128 * g + 32] * (
+            normed = normed_ref[32 * g : 32 * g + 32, :]
+            result = inverse_ref[32 * g : 32 * g + 32, :] * (
                 d_hat
                 - mm(d_hat.astype(BF), averager)
                 - normed * mm((d_hat * normed).astype(BF), averager)
@@ -393,6 +411,9 @@
 
 def vmem(count):
     return [pl.BlockSpec(memory_space=pltpu.VMEM)] * count
+
+
+LIMIT = pltpu.CompilerParams(vmem_limit_bytes=32 * 1024 * 1024)
 
 
 def gathered_body(
@@ -409,39 +430,68 @@
 ):
     shards, tokens, features = homolog_embedding.shape
     width = first_projection_matrix.shape[1]
+    first_t, second_t = first_projection_matrix.T, second_projection_matrix.T
     shape = lambda *dims: jax.ShapeDtypeStruct(dims, F32)
+    held = lambda *dims: pltpu.VMEM(dims, F32)
+    held_bf = lambda *dims: pltpu.VMEM(dims, BF)
+    place = lax.bitwise_xor(lax.axis_index("row"), lax.axis_index("col"))
+    place = place.astype(jnp.int32).reshape(1)
     packed = pl.pallas_call(
         pack_kernel,
-        out_shape=jax.ShapeDtypeStruct((192, 128), BF),
+        out_shape=held_bf(192, 128),
         in_specs=vmem(3),
         out_specs=vmem(1)[0],
     )(homolog_embedding, presence_indicator.T, coupling_change_derivative)
-    norm, back = pl.pallas_call(
+    pieces = [packed] + [
+        lax.ppermute(packed, "col", [(k, k ^ b) for k in range(n_col)]) for b in range(1, n_col)
+    ]
+    weights = pl.pallas_call(
         weights_kernel,
-        out_shape=(shape(8, 128), jax.ShapeDtypeStruct((256, 256), BF)),
-        in_specs=vmem(4),
-        out_specs=tuple(vmem(2)),
+        out_shape=(held(8, 128), held_bf(256, 256), held_bf(width * width, 128)),
+        in_specs=vmem(5),
+        out_specs=tuple(vmem(3)),
+        scratch_shapes=[pltpu.VMEM((width * width, 128), F32)],
+        compiler_params=LIMIT,
     )(
         standardizer_scale.reshape(1, features),
         standardizer_shift.reshape(1, features),
-        first_projection_matrix.T,
-        second_projection_matrix.T,
-    )
-
-    pieces = [packed] + [
-        lax.ppermute(packed, "col", [(k, k ^ b) for k in range(n_col)]) for b in range(1, n_col)
-    ]
+        first_t,
+        second_t,
+        final_projection_matrix,
+    )
+    pieces, weights = lax.optimization_barrier((pieces, weights))
+    norm, back, final_turned = weights
+
     sets = {0: jnp.stack(pieces)}
     step = n_row // 2
     while step:
-        for a, held in sorted(sets.items()):
-            sets[a ^ step] = lax.ppermute(held, "row", [(k, k ^ step) for k in range(n_row)])
+        for a, block in sorted(sets.items()):
+            sets[a ^ step] = lax.ppermute(block, "row", [(k, k ^ step) for k in range(n_row)])
         step //= 2
 
-    place = lax.bitwise_xor(lax.axis_index("row"), lax.axis_index("col")).astype(jnp.int32)
+    def stage(a):
+        outs = [
+            held_bf(512, 256), held_bf(128, 256), held_bf(256, 128), held(256, 128),
+            held_bf(256, 1024), held(8, 32, 128), held(128, 128),
+        ]
+        if a == 0:
+            outs += [held(128, 128)] * 2
+        return pl.pallas_call(
+            functools.partial(stage_kernel, n_col, a),
+            out_shape=tuple(outs),
+            in_specs=[pl.BlockSpec(memory_space=pltpu.SMEM)] + vmem(4),
+            out_specs=tuple(vmem(len(outs))),
+            compiler_params=LIMIT,
+            cost_estimate=pl.CostEstimate(
+                flops=1_000_000_000, bytes_accessed=4_000_000, transcendentals=0
+            ),
+        )(place, sets[a], norm, back, final_turned)
+
+    stages = [stage(a) for a in range(n_row)]
+    own = stages[0][7:]
     hbm = pl.BlockSpec(memory_space=pltpu.HBM)
     outs = pl.pallas_call(
-        functools.partial(part_kernel, n_row, n_col),
+        functools.partial(part_kernel, n_row),
         out_shape=(
             shape(shards, tokens, features),
             shape(width * width, 128),
@@ -451,37 +501,22 @@
             shape(1, features),
             shape(1, 128),
         ),
-        in_specs=[pl.BlockSpec(memory_space=pltpu.SMEM)] + vmem(n_row + 4) + [hbm],
+        in_specs=vmem(7 * n_row + 6),
         out_specs=(*vmem(1), hbm, *vmem(5)),
         scratch_shapes=[
-            pltpu.VMEM((32, 32, 128), F32),
-            pltpu.VMEM((512, 128), F32),
-            pltpu.VMEM((2048, 256), BF),
-            pltpu.VMEM((1024, 128), F32),
-            pltpu.VMEM((1024, 128), BF),
-            pltpu.VMEM((128, 1024), BF),
             pltpu.VMEM((1024, 128), BF),
             pltpu.VMEM((1024, 128), BF),
             pltpu.VMEM((1024, 1024), BF),
             pltpu.VMEM((1024, 1024), BF),
             pltpu.VMEM((1024, 128), F32),
             pltpu.VMEM((1024, 128), BF),
-            pltpu.VMEM((1024, 128), BF),
+            pltpu.VMEM((1024, 128), F32),
             pltpu.VMEM((1024, 128), BF),
             pltpu.VMEM((1024, 128), F32),
             pltpu.SemaphoreType.DMA,
-            pltpu.SemaphoreType.DMA,
         ],
-        compiler_params=pltpu.CompilerParams(vmem_limit_bytes=48 * 1024 * 1024),
-    )(
-        place.reshape(1),
-        *[sets[a] for a in range(n_row)],
-        norm,
-        back,
-        first_projection_matrix.T,
-        second_projection_matrix.T,
-        final_projection_matrix,
-    )
+        compiler_params=LIMIT,
+    )(*[x for s in stages for x in s[:7]], *own, norm, back, first_t, second_t)
     emb, final, first, second, gain, offset, bias = outs
     return emb, final, first.T, second.T, gain.reshape(-1), offset.reshape(-1), bias.reshape(-1)
 

time: 32.2 us -> 27.4 us (0.85)
  waiting for transfers between devices: 8.9 us -> 6.63 us
  Pallas kernels: 12.8 us -> 10.8 us
  other arithmetic: 0.83 us -> 0.03 us
    ppermute x3, waiting for transfers between devices: 4.63 us -> 2.37 us  [gathered_body(): lax.ppermute(packed, 'col', [(k, k ^ b) for k in range(n_col)])]
    pallas_call x3 -> x7, Pallas kernels: 12.8 us -> 10.8 us  [the longest x1 5.79 us: gathered_body(): pl.pallas_call(functools.partial(part_kernel, n_row), out_shape=(shape(sh...]
    another operation x1, other arithmetic: 0.83 us -> 0.03 us  [gathered_body(): sets = {0: jnp.stack(pieces)}]
  transfers between devices with their start and end apart: 6 -> 6, of which waited for: 3 -> 2; matrix products, arithmetic and copies ran while one was open for 0% -> 0% of each run, Pallas kernels for 5% -> 11%
where the time goes in v3:
time: 27.4 us; the launch traced here: 27.1 us
  Pallas kernels  10.8 us (39%)
  starting transfers between devices  7.32 us (27%)
  waiting for transfers between devices  6.63 us (24%)
  local copies, waits for them, and re-layouts  1.62 us (6%)
  between operations  0.72 us (3%)
    pallas_call x1, Pallas kernels, gathered_body(): pl.pallas_call(functools.partial(part_kernel, n_row), out_shape=(shape(sh...  5.79 us
    ppermute x3, starting transfers between devices, gathered_body(): lax.ppermute(packed, 'col', [(k, k ^ b) for k in range(n_col)])  5.76 us
    ppermute x3, waiting for transfers between devices, gathered_body(): lax.ppermute(block, 'row', [(k, k ^ step) for k in range(n_row)])  4.26 us
    pallas_call x4, Pallas kernels, stage(): pl.pallas_call(functools.partial(stage_kernel, n_col, a), out_shape=tuple...  3.62 us
    ppermute x3, waiting for transfers between devices, gathered_body(): lax.ppermute(packed, 'col', [(k, k ^ b) for k in range(n_col)])  2.37 us
    unnamed x10, local copies, waits for them, and re-layouts  1.62 us
    ppermute x3, starting transfers between devices, gathered_body(): lax.ppermute(block, 'row', [(k, k ^ step) for k in range(n_row)])  1.56 us
    pallas_call x1, Pallas kernels, gathered_body(): pl.pallas_call(pack_kernel, out_shape=held_bf(192, 128), in_specs=vmem(3)...  1.05 us
  transfers between devices with their start and end apart: 6, of which 2 were waited for; matrix products, arithmetic and copies ran while one was open for 0% of the time, Pallas kernels for 11%

profile of v3, /device:TPU:0, one launch (start us, length us, event | category | flops | bytes accessed | tf_op | source)
XLA Modules:
  0.0 27.1 jit_solution(11967767565712435516)
XLA Ops:
  0.6 0.0 copy-start.1
  0.6 0.0 copy-start.2
  0.7 1.0 %shard_map.135 = bf16[192,128]{1,0:T(8,128)(2,1)S(1)} custom-call(bf16[32,8,64]{2,1,0:T(8,128)(2,1)} %msa_ref.1, s32[8,32]{1,0:T(8,128)} %bitcast.25, bf16[8,8,128]{2,1,0:T(8,128)(2,1)} %pair_ref.1), custom_call_target="tpu_custom_call" | custom-call | tf_op jit(solution)/shard_map/pallas_call | solution.py:439
  1.7 5.1 %collective-permute-start.2 = (bf16[192,128]{1,0:T(8,128)(2,1)S(1)}, bf16[192,128]{1,0:T(8,128)(2,1)S(1)}, u32[]{:S(2)}, u32[]{:S(2)}) collective-permute-start(bf16[192,128]{1,0:T(8,128)(2,1)S(1)} %shard_map.135), channel_id=1, source_target_pairs={{0,3},{1,2},{2,1},{3,0},{4,7},{5,6},{6,5},{7,4},{8,11},{9,10},{10,... | collective-permute-start | bytes 147464 | tf_op jit(solution)/shard_map/ppermute | solution.py:446
  6.8 0.0 collective-permute-start.1
  6.8 0.6 %collective-permute-start = (bf16[192,128]{1,0:T(8,128)(2,1)S(1)}, bf16[192,128]{1,0:T(8,128)(2,1)S(1)}, u32[]{:S(2)}, u32[]{:S(2)}) collective-permute-start(bf16[192,128]{1,0:T(8,128)(2,1)S(1)} %shard_map.135), channel_id=1, source_target_pairs={{0,1},{1,0},{2,3},{3,2},{4,5},{5,4},{6,7},{7,6},{8,9},{9,8},{10,11... | collective-permute-start | bytes 147464 | tf_op jit(solution)/shard_map/ppermute | solution.py:446
  7.5 0.0 copy-start.3
  7.5 0.0 copy-start.4
  7.5 0.0 copy-done.1
  7.5 0.0 copy-done.2
  7.5 0.6 %copy-done.3 = f32[64]{0:T(128)S(1)} copy-done((f32[64]{0:T(128)S(1)}, f32[64]{0:T(128)}, u32[]{:S(2)}) %copy-start.3) | copy-done | bytes 280
  8.1 0.0 copy-done.4
  8.1 0.0 copy-start
  8.1 0.9 %copy-done = bf16[1024,128]{1,0:T(8,128)(2,1)S(1)} copy-done((bf16[1024,128]{1,0:T(8,128)(2,1)S(1)}, bf16[1024,128]{1,0:T(8,128)(2,1)}, u32[]{:S(2)}) %copy-start) | copy-done | bytes 262168
  9.1 0.3 %shard_map.136 = (f32[8,128]{1,0:T(8,128)S(1)}, bf16[256,256]{1,0:T(8,128)(2,1)S(1)}, bf16[1024,128]{1,0:T(8,128)(2,1)S(1)}) custom-call(f32[1,64]{1,0:T(1,128)S(1)} %bitcast.20, f32[1,64]{1,0:T(1,128)S(1)} %bitcast.21, bf16[32,64]{1,0:T(8,128)(2,1)S(1)} %bitcast.16, bf16[32,64]{1,0:T(8,128)(2,1)S(1)} %bitcast.18, bf16[1024,128]{1,0:T(8,128)(2,1)S(1)} %copy-done), custom_call_target="tpu_custom_call" | custom-call | tf_op jit(solution)/shard_map/pallas_call | solution.py:448
  9.4 0.0 collective-permute-done.2
  9.4 2.4 %collective-permute-done.1 = bf16[192,128]{1,0:T(8,128)(2,1)S(1)} collective-permute-done((bf16[192,128]{1,0:T(8,128)(2,1)S(1)}, bf16[192,128]{1,0:T(8,128)(2,1)S(1)}, u32[]{:S(2)}, u32[]{:S(2)}) %collective-permute-start.1) | collective-permute-done | bytes 49184 | tf_op jit(solution)/shard_map/ppermute | solution.py:446
  11.8 0.0 collective-permute-done
  11.8 1.6 %collective-permute-start.4 = (bf16[4,192,128]{2,1,0:T(8,128)(2,1)S(1)}, bf16[4,192,128]{2,1,0:T(8,128)(2,1)S(1)}, u32[]{:S(2)}, u32[]{:S(2)}) collective-permute-start(bf16[4,192,128]{2,1,0:T(8,128)(2,1)S(1)} %pad_maximum_fusion.set_ref), channel_id=1, source_target_pairs={{0,8},{4,12},{8,0},{12,4},{1,9},{5,13},{9,1},{13,5},{2,10},{6,14},... | collective-permute-start | bytes 589832 | tf_op jit(solution)/shard_map/ppermute | solution.py:469
  13.4 0.0 collective-permute-start.3
  13.4 4.3 %collective-permute-done.4.set_ref = bf16[4,192,128]{2,1,0:T(8,128)(2,1)S(1)} collective-permute-done((bf16[4,192,128]{2,1,0:T(8,128)(2,1)S(1)}, bf16[4,192,128]{2,1,0:T(8,128)(2,1)S(1)}, u32[]{:S(2)}, u32[]{:S(2)}) %collective-permute-start.4) | collective-permute-done | bytes 196640 | tf_op jit(solution)/shard_map/ppermute | solution.py:469
  17.7 0.0 collective-permute-start.5
  17.7 0.9 %shard_map.137 = (bf16[512,256]{1,0:T(8,128)(2,1)S(1)}, bf16[128,256]{1,0:T(8,128)(2,1)S(1)}, bf16[256,128]{1,0:T(8,128)(2,1)S(1)}, f32[256,128]{1,0:T(8,128)S(1...) custom-call(s32[1]{0:T(128)} %bitcast.place_ref, ...), custom_call_target="tpu_custom_call" | custom-call | flops 1000000000 | bytes 4000000 | tf_op jit(solution)/shard_map/pallas_call | solution.py:479
  18.6 0.9 %shard_map.139 = (bf16[512,256]{1,0:T(8,128)(2,1)S(1)}, bf16[128,256]{1,0:T(8,128)(2,1)S(1)}, bf16[256,128]{1,0:T(8,128)(2,1)S(1)}, f32[256,128]{1,0:T(8,128)S(1...) custom-call(s32[1]{0:T(128)} %bitcast.place_ref, ...), custom_call_target="tpu_custom_call" | custom-call | flops 1000000000 | bytes 4000000 | tf_op jit(solution)/shard_map/pallas_call | solution.py:479
  19.5 0.0 collective-permute-done.3.set_ref
  19.5 0.9 %shard_map.138 = (bf16[512,256]{1,0:T(8,128)(2,1)S(1)}, bf16[128,256]{1,0:T(8,128)(2,1)S(1)}, bf16[256,128]{1,0:T(8,128)(2,1)S(1)}, f32[256,128]{1,0:T(8,128)S(1...) custom-call(s32[1]{0:T(128)} %bitcast.place_ref, ...), custom_call_target="tpu_custom_call" | custom-call | flops 1000000000 | bytes 4000000 | tf_op jit(solution)/shard_map/pallas_call | solution.py:479
  20.4 0.0 collective-permute-done.5.set_ref
  20.4 0.9 %shard_map.140 = (bf16[512,256]{1,0:T(8,128)(2,1)S(1)}, bf16[128,256]{1,0:T(8,128)(2,1)S(1)}, bf16[256,128]{1,0:T(8,128)(2,1)S(1)}, f32[256,128]{1,0:T(8,128)S(1...) custom-call(s32[1]{0:T(128)} %bitcast.place_ref, ...), custom_call_target="tpu_custom_call" | custom-call | flops 1000000000 | bytes 4000000 | tf_op jit(solution)/shard_map/pallas_call | solution.py:479
  21.3 5.8 %shard_map.141 = (f32[32,8,64]{2,1,0:T(8,128)}, f32[1024,128]{1,0:T(8,128)}, f32[32,64]{1,0:T(8,128)}, f32[32,64]{1,0:T(8,128)}, f32[1,64]{1,0:T(1,128)}, /*index=5*/f32[1,64]{1,0:T(1,128)}, f32[1,128]{1,0:T(1,128)}) custom-call(bf16[512,256]{1,0:T(8,128)(2,1)S(1)} %get-tuple-element.64.refs_0_, bf16[128,256]{1,0:T(8,128)(2,1)S(1)} %get-tuple-element.65.refs_1_, ...), custom_call_target="tpu_custom_call" | custom-call | tf_op jit(solution)/shard_map/pallas_call | solution.py:493
  (1 shorter events, 0.0 us)
Async XLA Ops:
  0.6 6.8 %copy-start.1 = (bf16[64,32]{0,1:T(8,128)(2,1)S(1)}, bf16[64,32]{0,1:T(8,128)(2,1)}, u32[]{:S(2)}) copy-start(bf16[64,32]{0,1:T(8,128)(2,1)} %param.13) | copy-start | bytes 12292
  0.6 6.8 %copy-start.2 = (bf16[64,32]{0,1:T(8,128)(2,1)S(1)}, bf16[64,32]{0,1:T(8,128)(2,1)}, u32[]{:S(2)}) copy-start(bf16[64,32]{0,1:T(8,128)(2,1)} %param.14) | copy-start | bytes 12292
  1.7 7.7 %collective-permute-start.2 = (bf16[192,128]{1,0:T(8,128)(2,1)S(1)}, bf16[192,128]{1,0:T(8,128)(2,1)S(1)}, u32[]{:S(2)}, u32[]{:S(2)}) collective-permute-start(bf16[192,128]{1,0:T(8,128)(2,1)S(1)} %shard_map.135), channel_id=1, source_target_pairs={{0,3},{1,2},{2,1},{3,0},{4,7},{5,6},{6,5},{7,4},{8,11},{9,10},{10,... | collective-permute-start | bytes 147464 | tf_op jit(solution)/shard_map/ppermute | solution.py:446
  6.8 5.0 %collective-permute-start.1 = (bf16[192,128]{1,0:T(8,128)(2,1)S(1)}, bf16[192,128]{1,0:T(8,128)(2,1)S(1)}, u32[]{:S(2)}, u32[]{:S(2)}) collective-permute-start(bf16[192,128]{1,0:T(8,128)(2,1)S(1)} %shard_map.135), channel_id=1, source_target_pairs={{0,2},{1,3},{2,0},{3,1},{4,6},{5,7},{6,4},{7,5},{8,10},{9,11},{10,... | collective-permute-start | bytes 147464 | tf_op jit(solution)/shard_map/ppermute | solution.py:446
  6.8 5.0 %collective-permute-start = (bf16[192,128]{1,0:T(8,128)(2,1)S(1)}, bf16[192,128]{1,0:T(8,128)(2,1)S(1)}, u32[]{:S(2)}, u32[]{:S(2)}) collective-permute-start(bf16[192,128]{1,0:T(8,128)(2,1)S(1)} %shard_map.135), channel_id=1, source_target_pairs={{0,1},{1,0},{2,3},{3,2},{4,5},{5,4},{6,7},{7,6},{8,9},{9,8},{10,11... | collective-permute-start | bytes 147464 | tf_op jit(solution)/shard_map/ppermute | solution.py:446
  7.5 0.7 %copy-start.3 = (f32[64]{0:T(128)S(1)}, f32[64]{0:T(128)}, u32[]{:S(2)}) copy-start(f32[64]{0:T(128)} %param.11) | copy-start | bytes 772
  7.5 0.7 %copy-start.4 = (f32[64]{0:T(128)S(1)}, f32[64]{0:T(128)}, u32[]{:S(2)}) copy-start(f32[64]{0:T(128)} %param.12) | copy-start | bytes 772
  8.1 0.9 %copy-start = (bf16[1024,128]{1,0:T(8,128)(2,1)S(1)}, bf16[1024,128]{1,0:T(8,128)(2,1)}, u32[]{:S(2)}) copy-start(bf16[1024,128]{1,0:T(8,128)(2,1)} %final_ref.1) | copy-start | bytes 786436
  11.8 5.8 %collective-permute-start.4 = (bf16[4,192,128]{2,1,0:T(8,128)(2,1)S(1)}, bf16[4,192,128]{2,1,0:T(8,128)(2,1)S(1)}, u32[]{:S(2)}, u32[]{:S(2)}) collective-permute-start(bf16[4,192,128]{2,1,0:T(8,128)(2,1)S(1)} %pad_maximum_fusion.set_ref), channel_id=1, source_target_pairs={{0,8},{4,12},{8,0},{12,4},{1,9},{5,13},{9,1},{13,5},{2,10},{6,14},... | collective-permute-start | bytes 589832 | tf_op jit(solution)/shard_map/ppermute | solution.py:469
  13.4 6.1 %collective-permute-start.3 = (bf16[4,192,128]{2,1,0:T(8,128)(2,1)S(1)}, bf16[4,192,128]{2,1,0:T(8,128)(2,1)S(1)}, u32[]{:S(2)}, u32[]{:S(2)}) collective-permute-start(bf16[4,192,128]{2,1,0:T(8,128)(2,1)S(1)} %pad_maximum_fusion.set_ref), channel_id=1, source_target_pairs={{0,4},{4,0},{8,12},{12,8},{1,5},{5,1},{9,13},{13,9},{2,6},{6,2},{1... | collective-permute-start | bytes 589832 | tf_op jit(solution)/shard_map/ppermute | solution.py:469
  17.7 2.7 %collective-permute-start.5 = (bf16[4,192,128]{2,1,0:T(8,128)(2,1)S(1)}, bf16[4,192,128]{2,1,0:T(8,128)(2,1)S(1)}, u32[]{:S(2)}, u32[]{:S(2)}) collective-permute-start(bf16[4,192,128]{2,1,0:T(8,128)(2,1)S(1)} %collective-permute-done.4.set_ref), channel_id=1, source_target_pairs={{0,4},{4,0},{8,12},{12,8},{1,5},{5,1},{9,13},{13,9},{2,6},{6,2},{1... | collective-permute-start | bytes 589832 | tf_op jit(solution)/shard_map/ppermute | solution.py:469

commit v4 on v3

--- a/solution.py
+++ b/solution.py
@@ -218,7 +218,14 @@
     out_ref[128:192, :] = pair_ref[...].astype(F32).reshape(64, 128).astype(BF)
 
 
-def weights_kernel(gain_ref, offset_ref, first_ref, second_ref, final_ref, norm_out, back_out, final_out, scr):
+def weights_kernel(*refs):
+    sources, (norm_out, back_out, final_out), held, scr, sems = refs[:5], refs[5:8], refs[8:13], refs[13], refs[14]
+    copies = [pltpu.make_async_copy(sources[k], held[k], sems.at[k]) for k in range(5)]
+    for copy in copies:
+        copy.start()
+    for copy in copies:
+        copy.wait()
+    gain_ref, offset_ref, first_ref, second_ref, final_ref = held
     norm_out[...] = jnp.concatenate(
         [
             jnp.concatenate([ref[...]] * 2, axis=1)
@@ -241,19 +248,20 @@
 
 
 def stage_kernel(
-    n_col, a, place_ref, set_ref, norm_ref, back_ref, final_ref,
+    n_col, a, place_ref, even_ref, odd_ref, norm_ref, back_ref, final_ref,
     rhs_out, left_out, leftt_out, rightt_out, grad_out, pair_out, found_out, *own_out
 ):
     place = place_ref[0]
+    blocks = [(even_ref, odd_ref)[b % 2].at[b // 2] for b in range(n_col)]
     for b in range(n_col):
         at = pl.multiple_of(lax.bitwise_xor(place, b) * 8, 8)
-        pair_out[:, pl.ds(at, 8), :] = set_ref[b, 128:192, :].astype(F32).reshape(8, 8, 128)
+        pair_out[:, pl.ds(at, 8), :] = blocks[b][128:192, :].astype(F32).reshape(8, 8, 128)
 
     gain = norm_ref[0:1, :]
     offset = norm_ref[1:2, :]
     averager = averager_of()
     x = jnp.concatenate(
-        [set_ref[b, 32 * g : 32 * g + 32, :] for g in range(4) for b in range(n_col)], axis=0
+        [blocks[b][32 * g : 32 * g + 32, :] for g in range(4) for b in range(n_col)], axis=0
     )
     mean = mm(x, averager)
     present = mean < ABSENT / 2
@@ -434,6 +442,7 @@
     shape = lambda *dims: jax.ShapeDtypeStruct(dims, F32)
     held = lambda *dims: pltpu.VMEM(dims, F32)
     held_bf = lambda *dims: pltpu.VMEM(dims, BF)
+    hbm = pl.BlockSpec(memory_space=pltpu.HBM)
     place = lax.bitwise_xor(lax.axis_index("row"), lax.axis_index("col"))
     place = place.astype(jnp.int32).reshape(1)
     packed = pl.pallas_call(
@@ -442,15 +451,21 @@
         in_specs=vmem(3),
         out_specs=vmem(1)[0],
     )(homolog_embedding, presence_indicator.T, coupling_change_derivative)
-    pieces = [packed] + [
-        lax.ppermute(packed, "col", [(k, k ^ b) for k in range(n_col)]) for b in range(1, n_col)
-    ]
+    far = lax.ppermute(packed, "col", [(k, k ^ 2) for k in range(n_col)])
     weights = pl.pallas_call(
         weights_kernel,
         out_shape=(held(8, 128), held_bf(256, 256), held_bf(width * width, 128)),
-        in_specs=vmem(5),
+        in_specs=[hbm] * 5,
         out_specs=tuple(vmem(3)),
-        scratch_shapes=[pltpu.VMEM((width * width, 128), F32)],
+        scratch_shapes=[
+            pltpu.VMEM((1, features), F32),
+            pltpu.VMEM((1, features), F32),
+            pltpu.VMEM((width, features), BF),
+            pltpu.VMEM((width, features), BF),
+            pltpu.VMEM((width * width, 128), BF),
+            pltpu.VMEM((width * width, 128), F32),
+            pltpu.SemaphoreType.DMA((5,)),
+        ],
         compiler_params=LIMIT,
     )(
         standardizer_scale.reshape(1, features),
@@ -459,17 +474,19 @@
         second_t,
         final_projection_matrix,
     )
-    pieces, weights = lax.optimization_barrier((pieces, weights))
+    far, weights = lax.optimization_barrier((far, weights))
     norm, back, final_turned = weights
 
-    sets = {0: jnp.stack(pieces)}
-    step = n_row // 2
-    while step:
-        for a, block in sorted(sets.items()):
-            sets[a ^ step] = lax.ppermute(block, "row", [(k, k ^ step) for k in range(n_row)])
-        step //= 2
-
-    def stage(a):
+    def over(axis, size, step, array):
+        return lax.ppermute(array, axis, [(k, k ^ step) for k in range(size)])
+
+    even = jnp.stack([packed, far])
+    odd = over("col", n_col, 1, even)
+    chip_even = over("row", n_row, 2, even)
+    chip_odd = over("row", n_row, 2, odd)
+    core = over("row", n_row, 1, jnp.stack([even, odd]))
+
+    def stage(a, even, odd):
         outs = [
             held_bf(512, 256), held_bf(128, 256), held_bf(256, 128), held(256, 128),
             held_bf(256, 1024), held(8, 32, 128), held(128, 128),
@@ -479,17 +496,21 @@
         return pl.pallas_call(
             functools.partial(stage_kernel, n_col, a),
             out_shape=tuple(outs),
-            in_specs=[pl.BlockSpec(memory_space=pltpu.SMEM)] + vmem(4),
+            in_specs=[pl.BlockSpec(memory_space=pltpu.SMEM)] + vmem(5),
             out_specs=tuple(vmem(len(outs))),
             compiler_params=LIMIT,
             cost_estimate=pl.CostEstimate(
                 flops=1_000_000_000, bytes_accessed=4_000_000, transcendentals=0
             ),
-        )(place, sets[a], norm, back, final_turned)
-
-    stages = [stage(a) for a in range(n_row)]
+        )(place, even, odd, norm, back, final_turned)
+
+    own_stage = stage(0, even, odd)
+    core_stage = stage(1, core[0], core[1])
+    chip = jnp.stack([chip_even, chip_odd])
+    chip, own_stage, core_stage = lax.optimization_barrier((chip, own_stage, core_stage))
+    both = over("row", n_row, 1, chip)
+    stages = [own_stage, core_stage, stage(2, chip[0], chip[1]), stage(3, both[0], both[1])]
     own = stages[0][7:]
-    hbm = pl.BlockSpec(memory_space=pltpu.HBM)
     outs = pl.pallas_call(
         functools.partial(part_kernel, n_row),
         out_shape=(

time: 27.4 us -> 27.1 us (0.989)
  waiting for transfers between devices: 6.63 us -> 4.68 us
  starting transfers between devices: 7.32 us -> 8.88 us
    ppermute x6, waiting for transfers between devices: 6.63 us -> 4.68 us  [the longest x5 4.14 us: over(): return lax.ppermute(array, axis, [(k, k ^ step) for k in range(size)])]
    ppermute x6, starting transfers between devices: 7.32 us -> 8.88 us  [the longest x5 4.78 us: over(): return lax.ppermute(array, axis, [(k, k ^ step) for k in range(size)])]
  transfers between devices with their start and end apart: 6 -> 6, of which waited for: 2 -> 4; matrix products, arithmetic and copies ran while one was open for 0% -> 0% of each run, Pallas kernels for 11% -> 8%
where the time goes in v4:
time: 27.1 us; the launch traced here: 26.9 us
  Pallas kernels  10.9 us (40%)
  starting transfers between devices  8.88 us (33%)
  waiting for transfers between devices  4.68 us (17%)
  local copies, waits for them, and re-layouts  1.66 us (6%)
  between operations  0.76 us (3%)
    pallas_call x1, Pallas kernels, gathered_body(): pl.pallas_call(functools.partial(part_kernel, n_row), out_shape=(shape(sh...  5.79 us
    ppermute x5, starting transfers between devices, over(): return lax.ppermute(array, axis, [(k, k ^ step) for k in range(size)])  4.78 us
    ppermute x5, waiting for transfers between devices, over(): return lax.ppermute(array, axis, [(k, k ^ step) for k in range(size)])  4.14 us
    ppermute x1, starting transfers between devices, gathered_body(): far = lax.ppermute(packed, 'col', [(k, k ^ 2) for k in range(n_col)])  4.1 us
    pallas_call x4, Pallas kernels, stage(): pl.pallas_call(functools.partial(stage_kernel, n_col, a), out_shape=tuple...  3.63 us
    unnamed x10, local copies, waits for them, and re-layouts  1.62 us
    pallas_call x1, Pallas kernels, gathered_body(): pl.pallas_call(pack_kernel, out_shape=held_bf(192, 128), in_specs=vmem(3)...  1.05 us
    ppermute x1, waiting for transfers between devices, gathered_body(): far = lax.ppermute(packed, 'col', [(k, k ^ 2) for k in range(n_col)])  0.54 us
  transfers between devices with their start and end apart: 6, of which 4 were waited for; matrix products, arithmetic and copies ran while one was open for 0% of the time, Pallas kernels for 8%

profile of v4, /device:TPU:0, one launch (start us, length us, event | category | flops | bytes accessed | tf_op | source)
XLA Modules:
  0.0 26.9 jit_solution(14372258631713436903)
XLA Ops:
  0.6 0.0 copy-start.1
  0.6 0.0 copy-start.2
  0.7 1.0 %shard_map.135 = bf16[192,128]{1,0:T(8,128)(2,1)S(1)} custom-call(bf16[32,8,64]{2,1,0:T(8,128)(2,1)} %msa_ref.1, s32[8,32]{1,0:T(8,128)} %bitcast.41, bf16[8,8,128]{2,1,0:T(8,128)(2,1)} %pair_ref.1), custom_call_target="tpu_custom_call" | custom-call | tf_op jit(solution)/shard_map/pallas_call | solution.py:448
  1.7 4.1 %collective-permute-start = (bf16[192,128]{1,0:T(8,128)(2,1)S(1)}, bf16[192,128]{1,0:T(8,128)(2,1)S(1)}, u32[]{:S(2)}, u32[]{:S(2)}) collective-permute-start(bf16[192,128]{1,0:T(8,128)(2,1)S(1)} %shard_map.135), channel_id=1, source_target_pairs={{0,2},{1,3},{2,0},{3,1},{4,6},{5,7},{6,4},{7,5},{8,10},{9,11},{10,... | collective-permute-start | bytes 147464 | tf_op jit(solution)/shard_map/ppermute | solution.py:454
  5.8 0.0 copy-start.3
  5.8 0.0 copy-start.4
  5.8 0.0 copy-done.1
  5.8 0.0 copy-done.2
  5.8 0.6 %copy-done.3 = f32[64]{0:T(128)S(1)} copy-done((f32[64]{0:T(128)S(1)}, f32[64]{0:T(128)}, u32[]{:S(2)}) %copy-start.3) | copy-done | bytes 280
  6.5 0.0 copy-done.4
  6.5 0.0 copy-start
  6.5 0.9 %copy-done = bf16[1024,128]{1,0:T(8,128)(2,1)S(1)} copy-done((bf16[1024,128]{1,0:T(8,128)(2,1)S(1)}, bf16[1024,128]{1,0:T(8,128)(2,1)}, u32[]{:S(2)}) %copy-start) | copy-done | bytes 262168
  7.4 0.4 %shard_map.136 = (f32[8,128]{1,0:T(8,128)S(1)}, bf16[256,256]{1,0:T(8,128)(2,1)S(1)}, bf16[1024,128]{1,0:T(8,128)(2,1)S(1)}) custom-call(f32[1,64]{1,0:T(1,128)S(1)} %bitcast.36, f32[1,64]{1,0:T(1,128)S(1)} %bitcast.37, bf16[32,64]{1,0:T(8,128)(2,1)S(1)} %bitcast.32, bf16[32,64]{1,0:T(8,128)(2,1)S(1)} %bitcast.34, bf16[1024,128]{1,0:T(8,128)(2,1)S(1)} %copy-done), custom_call_target="tpu_custom_call" | custom-call | tf_op jit(solution)/shard_map/pallas_call | solution.py:455
  7.9 0.5 %collective-permute-done = bf16[192,128]{1,0:T(8,128)(2,1)S(1)} collective-permute-done((bf16[192,128]{1,0:T(8,128)(2,1)S(1)}, bf16[192,128]{1,0:T(8,128)(2,1)S(1)}, u32[]{:S(2)}, u32[]{:S(2)}) %collective-permute-start) | collective-permute-done | bytes 49184 | tf_op jit(solution)/shard_map/ppermute | solution.py:454
  8.4 1.4 %collective-permute-start.2 = (bf16[2,192,128]{2,1,0:T(8,128)(2,1)S(1)}, bf16[2,192,128]{2,1,0:T(8,128)(2,1)S(1)}, u32[]{:S(2)}, u32[]{:S(2)}) collective-permute-start(bf16[2,192,128]{2,1,0:T(8,128)(2,1)S(1)} %get-tuple-element.136.even_ref), channel_id=1, source_target_pairs={{0,1},{1,0},{2,3},{3,2},{4,5},{5,4},{6,7},{7,6},{8,9},{9,8},{10,11... | collective-permute-start | bytes 294920 | tf_op jit(solution)/shard_map/ppermute | solution.py:481
  9.9 1.5 %collective-permute-start.1 = (bf16[2,192,128]{2,1,0:T(8,128)(2,1)S(1)}, bf16[2,192,128]{2,1,0:T(8,128)(2,1)S(1)}, u32[]{:S(2)}, u32[]{:S(2)}) collective-permute-start(bf16[2,192,128]{2,1,0:T(8,128)(2,1)S(1)} %get-tuple-element.136.even_ref), channel_id=1, source_target_pairs={{0,8},{4,12},{8,0},{12,4},{1,9},{5,13},{9,1},{13,5},{2,10},{6,14},... | collective-permute-start | bytes 294920 | tf_op jit(solution)/shard_map/ppermute | solution.py:481
  11.4 1.7 %collective-permute-done.2.odd_ref = bf16[2,192,128]{2,1,0:T(8,128)(2,1)S(1)} collective-permute-done((bf16[2,192,128]{2,1,0:T(8,128)(2,1)S(1)}, bf16[2,192,128]{2,1,0:T(8,128)(2,1)S(1)}, u32[]{:S(2)}, u32[]{:S(2)}) %collective-permute-start.2) | collective-permute-done | bytes 98336 | tf_op jit(solution)/shard_map/ppermute | solution.py:481
  13.1 1.7 %collective-permute-start.3 = (bf16[2,192,128]{2,1,0:T(8,128)(2,1)S(1)}, bf16[2,192,128]{2,1,0:T(8,128)(2,1)S(1)}, u32[]{:S(2)}, u32[]{:S(2)}) collective-permute-start(bf16[2,192,128]{2,1,0:T(8,128)(2,1)S(1)} %collective-permute-done.2.odd_ref), channel_id=1, source_target_pairs={{0,8},{4,12},{8,0},{12,4},{1,9},{5,13},{9,1},{13,5},{2,10},{6,14},... | collective-permute-start | bytes 294920 | tf_op jit(solution)/shard_map/ppermute | solution.py:481
  14.8 0.1 collective-permute-start.4
  14.9 0.9 %shard_map.137 = (bf16[512,256]{1,0:T(8,128)(2,1)S(1)}, bf16[128,256]{1,0:T(8,128)(2,1)S(1)}, bf16[256,128]{1,0:T(8,128)(2,1)S(1)}, f32[256,128]{1,0:T(8,128)S(1...) custom-call(s32[1]{0:T(128)} %bitcast.9.place_ref, ...), custom_call_target="tpu_custom_call" | custom-call | flops 1000000000 | bytes 4000000 | tf_op jit(solution)/shard_map/pallas_call | solution.py:496
  15.8 0.0 collective-permute-done.1
  15.8 1.9 %collective-permute-done.3 = bf16[2,192,128]{2,1,0:T(8,128)(2,1)S(1)} collective-permute-done((bf16[2,192,128]{2,1,0:T(8,128)(2,1)S(1)}, bf16[2,192,128]{2,1,0:T(8,128)(2,1)S(1)}, u32[]{:S(2)}, u32[]{:S(2)}) %collective-permute-start.3) | collective-permute-done | bytes 98336 | tf_op jit(solution)/shard_map/ppermute | solution.py:481
  17.7 0.0 collective-permute-done.4
  17.8 0.9 %shard_map.138 = (bf16[512,256]{1,0:T(8,128)(2,1)S(1)}, bf16[128,256]{1,0:T(8,128)(2,1)S(1)}, bf16[256,128]{1,0:T(8,128)(2,1)S(1)}, f32[256,128]{1,0:T(8,128)S(1...) custom-call(s32[1]{0:T(128)} %bitcast.9.place_ref, ...), custom_call_target="tpu_custom_call" | custom-call | flops 1000000000 | bytes 4000000 | tf_op jit(solution)/shard_map/pallas_call | solution.py:496
  18.7 0.1 collective-permute-start.5
  18.8 0.9 %shard_map.139 = (bf16[512,256]{1,0:T(8,128)(2,1)S(1)}, bf16[128,256]{1,0:T(8,128)(2,1)S(1)}, bf16[256,128]{1,0:T(8,128)(2,1)S(1)}, f32[256,128]{1,0:T(8,128)S(1...) custom-call(s32[1]{0:T(128)} %bitcast.9.place_ref, ...), custom_call_target="tpu_custom_call" | custom-call | flops 1000000000 | bytes 4000000 | tf_op jit(solution)/shard_map/pallas_call | solution.py:496
  19.7 0.5 %collective-permute-done.5 = bf16[2,2,192,128]{3,2,1,0:T(8,128)(2,1)S(1)} collective-permute-done((bf16[2,2,192,128]{3,2,1,0:T(8,128)(2,1)S(1)}, bf16[2,2,192,128]{3,2,1,0:T(8,128)(2,1)S(1)}, u32[]{:S(2)}, u32[]{:S(2)}) %collective-permute-start.5) | collective-permute-done | bytes 196640 | tf_op jit(solution)/shard_map/ppermute | solution.py:481
  20.2 0.9 %shard_map.140 = (bf16[512,256]{1,0:T(8,128)(2,1)S(1)}, bf16[128,256]{1,0:T(8,128)(2,1)S(1)}, bf16[256,128]{1,0:T(8,128)(2,1)S(1)}, f32[256,128]{1,0:T(8,128)S(1...) custom-call(s32[1]{0:T(128)} %bitcast.9.place_ref, ...), custom_call_target="tpu_custom_call" | custom-call | flops 1000000000 | bytes 4000000 | tf_op jit(solution)/shard_map/pallas_call | solution.py:496
  21.1 5.8 %shard_map.141 = (f32[32,8,64]{2,1,0:T(8,128)}, f32[1024,128]{1,0:T(8,128)}, f32[32,64]{1,0:T(8,128)}, f32[32,64]{1,0:T(8,128)}, f32[1,64]{1,0:T(1,128)}, /*index=5*/f32[1,64]{1,0:T(1,128)}, f32[1,128]{1,0:T(1,128)}) custom-call(bf16[512,256]{1,0:T(8,128)(2,1)S(1)} %get-tuple-element.91.refs_0_, bf16[128,256]{1,0:T(8,128)(2,1)S(1)} %get-tuple-element.92.refs_1_, ...), custom_call_target="tpu_custom_call" | custom-call | tf_op jit(solution)/shard_map/pallas_call | solution.py:514
  (6 shorter events, 0.1 us)
Async XLA Ops:
  0.6 5.2 %copy-start.1 = (bf16[64,32]{0,1:T(8,128)(2,1)S(1)}, bf16[64,32]{0,1:T(8,128)(2,1)}, u32[]{:S(2)}) copy-start(bf16[64,32]{0,1:T(8,128)(2,1)} %param.13) | copy-start | bytes 12292
  0.6 5.2 %copy-start.2 = (bf16[64,32]{0,1:T(8,128)(2,1)S(1)}, bf16[64,32]{0,1:T(8,128)(2,1)}, u32[]{:S(2)}) copy-start(bf16[64,32]{0,1:T(8,128)(2,1)} %param.14) | copy-start | bytes 12292
  1.7 6.7 %collective-permute-start = (bf16[192,128]{1,0:T(8,128)(2,1)S(1)}, bf16[192,128]{1,0:T(8,128)(2,1)S(1)}, u32[]{:S(2)}, u32[]{:S(2)}) collective-permute-start(bf16[192,128]{1,0:T(8,128)(2,1)S(1)} %shard_map.135), channel_id=1, source_target_pairs={{0,2},{1,3},{2,0},{3,1},{4,6},{5,7},{6,4},{7,5},{8,10},{9,11},{10,... | collective-permute-start | bytes 147464 | tf_op jit(solution)/shard_map/ppermute | solution.py:454
  5.8 0.7 %copy-start.3 = (f32[64]{0:T(128)S(1)}, f32[64]{0:T(128)}, u32[]{:S(2)}) copy-start(f32[64]{0:T(128)} %param.11) | copy-start | bytes 772
  5.8 0.7 %copy-start.4 = (f32[64]{0:T(128)S(1)}, f32[64]{0:T(128)}, u32[]{:S(2)}) copy-start(f32[64]{0:T(128)} %param.12) | copy-start | bytes 772
  6.5 0.9 %copy-start = (bf16[1024,128]{1,0:T(8,128)(2,1)S(1)}, bf16[1024,128]{1,0:T(8,128)(2,1)}, u32[]{:S(2)}) copy-start(bf16[1024,128]{1,0:T(8,128)(2,1)} %refs_4_.1) | copy-start | bytes 786436
  8.4 4.7 %collective-permute-start.2 = (bf16[2,192,128]{2,1,0:T(8,128)(2,1)S(1)}, bf16[2,192,128]{2,1,0:T(8,128)(2,1)S(1)}, u32[]{:S(2)}, u32[]{:S(2)}) collective-permute-start(bf16[2,192,128]{2,1,0:T(8,128)(2,1)S(1)} %get-tuple-element.136.even_ref), channel_id=1, source_target_pairs={{0,1},{1,0},{2,3},{3,2},{4,5},{5,4},{6,7},{7,6},{8,9},{9,8},{10,11... | collective-permute-start | bytes 294920 | tf_op jit(solution)/shard_map/ppermute | solution.py:481
  9.9 6.0 %collective-permute-start.1 = (bf16[2,192,128]{2,1,0:T(8,128)(2,1)S(1)}, bf16[2,192,128]{2,1,0:T(8,128)(2,1)S(1)}, u32[]{:S(2)}, u32[]{:S(2)}) collective-permute-start(bf16[2,192,128]{2,1,0:T(8,128)(2,1)S(1)} %get-tuple-element.136.even_ref), channel_id=1, source_target_pairs={{0,8},{4,12},{8,0},{12,4},{1,9},{5,13},{9,1},{13,5},{2,10},{6,14},... | collective-permute-start | bytes 294920 | tf_op jit(solution)/shard_map/ppermute | solution.py:481
  13.1 4.6 %collective-permute-start.3 = (bf16[2,192,128]{2,1,0:T(8,128)(2,1)S(1)}, bf16[2,192,128]{2,1,0:T(8,128)(2,1)S(1)}, u32[]{:S(2)}, u32[]{:S(2)}) collective-permute-start(bf16[2,192,128]{2,1,0:T(8,128)(2,1)S(1)} %collective-permute-done.2.odd_ref), channel_id=1, source_target_pairs={{0,8},{4,12},{8,0},{12,4},{1,9},{5,13},{9,1},{13,5},{2,10},{6,14},... | collective-permute-start | bytes 294920 | tf_op jit(solution)/shard_map/ppermute | solution.py:481
  14.8 2.9 %collective-permute-start.4 = (bf16[2,2,192,128]{3,2,1,0:T(8,128)(2,1)S(1)}, bf16[2,2,192,128]{3,2,1,0:T(8,128)(2,1)S(1)}, u32[]{:S(2)}, u32[]{:S(2)}) collective-permute-start(bf16[2,2,192,128]{3,2,1,0:T(8,128)(2,1)S(1)} %pad_maximum_fusion.1), channel_id=1, source_target_pairs={{0,4},{4,0},{8,12},{12,8},{1,5},{5,1},{9,13},{13,9},{2,6},{6,2},{1... | collective-permute-start | bytes 589832 | tf_op jit(solution)/shard_map/ppermute | solution.py:481
  18.7 1.5 %collective-permute-start.5 = (bf16[2,2,192,128]{3,2,1,0:T(8,128)(2,1)S(1)}, bf16[2,2,192,128]{3,2,1,0:T(8,128)(2,1)S(1)}, u32[]{:S(2)}, u32[]{:S(2)}) collective-permute-start(bf16[2,2,192,128]{3,2,1,0:T(8,128)(2,1)S(1)} %pad_maximum_fusion), channel_id=1, source_target_pairs={{0,4},{4,0},{8,12},{12,8},{1,5},{5,1},{9,13},{13,9},{2,6},{6,2},{1... | collective-permute-start | bytes 589832 | tf_op jit(solution)/shard_map/ppermute | solution.py:481

commit v5 on v4

--- a/solution.py
+++ b/solution.py
@@ -248,20 +248,20 @@
 
 
 def stage_kernel(
-    n_col, a, place_ref, even_ref, odd_ref, norm_ref, back_ref, final_ref,
-    rhs_out, left_out, leftt_out, rightt_out, grad_out, pair_out, found_out, *own_out
+    n_col, a, place_ref, set_ref, norm_ref, back_ref, final_ref,
+    rhs_out, left_out, leftt_out, rightt_out, grad_out, pair_out, found_out, *rest
 ):
+    *own_out, turn_scr = rest
     place = place_ref[0]
-    blocks = [(even_ref, odd_ref)[b % 2].at[b // 2] for b in range(n_col)]
     for b in range(n_col):
         at = pl.multiple_of(lax.bitwise_xor(place, b) * 8, 8)
-        pair_out[:, pl.ds(at, 8), :] = blocks[b][128:192, :].astype(F32).reshape(8, 8, 128)
+        pair_out[:, pl.ds(at, 8), :] = set_ref[b, 128:192, :].astype(F32).reshape(8, 8, 128)
 
     gain = norm_ref[0:1, :]
     offset = norm_ref[1:2, :]
     averager = averager_of()
     x = jnp.concatenate(
-        [blocks[b][32 * g : 32 * g + 32, :] for g in range(4) for b in range(n_col)], axis=0
+        [set_ref[b, 32 * g : 32 * g + 32, :] for g in range(4) for b in range(n_col)], axis=0
     )
     mean = mm(x, averager)
     present = mean < ABSENT / 2
@@ -289,7 +289,10 @@
         left_out[:, at] = mm_nt(masked, back_ref[:128, :]).astype(BF)
         both = mm_nt(back_ref[...], masked)
         leftt_out[at, :] = both[:128].astype(BF)
-        rightt_out[at, :] = both[128:]
+        turn_scr[at, :] = both[128:]
+
+    for e in range(32):
+        rightt_out[e] = turn_scr[pl.ds(e, 8, stride=32), :]
 
     grad = mm_nt(final_ref[...], pair_out[...].reshape(256, 128).astype(BF)).astype(BF)
     for q in range(8):
@@ -316,10 +319,10 @@
     mask = jnp.where((lane % 2 == 0) == (lane < 64), found, turned)
     mask_t = mask.T
 
-    for a, stage in enumerate(stages):
-        wide_scr[256 * a : 256 * a + 256, :] = stage[3][...]
     for e in range(32):
-        right_scr[32 * e : 32 * e + 32, :] = wide_scr[pl.ds(e, 32, stride=32), :].astype(BF)
+        right_scr[32 * e : 32 * e + 32, :] = jnp.concatenate(
+            [stage[3][e] for stage in stages], axis=0
+        ).astype(BF)
 
     bias = jnp.zeros((1, 128), F32)
     ones = jnp.ones((128, 128), BF)
@@ -349,14 +352,13 @@
     final_send.start()
 
     mask_bf = mask.astype(BF)
-    share = 1.0 / (mm_tn(mask_bf, mask_bf)[0:32] + 0.001)
+    share = (1.0 / (mm_tn(mask_bf, mask_bf)[0:32] + 0.001)).astype(BF)
     for i in range(32):
         a, at = i // 8, 32 * (i % 8)
         for q in range(8):
-            block = stages[a][4][at : at + 32, 128 * q : 128 * q + 128].astype(F32)
             grad_scr[32 * i : 32 * i + 32, 128 * q : 128 * q + 128] = (
-                block * share[i : i + 1]
-            ).astype(BF)
+                stages[a][4][at : at + 32, 128 * q : 128 * q + 128] * share[i : i + 1]
+            )
     left_grad = mm(grad_scr[...], right_scr[...])
     left = jnp.concatenate([stage[1][...] for stage in stages], axis=1)
     right_grad = mm(left, grad_scr[...])
@@ -451,7 +453,10 @@
         in_specs=vmem(3),
         out_specs=vmem(1)[0],
     )(homolog_embedding, presence_indicator.T, coupling_change_derivative)
-    far = lax.ppermute(packed, "col", [(k, k ^ 2) for k in range(n_col)])
+    def over(axis, size, step, array):
+        return lax.ppermute(array, axis, [(k, k ^ step) for k in range(size)])
+
+    pieces = [packed] + [over("col", n_col, b, packed) for b in range(1, n_col)]
     weights = pl.pallas_call(
         weights_kernel,
         out_shape=(held(8, 128), held_bf(256, 256), held_bf(width * width, 128)),
@@ -474,21 +479,15 @@
         second_t,
         final_projection_matrix,
     )
-    far, weights = lax.optimization_barrier((far, weights))
+    pieces, weights = lax.optimization_barrier((pieces, weights))
     norm, back, final_turned = weights
-
-    def over(axis, size, step, array):
-        return lax.ppermute(array, axis, [(k, k ^ step) for k in range(size)])
-
-    even = jnp.stack([packed, far])
-    odd = over("col", n_col, 1, even)
-    chip_even = over("row", n_row, 2, even)
-    chip_odd = over("row", n_row, 2, odd)
-    core = over("row", n_row, 1, jnp.stack([even, odd]))
-
-    def stage(a, even, odd):
+    own = jnp.stack(pieces)
+    chip = over("row", n_row, 2, own)
+    core = over("row", n_row, 1, own)
+
+    def stage(a, block):
         outs = [
-            held_bf(512, 256), held_bf(128, 256), held_bf(256, 128), held(256, 128),
+            held_bf(512, 256), held_bf(128, 256), held_bf(256, 128), held(width, 8, 128),
             held_bf(256, 1024), held(8, 32, 128), held(128, 128),
         ]
         if a == 0:
@@ -496,21 +495,21 @@
         return pl.pallas_call(
             functools.partial(stage_kernel, n_col, a),
             out_shape=tuple(outs),
-            in_specs=[pl.BlockSpec(memory_space=pltpu.SMEM)] + vmem(5),
+            in_specs=[pl.BlockSpec(memory_space=pltpu.SMEM)] + vmem(4),
             out_specs=tuple(vmem(len(outs))),
+            scratch_shapes=[pltpu.VMEM((256, 128), F32)],
             compiler_params=LIMIT,
             cost_estimate=pl.CostEstimate(
                 flops=1_000_000_000, bytes_accessed=4_000_000, transcendentals=0
             ),
-        )(place, even, odd, norm, back, final_turned)
-
-    own_stage = stage(0, even, odd)
-    core_stage = stage(1, core[0], core[1])
-    chip = jnp.stack([chip_even, chip_odd])
+        )(place, block, norm, back, final_turned)
+
+    own_stage = stage(0, own)
+    core_stage = stage(1, core)
     chip, own_stage, core_stage = lax.optimization_barrier((chip, own_stage, core_stage))
     both = over("row", n_row, 1, chip)
-    stages = [own_stage, core_stage, stage(2, chip[0], chip[1]), stage(3, both[0], both[1])]
-    own = stages[0][7:]
+    stages = [own_stage, core_stage, stage(2, chip), stage(3, both)]
+    own_norm = stages[0][7:]
     outs = pl.pallas_call(
         functools.partial(part_kernel, n_row),
         out_shape=(
@@ -537,7 +536,7 @@
             pltpu.SemaphoreType.DMA,
         ],
         compiler_params=LIMIT,
-    )(*[x for s in stages for x in s[:7]], *own, norm, back, first_t, second_t)
+    )(*[x for s in stages for x in s[:7]], *own_norm, norm, back, first_t, second_t)
     emb, final, first, second, gain, offset, bias = outs
     return emb, final, first.T, second.T, gain.reshape(-1), offset.reshape(-1), bias.reshape(-1)
 

time: 27.1 us -> 27.5 us (1.015)
  waiting for transfers between devices: 4.68 us -> 6.63 us
  starting transfers between devices: 8.88 us -> 7.39 us
    ppermute x1 -> x0, starting transfers between devices: 4.1 us -> none  [gathered_body(): far = lax.ppermute(packed, 'col', [(k, k ^ 2) for k in range(n_col)])]
    ppermute x5 -> x6, starting transfers between devices: 4.78 us -> 7.39 us  [over(): return lax.ppermute(array, axis, [(k, k ^ step) for k in range(size)])]
    ppermute x5 -> x6, waiting for transfers between devices: 4.14 us -> 6.63 us  [over(): return lax.ppermute(array, axis, [(k, k ^ step) for k in range(size)])]
    ppermute x1 -> x0, waiting for transfers between devices: 0.54 us -> none  [gathered_body(): far = lax.ppermute(packed, 'col', [(k, k ^ 2) for k in range(n_col)])]
  transfers between devices with their start and end apart: 6 -> 6, of which waited for: 4 -> 3; matrix products, arithmetic and copies ran while one was open for 0% -> 0% of each run, Pallas kernels for 8% -> 12%
where the time goes in v5:
time: 27.5 us; the launch traced here: 27.2 us
  Pallas kernels  10.9 us (40%)
  starting transfers between devices  7.39 us (27%)
  waiting for transfers between devices  6.63 us (24%)
  local copies, waits for them, and re-layouts  1.62 us (6%)
  between operations  0.72 us (3%)
    ppermute x6, starting transfers between devices, over(): return lax.ppermute(array, axis, [(k, k ^ step) for k in range(size)])  7.39 us
    ppermute x6, waiting for transfers between devices, over(): return lax.ppermute(array, axis, [(k, k ^ step) for k in range(size)])  6.63 us
    pallas_call x1, Pallas kernels, gathered_body(): pl.pallas_call(functools.partial(part_kernel, n_row), out_shape=(shape(sh...  5.61 us
    pallas_call x4, Pallas kernels, stage(): pl.pallas_call(functools.partial(stage_kernel, n_col, a), out_shape=tuple...  3.78 us
    unnamed x10, local copies, waits for them, and re-layouts  1.62 us
    pallas_call x1, Pallas kernels, gathered_body(): pl.pallas_call(pack_kernel, out_shape=held_bf(192, 128), in_specs=vmem(3)...  1.05 us
  transfers between devices with their start and end apart: 6, of which 3 were waited for; matrix products, arithmetic and copies ran while one was open for 0% of the time, Pallas kernels for 12%

profile of v5, /device:TPU:0, one launch (start us, length us, event | category | flops | bytes accessed | tf_op | source)
XLA Modules:
  0.0 27.2 jit_solution(11051450254254069019)
XLA Ops:
  0.6 0.0 copy-start.1
  0.6 0.0 copy-start.2
  0.7 1.0 %shard_map.135 = bf16[192,128]{1,0:T(8,128)(2,1)S(1)} custom-call(bf16[32,8,64]{2,1,0:T(8,128)(2,1)} %msa_ref.1, s32[8,32]{1,0:T(8,128)} %bitcast.25, bf16[8,8,128]{2,1,0:T(8,128)(2,1)} %pair_ref.1), custom_call_target="tpu_custom_call" | custom-call | tf_op jit(solution)/shard_map/pallas_call | solution.py:450
  1.7 5.1 %collective-permute-start.2 = (bf16[192,128]{1,0:T(8,128)(2,1)S(1)}, bf16[192,128]{1,0:T(8,128)(2,1)S(1)}, u32[]{:S(2)}, u32[]{:S(2)}) collective-permute-start(bf16[192,128]{1,0:T(8,128)(2,1)S(1)} %shard_map.135), channel_id=1, source_target_pairs={{0,3},{1,2},{2,1},{3,0},{4,7},{5,6},{6,5},{7,4},{8,11},{9,10},{10,... | collective-permute-start | bytes 147464 | tf_op jit(solution)/shard_map/ppermute | solution.py:457
  6.8 0.0 collective-permute-start.1
  6.8 0.6 %collective-permute-start = (bf16[192,128]{1,0:T(8,128)(2,1)S(1)}, bf16[192,128]{1,0:T(8,128)(2,1)S(1)}, u32[]{:S(2)}, u32[]{:S(2)}) collective-permute-start(bf16[192,128]{1,0:T(8,128)(2,1)S(1)} %shard_map.135), channel_id=1, source_target_pairs={{0,1},{1,0},{2,3},{3,2},{4,5},{5,4},{6,7},{7,6},{8,9},{9,8},{10,11... | collective-permute-start | bytes 147464 | tf_op jit(solution)/shard_map/ppermute | solution.py:457
  7.5 0.0 copy-start.3
  7.5 0.0 copy-start.4
  7.5 0.0 copy-done.1
  7.5 0.0 copy-done.2
  7.5 0.6 %copy-done.3 = f32[64]{0:T(128)S(1)} copy-done((f32[64]{0:T(128)S(1)}, f32[64]{0:T(128)}, u32[]{:S(2)}) %copy-start.3) | copy-done | bytes 280
  8.1 0.0 copy-done.4
  8.1 0.0 copy-start
  8.1 0.9 %copy-done = bf16[1024,128]{1,0:T(8,128)(2,1)S(1)} copy-done((bf16[1024,128]{1,0:T(8,128)(2,1)S(1)}, bf16[1024,128]{1,0:T(8,128)(2,1)}, u32[]{:S(2)}) %copy-start) | copy-done | bytes 262168
  9.1 0.4 %shard_map.136 = (f32[8,128]{1,0:T(8,128)S(1)}, bf16[256,256]{1,0:T(8,128)(2,1)S(1)}, bf16[1024,128]{1,0:T(8,128)(2,1)S(1)}) custom-call(f32[1,64]{1,0:T(1,128)S(1)} %bitcast.20, f32[1,64]{1,0:T(1,128)S(1)} %bitcast.21, bf16[32,64]{1,0:T(8,128)(2,1)S(1)} %bitcast.16, bf16[32,64]{1,0:T(8,128)(2,1)S(1)} %bitcast.18, bf16[1024,128]{1,0:T(8,128)(2,1)S(1)} %copy-done), custom_call_target="tpu_custom_call" | custom-call | tf_op jit(solution)/shard_map/pallas_call | solution.py:460
  9.5 0.0 collective-permute-done.2
  9.5 2.3 %collective-permute-done.1 = bf16[192,128]{1,0:T(8,128)(2,1)S(1)} collective-permute-done((bf16[192,128]{1,0:T(8,128)(2,1)S(1)}, bf16[192,128]{1,0:T(8,128)(2,1)S(1)}, u32[]{:S(2)}, u32[]{:S(2)}) %collective-permute-start.1) | collective-permute-done | bytes 49184 | tf_op jit(solution)/shard_map/ppermute | solution.py:457
  11.8 0.0 collective-permute-done
  11.8 0.1 collective-permute-start.4
  11.9 1.6 %collective-permute-start.3 = (bf16[4,192,128]{2,1,0:T(8,128)(2,1)S(1)}, bf16[4,192,128]{2,1,0:T(8,128)(2,1)S(1)}, u32[]{:S(2)}, u32[]{:S(2)}) collective-permute-start(bf16[4,192,128]{2,1,0:T(8,128)(2,1)S(1)} %pad_maximum_fusion.set_ref), channel_id=1, source_target_pairs={{0,8},{4,12},{8,0},{12,4},{1,9},{5,13},{9,1},{13,5},{2,10},{6,14},... | collective-permute-start | bytes 589832 | tf_op jit(solution)/shard_map/ppermute | solution.py:457
  13.5 0.9 %shard_map.137 = (bf16[512,256]{1,0:T(8,128)(2,1)S(1)}, bf16[128,256]{1,0:T(8,128)(2,1)S(1)}, bf16[256,128]{1,0:T(8,128)(2,1)S(1)}, f32[32,8,128]{2,1,0:T(8,128)...) custom-call(s32[1]{0:T(128)} %bitcast.9.place_ref, ...), custom_call_target="tpu_custom_call" | custom-call | flops 1000000000 | bytes 4000000 | tf_op jit(solution)/shard_map/pallas_call | solution.py:495
  14.4 0.0 collective-permute-done.4.set_ref
  14.4 1.0 %shard_map.138 = (bf16[512,256]{1,0:T(8,128)(2,1)S(1)}, bf16[128,256]{1,0:T(8,128)(2,1)S(1)}, bf16[256,128]{1,0:T(8,128)(2,1)S(1)}, f32[32,8,128]{2,1,0:T(8,128)...) custom-call(s32[1]{0:T(128)} %bitcast.9.place_ref, ...), custom_call_target="tpu_custom_call" | custom-call | flops 1000000000 | bytes 4000000 | tf_op jit(solution)/shard_map/pallas_call | solution.py:495
  15.4 3.8 %collective-permute-done.3.set_ref = bf16[4,192,128]{2,1,0:T(8,128)(2,1)S(1)} collective-permute-done((bf16[4,192,128]{2,1,0:T(8,128)(2,1)S(1)}, bf16[4,192,128]{2,1,0:T(8,128)(2,1)S(1)}, u32[]{:S(2)}, u32[]{:S(2)}) %collective-permute-start.3) | collective-permute-done | bytes 196640 | tf_op jit(solution)/shard_map/ppermute | solution.py:457
  19.2 0.0 collective-permute-start.5
  19.2 0.9 %shard_map.139 = (bf16[512,256]{1,0:T(8,128)(2,1)S(1)}, bf16[128,256]{1,0:T(8,128)(2,1)S(1)}, bf16[256,128]{1,0:T(8,128)(2,1)S(1)}, f32[32,8,128]{2,1,0:T(8,128)...) custom-call(s32[1]{0:T(128)} %bitcast.9.place_ref, ...), custom_call_target="tpu_custom_call" | custom-call | flops 1000000000 | bytes 4000000 | tf_op jit(solution)/shard_map/pallas_call | solution.py:495
  20.2 0.5 %collective-permute-done.5.set_ref = bf16[4,192,128]{2,1,0:T(8,128)(2,1)S(1)} collective-permute-done((bf16[4,192,128]{2,1,0:T(8,128)(2,1)S(1)}, bf16[4,192,128]{2,1,0:T(8,128)(2,1)S(1)}, u32[]{:S(2)}, u32[]{:S(2)}) %collective-permute-start.5) | collective-permute-done | bytes 196640 | tf_op jit(solution)/shard_map/ppermute | solution.py:457
  20.7 0.9 %shard_map.140 = (bf16[512,256]{1,0:T(8,128)(2,1)S(1)}, bf16[128,256]{1,0:T(8,128)(2,1)S(1)}, bf16[256,128]{1,0:T(8,128)(2,1)S(1)}, f32[32,8,128]{2,1,0:T(8,128)...) custom-call(s32[1]{0:T(128)} %bitcast.9.place_ref, ...), custom_call_target="tpu_custom_call" | custom-call | flops 1000000000 | bytes 4000000 | tf_op jit(solution)/shard_map/pallas_call | solution.py:495
  21.6 5.6 %shard_map.141 = (f32[32,8,64]{2,1,0:T(8,128)}, f32[1024,128]{1,0:T(8,128)}, f32[32,64]{1,0:T(8,128)}, f32[32,64]{1,0:T(8,128)}, f32[1,64]{1,0:T(1,128)}, /*index=5*/f32[1,64]{1,0:T(1,128)}, f32[1,128]{1,0:T(1,128)}) custom-call(bf16[512,256]{1,0:T(8,128)(2,1)S(1)} %get-tuple-element.97.refs_0_, bf16[128,256]{1,0:T(8,128)(2,1)S(1)} %get-tuple-element.98.refs_1_, ...), custom_call_target="tpu_custom_call" | custom-call | tf_op jit(solution)/shard_map/pallas_call | solution.py:513
  (1 shorter events, 0.0 us)
Async XLA Ops:
  0.6 6.8 %copy-start.1 = (bf16[64,32]{0,1:T(8,128)(2,1)S(1)}, bf16[64,32]{0,1:T(8,128)(2,1)}, u32[]{:S(2)}) copy-start(bf16[64,32]{0,1:T(8,128)(2,1)} %param.13) | copy-start | bytes 12292
  0.6 6.8 %copy-start.2 = (bf16[64,32]{0,1:T(8,128)(2,1)S(1)}, bf16[64,32]{0,1:T(8,128)(2,1)}, u32[]{:S(2)}) copy-start(bf16[64,32]{0,1:T(8,128)(2,1)} %param.14) | copy-start | bytes 12292
  1.7 7.8 %collective-permute-start.2 = (bf16[192,128]{1,0:T(8,128)(2,1)S(1)}, bf16[192,128]{1,0:T(8,128)(2,1)S(1)}, u32[]{:S(2)}, u32[]{:S(2)}) collective-permute-start(bf16[192,128]{1,0:T(8,128)(2,1)S(1)} %shard_map.135), channel_id=1, source_target_pairs={{0,3},{1,2},{2,1},{3,0},{4,7},{5,6},{6,5},{7,4},{8,11},{9,10},{10,... | collective-permute-start | bytes 147464 | tf_op jit(solution)/shard_map/ppermute | solution.py:457
  6.8 5.0 %collective-permute-start.1 = (bf16[192,128]{1,0:T(8,128)(2,1)S(1)}, bf16[192,128]{1,0:T(8,128)(2,1)S(1)}, u32[]{:S(2)}, u32[]{:S(2)}) collective-permute-start(bf16[192,128]{1,0:T(8,128)(2,1)S(1)} %shard_map.135), channel_id=1, source_target_pairs={{0,2},{1,3},{2,0},{3,1},{4,6},{5,7},{6,4},{7,5},{8,10},{9,11},{10,... | collective-permute-start | bytes 147464 | tf_op jit(solution)/shard_map/ppermute | solution.py:457
  6.8 5.0 %collective-permute-start = (bf16[192,128]{1,0:T(8,128)(2,1)S(1)}, bf16[192,128]{1,0:T(8,128)(2,1)S(1)}, u32[]{:S(2)}, u32[]{:S(2)}) collective-permute-start(bf16[192,128]{1,0:T(8,128)(2,1)S(1)} %shard_map.135), channel_id=1, source_target_pairs={{0,1},{1,0},{2,3},{3,2},{4,5},{5,4},{6,7},{7,6},{8,9},{9,8},{10,11... | collective-permute-start | bytes 147464 | tf_op jit(solution)/shard_map/ppermute | solution.py:457
  7.5 0.7 %copy-start.3 = (f32[64]{0:T(128)S(1)}, f32[64]{0:T(128)}, u32[]{:S(2)}) copy-start(f32[64]{0:T(128)} %param.11) | copy-start | bytes 772
  7.5 0.7 %copy-start.4 = (f32[64]{0:T(128)S(1)}, f32[64]{0:T(128)}, u32[]{:S(2)}) copy-start(f32[64]{0:T(128)} %param.12) | copy-start | bytes 772
  8.1 0.9 %copy-start = (bf16[1024,128]{1,0:T(8,128)(2,1)S(1)}, bf16[1024,128]{1,0:T(8,128)(2,1)}, u32[]{:S(2)}) copy-start(bf16[1024,128]{1,0:T(8,128)(2,1)} %refs_4_.1) | copy-start | bytes 786436
  11.8 2.6 %collective-permute-start.4 = (bf16[4,192,128]{2,1,0:T(8,128)(2,1)S(1)}, bf16[4,192,128]{2,1,0:T(8,128)(2,1)S(1)}, u32[]{:S(2)}, u32[]{:S(2)}) collective-permute-start(bf16[4,192,128]{2,1,0:T(8,128)(2,1)S(1)} %pad_maximum_fusion.set_ref), channel_id=1, source_target_pairs={{0,4},{4,0},{8,12},{12,8},{1,5},{5,1},{9,13},{13,9},{2,6},{6,2},{1... | collective-permute-start | bytes 589832 | tf_op jit(solution)/shard_map/ppermute | solution.py:457
  11.9 7.3 %collective-permute-start.3 = (bf16[4,192,128]{2,1,0:T(8,128)(2,1)S(1)}, bf16[4,192,128]{2,1,0:T(8,128)(2,1)S(1)}, u32[]{:S(2)}, u32[]{:S(2)}) collective-permute-start(bf16[4,192,128]{2,1,0:T(8,128)(2,1)S(1)} %pad_maximum_fusion.set_ref), channel_id=1, source_target_pairs={{0,8},{4,12},{8,0},{12,4},{1,9},{5,13},{9,1},{13,5},{2,10},{6,14},... | collective-permute-start | bytes 589832 | tf_op jit(solution)/shard_map/ppermute | solution.py:457
  19.2 1.4 %collective-permute-start.5 = (bf16[4,192,128]{2,1,0:T(8,128)(2,1)S(1)}, bf16[4,192,128]{2,1,0:T(8,128)(2,1)S(1)}, u32[]{:S(2)}, u32[]{:S(2)}) collective-permute-start(bf16[4,192,128]{2,1,0:T(8,128)(2,1)S(1)} %collective-permute-done.3.set_ref), channel_id=1, source_target_pairs={{0,4},{4,0},{8,12},{12,8},{1,5},{5,1},{9,13},{13,9},{2,6},{6,2},{1... | collective-permute-start | bytes 589832 | tf_op jit(solution)/shard_map/ppermute | solution.py:457

commit v6 on v5

--- a/solution.py
+++ b/solution.py
@@ -252,9 +252,9 @@
     rhs_out, left_out, leftt_out, rightt_out, grad_out, pair_out, found_out, *rest
 ):
     *own_out, turn_scr = rest
-    place = place_ref[0]
     for b in range(n_col):
-        at = pl.multiple_of(lax.bitwise_xor(place, b) * 8, 8)
+        source = lax.rem(place_ref[1] + n_col - b, n_col)
+        at = pl.multiple_of(lax.bitwise_xor(place_ref[0], source) * 8, 8)
         pair_out[:, pl.ds(at, 8), :] = set_ref[b, 128:192, :].astype(F32).reshape(8, 8, 128)
 
     gain = norm_ref[0:1, :]
@@ -445,8 +445,7 @@
     held = lambda *dims: pltpu.VMEM(dims, F32)
     held_bf = lambda *dims: pltpu.VMEM(dims, BF)
     hbm = pl.BlockSpec(memory_space=pltpu.HBM)
-    place = lax.bitwise_xor(lax.axis_index("row"), lax.axis_index("col"))
-    place = place.astype(jnp.int32).reshape(1)
+    place = jnp.stack([lax.axis_index("row"), lax.axis_index("col")]).astype(jnp.int32)
     packed = pl.pallas_call(
         pack_kernel,
         out_shape=held_bf(192, 128),
@@ -456,7 +455,11 @@
     def over(axis, size, step, array):
         return lax.ppermute(array, axis, [(k, k ^ step) for k in range(size)])
 
-    pieces = [packed] + [over("col", n_col, b, packed) for b in range(1, n_col)]
+    pieces = [
+        lax.ppermute(packed, "col", [(k, (k + b) % n_col) for k in range(n_col)])
+        for b in reversed(range(1, n_col))
+    ]
+    pieces = [packed] + pieces[::-1]
     weights = pl.pallas_call(
         weights_kernel,
         out_shape=(held(8, 128), held_bf(256, 256), held_bf(width * width, 128)),
@@ -506,7 +509,7 @@
 
     own_stage = stage(0, own)
     core_stage = stage(1, core)
-    chip, own_stage, core_stage = lax.optimization_barrier((chip, own_stage, core_stage))
+    chip, own_stage = lax.optimization_barrier((chip, own_stage))
     both = over("row", n_row, 1, chip)
     stages = [own_stage, core_stage, stage(2, chip), stage(3, both)]
     own_norm = stages[0][7:]

time: 27.5 us -> 28.9 us (1.051)
  Pallas kernels: 10.9 us -> 13 us
  waiting for transfers between devices: 6.63 us -> 5.37 us
  starting transfers between devices: 7.39 us -> 7.68 us
    ppermute x0 -> x3, starting transfers between devices: none -> 6.11 us  [gathered_body(): lax.ppermute(packed, 'col', [(k, (k + b) % n_col) for k in range(n_col)])]
    ppermute x6 -> x3, starting transfers between devices: 7.39 us -> 1.56 us  [over(): return lax.ppermute(array, axis, [(k, k ^ step) for k in range(size)])]
    ppermute x6 -> x3, waiting for transfers between devices: 6.63 us -> 2.6 us  [over(): return lax.ppermute(array, axis, [(k, k ^ step) for k in range(size)])]
    ppermute x0 -> x3, waiting for transfers between devices: none -> 2.77 us  [gathered_body(): lax.ppermute(packed, 'col', [(k, (k + b) % n_col) for k in range(n_col)])]
    pallas_call x4, Pallas kernels: 3.78 us -> 5.96 us  [stage(): pl.pallas_call(functools.partial(stage_kernel, n_col, a), out_shape=tuple...]
  transfers between devices with their start and end apart: 6 -> 6, of which waited for: 3 -> 3; matrix products, arithmetic and copies ran while one was open for 0% -> 0% of each run, Pallas kernels for 12% -> 17%
where the time goes in v6:
time: 28.9 us; the launch traced here: 28.5 us
  Pallas kernels  13 us (45%)
  starting transfers between devices  7.68 us (27%)
  waiting for transfers between devices  5.37 us (19%)
  local copies, waits for them, and re-layouts  1.66 us (6%)
  between operations  0.71 us (2%)
    ppermute x3, starting transfers between devices, gathered_body(): lax.ppermute(packed, 'col', [(k, (k + b) % n_col) for k in range(n_col)])  6.11 us
    pallas_call x4, Pallas kernels, stage(): pl.pallas_call(functools.partial(stage_kernel, n_col, a), out_shape=tuple...  5.96 us
    pallas_call x1, Pallas kernels, gathered_body(): pl.pallas_call(functools.partial(part_kernel, n_row), out_shape=(shape(sh...  5.61 us
    ppermute x3, waiting for transfers between devices, gathered_body(): lax.ppermute(packed, 'col', [(k, (k + b) % n_col) for k in range(n_col)])  2.77 us
    ppermute x3, waiting for transfers between devices, over(): return lax.ppermute(array, axis, [(k, k ^ step) for k in range(size)])  2.6 us
    unnamed x10, local copies, waits for them, and re-layouts  1.66 us
    ppermute x3, starting transfers between devices, over(): return lax.ppermute(array, axis, [(k, k ^ step) for k in range(size)])  1.56 us
    pallas_call x1, Pallas kernels, gathered_body(): pl.pallas_call(pack_kernel, out_shape=held_bf(192, 128), in_specs=vmem(3)...  1.04 us
  transfers between devices with their start and end apart: 6, of which 3 were waited for; matrix products, arithmetic and copies ran while one was open for 0% of the time, Pallas kernels for 17%

profile of v6, /device:TPU:0, one launch (start us, length us, event | category | flops | bytes accessed | tf_op | source)
XLA Modules:
  0.0 28.5 jit_solution(14439761809122551707)
XLA Ops:
  0.6 1.0 %shard_map.135 = bf16[192,128]{1,0:T(8,128)(2,1)S(1)} custom-call(bf16[32,8,64]{2,1,0:T(8,128)(2,1)} %msa_ref.1, s32[8,32]{1,0:T(8,128)} %bitcast.26, bf16[8,8,128]{2,1,0:T(8,128)(2,1)} %pair_ref.1), custom_call_target="tpu_custom_call" | custom-call | tf_op jit(solution)/shard_map/pallas_call | solution.py:449
  1.7 5.1 %collective-permute-start.2 = (bf16[192,128]{1,0:T(8,128)(2,1)S(1)}, bf16[192,128]{1,0:T(8,128)(2,1)S(1)}, u32[]{:S(2)}, u32[]{:S(2)}) collective-permute-start(bf16[192,128]{1,0:T(8,128)(2,1)S(1)} %shard_map.135), channel_id=1, source_target_pairs={{0,3},{1,0},{2,1},{3,2},{4,7},{5,4},{6,5},{7,6},{8,11},{9,8},{10,9... | collective-permute-start | bytes 147464 | tf_op jit(solution)/shard_map/ppermute | solution.py:459
  6.8 0.0 collective-permute-start.1
  6.8 1.0 %collective-permute-start = (bf16[192,128]{1,0:T(8,128)(2,1)S(1)}, bf16[192,128]{1,0:T(8,128)(2,1)S(1)}, u32[]{:S(2)}, u32[]{:S(2)}) collective-permute-start(bf16[192,128]{1,0:T(8,128)(2,1)S(1)} %shard_map.135), channel_id=1, source_target_pairs={{0,1},{1,2},{2,3},{3,0},{4,5},{5,6},{6,7},{7,4},{8,9},{9,10},{10,1... | collective-permute-start | bytes 147464 | tf_op jit(solution)/shard_map/ppermute | solution.py:459
  7.8 0.0 copy-start.2
  7.8 0.0 copy-start.1
  7.8 0.0 copy-start.3
  7.8 0.0 copy-start.4
  7.8 0.7 %copy-done.2 = bf16[64,32]{0,1:T(8,128)(2,1)S(1)} copy-done((bf16[64,32]{0,1:T(8,128)(2,1)S(1)}, bf16[64,32]{0,1:T(8,128)(2,1)}, u32[]{:S(2)}) %copy-start.2) | copy-done | bytes 4120
  8.5 0.0 copy-done.1
  8.5 0.0 copy-done.3
  8.5 0.0 copy-done.4
  8.5 0.0 copy-start
  8.5 0.9 %copy-done = bf16[1024,128]{1,0:T(8,128)(2,1)S(1)} copy-done((bf16[1024,128]{1,0:T(8,128)(2,1)S(1)}, bf16[1024,128]{1,0:T(8,128)(2,1)}, u32[]{:S(2)}) %copy-start) | copy-done | bytes 262168
  9.5 0.4 %shard_map.136 = (f32[8,128]{1,0:T(8,128)S(1)}, bf16[256,256]{1,0:T(8,128)(2,1)S(1)}, bf16[1024,128]{1,0:T(8,128)(2,1)S(1)}) custom-call(f32[1,64]{1,0:T(1,128)S(1)} %bitcast.21, f32[1,64]{1,0:T(1,128)S(1)} %bitcast.22, bf16[32,64]{1,0:T(8,128)(2,1)S(1)} %bitcast.17, bf16[32,64]{1,0:T(8,128)(2,1)S(1)} %bitcast.19, bf16[1024,128]{1,0:T(8,128)(2,1)S(1)} %copy-done), custom_call_target="tpu_custom_call" | custom-call | tf_op jit(solution)/shard_map/pallas_call | solution.py:463
  9.9 0.0 collective-permute-done.2
  9.9 1.9 %collective-permute-done.1 = bf16[192,128]{1,0:T(8,128)(2,1)S(1)} collective-permute-done((bf16[192,128]{1,0:T(8,128)(2,1)S(1)}, bf16[192,128]{1,0:T(8,128)(2,1)S(1)}, u32[]{:S(2)}, u32[]{:S(2)}) %collective-permute-start.1) | collective-permute-done | bytes 49184 | tf_op jit(solution)/shard_map/ppermute | solution.py:459
  11.8 0.9 %collective-permute-done = bf16[192,128]{1,0:T(8,128)(2,1)S(1)} collective-permute-done((bf16[192,128]{1,0:T(8,128)(2,1)S(1)}, bf16[192,128]{1,0:T(8,128)(2,1)S(1)}, u32[]{:S(2)}, u32[]{:S(2)}) %collective-permute-start) | collective-permute-done | bytes 49184 | tf_op jit(solution)/shard_map/ppermute | solution.py:459
  12.7 1.6 %collective-permute-start.3 = (bf16[4,192,128]{2,1,0:T(8,128)(2,1)S(1)}, bf16[4,192,128]{2,1,0:T(8,128)(2,1)S(1)}, u32[]{:S(2)}, u32[]{:S(2)}) collective-permute-start(bf16[4,192,128]{2,1,0:T(8,128)(2,1)S(1)} %pad_maximum_fusion.set_ref), channel_id=1, source_target_pairs={{0,8},{4,12},{8,0},{12,4},{1,9},{5,13},{9,1},{13,5},{2,10},{6,14},... | collective-permute-start | bytes 589832 | tf_op jit(solution)/shard_map/ppermute | solution.py:456
  14.3 0.1 pad_add_fusion.place_ref
  14.3 0.0 collective-permute-start.4
  14.3 1.5 %shard_map.137 = (bf16[512,256]{1,0:T(8,128)(2,1)S(1)}, bf16[128,256]{1,0:T(8,128)(2,1)S(1)}, bf16[256,128]{1,0:T(8,128)(2,1)S(1)}, f32[32,8,128]{2,1,0:T(8,128)...) custom-call(s32[2]{0:T(128)S(1)} %pad_add_fusion.place_ref, ...), custom_call_target="tpu_custom_call" | custom-call | flops 1000000000 | bytes 4000000 | tf_op jit(solution)/shard_map/pallas_call | solution.py:498
  15.8 2.6 %collective-permute-done.3.set_ref = bf16[4,192,128]{2,1,0:T(8,128)(2,1)S(1)} collective-permute-done((bf16[4,192,128]{2,1,0:T(8,128)(2,1)S(1)}, bf16[4,192,128]{2,1,0:T(8,128)(2,1)S(1)}, u32[]{:S(2)}, u32[]{:S(2)}) %collective-permute-start.3) | collective-permute-done | bytes 196640 | tf_op jit(solution)/shard_map/ppermute | solution.py:456
  18.4 0.0 collective-permute-start.5
  18.4 1.5 %shard_map.139 = (bf16[512,256]{1,0:T(8,128)(2,1)S(1)}, bf16[128,256]{1,0:T(8,128)(2,1)S(1)}, bf16[256,128]{1,0:T(8,128)(2,1)S(1)}, f32[32,8,128]{2,1,0:T(8,128)...) custom-call(s32[2]{0:T(128)S(1)} %pad_add_fusion.place_ref, ...), custom_call_target="tpu_custom_call" | custom-call | flops 1000000000 | bytes 4000000 | tf_op jit(solution)/shard_map/pallas_call | solution.py:498
  19.9 0.0 collective-permute-done.4.set_ref
  19.9 1.5 %shard_map.138 = (bf16[512,256]{1,0:T(8,128)(2,1)S(1)}, bf16[128,256]{1,0:T(8,128)(2,1)S(1)}, bf16[256,128]{1,0:T(8,128)(2,1)S(1)}, f32[32,8,128]{2,1,0:T(8,128)...) custom-call(s32[2]{0:T(128)S(1)} %pad_add_fusion.place_ref, ...), custom_call_target="tpu_custom_call" | custom-call | flops 1000000000 | bytes 4000000 | tf_op jit(solution)/shard_map/pallas_call | solution.py:498
  21.4 0.0 collective-permute-done.5.set_ref
  21.4 1.5 %shard_map.140 = (bf16[512,256]{1,0:T(8,128)(2,1)S(1)}, bf16[128,256]{1,0:T(8,128)(2,1)S(1)}, bf16[256,128]{1,0:T(8,128)(2,1)S(1)}, f32[32,8,128]{2,1,0:T(8,128)...) custom-call(s32[2]{0:T(128)S(1)} %pad_add_fusion.place_ref, ...), custom_call_target="tpu_custom_call" | custom-call | flops 1000000000 | bytes 4000000 | tf_op jit(solution)/shard_map/pallas_call | solution.py:498
  22.9 5.6 %shard_map.141 = (f32[32,8,64]{2,1,0:T(8,128)}, f32[1024,128]{1,0:T(8,128)}, f32[32,64]{1,0:T(8,128)}, f32[32,64]{1,0:T(8,128)}, f32[1,64]{1,0:T(1,128)}, /*index=5*/f32[1,64]{1,0:T(1,128)}, f32[1,128]{1,0:T(1,128)}) custom-call(bf16[512,256]{1,0:T(8,128)(2,1)S(1)} %get-tuple-element.83.refs_0_, bf16[128,256]{1,0:T(8,128)(2,1)S(1)} %get-tuple-element.84.refs_1_, ...), custom_call_target="tpu_custom_call" | custom-call | tf_op jit(solution)/shard_map/pallas_call | solution.py:516
  (1 shorter events, 0.0 us)
Async XLA Ops:
  1.7 8.2 %collective-permute-start.2 = (bf16[192,128]{1,0:T(8,128)(2,1)S(1)}, bf16[192,128]{1,0:T(8,128)(2,1)S(1)}, u32[]{:S(2)}, u32[]{:S(2)}) collective-permute-start(bf16[192,128]{1,0:T(8,128)(2,1)S(1)} %shard_map.135), channel_id=1, source_target_pairs={{0,3},{1,0},{2,1},{3,2},{4,7},{5,4},{6,5},{7,6},{8,11},{9,8},{10,9... | collective-permute-start | bytes 147464 | tf_op jit(solution)/shard_map/ppermute | solution.py:459
  6.8 5.0 %collective-permute-start.1 = (bf16[192,128]{1,0:T(8,128)(2,1)S(1)}, bf16[192,128]{1,0:T(8,128)(2,1)S(1)}, u32[]{:S(2)}, u32[]{:S(2)}) collective-permute-start(bf16[192,128]{1,0:T(8,128)(2,1)S(1)} %shard_map.135), channel_id=1, source_target_pairs={{0,2},{1,3},{2,0},{3,1},{4,6},{5,7},{6,4},{7,5},{8,10},{9,11},{10,... | collective-permute-start | bytes 147464 | tf_op jit(solution)/shard_map/ppermute | solution.py:459
  6.8 5.9 %collective-permute-start = (bf16[192,128]{1,0:T(8,128)(2,1)S(1)}, bf16[192,128]{1,0:T(8,128)(2,1)S(1)}, u32[]{:S(2)}, u32[]{:S(2)}) collective-permute-start(bf16[192,128]{1,0:T(8,128)(2,1)S(1)} %shard_map.135), channel_id=1, source_target_pairs={{0,1},{1,2},{2,3},{3,0},{4,5},{5,6},{6,7},{7,4},{8,9},{9,10},{10,1... | collective-permute-start | bytes 147464 | tf_op jit(solution)/shard_map/ppermute | solution.py:459
  7.8 0.7 %copy-start.2 = (bf16[64,32]{0,1:T(8,128)(2,1)S(1)}, bf16[64,32]{0,1:T(8,128)(2,1)}, u32[]{:S(2)}) copy-start(bf16[64,32]{0,1:T(8,128)(2,1)} %param.14) | copy-start | bytes 12292
  7.8 0.7 %copy-start.1 = (bf16[64,32]{0,1:T(8,128)(2,1)S(1)}, bf16[64,32]{0,1:T(8,128)(2,1)}, u32[]{:S(2)}) copy-start(bf16[64,32]{0,1:T(8,128)(2,1)} %param.13) | copy-start | bytes 12292
  7.8 0.7 %copy-start.3 = (f32[64]{0:T(128)S(1)}, f32[64]{0:T(128)}, u32[]{:S(2)}) copy-start(f32[64]{0:T(128)} %param.11) | copy-start | bytes 772
  7.8 0.7 %copy-start.4 = (f32[64]{0:T(128)S(1)}, f32[64]{0:T(128)}, u32[]{:S(2)}) copy-start(f32[64]{0:T(128)} %param.12) | copy-start | bytes 772
  8.5 1.0 %copy-start = (bf16[1024,128]{1,0:T(8,128)(2,1)S(1)}, bf16[1024,128]{1,0:T(8,128)(2,1)}, u32[]{:S(2)}) copy-start(bf16[1024,128]{1,0:T(8,128)(2,1)} %refs_4_.1) | copy-start | bytes 786436
  12.7 5.7 %collective-permute-start.3 = (bf16[4,192,128]{2,1,0:T(8,128)(2,1)S(1)}, bf16[4,192,128]{2,1,0:T(8,128)(2,1)S(1)}, u32[]{:S(2)}, u32[]{:S(2)}) collective-permute-start(bf16[4,192,128]{2,1,0:T(8,128)(2,1)S(1)} %pad_maximum_fusion.set_ref), channel_id=1, source_target_pairs={{0,8},{4,12},{8,0},{12,4},{1,9},{5,13},{9,1},{13,5},{2,10},{6,14},... | collective-permute-start | bytes 589832 | tf_op jit(solution)/shard_map/ppermute | solution.py:456
  14.3 5.6 %collective-permute-start.4 = (bf16[4,192,128]{2,1,0:T(8,128)(2,1)S(1)}, bf16[4,192,128]{2,1,0:T(8,128)(2,1)S(1)}, u32[]{:S(2)}, u32[]{:S(2)}) collective-permute-start(bf16[4,192,128]{2,1,0:T(8,128)(2,1)S(1)} %pad_maximum_fusion.set_ref), channel_id=1, source_target_pairs={{0,4},{4,0},{8,12},{12,8},{1,5},{5,1},{9,13},{13,9},{2,6},{6,2},{1... | collective-permute-start | bytes 589832 | tf_op jit(solution)/shard_map/ppermute | solution.py:456
  18.4 3.0 %collective-permute-start.5 = (bf16[4,192,128]{2,1,0:T(8,128)(2,1)S(1)}, bf16[4,192,128]{2,1,0:T(8,128)(2,1)S(1)}, u32[]{:S(2)}, u32[]{:S(2)}) collective-permute-start(bf16[4,192,128]{2,1,0:T(8,128)(2,1)S(1)} %collective-permute-done.3.set_ref), channel_id=1, source_target_pairs={{0,4},{4,0},{8,12},{12,8},{1,5},{5,1},{9,13},{13,9},{2,6},{6,2},{1... | collective-permute-start | bytes 589832 | tf_op jit(solution)/shard_map/ppermute | solution.py:456

commit v7 on v5

--- a/solution.py
+++ b/solution.py
@@ -252,9 +252,8 @@
     rhs_out, left_out, leftt_out, rightt_out, grad_out, pair_out, found_out, *rest
 ):
     *own_out, turn_scr = rest
-    place = place_ref[0]
     for b in range(n_col):
-        at = pl.multiple_of(lax.bitwise_xor(place, b) * 8, 8)
+        at = pl.multiple_of(lax.bitwise_xor(place_ref[0], b) * 8, 8)
         pair_out[:, pl.ds(at, 8), :] = set_ref[b, 128:192, :].astype(F32).reshape(8, 8, 128)
 
     gain = norm_ref[0:1, :]
@@ -457,6 +456,9 @@
         return lax.ppermute(array, axis, [(k, k ^ step) for k in range(size)])
 
     pieces = [packed] + [over("col", n_col, b, packed) for b in range(1, n_col)]
+    chip_first = over("row", n_row, 2, packed)
+    rest = jnp.stack(pieces[1:])
+    chip_rest = over("row", n_row, 2, rest)
     weights = pl.pallas_call(
         weights_kernel,
         out_shape=(held(8, 128), held_bf(256, 256), held_bf(width * width, 128)),
@@ -473,16 +475,20 @@
         ],
         compiler_params=LIMIT,
     )(
-        standardizer_scale.reshape(1, features),
-        standardizer_shift.reshape(1, features),
-        first_t,
-        second_t,
-        final_projection_matrix,
-    )
-    pieces, weights = lax.optimization_barrier((pieces, weights))
+        *[
+            pltpu.with_memory_space_constraint(x, pltpu.HBM)
+            for x in (
+                standardizer_scale.reshape(1, features),
+                standardizer_shift.reshape(1, features),
+                first_t,
+                second_t,
+                final_projection_matrix,
+            )
+        ]
+    )
     norm, back, final_turned = weights
-    own = jnp.stack(pieces)
-    chip = over("row", n_row, 2, own)
+    own = jnp.concatenate([packed[None], rest])
+    own, chip_first = lax.optimization_barrier((own, chip_first))
     core = over("row", n_row, 1, own)
 
     def stage(a, block):
@@ -506,7 +512,8 @@
 
     own_stage = stage(0, own)
     core_stage = stage(1, core)
-    chip, own_stage, core_stage = lax.optimization_barrier((chip, own_stage, core_stage))
+    chip = jnp.concatenate([chip_first[None], chip_rest])
+    chip, own_stage = lax.optimization_barrier((chip, own_stage))
     both = over("row", n_row, 1, chip)
     stages = [own_stage, core_stage, stage(2, chip), stage(3, both)]
     own_norm = stages[0][7:]

time: 27.5 us -> 26.6 us (0.967)
  waiting for transfers between devices: 6.63 us -> 3.88 us
  starting transfers between devices: 7.39 us -> 9.09 us
  local copies, waits for them, and re-layouts: 1.62 us -> 0.7 us
  Pallas kernels: 10.9 us -> 11.8 us
    ppermute x6 -> x7, waiting for transfers between devices: 6.63 us -> 3.88 us  [over(): return lax.ppermute(array, axis, [(k, k ^ step) for k in range(size)])]
    ppermute x6 -> x7, starting transfers between devices: 7.39 us -> 9.09 us  [over(): return lax.ppermute(array, axis, [(k, k ^ step) for k in range(size)])]
    pallas_call x1, Pallas kernels: 0.42 us -> 1.4 us  [gathered_body(): pl.pallas_call(weights_kernel, out_shape=(held(8, 128), held_bf(256, 256)...]
    unnamed x10 -> x4, local copies, waits for them, and re-layouts: 1.62 us -> 0.7 us
  transfers between devices with their start and end apart: 6 -> 7, of which waited for: 3 -> 2; matrix products, arithmetic and copies ran while one was open for 0% -> 0% of each run, Pallas kernels for 12% -> 16%
where the time goes in v7:
time: 26.6 us; the launch traced here: 26.3 us
  Pallas kernels  11.8 us (44%)
  starting transfers between devices  9.09 us (34%)
  waiting for transfers between devices  3.88 us (15%)
  between operations  0.74 us (3%)
  local copies, waits for them, and re-layouts  0.7 us (3%)
    ppermute x7, starting transfers between devices, over(): return lax.ppermute(array, axis, [(k, k ^ step) for k in range(size)])  9.09 us
    pallas_call x1, Pallas kernels, gathered_body(): pl.pallas_call(functools.partial(part_kernel, n_row), out_shape=(shape(sh...  5.56 us
    ppermute x7, waiting for transfers between devices, over(): return lax.ppermute(array, axis, [(k, k ^ step) for k in range(size)])  3.88 us
    pallas_call x4, Pallas kernels, stage(): pl.pallas_call(functools.partial(stage_kernel, n_col, a), out_shape=tuple...  3.8 us
    pallas_call x1, Pallas kernels, gathered_body(): pl.pallas_call(weights_kernel, out_shape=(held(8, 128), held_bf(256, 256)...  1.4 us
    pallas_call x1, Pallas kernels, gathered_body(): pl.pallas_call(pack_kernel, out_shape=held_bf(192, 128), in_specs=vmem(3)...  1.04 us
    unnamed x4, local copies, waits for them, and re-layouts  0.7 us
  transfers between devices with their start and end apart: 7, of which 2 were waited for; matrix products, arithmetic and copies ran while one was open for 0% of the time, Pallas kernels for 16%

profile of v7, /device:TPU:0, one launch (start us, length us, event | category | flops | bytes accessed | tf_op | source)
XLA Modules:
  0.0 26.3 jit_solution(7783939948990077556)
XLA Ops:
  0.6 1.0 %shard_map.135 = bf16[192,128]{1,0:T(8,128)(2,1)S(1)} custom-call(bf16[32,8,64]{2,1,0:T(8,128)(2,1)} %msa_ref.1, s32[8,32]{1,0:T(8,128)} %bitcast.28, bf16[8,8,128]{2,1,0:T(8,128)(2,1)} %pair_ref.1), custom_call_target="tpu_custom_call" | custom-call | tf_op jit(solution)/shard_map/pallas_call | solution.py:449
  1.7 5.1 %collective-permute-start.2 = (bf16[192,128]{1,0:T(8,128)(2,1)S(1)}, bf16[192,128]{1,0:T(8,128)(2,1)S(1)}, u32[]{:S(2)}, u32[]{:S(2)}) collective-permute-start(bf16[192,128]{1,0:T(8,128)(2,1)S(1)} %shard_map.135), channel_id=1, source_target_pairs={{0,3},{1,2},{2,1},{3,0},{4,7},{5,6},{6,5},{7,4},{8,11},{9,10},{10,... | collective-permute-start | bytes 147464 | tf_op jit(solution)/shard_map/ppermute | solution.py:456
  6.8 0.0 collective-permute-start.1
  6.8 0.6 %collective-permute-start = (bf16[192,128]{1,0:T(8,128)(2,1)S(1)}, bf16[192,128]{1,0:T(8,128)(2,1)S(1)}, u32[]{:S(2)}, u32[]{:S(2)}) collective-permute-start(bf16[192,128]{1,0:T(8,128)(2,1)S(1)} %shard_map.135), channel_id=1, source_target_pairs={{0,1},{1,0},{2,3},{3,2},{4,5},{5,4},{6,7},{7,6},{8,9},{9,8},{10,11... | collective-permute-start | bytes 147464 | tf_op jit(solution)/shard_map/ppermute | solution.py:456
  7.4 1.6 %collective-permute-start.3 = (bf16[192,128]{1,0:T(8,128)(2,1)S(1)}, bf16[192,128]{1,0:T(8,128)(2,1)S(1)}, u32[]{:S(2)}, u32[]{:S(2)}) collective-permute-start(bf16[192,128]{1,0:T(8,128)(2,1)S(1)} %shard_map.135), channel_id=1, source_target_pairs={{0,8},{4,12},{8,0},{12,4},{1,9},{5,13},{9,1},{13,5},{2,10},{6,14},... | collective-permute-start | bytes 147464 | tf_op jit(solution)/shard_map/ppermute | solution.py:456
  9.1 1.4 %shard_map.136 = (f32[8,128]{1,0:T(8,128)S(1)}, bf16[256,256]{1,0:T(8,128)(2,1)S(1)}, bf16[1024,128]{1,0:T(8,128)(2,1)S(1)}) custom-call(f32[1,64]{1,0:T(1,128)} %bitcast.29, f32[1,64]{1,0:T(1,128)} %bitcast.30, bf16[32,64]{1,0:T(8,128)(2,1)} %bitcast.17, bf16[32,64]{1,0:T(8,128)(2,1)} %bitcast.19, bf16[1024,128]{1,0:T(8,128)(2,1)} %refs_4_.1), custom_call_target="tpu_custom_call" | custom-call | tf_op jit(solution)/shard_map/pallas_call | solution.py:462
  10.5 0.0 collective-permute-done.2
  10.5 1.3 %collective-permute-done.1 = bf16[192,128]{1,0:T(8,128)(2,1)S(1)} collective-permute-done((bf16[192,128]{1,0:T(8,128)(2,1)S(1)}, bf16[192,128]{1,0:T(8,128)(2,1)S(1)}, u32[]{:S(2)}, u32[]{:S(2)}) %collective-permute-start.1) | collective-permute-done | bytes 49184 | tf_op jit(solution)/shard_map/ppermute | solution.py:456
  11.8 0.0 collective-permute-done
  11.8 1.6 %collective-permute-start.4 = (bf16[3,192,128]{2,1,0:T(8,128)(2,1)S(1)}, bf16[3,192,128]{2,1,0:T(8,128)(2,1)S(1)}, u32[]{:S(2)}, u32[]{:S(2)}) collective-permute-start(bf16[3,192,128]{2,1,0:T(8,128)(2,1)S(1)} %pad_maximum_fusion.2), channel_id=1, source_target_pairs={{0,8},{4,12},{8,0},{12,4},{1,9},{5,13},{9,1},{13,5},{2,10},{6,14},... | collective-permute-start | bytes 442376 | tf_op jit(solution)/shard_map/ppermute | solution.py:456
  13.4 0.0 collective-permute-done.3
  13.4 0.1 collective-permute-start.5
  13.5 1.0 %shard_map.137 = (bf16[512,256]{1,0:T(8,128)(2,1)S(1)}, bf16[128,256]{1,0:T(8,128)(2,1)S(1)}, bf16[256,128]{1,0:T(8,128)(2,1)S(1)}, f32[32,8,128]{2,1,0:T(8,128)...) custom-call(s32[1]{0:T(128)} %bitcast.6.place_ref, ...), custom_call_target="tpu_custom_call" | custom-call | flops 1000000000 | bytes 4000000 | tf_op jit(solution)/shard_map/pallas_call | solution.py:501
  14.4 2.6 %collective-permute-done.4 = bf16[3,192,128]{2,1,0:T(8,128)(2,1)S(1)} collective-permute-done((bf16[3,192,128]{2,1,0:T(8,128)(2,1)S(1)}, bf16[3,192,128]{2,1,0:T(8,128)(2,1)S(1)}, u32[]{:S(2)}, u32[]{:S(2)}) %collective-permute-start.4) | collective-permute-done | bytes 147488 | tf_op jit(solution)/shard_map/ppermute | solution.py:456
  17.0 0.1 collective-permute-start.6
  17.1 1.0 %shard_map.139 = (bf16[512,256]{1,0:T(8,128)(2,1)S(1)}, bf16[128,256]{1,0:T(8,128)(2,1)S(1)}, bf16[256,128]{1,0:T(8,128)(2,1)S(1)}, f32[32,8,128]{2,1,0:T(8,128)...) custom-call(s32[1]{0:T(128)} %bitcast.6.place_ref, ...), custom_call_target="tpu_custom_call" | custom-call | flops 1000000000 | bytes 4000000 | tf_op jit(solution)/shard_map/pallas_call | solution.py:501
  18.1 0.0 collective-permute-done.5.set_ref
  18.1 0.9 %shard_map.138 = (bf16[512,256]{1,0:T(8,128)(2,1)S(1)}, bf16[128,256]{1,0:T(8,128)(2,1)S(1)}, bf16[256,128]{1,0:T(8,128)(2,1)S(1)}, f32[32,8,128]{2,1,0:T(8,128)...) custom-call(s32[1]{0:T(128)} %bitcast.6.place_ref, ...), custom_call_target="tpu_custom_call" | custom-call | flops 1000000000 | bytes 4000000 | tf_op jit(solution)/shard_map/pallas_call | solution.py:501
  19.0 0.0 collective-permute-done.6.set_ref
  19.0 1.0 %shard_map.140 = (bf16[512,256]{1,0:T(8,128)(2,1)S(1)}, bf16[128,256]{1,0:T(8,128)(2,1)S(1)}, bf16[256,128]{1,0:T(8,128)(2,1)S(1)}, f32[32,8,128]{2,1,0:T(8,128)...) custom-call(s32[1]{0:T(128)} %bitcast.6.place_ref, ...), custom_call_target="tpu_custom_call" | custom-call | flops 1000000000 | bytes 4000000 | tf_op jit(solution)/shard_map/pallas_call | solution.py:501
  20.0 0.0 copy-start.1
  20.0 0.0 copy-start
  20.0 0.7 %copy-done.1 = bf16[64,32]{0,1:T(8,128)(2,1)S(1)} copy-done((bf16[64,32]{0,1:T(8,128)(2,1)S(1)}, bf16[64,32]{0,1:T(8,128)(2,1)}, u32[]{:S(2)}) %copy-start.1) | copy-done | bytes 4120
  20.7 0.0 copy-done
  20.7 5.6 %shard_map.141 = (f32[32,8,64]{2,1,0:T(8,128)}, f32[1024,128]{1,0:T(8,128)}, f32[32,64]{1,0:T(8,128)}, f32[32,64]{1,0:T(8,128)}, f32[1,64]{1,0:T(1,128)}, /*index=5*/f32[1,64]{1,0:T(1,128)}, f32[1,128]{1,0:T(1,128)}) custom-call(bf16[512,256]{1,0:T(8,128)(2,1)S(1)} %get-tuple-element.73.refs_0_, bf16[128,256]{1,0:T(8,128)(2,1)S(1)} %get-tuple-element.74.refs_1_, ...), custom_call_target="tpu_custom_call" | custom-call | tf_op jit(solution)/shard_map/pallas_call | solution.py:520
  (3 shorter events, 0.1 us)
Async XLA Ops:
  1.7 8.8 %collective-permute-start.2 = (bf16[192,128]{1,0:T(8,128)(2,1)S(1)}, bf16[192,128]{1,0:T(8,128)(2,1)S(1)}, u32[]{:S(2)}, u32[]{:S(2)}) collective-permute-start(bf16[192,128]{1,0:T(8,128)(2,1)S(1)} %shard_map.135), channel_id=1, source_target_pairs={{0,3},{1,2},{2,1},{3,0},{4,7},{5,6},{6,5},{7,4},{8,11},{9,10},{10,... | collective-permute-start | bytes 147464 | tf_op jit(solution)/shard_map/ppermute | solution.py:456
  6.8 5.0 %collective-permute-start.1 = (bf16[192,128]{1,0:T(8,128)(2,1)S(1)}, bf16[192,128]{1,0:T(8,128)(2,1)S(1)}, u32[]{:S(2)}, u32[]{:S(2)}) collective-permute-start(bf16[192,128]{1,0:T(8,128)(2,1)S(1)} %shard_map.135), channel_id=1, source_target_pairs={{0,2},{1,3},{2,0},{3,1},{4,6},{5,7},{6,4},{7,5},{8,10},{9,11},{10,... | collective-permute-start | bytes 147464 | tf_op jit(solution)/shard_map/ppermute | solution.py:456
  6.8 5.0 %collective-permute-start = (bf16[192,128]{1,0:T(8,128)(2,1)S(1)}, bf16[192,128]{1,0:T(8,128)(2,1)S(1)}, u32[]{:S(2)}, u32[]{:S(2)}) collective-permute-start(bf16[192,128]{1,0:T(8,128)(2,1)S(1)} %shard_map.135), channel_id=1, source_target_pairs={{0,1},{1,0},{2,3},{3,2},{4,5},{5,4},{6,7},{7,6},{8,9},{9,8},{10,11... | collective-permute-start | bytes 147464 | tf_op jit(solution)/shard_map/ppermute | solution.py:456
  7.4 6.0 %collective-permute-start.3 = (bf16[192,128]{1,0:T(8,128)(2,1)S(1)}, bf16[192,128]{1,0:T(8,128)(2,1)S(1)}, u32[]{:S(2)}, u32[]{:S(2)}) collective-permute-start(bf16[192,128]{1,0:T(8,128)(2,1)S(1)} %shard_map.135), channel_id=1, source_target_pairs={{0,8},{4,12},{8,0},{12,4},{1,9},{5,13},{9,1},{13,5},{2,10},{6,14},... | collective-permute-start | bytes 147464 | tf_op jit(solution)/shard_map/ppermute | solution.py:456
  11.8 5.2 %collective-permute-start.4 = (bf16[3,192,128]{2,1,0:T(8,128)(2,1)S(1)}, bf16[3,192,128]{2,1,0:T(8,128)(2,1)S(1)}, u32[]{:S(2)}, u32[]{:S(2)}) collective-permute-start(bf16[3,192,128]{2,1,0:T(8,128)(2,1)S(1)} %pad_maximum_fusion.2), channel_id=1, source_target_pairs={{0,8},{4,12},{8,0},{12,4},{1,9},{5,13},{9,1},{13,5},{2,10},{6,14},... | collective-permute-start | bytes 442376 | tf_op jit(solution)/shard_map/ppermute | solution.py:456
  13.4 4.7 %collective-permute-start.5 = (bf16[4,192,128]{2,1,0:T(8,128)(2,1)S(1)}, bf16[4,192,128]{2,1,0:T(8,128)(2,1)S(1)}, u32[]{:S(2)}, u32[]{:S(2)}) collective-permute-start(bf16[4,192,128]{2,1,0:T(8,128)(2,1)S(1)} %pad_maximum_fusion.set_ref), channel_id=1, source_target_pairs={{0,4},{4,0},{8,12},{12,8},{1,5},{5,1},{9,13},{13,9},{2,6},{6,2},{1... | collective-permute-start | bytes 589832 | tf_op jit(solution)/shard_map/ppermute | solution.py:456
  17.0 2.0 %collective-permute-start.6 = (bf16[4,192,128]{2,1,0:T(8,128)(2,1)S(1)}, bf16[4,192,128]{2,1,0:T(8,128)(2,1)S(1)}, u32[]{:S(2)}, u32[]{:S(2)}) collective-permute-start(bf16[4,192,128]{2,1,0:T(8,128)(2,1)S(1)} %pad_maximum_fusion.1.set_ref), channel_id=1, source_target_pairs={{0,4},{4,0},{8,12},{12,8},{1,5},{5,1},{9,13},{13,9},{2,6},{6,2},{1... | collective-permute-start | bytes 589832 | tf_op jit(solution)/shard_map/ppermute | solution.py:456
  20.0 0.7 %copy-start.1 = (bf16[64,32]{0,1:T(8,128)(2,1)S(1)}, bf16[64,32]{0,1:T(8,128)(2,1)}, u32[]{:S(2)}) copy-start(bf16[64,32]{0,1:T(8,128)(2,1)} %param.14) | copy-start | bytes 12292
  20.0 0.7 %copy-start = (bf16[64,32]{0,1:T(8,128)(2,1)S(1)}, bf16[64,32]{0,1:T(8,128)(2,1)}, u32[]{:S(2)}) copy-start(bf16[64,32]{0,1:T(8,128)(2,1)} %param.13) | copy-start | bytes 12292

commit v8 on v7

--- a/solution.py
+++ b/solution.py
@@ -187,20 +187,19 @@
     return lax.dot_general(a, b, (((0,), (0,)), ((), ())), preferred_element_type=F32)
 
 
-def swap_blocks(block):
-    lane = lax.broadcasted_iota(jnp.int32, (32, 128), 1)
-    upper = lane >= 64
-    odd = (lane // 32) % 2 == 1
-    piece = [block[32 * a : 32 * a + 32] for a in range(4)]
-    for a in (0, 1):
-        x, y = piece[a], piece[a + 2]
-        piece[a] = jnp.where(upper, pltpu.roll(y, 64, 1), x)
-        piece[a + 2] = jnp.where(upper, y, pltpu.roll(x, 64, 1))
-    for a in (0, 2):
-        x, y = piece[a], piece[a + 1]
-        piece[a] = jnp.where(odd, pltpu.roll(y, 32, 1), x)
-        piece[a + 1] = jnp.where(odd, y, pltpu.roll(x, 96, 1))
-    return jnp.concatenate(piece, axis=0)
+def interleave(first, second):
+    odd = lax.broadcasted_iota(jnp.int16, (32, 128), 1) & 32 != 0
+    return (
+        jnp.where(odd, pltpu.roll(second, 32, 1), first),
+        jnp.where(odd, second, pltpu.roll(first, 96, 1)),
+    )
+
+
+def diagonal_pair(block):
+    zero = jnp.zeros_like(block)
+    return jnp.concatenate(
+        [jnp.concatenate([block, zero], axis=1), jnp.concatenate([zero, block], axis=1)], axis=0
+    )
 
 
 ABSENT = 1024.0
@@ -219,7 +218,8 @@
 
 
 def weights_kernel(*refs):
-    sources, (norm_out, back_out, final_out), held, scr, sems = refs[:5], refs[5:8], refs[8:13], refs[13], refs[14]
+    sources, (norm_out, back_out, final_out, first_out) = refs[:5], refs[5:9]
+    held, scr, sems = refs[9:14], refs[14], refs[15]
     copies = [pltpu.make_async_copy(sources[k], held[k], sems.at[k]) for k in range(5)]
     for copy in copies:
         copy.start()
@@ -234,13 +234,18 @@
         axis=0,
     )
     for k, ref in enumerate((first_ref, second_ref)):
-        wide = jnp.concatenate([ref[...].astype(F32)] * 4, axis=1)
+        narrow = ref[...].astype(F32)
+        first_out[32 * k : 32 * k + 32, :] = narrow
+        wide = jnp.concatenate([narrow] * 4, axis=1)
         wide = jnp.concatenate([wide] * 4, axis=0)
         own = spread(128, 256, lambda r, c: r // 32 == c // 64)
         back_out[128 * k : 128 * k + 128, :] = jnp.where(own, wide, 0.0).astype(BF)
     scr[...] = final_ref[...].astype(F32)
-    for e in range(32):
-        final_out[32 * e : 32 * e + 32, :] = scr[pl.ds(e, 32, stride=32), :].astype(BF)
+    for k in range(16):
+        e = 4 * (k // 2) + k % 2
+        final_out[32 * k : 32 * k + 32, :] = jnp.concatenate(
+            [scr[pl.ds(e, 32, stride=32), :], scr[pl.ds(e + 2, 32, stride=32), :]], axis=1
+        ).astype(BF)
 
 
 def averager_of():
@@ -287,28 +292,42 @@
         at = slice(128 * h, 128 * h + 128)
         left_out[:, at] = mm_nt(masked, back_ref[:128, :]).astype(BF)
         both = mm_nt(back_ref[...], masked)
-        leftt_out[at, :] = both[:128].astype(BF)
         turn_scr[at, :] = both[128:]
+        for k in range(2):
+            leftt_out[64 * h + 32 * k : 64 * h + 32 * k + 32, :] = jnp.concatenate(
+                [both[32 * k : 32 * k + 32], both[32 * k + 64 : 32 * k + 96]], axis=1
+            ).astype(BF)
 
     for e in range(32):
         rightt_out[e] = turn_scr[pl.ds(e, 8, stride=32), :]
 
-    grad = mm_nt(final_ref[...], pair_out[...].reshape(256, 128).astype(BF)).astype(BF)
-    for q in range(8):
+    pair = pair_out[...].reshape(256, 128).astype(BF)
+    for n in range(2):
+        pairs = jnp.concatenate(
+            [diagonal_pair(pair[64 * p : 64 * p + 64]) for p in (2 * n, 2 * n + 1)], axis=0
+        )
+        grad = mm_nt(final_ref[...], pairs).astype(BF)
         for p in range(2):
-            grad_out[128 * p : 128 * p + 128, 128 * q : 128 * q + 128] = swap_blocks(
-                grad[128 * q : 128 * q + 128, 128 * p : 128 * p + 128]
-            )
-
-
-def part_kernel(n_row, *refs):
-    stages = [refs[7 * a : 7 * a + 7] for a in range(n_row)]
+            for q in range(8):
+                rows = 64 * (2 * n + p)
+                block = grad[64 * q : 64 * q + 64, 128 * p : 128 * p + 128]
+                even, odd = interleave(block[:32], block[32:])
+                grad_out[rows : rows + 32, 128 * q : 128 * q + 128] = even
+                grad_out[rows + 32 : rows + 64, 128 * q : 128 * q + 128] = odd
+
+
+def part_kernel(n_row, n_col, place_ref, last_ref, *refs):
+    stages = [refs[7 * a : 7 * a + 7] for a in range(n_row - 1)]
     (
-        normed_ref, inverse_ref, norm_ref, back_ref, first_ref, second_ref,
+        normed_ref, inverse_ref, norm_ref, back_ref, final_ref, first_ref,
         emb_out, final_hbm_out, first_out, second_out, gain_out, offset_out, bias_out,
-        right_scr, scaled_scr, grad_scr, outer_scr, wide_scr, linc_scr, rin_scr, rinc_scr,
-        final_out, out_sem,
-    ) = refs[7 * n_row :]
+        right_scr, scaled_scr, grad_scr, outer_scr, wide_scr, rin_scr, all_scr,
+        final_out, out_sem, turn_scr,
+    ) = refs[7 * (n_row - 1) : -7]
+    stages.append(refs[-7:])
+    stage_kernel(
+        n_col, n_row - 1, place_ref, last_ref, norm_ref, back_ref, final_ref, *stages[-1], turn_scr
+    )
     gain = norm_ref[0:1, :]
     averager = averager_of()
     lane = lax.broadcasted_iota(jnp.int32, (128, 128), 1)
@@ -322,6 +341,30 @@
         right_scr[32 * e : 32 * e + 32, :] = jnp.concatenate(
             [stage[3][e] for stage in stages], axis=0
         ).astype(BF)
+
+    mask_bf = mask.astype(BF)
+    share = (1.0 / (mm_tn(mask_bf, mask_bf)[0:32] + 0.001)).astype(BF)
+    for i in range(32):
+        a, at = i // 8, 32 * (i % 8)
+        for q in range(8):
+            grad_scr[32 * i : 32 * i + 32, 128 * q : 128 * q + 128] = (
+                stages[a][4][at : at + 32, 128 * q : 128 * q + 128] * share[i : i + 1]
+            )
+    left = jnp.concatenate([stage[1][...] for stage in stages], axis=1)
+    right_grad = mm(left, grad_scr[...])
+    left_grad = mm(grad_scr[...], right_scr[...])
+
+    identity = spread(128, 128, lambda r, c: jnp.where(r == c, 1.0, 0.0)).astype(BF)
+    for q in range(8):
+        at = slice(128 * q, 128 * q + 128)
+        rin_scr[at, :] = mm_nt(identity, (right_grad[:, at] * mask).astype(BF))
+    for t in range(32):
+        at = slice(128 * (t // 2), 128 * (t // 2) + 128)
+        row = 32 * (t % 2)
+        all_scr[row : row + 32, at] = (
+            left_grad[32 * t : 32 * t + 32] * mask_t[t : t + 1]
+        ).astype(BF)
+        all_scr[row + 64 : row + 96, at] = rin_scr[pl.ds(t, 32, stride=32), :].astype(BF)
 
     bias = jnp.zeros((1, 128), F32)
     ones = jnp.ones((128, 128), BF)
@@ -336,54 +379,31 @@
         scaled_scr[128 * p : 128 * p + 128, :] = scaled.astype(BF)
     bias_out[...] = bias
 
-    for a, stage in enumerate(stages):
-        outer = mm_nt(stage[2][...], right_scr[...]).astype(BF)
+    left_t = jnp.concatenate([stage[2][...] for stage in stages], axis=0)
+    for n in range(8):
+        rights = jnp.concatenate(
+            [diagonal_pair(right_scr[64 * p : 64 * p + 64, :]) for p in (2 * n, 2 * n + 1)], axis=0
+        )
+        outer = mm_nt(left_t, rights).astype(BF)
         for p in range(2):
             for q in range(8):
-                to = 256 * a + 128 * p
-                outer_scr[128 * q : 128 * q + 128, to : to + 128] = swap_blocks(
-                    outer[128 * p : 128 * p + 128, 128 * q : 128 * q + 128]
-                )
+                rows = 64 * (2 * n + p)
+                block = outer[64 * q : 64 * q + 64, 128 * p : 128 * p + 128]
+                even, odd = interleave(block[:32], block[32:])
+                outer_scr[rows : rows + 32, 128 * q : 128 * q + 128] = even
+                outer_scr[rows + 32 : rows + 64, 128 * q : 128 * q + 128] = odd
     wide_scr[...] = mm(outer_scr[...], scaled_scr[...])
     for c in range(32):
         final_out[32 * c : 32 * c + 32, :] = wide_scr[pl.ds(c, 32, stride=32), :]
     final_send = pltpu.make_async_copy(final_out, final_hbm_out, out_sem)
     final_send.start()
 
-    mask_bf = mask.astype(BF)
-    share = (1.0 / (mm_tn(mask_bf, mask_bf)[0:32] + 0.001)).astype(BF)
-    for i in range(32):
-        a, at = i // 8, 32 * (i % 8)
-        for q in range(8):
-            grad_scr[32 * i : 32 * i + 32, 128 * q : 128 * q + 128] = (
-                stages[a][4][at : at + 32, 128 * q : 128 * q + 128] * share[i : i + 1]
-            )
-    left_grad = mm(grad_scr[...], right_scr[...])
-    left = jnp.concatenate([stage[1][...] for stage in stages], axis=1)
-    right_grad = mm(left, grad_scr[...])
-
-    identity = spread(128, 128, lambda r, c: jnp.where(r == c, 1.0, 0.0)).astype(BF)
-    for q in range(8):
-        at = slice(128 * q, 128 * q + 128)
-        rin_scr[at, :] = mm_nt(identity, (right_grad[:, at] * mask).astype(BF))
-    for k in range(8):
-        rows = []
-        for t in range(4 * k, 4 * k + 4):
-            rows.append(left_grad[32 * t : 32 * t + 32] * mask_t[t : t + 1])
-        at = slice(128 * k, 128 * k + 128)
-        linc_scr[at, :] = jnp.concatenate(rows, axis=0).astype(BF)
-        rinc_scr[at, :] = jnp.concatenate(
-            [rin_scr[pl.ds(t, 32, stride=32), :] for t in range(4 * k, 4 * k + 4)], axis=0
-        ).astype(BF)
-
-    total = jnp.zeros((128, 256), F32)
-    sums = jnp.zeros((128, 128), F32)
-    for g in range(16):
-        grads = jnp.concatenate(
-            [linc_scr[64 * g : 64 * g + 64, :], rinc_scr[64 * g : 64 * g + 64, :]], axis=0
-        )
-        sums = sums + grads.astype(F32)
-        total = total + mm(grads, stages[g // 4][0][128 * (g % 4) : 128 * (g % 4) + 128, :])
+    total = mm(
+        all_scr[...], jnp.concatenate([stage[0][...] for stage in stages], axis=0)
+    )
+    sums = all_scr[:, 0:128].astype(F32)
+    for g in range(1, 16):
+        sums = sums + all_scr[:, 128 * g : 128 * g + 128].astype(F32)
 
     def fold(block):
         return block[0:32, 0:64] + block[32:64, 64:128]
@@ -393,28 +413,30 @@
     sums = jnp.sum(sums, axis=1, keepdims=True)
     left_sum = sums[0:32] + sums[32:64]
     right_sum = sums[64:96] + sums[96:128]
-    first = first_ref[...].astype(F32)
-    second = second_ref[...].astype(F32)
+    first, second = first_ref[0:32, :], first_ref[32:64, :]
     gain_out[...] = jnp.sum(
         first * fold(total[0:64, 128:256]) + second * fold(total[64:128, 128:256]),
         axis=0, keepdims=True,
     )
     offset_out[...] = jnp.sum(first * left_sum + second * right_sum, axis=0, keepdims=True)
 
+    d_hat = []
     for h in range(2):
-        at = slice(128 * h, 128 * h + 128)
-        d_normal = mm_tn(linc_scr[at, :], back_ref[:128, :]) + mm_tn(rinc_scr[at, :], back_ref[128:, :])
-        for half in range(2):
-            g = 2 * h + half
-            d_hat = d_normal[0:32, 128 * half : 128 * half + 128] * gain
-            normed = normed_ref[32 * g : 32 * g + 32, :]
-            result = inverse_ref[32 * g : 32 * g + 32, :] * (
-                d_hat
-                - mm(d_hat.astype(BF), averager)
-                - normed * mm((d_hat * normed).astype(BF), averager)
+        sides = [
+            jnp.concatenate(
+                [all_scr[row : row + 64, 128 * g : 128 * g + 128] for g in (2 * h, 2 * h + 1)], axis=0
             )
-            emb_out[:, 2 * g, :] = result[:, 0:64]
-            emb_out[:, 2 * g + 1, :] = result[:, 64:128]
+            for row in (0, 64)
+        ]
+        d_normal = mm_tn(jnp.concatenate(sides, axis=0), back_ref[...])
+        d_hat += [d_normal[0:32, 0:128] * gain, d_normal[0:32, 128:256] * gain]
+    d_hat = jnp.concatenate(d_hat, axis=0)
+    normed = normed_ref[...]
+    means = mm(jnp.concatenate([d_hat, d_hat * normed], axis=0).astype(BF), averager)
+    result = inverse_ref[...] * (d_hat - means[:128] - normed * means[128:])
+    for g in range(4):
+        emb_out[:, 2 * g, :] = result[32 * g : 32 * g + 32, 0:64]
+        emb_out[:, 2 * g + 1, :] = result[32 * g : 32 * g + 32, 64:128]
     final_send.wait()
 
 
@@ -461,9 +483,11 @@
     chip_rest = over("row", n_row, 2, rest)
     weights = pl.pallas_call(
         weights_kernel,
-        out_shape=(held(8, 128), held_bf(256, 256), held_bf(width * width, 128)),
+        out_shape=(
+            held(8, 128), held_bf(256, 256), held_bf(width * width // 2, 256), held(2 * width, features),
+        ),
         in_specs=[hbm] * 5,
-        out_specs=tuple(vmem(3)),
+        out_specs=tuple(vmem(4)),
         scratch_shapes=[
             pltpu.VMEM((1, features), F32),
             pltpu.VMEM((1, features), F32),
@@ -486,22 +510,23 @@
             )
         ]
     )
-    norm, back, final_turned = weights
+    norm, back, final_turned, first = weights
     own = jnp.concatenate([packed[None], rest])
     own, chip_first = lax.optimization_barrier((own, chip_first))
     core = over("row", n_row, 1, own)
 
+    stage_outs = [
+        held_bf(512, 256), held_bf(128, 256), held_bf(128, 256), held(width, 8, 128),
+        held_bf(256, 1024), held(8, 32, 128), held(128, 128),
+    ]
+    scalar = pl.BlockSpec(memory_space=pltpu.SMEM)
+
     def stage(a, block):
-        outs = [
-            held_bf(512, 256), held_bf(128, 256), held_bf(256, 128), held(width, 8, 128),
-            held_bf(256, 1024), held(8, 32, 128), held(128, 128),
-        ]
-        if a == 0:
-            outs += [held(128, 128)] * 2
+        outs = stage_outs + [held(128, 128)] * 2 * (a == 0)
         return pl.pallas_call(
             functools.partial(stage_kernel, n_col, a),
             out_shape=tuple(outs),
-            in_specs=[pl.BlockSpec(memory_space=pltpu.SMEM)] + vmem(4),
+            in_specs=[scalar] + vmem(4),
             out_specs=tuple(vmem(len(outs))),
             scratch_shapes=[pltpu.VMEM((256, 128), F32)],
             compiler_params=LIMIT,
@@ -515,10 +540,9 @@
     chip = jnp.concatenate([chip_first[None], chip_rest])
     chip, own_stage = lax.optimization_barrier((chip, own_stage))
     both = over("row", n_row, 1, chip)
-    stages = [own_stage, core_stage, stage(2, chip), stage(3, both)]
-    own_norm = stages[0][7:]
+    stages = [own_stage[:7], core_stage, stage(2, chip)]
     outs = pl.pallas_call(
-        functools.partial(part_kernel, n_row),
+        functools.partial(part_kernel, n_row, n_col),
         out_shape=(
             shape(shards, tokens, features),
             shape(width * width, 128),
@@ -528,7 +552,7 @@
             shape(1, features),
             shape(1, 128),
         ),
-        in_specs=vmem(7 * n_row + 6),
+        in_specs=[scalar] + vmem(7 * (n_row - 1) + 7),
         out_specs=(*vmem(1), hbm, *vmem(5)),
         scratch_shapes=[
             pltpu.VMEM((1024, 128), BF),
@@ -536,14 +560,15 @@
             pltpu.VMEM((1024, 1024), BF),
             pltpu.VMEM((1024, 1024), BF),
             pltpu.VMEM((1024, 128), F32),
-            pltpu.VMEM((1024, 128), BF),
             pltpu.VMEM((1024, 128), F32),
-            pltpu.VMEM((1024, 128), BF),
+            pltpu.VMEM((128, 2048), BF),
             pltpu.VMEM((1024, 128), F32),
             pltpu.SemaphoreType.DMA,
+            pltpu.VMEM((256, 128), F32),
+            *stage_outs,
         ],
         compiler_params=LIMIT,
-    )(*[x for s in stages for x in s[:7]], *own_norm, norm, back, first_t, second_t)
+    )(place, both, *[x for s in stages for x in s], *own_stage[7:], norm, back, final_turned, first)
     emb, final, first, second, gain, offset, bias = outs
     return emb, final, first.T, second.T, gain.reshape(-1), offset.reshape(-1), bias.reshape(-1)
 

time: 26.6 us -> 24.8 us (0.932)
  Pallas kernels: 11.8 us -> 10.6 us
  local copies, waits for them, and re-layouts: 0.7 us -> 0 us
    pallas_call x4 -> x3, Pallas kernels: 3.8 us -> 2.44 us  [stage(): pl.pallas_call(functools.partial(stage_kernel, n_col, a), out_shape=tuple...]
    unnamed x4 -> x0, local copies, waits for them, and re-layouts: 0.7 us -> none
where the time goes in v8:
time: 24.8 us; the launch traced here: 24.5 us
  Pallas kernels  10.6 us (43%)
  starting transfers between devices  9.09 us (37%)
  waiting for transfers between devices  4.02 us (16%)
  between operations  0.73 us (3%)
    ppermute x7, starting transfers between devices, over(): return lax.ppermute(array, axis, [(k, k ^ step) for k in range(size)])  9.09 us
    pallas_call x1, Pallas kernels, gathered_body(): pl.pallas_call(functools.partial(part_kernel, n_row, n_col), out_shape=(s...  5.75 us
    ppermute x7, waiting for transfers between devices, over(): return lax.ppermute(array, axis, [(k, k ^ step) for k in range(size)])  4.02 us
    pallas_call x3, Pallas kernels, stage(): pl.pallas_call(functools.partial(stage_kernel, n_col, a), out_shape=tuple...  2.44 us
    pallas_call x1, Pallas kernels, gathered_body(): pl.pallas_call(weights_kernel, out_shape=(held(8, 128), held_bf(256, 256)...  1.39 us
    pallas_call x1, Pallas kernels, gathered_body(): pl.pallas_call(pack_kernel, out_shape=held_bf(192, 128), in_specs=vmem(3)...  1.04 us
  transfers between devices with their start and end apart: 7, of which 2 were waited for; matrix products, arithmetic and copies ran while one was open for 0% of the time, Pallas kernels for 16%

profile of v8, /device:TPU:0, one launch (start us, length us, event | category | flops | bytes accessed | tf_op | source)
XLA Modules:
  0.0 24.5 jit_solution(10092886599258529282)
XLA Ops:
  0.6 1.0 %shard_map.135 = bf16[192,128]{1,0:T(8,128)(2,1)S(1)} custom-call(bf16[32,8,64]{2,1,0:T(8,128)(2,1)} %msa_ref.1, s32[8,32]{1,0:T(8,128)} %bitcast.26, bf16[8,8,128]{2,1,0:T(8,128)(2,1)} %pair_ref.1), custom_call_target="tpu_custom_call" | custom-call | tf_op jit(solution)/shard_map/pallas_call | solution.py:471
  1.7 5.1 %collective-permute-start.2 = (bf16[192,128]{1,0:T(8,128)(2,1)S(1)}, bf16[192,128]{1,0:T(8,128)(2,1)S(1)}, u32[]{:S(2)}, u32[]{:S(2)}) collective-permute-start(bf16[192,128]{1,0:T(8,128)(2,1)S(1)} %shard_map.135), channel_id=1, source_target_pairs={{0,3},{1,2},{2,1},{3,0},{4,7},{5,6},{6,5},{7,4},{8,11},{9,10},{10,... | collective-permute-start | bytes 147464 | tf_op jit(solution)/shard_map/ppermute | solution.py:478
  6.8 0.0 collective-permute-start.1
  6.8 0.6 %collective-permute-start = (bf16[192,128]{1,0:T(8,128)(2,1)S(1)}, bf16[192,128]{1,0:T(8,128)(2,1)S(1)}, u32[]{:S(2)}, u32[]{:S(2)}) collective-permute-start(bf16[192,128]{1,0:T(8,128)(2,1)S(1)} %shard_map.135), channel_id=1, source_target_pairs={{0,1},{1,0},{2,3},{3,2},{4,5},{5,4},{6,7},{7,6},{8,9},{9,8},{10,11... | collective-permute-start | bytes 147464 | tf_op jit(solution)/shard_map/ppermute | solution.py:478
  7.4 1.6 %collective-permute-start.3 = (bf16[192,128]{1,0:T(8,128)(2,1)S(1)}, bf16[192,128]{1,0:T(8,128)(2,1)S(1)}, u32[]{:S(2)}, u32[]{:S(2)}) collective-permute-start(bf16[192,128]{1,0:T(8,128)(2,1)S(1)} %shard_map.135), channel_id=1, source_target_pairs={{0,8},{4,12},{8,0},{12,4},{1,9},{5,13},{9,1},{13,5},{2,10},{6,14},... | collective-permute-start | bytes 147464 | tf_op jit(solution)/shard_map/ppermute | solution.py:478
  9.1 1.4 %shard_map.136 = (f32[8,128]{1,0:T(8,128)S(1)}, bf16[256,256]{1,0:T(8,128)(2,1)S(1)}, bf16[512,256]{1,0:T(8,128)(2,1)S(1)}, f32[64,64]{1,0:T(8,128)S(1)}) custom-call(f32[1,64]{1,0:T(1,128)} %bitcast.27, f32[1,64]{1,0:T(1,128)} %bitcast.28, bf16[32,64]{1,0:T(8,128)(2,1)} %bitcast.24, bf16[32,64]{1,0:T(8,128)(2,1)} %bitcast.25, bf16[1024,128]{1,0:T(8,128)(2,1)} %refs_4_.1), custom_call_target="tpu_custom_call" | custom-call | tf_op jit(solution)/shard_map/pallas_call | solution.py:484
  10.5 0.0 collective-permute-done.2
  10.5 1.3 %collective-permute-done.1 = bf16[192,128]{1,0:T(8,128)(2,1)S(1)} collective-permute-done((bf16[192,128]{1,0:T(8,128)(2,1)S(1)}, bf16[192,128]{1,0:T(8,128)(2,1)S(1)}, u32[]{:S(2)}, u32[]{:S(2)}) %collective-permute-start.1) | collective-permute-done | bytes 49184 | tf_op jit(solution)/shard_map/ppermute | solution.py:478
  11.8 0.0 collective-permute-done
  11.8 1.6 %collective-permute-start.4 = (bf16[3,192,128]{2,1,0:T(8,128)(2,1)S(1)}, bf16[3,192,128]{2,1,0:T(8,128)(2,1)S(1)}, u32[]{:S(2)}, u32[]{:S(2)}) collective-permute-start(bf16[3,192,128]{2,1,0:T(8,128)(2,1)S(1)} %pad_maximum_fusion.2), channel_id=1, source_target_pairs={{0,8},{4,12},{8,0},{12,4},{1,9},{5,13},{9,1},{13,5},{2,10},{6,14},... | collective-permute-start | bytes 442376 | tf_op jit(solution)/shard_map/ppermute | solution.py:478
  13.4 0.0 collective-permute-done.3
  13.4 0.1 collective-permute-start.6
  13.5 0.8 %shard_map.137 = (bf16[512,256]{1,0:T(8,128)(2,1)S(1)}, bf16[128,256]{1,0:T(8,128)(2,1)S(1)}, bf16[128,256]{1,0:T(8,128)(2,1)S(1)}, f32[32,8,128]{2,1,0:T(8,128)...) custom-call(s32[1]{0:T(128)} %bitcast.place_ref, ...), custom_call_target="tpu_custom_call" | custom-call | flops 1000000000 | bytes 4000000 | tf_op jit(solution)/shard_map/pallas_call | solution.py:526
  14.3 2.7 %collective-permute-done.4 = bf16[3,192,128]{2,1,0:T(8,128)(2,1)S(1)} collective-permute-done((bf16[3,192,128]{2,1,0:T(8,128)(2,1)S(1)}, bf16[3,192,128]{2,1,0:T(8,128)(2,1)S(1)}, u32[]{:S(2)}, u32[]{:S(2)}) %collective-permute-start.4) | collective-permute-done | bytes 147488 | tf_op jit(solution)/shard_map/ppermute | solution.py:478
  17.0 0.1 collective-permute-start.5
  17.1 0.8 %shard_map.139 = (bf16[512,256]{1,0:T(8,128)(2,1)S(1)}, bf16[128,256]{1,0:T(8,128)(2,1)S(1)}, bf16[128,256]{1,0:T(8,128)(2,1)S(1)}, f32[32,8,128]{2,1,0:T(8,128)...) custom-call(s32[1]{0:T(128)} %bitcast.place_ref, ...), custom_call_target="tpu_custom_call" | custom-call | flops 1000000000 | bytes 4000000 | tf_op jit(solution)/shard_map/pallas_call | solution.py:526
  17.9 0.0 collective-permute-done.6.set_ref
  17.9 0.8 %shard_map.138 = (bf16[512,256]{1,0:T(8,128)(2,1)S(1)}, bf16[128,256]{1,0:T(8,128)(2,1)S(1)}, bf16[128,256]{1,0:T(8,128)(2,1)S(1)}, f32[32,8,128]{2,1,0:T(8,128)...) custom-call(s32[1]{0:T(128)} %bitcast.place_ref, ...), custom_call_target="tpu_custom_call" | custom-call | flops 1000000000 | bytes 4000000 | tf_op jit(solution)/shard_map/pallas_call | solution.py:526
  18.8 0.0 collective-permute-done.5.last_ref
  18.8 5.7 %shard_map.140 = (f32[32,8,64]{2,1,0:T(8,128)}, f32[1024,128]{1,0:T(8,128)}, f32[32,64]{1,0:T(8,128)}, f32[32,64]{1,0:T(8,128)}, f32[1,64]{1,0:T(1,128)}, /*index=5*/f32[1,64]{1,0:T(1,128)}, f32[1,128]{1,0:T(1,128)}) custom-call(s32[1]{0:T(128)} %bitcast.place_ref, bf16[4,192,128]{2,1,0:T(8,128)(2,1)S(1)} %collective-permute-done.5.last_ref, ...), custom_call_target="tpu_custom_call" | custom-call | tf_op jit(solution)/shard_map/pallas_call | solution.py:544
  (3 shorter events, 0.1 us)
Async XLA Ops:
  1.7 8.8 %collective-permute-start.2 = (bf16[192,128]{1,0:T(8,128)(2,1)S(1)}, bf16[192,128]{1,0:T(8,128)(2,1)S(1)}, u32[]{:S(2)}, u32[]{:S(2)}) collective-permute-start(bf16[192,128]{1,0:T(8,128)(2,1)S(1)} %shard_map.135), channel_id=1, source_target_pairs={{0,3},{1,2},{2,1},{3,0},{4,7},{5,6},{6,5},{7,4},{8,11},{9,10},{10,... | collective-permute-start | bytes 147464 | tf_op jit(solution)/shard_map/ppermute | solution.py:478
  6.8 5.0 %collective-permute-start.1 = (bf16[192,128]{1,0:T(8,128)(2,1)S(1)}, bf16[192,128]{1,0:T(8,128)(2,1)S(1)}, u32[]{:S(2)}, u32[]{:S(2)}) collective-permute-start(bf16[192,128]{1,0:T(8,128)(2,1)S(1)} %shard_map.135), channel_id=1, source_target_pairs={{0,2},{1,3},{2,0},{3,1},{4,6},{5,7},{6,4},{7,5},{8,10},{9,11},{10,... | collective-permute-start | bytes 147464 | tf_op jit(solution)/shard_map/ppermute | solution.py:478
  6.8 5.0 %collective-permute-start = (bf16[192,128]{1,0:T(8,128)(2,1)S(1)}, bf16[192,128]{1,0:T(8,128)(2,1)S(1)}, u32[]{:S(2)}, u32[]{:S(2)}) collective-permute-start(bf16[192,128]{1,0:T(8,128)(2,1)S(1)} %shard_map.135), channel_id=1, source_target_pairs={{0,1},{1,0},{2,3},{3,2},{4,5},{5,4},{6,7},{7,6},{8,9},{9,8},{10,11... | collective-permute-start | bytes 147464 | tf_op jit(solution)/shard_map/ppermute | solution.py:478
  7.4 6.0 %collective-permute-start.3 = (bf16[192,128]{1,0:T(8,128)(2,1)S(1)}, bf16[192,128]{1,0:T(8,128)(2,1)S(1)}, u32[]{:S(2)}, u32[]{:S(2)}) collective-permute-start(bf16[192,128]{1,0:T(8,128)(2,1)S(1)} %shard_map.135), channel_id=1, source_target_pairs={{0,8},{4,12},{8,0},{12,4},{1,9},{5,13},{9,1},{13,5},{2,10},{6,14},... | collective-permute-start | bytes 147464 | tf_op jit(solution)/shard_map/ppermute | solution.py:478
  11.8 5.2 %collective-permute-start.4 = (bf16[3,192,128]{2,1,0:T(8,128)(2,1)S(1)}, bf16[3,192,128]{2,1,0:T(8,128)(2,1)S(1)}, u32[]{:S(2)}, u32[]{:S(2)}) collective-permute-start(bf16[3,192,128]{2,1,0:T(8,128)(2,1)S(1)} %pad_maximum_fusion.2), channel_id=1, source_target_pairs={{0,8},{4,12},{8,0},{12,4},{1,9},{5,13},{9,1},{13,5},{2,10},{6,14},... | collective-permute-start | bytes 442376 | tf_op jit(solution)/shard_map/ppermute | solution.py:478
  13.4 4.5 %collective-permute-start.6 = (bf16[4,192,128]{2,1,0:T(8,128)(2,1)S(1)}, bf16[4,192,128]{2,1,0:T(8,128)(2,1)S(1)}, u32[]{:S(2)}, u32[]{:S(2)}) collective-permute-start(bf16[4,192,128]{2,1,0:T(8,128)(2,1)S(1)} %pad_maximum_fusion.set_ref), channel_id=1, source_target_pairs={{0,4},{4,0},{8,12},{12,8},{1,5},{5,1},{9,13},{13,9},{2,6},{6,2},{1... | collective-permute-start | bytes 589832 | tf_op jit(solution)/shard_map/ppermute | solution.py:478
  17.0 1.7 %collective-permute-start.5 = (bf16[4,192,128]{2,1,0:T(8,128)(2,1)S(1)}, bf16[4,192,128]{2,1,0:T(8,128)(2,1)S(1)}, u32[]{:S(2)}, u32[]{:S(2)}) collective-permute-start(bf16[4,192,128]{2,1,0:T(8,128)(2,1)S(1)} %pad_maximum_fusion.1.set_ref), channel_id=1, source_target_pairs={{0,4},{4,0},{8,12},{12,8},{1,5},{5,1},{9,13},{13,9},{2,6},{6,2},{1... | collective-permute-start | bytes 589832 | tf_op jit(solution)/shard_map/ppermute | solution.py:478

commit v9 on v8

--- a/solution.py
+++ b/solution.py
@@ -252,13 +252,16 @@
     return spread(128, 128, lambda r, c: jnp.where(r // 64 == c // 64, 1.0 / 64, 0.0)).astype(BF)
 
 
+ORDER = (0, 1, 3, 2)
+
+
 def stage_kernel(
     n_col, a, place_ref, set_ref, norm_ref, back_ref, final_ref,
     rhs_out, left_out, leftt_out, rightt_out, grad_out, pair_out, found_out, *rest
 ):
     *own_out, turn_scr = rest
     for b in range(n_col):
-        at = pl.multiple_of(lax.bitwise_xor(place_ref[0], b) * 8, 8)
+        at = pl.multiple_of(lax.bitwise_xor(place_ref[0], ORDER[b]) * 8, 8)
         pair_out[:, pl.ds(at, 8), :] = set_ref[b, 128:192, :].astype(F32).reshape(8, 8, 128)
 
     gain = norm_ref[0:1, :]
@@ -321,7 +324,7 @@
     (
         normed_ref, inverse_ref, norm_ref, back_ref, final_ref, first_ref,
         emb_out, final_hbm_out, first_out, second_out, gain_out, offset_out, bias_out,
-        right_scr, scaled_scr, grad_scr, outer_scr, wide_scr, rin_scr, all_scr,
+        right_scr, scaled_scr, grad_scr, outer_scr, wide_scr, all_scr,
         final_out, out_sem, turn_scr,
     ) = refs[7 * (n_row - 1) : -7]
     stages.append(refs[-7:])
@@ -354,17 +357,23 @@
     right_grad = mm(left, grad_scr[...])
     left_grad = mm(grad_scr[...], right_scr[...])
 
-    identity = spread(128, 128, lambda r, c: jnp.where(r == c, 1.0, 0.0)).astype(BF)
-    for q in range(8):
-        at = slice(128 * q, 128 * q + 128)
-        rin_scr[at, :] = mm_nt(identity, (right_grad[:, at] * mask).astype(BF))
+    turn = spread(
+        256, 256, lambda r, c: jnp.where((r // 8 == c % 32) & (r % 8 == c // 32), 1.0, 0.0)
+    ).astype(BF)
+    mask_two = jnp.concatenate([mask, mask], axis=1)
+    right_in = [
+        mm_nt(turn, (right_grad[:, 256 * q : 256 * q + 256] * mask_two).astype(BF))
+        for q in range(4)
+    ]
     for t in range(32):
         at = slice(128 * (t // 2), 128 * (t // 2) + 128)
         row = 32 * (t % 2)
         all_scr[row : row + 32, at] = (
             left_grad[32 * t : 32 * t + 32] * mask_t[t : t + 1]
         ).astype(BF)
-        all_scr[row + 64 : row + 96, at] = rin_scr[pl.ds(t, 32, stride=32), :].astype(BF)
+        all_scr[row + 64 : row + 96, at] = jnp.concatenate(
+            [part[8 * t : 8 * t + 8] for part in right_in], axis=0
+        ).astype(BF)
 
     bias = jnp.zeros((1, 128), F32)
     ones = jnp.ones((128, 128), BF)
@@ -477,10 +486,14 @@
     def over(axis, size, step, array):
         return lax.ppermute(array, axis, [(k, k ^ step) for k in range(size)])
 
-    pieces = [packed] + [over("col", n_col, b, packed) for b in range(1, n_col)]
-    chip_first = over("row", n_row, 2, packed)
-    rest = jnp.stack(pieces[1:])
-    chip_rest = over("row", n_row, 2, rest)
+    far = over("col", n_col, 2, packed)
+    last = over("col", n_col, 3, packed)
+    near = over("col", n_col, 1, packed)
+    front = jnp.stack([packed, near])
+    chip_front = over("row", n_row, 2, front)
+    rear = jnp.stack([last, far])
+    chip_rear = over("row", n_row, 2, rear)
+    rear, final_projection_matrix = lax.optimization_barrier((rear, final_projection_matrix))
     weights = pl.pallas_call(
         weights_kernel,
         out_shape=(
@@ -511,10 +524,8 @@
         ]
     )
     norm, back, final_turned, first = weights
-    own = jnp.concatenate([packed[None], rest])
-    own, chip_first = lax.optimization_barrier((own, chip_first))
+    own = jnp.concatenate([front, rear])
     core = over("row", n_row, 1, own)
-
     stage_outs = [
         held_bf(512, 256), held_bf(128, 256), held_bf(128, 256), held(width, 8, 128),
         held_bf(256, 1024), held(8, 32, 128), held(128, 128),
@@ -537,7 +548,7 @@
 
     own_stage = stage(0, own)
     core_stage = stage(1, core)
-    chip = jnp.concatenate([chip_first[None], chip_rest])
+    chip = jnp.concatenate([chip_front, chip_rear])
     chip, own_stage = lax.optimization_barrier((chip, own_stage))
     both = over("row", n_row, 1, chip)
     stages = [own_stage[:7], core_stage, stage(2, chip)]
@@ -560,7 +571,6 @@
             pltpu.VMEM((1024, 1024), BF),
             pltpu.VMEM((1024, 1024), BF),
             pltpu.VMEM((1024, 128), F32),
-            pltpu.VMEM((1024, 128), F32),
             pltpu.VMEM((128, 2048), BF),
             pltpu.VMEM((1024, 128), F32),
             pltpu.SemaphoreType.DMA,

time: 24.8 us -> 25.6 us (1.032)
  waiting for transfers between devices: 4.02 us -> 6.15 us
  starting transfers between devices: 9.09 us -> 7.98 us
    ppermute x7, waiting for transfers between devices: 4.02 us -> 6.15 us  [over(): return lax.ppermute(array, axis, [(k, k ^ step) for k in range(size)])]
    ppermute x7, starting transfers between devices: 9.09 us -> 7.98 us  [over(): return lax.ppermute(array, axis, [(k, k ^ step) for k in range(size)])]
  transfers between devices with their start and end apart: 7 -> 7, of which waited for: 2 -> 3; matrix products, arithmetic and copies ran while one was open for 0% -> 0% of each run, Pallas kernels for 16% -> 15%
where the time goes in v9:
time: 25.6 us; the launch traced here: 25.4 us
  Pallas kernels  10.5 us (41%)
  starting transfers between devices  7.98 us (31%)
  waiting for transfers between devices  6.15 us (24%)
  between operations  0.72 us (3%)
    ppermute x7, starting transfers between devices, over(): return lax.ppermute(array, axis, [(k, k ^ step) for k in range(size)])  7.98 us
    ppermute x7, waiting for transfers between devices, over(): return lax.ppermute(array, axis, [(k, k ^ step) for k in range(size)])  6.15 us
    pallas_call x1, Pallas kernels, gathered_body(): pl.pallas_call(functools.partial(part_kernel, n_row, n_col), out_shape=(s...  5.57 us
    pallas_call x3, Pallas kernels, stage(): pl.pallas_call(functools.partial(stage_kernel, n_col, a), out_shape=tuple...  2.44 us
    pallas_call x1, Pallas kernels, gathered_body(): pl.pallas_call(weights_kernel, out_shape=(held(8, 128), held_bf(256, 256)...  1.4 us
    pallas_call x1, Pallas kernels, gathered_body(): pl.pallas_call(pack_kernel, out_shape=held_bf(192, 128), in_specs=vmem(3)...  1.04 us
  transfers between devices with their start and end apart: 7, of which 3 were waited for; matrix products, arithmetic and copies ran while one was open for 0% of the time, Pallas kernels for 15%

profile of v9, /device:TPU:0, one launch (start us, length us, event | category | flops | bytes accessed | tf_op | source)
XLA Modules:
  0.0 25.4 jit_solution(11919765094950360632)
XLA Ops:
  0.6 1.0 %shard_map.135 = bf16[192,128]{1,0:T(8,128)(2,1)S(1)} custom-call(bf16[32,8,64]{2,1,0:T(8,128)(2,1)} %msa_ref.1, s32[8,32]{1,0:T(8,128)} %bitcast.23, bf16[8,8,128]{2,1,0:T(8,128)(2,1)} %pair_ref.1), custom_call_target="tpu_custom_call" | custom-call | tf_op jit(solution)/shard_map/pallas_call | solution.py:480
  1.7 4.1 %collective-permute-start.3 = (bf16[192,128]{1,0:T(8,128)(2,1)S(1)}, bf16[192,128]{1,0:T(8,128)(2,1)S(1)}, u32[]{:S(2)}, u32[]{:S(2)}) collective-permute-start(bf16[192,128]{1,0:T(8,128)(2,1)S(1)} %shard_map.135), channel_id=1, source_target_pairs={{0,2},{1,3},{2,0},{3,1},{4,6},{5,7},{6,4},{7,5},{8,10},{9,11},{10,... | collective-permute-start | bytes 147464 | tf_op jit(solution)/shard_map/ppermute | solution.py:487
  5.8 1.3 %collective-permute-start.2 = (bf16[192,128]{1,0:T(8,128)(2,1)S(1)}, bf16[192,128]{1,0:T(8,128)(2,1)S(1)}, u32[]{:S(2)}, u32[]{:S(2)}) collective-permute-start(bf16[192,128]{1,0:T(8,128)(2,1)S(1)} %shard_map.135), channel_id=1, source_target_pairs={{0,3},{1,2},{2,1},{3,0},{4,7},{5,6},{6,5},{7,4},{8,11},{9,10},{10,... | collective-permute-start | bytes 147464 | tf_op jit(solution)/shard_map/ppermute | solution.py:487
  7.1 0.2 collective-permute-start
  7.4 1.0 %collective-permute-done.3 = bf16[192,128]{1,0:T(8,128)(2,1)S(1)} collective-permute-done((bf16[192,128]{1,0:T(8,128)(2,1)S(1)}, bf16[192,128]{1,0:T(8,128)(2,1)S(1)}, u32[]{:S(2)}, u32[]{:S(2)}) %collective-permute-start.3) | collective-permute-done | bytes 49184 | tf_op jit(solution)/shard_map/ppermute | solution.py:487
  8.4 3.4 %collective-permute-done.2 = bf16[192,128]{1,0:T(8,128)(2,1)S(1)} collective-permute-done((bf16[192,128]{1,0:T(8,128)(2,1)S(1)}, bf16[192,128]{1,0:T(8,128)(2,1)S(1)}, u32[]{:S(2)}, u32[]{:S(2)}) %collective-permute-start.2) | collective-permute-done | bytes 49184 | tf_op jit(solution)/shard_map/ppermute | solution.py:487
  11.8 1.6 %collective-permute-start.4 = (bf16[2,192,128]{2,1,0:T(8,128)(2,1)S(1)}, bf16[2,192,128]{2,1,0:T(8,128)(2,1)S(1)}, u32[]{:S(2)}, u32[]{:S(2)}) collective-permute-start(bf16[2,192,128]{2,1,0:T(8,128)(2,1)S(1)} %pad_maximum_fusion.3), channel_id=1, source_target_pairs={{0,8},{4,12},{8,0},{12,4},{1,9},{5,13},{9,1},{13,5},{2,10},{6,14},... | collective-permute-start | bytes 294920 | tf_op jit(solution)/shard_map/ppermute | solution.py:487
  13.3 0.0 collective-permute-done
  13.3 0.6 %collective-permute-start.1 = (bf16[2,192,128]{2,1,0:T(8,128)(2,1)S(1)}, bf16[2,192,128]{2,1,0:T(8,128)(2,1)S(1)}, u32[]{:S(2)}, u32[]{:S(2)}) collective-permute-start(bf16[2,192,128]{2,1,0:T(8,128)(2,1)S(1)} %pad_maximum_fusion.2), channel_id=1, source_target_pairs={{0,8},{4,12},{8,0},{12,4},{1,9},{5,13},{9,1},{13,5},{2,10},{6,14},... | collective-permute-start | bytes 294920 | tf_op jit(solution)/shard_map/ppermute | solution.py:487
  14.0 0.1 collective-permute-start.6
  14.0 1.4 %shard_map.136 = (f32[8,128]{1,0:T(8,128)S(1)}, bf16[256,256]{1,0:T(8,128)(2,1)S(1)}, bf16[512,256]{1,0:T(8,128)(2,1)S(1)}, f32[64,64]{1,0:T(8,128)S(1)}) custom-call(f32[1,64]{1,0:T(1,128)} %bitcast.24, f32[1,64]{1,0:T(1,128)} %bitcast.25, bf16[32,64]{1,0:T(8,128)(2,1)} %bitcast.21, bf16[32,64]{1,0:T(8,128)(2,1)} %bitcast.22, bf16[1024,128]{1,0:T(8,128)(2,1)} %refs_4_), custom_call_target="tpu_custom_call" | custom-call | tf_op jit(solution)/shard_map/pallas_call | solution.py:497
  15.4 0.8 %shard_map.137 = (bf16[512,256]{1,0:T(8,128)(2,1)S(1)}, bf16[128,256]{1,0:T(8,128)(2,1)S(1)}, bf16[128,256]{1,0:T(8,128)(2,1)S(1)}, f32[32,8,128]{2,1,0:T(8,128)...) custom-call(s32[1]{0:T(128)} %bitcast.place_ref, ...), custom_call_target="tpu_custom_call" | custom-call | flops 1000000000 | bytes 4000000 | tf_op jit(solution)/shard_map/pallas_call | solution.py:537
  16.3 1.8 %collective-permute-done.1 = bf16[2,192,128]{2,1,0:T(8,128)(2,1)S(1)} collective-permute-done((bf16[2,192,128]{2,1,0:T(8,128)(2,1)S(1)}, bf16[2,192,128]{2,1,0:T(8,128)(2,1)S(1)}, u32[]{:S(2)}, u32[]{:S(2)}) %collective-permute-start.1) | collective-permute-done | bytes 98336 | tf_op jit(solution)/shard_map/ppermute | solution.py:487
  18.0 0.0 collective-permute-done.4
  18.0 0.1 collective-permute-start.5
  18.1 0.8 %shard_map.139 = (bf16[512,256]{1,0:T(8,128)(2,1)S(1)}, bf16[128,256]{1,0:T(8,128)(2,1)S(1)}, bf16[128,256]{1,0:T(8,128)(2,1)S(1)}, f32[32,8,128]{2,1,0:T(8,128)...) custom-call(s32[1]{0:T(128)} %bitcast.place_ref, ...), custom_call_target="tpu_custom_call" | custom-call | flops 1000000000 | bytes 4000000 | tf_op jit(solution)/shard_map/pallas_call | solution.py:537
  18.9 0.0 collective-permute-done.6.set_ref
  19.0 0.8 %shard_map.138 = (bf16[512,256]{1,0:T(8,128)(2,1)S(1)}, bf16[128,256]{1,0:T(8,128)(2,1)S(1)}, bf16[128,256]{1,0:T(8,128)(2,1)S(1)}, f32[32,8,128]{2,1,0:T(8,128)...) custom-call(s32[1]{0:T(128)} %bitcast.place_ref, ...), custom_call_target="tpu_custom_call" | custom-call | flops 1000000000 | bytes 4000000 | tf_op jit(solution)/shard_map/pallas_call | solution.py:537
  19.8 0.0 collective-permute-done.5.last_ref
  19.8 5.6 %shard_map.140 = (f32[32,8,64]{2,1,0:T(8,128)}, f32[1024,128]{1,0:T(8,128)}, f32[32,64]{1,0:T(8,128)}, f32[32,64]{1,0:T(8,128)}, f32[1,64]{1,0:T(1,128)}, /*index=5*/f32[1,64]{1,0:T(1,128)}, f32[1,128]{1,0:T(1,128)}) custom-call(s32[1]{0:T(128)} %bitcast.place_ref, bf16[4,192,128]{2,1,0:T(8,128)(2,1)S(1)} %collective-permute-done.5.last_ref, ...), custom_call_target="tpu_custom_call" | custom-call | tf_op jit(solution)/shard_map/pallas_call | solution.py:555
  (4 shorter events, 0.1 us)
Async XLA Ops:
  1.7 6.7 %collective-permute-start.3 = (bf16[192,128]{1,0:T(8,128)(2,1)S(1)}, bf16[192,128]{1,0:T(8,128)(2,1)S(1)}, u32[]{:S(2)}, u32[]{:S(2)}) collective-permute-start(bf16[192,128]{1,0:T(8,128)(2,1)S(1)} %shard_map.135), channel_id=1, source_target_pairs={{0,2},{1,3},{2,0},{3,1},{4,6},{5,7},{6,4},{7,5},{8,10},{9,11},{10,... | collective-permute-start | bytes 147464 | tf_op jit(solution)/shard_map/ppermute | solution.py:487
  5.8 6.0 %collective-permute-start.2 = (bf16[192,128]{1,0:T(8,128)(2,1)S(1)}, bf16[192,128]{1,0:T(8,128)(2,1)S(1)}, u32[]{:S(2)}, u32[]{:S(2)}) collective-permute-start(bf16[192,128]{1,0:T(8,128)(2,1)S(1)} %shard_map.135), channel_id=1, source_target_pairs={{0,3},{1,2},{2,1},{3,0},{4,7},{5,6},{6,5},{7,4},{8,11},{9,10},{10,... | collective-permute-start | bytes 147464 | tf_op jit(solution)/shard_map/ppermute | solution.py:487
  7.1 6.2 %collective-permute-start = (bf16[192,128]{1,0:T(8,128)(2,1)S(1)}, bf16[192,128]{1,0:T(8,128)(2,1)S(1)}, u32[]{:S(2)}, u32[]{:S(2)}) collective-permute-start(bf16[192,128]{1,0:T(8,128)(2,1)S(1)} %shard_map.135), channel_id=1, source_target_pairs={{0,1},{1,0},{2,3},{3,2},{4,5},{5,4},{6,7},{7,6},{8,9},{9,8},{10,11... | collective-permute-start | bytes 147464 | tf_op jit(solution)/shard_map/ppermute | solution.py:487
  11.8 6.3 %collective-permute-start.4 = (bf16[2,192,128]{2,1,0:T(8,128)(2,1)S(1)}, bf16[2,192,128]{2,1,0:T(8,128)(2,1)S(1)}, u32[]{:S(2)}, u32[]{:S(2)}) collective-permute-start(bf16[2,192,128]{2,1,0:T(8,128)(2,1)S(1)} %pad_maximum_fusion.3), channel_id=1, source_target_pairs={{0,8},{4,12},{8,0},{12,4},{1,9},{5,13},{9,1},{13,5},{2,10},{6,14},... | collective-permute-start | bytes 294920 | tf_op jit(solution)/shard_map/ppermute | solution.py:487
  13.3 4.7 %collective-permute-start.1 = (bf16[2,192,128]{2,1,0:T(8,128)(2,1)S(1)}, bf16[2,192,128]{2,1,0:T(8,128)(2,1)S(1)}, u32[]{:S(2)}, u32[]{:S(2)}) collective-permute-start(bf16[2,192,128]{2,1,0:T(8,128)(2,1)S(1)} %pad_maximum_fusion.2), channel_id=1, source_target_pairs={{0,8},{4,12},{8,0},{12,4},{1,9},{5,13},{9,1},{13,5},{2,10},{6,14},... | collective-permute-start | bytes 294920 | tf_op jit(solution)/shard_map/ppermute | solution.py:487
  14.0 5.0 %collective-permute-start.6 = (bf16[4,192,128]{2,1,0:T(8,128)(2,1)S(1)}, bf16[4,192,128]{2,1,0:T(8,128)(2,1)S(1)}, u32[]{:S(2)}, u32[]{:S(2)}) collective-permute-start(bf16[4,192,128]{2,1,0:T(8,128)(2,1)S(1)} %pad_maximum_fusion.1.set_ref), channel_id=1, source_target_pairs={{0,4},{4,0},{8,12},{12,8},{1,5},{5,1},{9,13},{13,9},{2,6},{6,2},{1... | collective-permute-start | bytes 589832 | tf_op jit(solution)/shard_map/ppermute | solution.py:487
  18.0 1.7 %collective-permute-start.5 = (bf16[4,192,128]{2,1,0:T(8,128)(2,1)S(1)}, bf16[4,192,128]{2,1,0:T(8,128)(2,1)S(1)}, u32[]{:S(2)}, u32[]{:S(2)}) collective-permute-start(bf16[4,192,128]{2,1,0:T(8,128)(2,1)S(1)} %pad_maximum_fusion.set_ref), channel_id=1, source_target_pairs={{0,4},{4,0},{8,12},{12,8},{1,5},{5,1},{9,13},{13,9},{2,6},{6,2},{1... | collective-permute-start | bytes 589832 | tf_op jit(solution)/shard_map/ppermute | solution.py:487

commit v10 on v9

--- a/solution.py
+++ b/solution.py
@@ -252,7 +252,7 @@
     return spread(128, 128, lambda r, c: jnp.where(r // 64 == c // 64, 1.0 / 64, 0.0)).astype(BF)
 
 
-ORDER = (0, 1, 3, 2)
+ORDER = (0, 3, 1, 2)
 
 
 def stage_kernel(
@@ -487,13 +487,13 @@
         return lax.ppermute(array, axis, [(k, k ^ step) for k in range(size)])
 
     far = over("col", n_col, 2, packed)
+    near = over("col", n_col, 1, packed)
     last = over("col", n_col, 3, packed)
-    near = over("col", n_col, 1, packed)
-    front = jnp.stack([packed, near])
+    front = jnp.stack([packed, last])
     chip_front = over("row", n_row, 2, front)
-    rear = jnp.stack([last, far])
+    rear = jnp.stack([near, far])
     chip_rear = over("row", n_row, 2, rear)
-    rear, final_projection_matrix = lax.optimization_barrier((rear, final_projection_matrix))
+    front, final_projection_matrix = lax.optimization_barrier((front, final_projection_matrix))
     weights = pl.pallas_call(
         weights_kernel,
         out_shape=(

time: 25.6 us -> 24.1 us (0.941)
  waiting for transfers between devices: 6.15 us -> 3.27 us
  starting transfers between devices: 7.98 us -> 9.32 us
    ppermute x7, waiting for transfers between devices: 6.15 us -> 3.27 us  [over(): return lax.ppermute(array, axis, [(k, k ^ step) for k in range(size)])]
    ppermute x7, starting transfers between devices: 7.98 us -> 9.32 us  [over(): return lax.ppermute(array, axis, [(k, k ^ step) for k in range(size)])]
  transfers between devices with their start and end apart: 7 -> 7, of which waited for: 3 -> 3; matrix products, arithmetic and copies ran while one was open for 0% -> 0% of each run, Pallas kernels for 15% -> 16%
where the time goes in v10:
time: 24.1 us; the launch traced here: 23.8 us
  Pallas kernels  10.5 us (44%)
  starting transfers between devices  9.32 us (39%)
  waiting for transfers between devices  3.27 us (14%)
  between operations  0.72 us (3%)
    ppermute x7, starting transfers between devices, over(): return lax.ppermute(array, axis, [(k, k ^ step) for k in range(size)])  9.32 us
    pallas_call x1, Pallas kernels, gathered_body(): pl.pallas_call(functools.partial(part_kernel, n_row, n_col), out_shape=(s...  5.57 us
    ppermute x7, waiting for transfers between devices, over(): return lax.ppermute(array, axis, [(k, k ^ step) for k in range(size)])  3.27 us
    pallas_call x3, Pallas kernels, stage(): pl.pallas_call(functools.partial(stage_kernel, n_col, a), out_shape=tuple...  2.44 us
    pallas_call x1, Pallas kernels, gathered_body(): pl.pallas_call(weights_kernel, out_shape=(held(8, 128), held_bf(256, 256)...  1.4 us
    pallas_call x1, Pallas kernels, gathered_body(): pl.pallas_call(pack_kernel, out_shape=held_bf(192, 128), in_specs=vmem(3)...  1.04 us
  transfers between devices with their start and end apart: 7, of which 3 were waited for; matrix products, arithmetic and copies ran while one was open for 0% of the time, Pallas kernels for 16%

profile of v10, /device:TPU:0, one launch (start us, length us, event | category | flops | bytes accessed | tf_op | source)
XLA Modules:
  0.0 23.8 jit_solution(16995398249998462848)
XLA Ops:
  0.6 1.0 %shard_map.135 = bf16[192,128]{1,0:T(8,128)(2,1)S(1)} custom-call(bf16[32,8,64]{2,1,0:T(8,128)(2,1)} %msa_ref.1, s32[8,32]{1,0:T(8,128)} %bitcast.23, bf16[8,8,128]{2,1,0:T(8,128)(2,1)} %pair_ref.1), custom_call_target="tpu_custom_call" | custom-call | tf_op jit(solution)/shard_map/pallas_call | solution.py:480
  1.7 5.1 %collective-permute-start = (bf16[192,128]{1,0:T(8,128)(2,1)S(1)}, bf16[192,128]{1,0:T(8,128)(2,1)S(1)}, u32[]{:S(2)}, u32[]{:S(2)}) collective-permute-start(bf16[192,128]{1,0:T(8,128)(2,1)S(1)} %shard_map.135), channel_id=1, source_target_pairs={{0,3},{1,2},{2,1},{3,0},{4,7},{5,6},{6,5},{7,4},{8,11},{9,10},{10,... | collective-permute-start | bytes 147464 | tf_op jit(solution)/shard_map/ppermute | solution.py:487
  6.8 0.0 collective-permute-start.3
  6.8 0.6 %collective-permute-start.2 = (bf16[192,128]{1,0:T(8,128)(2,1)S(1)}, bf16[192,128]{1,0:T(8,128)(2,1)S(1)}, u32[]{:S(2)}, u32[]{:S(2)}) collective-permute-start(bf16[192,128]{1,0:T(8,128)(2,1)S(1)} %shard_map.135), channel_id=1, source_target_pairs={{0,1},{1,0},{2,3},{3,2},{4,5},{5,4},{6,7},{7,6},{8,9},{9,8},{10,11... | collective-permute-start | bytes 147464 | tf_op jit(solution)/shard_map/ppermute | solution.py:487
  7.4 1.6 %collective-permute-done = bf16[192,128]{1,0:T(8,128)(2,1)S(1)} collective-permute-done((bf16[192,128]{1,0:T(8,128)(2,1)S(1)}, bf16[192,128]{1,0:T(8,128)(2,1)S(1)}, u32[]{:S(2)}, u32[]{:S(2)}) %collective-permute-start) | collective-permute-done | bytes 49184 | tf_op jit(solution)/shard_map/ppermute | solution.py:487
  9.0 1.9 %collective-permute-start.1 = (bf16[2,192,128]{2,1,0:T(8,128)(2,1)S(1)}, bf16[2,192,128]{2,1,0:T(8,128)(2,1)S(1)}, u32[]{:S(2)}, u32[]{:S(2)}) collective-permute-start(bf16[2,192,128]{2,1,0:T(8,128)(2,1)S(1)} %pad_maximum_fusion.2), channel_id=1, source_target_pairs={{0,8},{4,12},{8,0},{12,4},{1,9},{5,13},{9,1},{13,5},{2,10},{6,14},... | collective-permute-start | bytes 294920 | tf_op jit(solution)/shard_map/ppermute | solution.py:487
  10.9 0.9 %collective-permute-done.3 = bf16[192,128]{1,0:T(8,128)(2,1)S(1)} collective-permute-done((bf16[192,128]{1,0:T(8,128)(2,1)S(1)}, bf16[192,128]{1,0:T(8,128)(2,1)S(1)}, u32[]{:S(2)}, u32[]{:S(2)}) %collective-permute-start.3) | collective-permute-done | bytes 49184 | tf_op jit(solution)/shard_map/ppermute | solution.py:487
  11.8 0.0 collective-permute-done.2
  11.8 1.6 %collective-permute-start.4 = (bf16[2,192,128]{2,1,0:T(8,128)(2,1)S(1)}, bf16[2,192,128]{2,1,0:T(8,128)(2,1)S(1)}, u32[]{:S(2)}, u32[]{:S(2)}) collective-permute-start(bf16[2,192,128]{2,1,0:T(8,128)(2,1)S(1)} %pad_maximum_fusion.3), channel_id=1, source_target_pairs={{0,8},{4,12},{8,0},{12,4},{1,9},{5,13},{9,1},{13,5},{2,10},{6,14},... | collective-permute-start | bytes 294920 | tf_op jit(solution)/shard_map/ppermute | solution.py:487
  13.4 0.1 collective-permute-start.6
  13.5 1.4 %shard_map.136 = (f32[8,128]{1,0:T(8,128)S(1)}, bf16[256,256]{1,0:T(8,128)(2,1)S(1)}, bf16[512,256]{1,0:T(8,128)(2,1)S(1)}, f32[64,64]{1,0:T(8,128)S(1)}) custom-call(f32[1,64]{1,0:T(1,128)} %bitcast.24, f32[1,64]{1,0:T(1,128)} %bitcast.25, bf16[32,64]{1,0:T(8,128)(2,1)} %bitcast.21, bf16[32,64]{1,0:T(8,128)(2,1)} %bitcast.22, bf16[1024,128]{1,0:T(8,128)(2,1)} %refs_4_), custom_call_target="tpu_custom_call" | custom-call | tf_op jit(solution)/shard_map/pallas_call | solution.py:497
  14.9 0.8 %shard_map.137 = (bf16[512,256]{1,0:T(8,128)(2,1)S(1)}, bf16[128,256]{1,0:T(8,128)(2,1)S(1)}, bf16[128,256]{1,0:T(8,128)(2,1)S(1)}, f32[32,8,128]{2,1,0:T(8,128)...) custom-call(s32[1]{0:T(128)} %bitcast.place_ref, ...), custom_call_target="tpu_custom_call" | custom-call | flops 1000000000 | bytes 4000000 | tf_op jit(solution)/shard_map/pallas_call | solution.py:537
  15.7 0.8 %collective-permute-done.4 = bf16[2,192,128]{2,1,0:T(8,128)(2,1)S(1)} collective-permute-done((bf16[2,192,128]{2,1,0:T(8,128)(2,1)S(1)}, bf16[2,192,128]{2,1,0:T(8,128)(2,1)S(1)}, u32[]{:S(2)}, u32[]{:S(2)}) %collective-permute-start.4) | collective-permute-done | bytes 98336 | tf_op jit(solution)/shard_map/ppermute | solution.py:487
  16.5 0.0 collective-permute-done.1
  16.5 0.1 collective-permute-start.5
  16.6 0.8 %shard_map.139 = (bf16[512,256]{1,0:T(8,128)(2,1)S(1)}, bf16[128,256]{1,0:T(8,128)(2,1)S(1)}, bf16[128,256]{1,0:T(8,128)(2,1)S(1)}, f32[32,8,128]{2,1,0:T(8,128)...) custom-call(s32[1]{0:T(128)} %bitcast.place_ref, ...), custom_call_target="tpu_custom_call" | custom-call | flops 1000000000 | bytes 4000000 | tf_op jit(solution)/shard_map/pallas_call | solution.py:537
  17.4 0.0 collective-permute-done.6.set_ref
  17.4 0.8 %shard_map.138 = (bf16[512,256]{1,0:T(8,128)(2,1)S(1)}, bf16[128,256]{1,0:T(8,128)(2,1)S(1)}, bf16[128,256]{1,0:T(8,128)(2,1)S(1)}, f32[32,8,128]{2,1,0:T(8,128)...) custom-call(s32[1]{0:T(128)} %bitcast.place_ref, ...), custom_call_target="tpu_custom_call" | custom-call | flops 1000000000 | bytes 4000000 | tf_op jit(solution)/shard_map/pallas_call | solution.py:537
  18.2 0.0 collective-permute-done.5.last_ref
  18.3 5.6 %shard_map.140 = (f32[32,8,64]{2,1,0:T(8,128)}, f32[1024,128]{1,0:T(8,128)}, f32[32,64]{1,0:T(8,128)}, f32[32,64]{1,0:T(8,128)}, f32[1,64]{1,0:T(1,128)}, /*index=5*/f32[1,64]{1,0:T(1,128)}, f32[1,128]{1,0:T(1,128)}) custom-call(s32[1]{0:T(128)} %bitcast.place_ref, bf16[4,192,128]{2,1,0:T(8,128)(2,1)S(1)} %collective-permute-done.5.last_ref, ...), custom_call_target="tpu_custom_call" | custom-call | tf_op jit(solution)/shard_map/pallas_call | solution.py:555
  (4 shorter events, 0.1 us)
Async XLA Ops:
  1.7 7.3 %collective-permute-start = (bf16[192,128]{1,0:T(8,128)(2,1)S(1)}, bf16[192,128]{1,0:T(8,128)(2,1)S(1)}, u32[]{:S(2)}, u32[]{:S(2)}) collective-permute-start(bf16[192,128]{1,0:T(8,128)(2,1)S(1)} %shard_map.135), channel_id=1, source_target_pairs={{0,3},{1,2},{2,1},{3,0},{4,7},{5,6},{6,5},{7,4},{8,11},{9,10},{10,... | collective-permute-start | bytes 147464 | tf_op jit(solution)/shard_map/ppermute | solution.py:487
  6.8 5.0 %collective-permute-start.3 = (bf16[192,128]{1,0:T(8,128)(2,1)S(1)}, bf16[192,128]{1,0:T(8,128)(2,1)S(1)}, u32[]{:S(2)}, u32[]{:S(2)}) collective-permute-start(bf16[192,128]{1,0:T(8,128)(2,1)S(1)} %shard_map.135), channel_id=1, source_target_pairs={{0,2},{1,3},{2,0},{3,1},{4,6},{5,7},{6,4},{7,5},{8,10},{9,11},{10,... | collective-permute-start | bytes 147464 | tf_op jit(solution)/shard_map/ppermute | solution.py:487
  6.8 5.0 %collective-permute-start.2 = (bf16[192,128]{1,0:T(8,128)(2,1)S(1)}, bf16[192,128]{1,0:T(8,128)(2,1)S(1)}, u32[]{:S(2)}, u32[]{:S(2)}) collective-permute-start(bf16[192,128]{1,0:T(8,128)(2,1)S(1)} %shard_map.135), channel_id=1, source_target_pairs={{0,1},{1,0},{2,3},{3,2},{4,5},{5,4},{6,7},{7,6},{8,9},{9,8},{10,11... | collective-permute-start | bytes 147464 | tf_op jit(solution)/shard_map/ppermute | solution.py:487
  9.0 7.5 %collective-permute-start.1 = (bf16[2,192,128]{2,1,0:T(8,128)(2,1)S(1)}, bf16[2,192,128]{2,1,0:T(8,128)(2,1)S(1)}, u32[]{:S(2)}, u32[]{:S(2)}) collective-permute-start(bf16[2,192,128]{2,1,0:T(8,128)(2,1)S(1)} %pad_maximum_fusion.2), channel_id=1, source_target_pairs={{0,8},{4,12},{8,0},{12,4},{1,9},{5,13},{9,1},{13,5},{2,10},{6,14},... | collective-permute-start | bytes 294920 | tf_op jit(solution)/shard_map/ppermute | solution.py:487
  11.8 4.7 %collective-permute-start.4 = (bf16[2,192,128]{2,1,0:T(8,128)(2,1)S(1)}, bf16[2,192,128]{2,1,0:T(8,128)(2,1)S(1)}, u32[]{:S(2)}, u32[]{:S(2)}) collective-permute-start(bf16[2,192,128]{2,1,0:T(8,128)(2,1)S(1)} %pad_maximum_fusion.3), channel_id=1, source_target_pairs={{0,8},{4,12},{8,0},{12,4},{1,9},{5,13},{9,1},{13,5},{2,10},{6,14},... | collective-permute-start | bytes 294920 | tf_op jit(solution)/shard_map/ppermute | solution.py:487
  13.4 4.0 %collective-permute-start.6 = (bf16[4,192,128]{2,1,0:T(8,128)(2,1)S(1)}, bf16[4,192,128]{2,1,0:T(8,128)(2,1)S(1)}, u32[]{:S(2)}, u32[]{:S(2)}) collective-permute-start(bf16[4,192,128]{2,1,0:T(8,128)(2,1)S(1)} %pad_maximum_fusion.1.set_ref), channel_id=1, source_target_pairs={{0,4},{4,0},{8,12},{12,8},{1,5},{5,1},{9,13},{13,9},{2,6},{6,2},{1... | collective-permute-start | bytes 589832 | tf_op jit(solution)/shard_map/ppermute | solution.py:487
  16.5 1.7 %collective-permute-start.5 = (bf16[4,192,128]{2,1,0:T(8,128)(2,1)S(1)}, bf16[4,192,128]{2,1,0:T(8,128)(2,1)S(1)}, u32[]{:S(2)}, u32[]{:S(2)}) collective-permute-start(bf16[4,192,128]{2,1,0:T(8,128)(2,1)S(1)} %pad_maximum_fusion.set_ref), channel_id=1, source_target_pairs={{0,4},{4,0},{8,12},{12,8},{1,5},{5,1},{9,13},{13,9},{2,6},{6,2},{1... | collective-permute-start | bytes 589832 | tf_op jit(solution)/shard_map/ppermute | solution.py:487

commit v11 on v10

--- a/solution.py
+++ b/solution.py
@@ -324,7 +324,7 @@
     (
         normed_ref, inverse_ref, norm_ref, back_ref, final_ref, first_ref,
         emb_out, final_hbm_out, first_out, second_out, gain_out, offset_out, bias_out,
-        right_scr, scaled_scr, grad_scr, outer_scr, wide_scr, all_scr,
+        right_scr, scaled_scr, grad_scr, outer_scr, all_scr,
         final_out, out_sem, turn_scr,
     ) = refs[7 * (n_row - 1) : -7]
     stages.append(refs[-7:])
@@ -346,12 +346,13 @@
         ).astype(BF)
 
     mask_bf = mask.astype(BF)
-    share = (1.0 / (mm_tn(mask_bf, mask_bf)[0:32] + 0.001)).astype(BF)
+    share = 1.0 / (mm_tn(mask_bf, mask_bf)[0:32] + 0.001)
+    share_bf = share.astype(BF)
     for i in range(32):
         a, at = i // 8, 32 * (i % 8)
         for q in range(8):
             grad_scr[32 * i : 32 * i + 32, 128 * q : 128 * q + 128] = (
-                stages[a][4][at : at + 32, 128 * q : 128 * q + 128] * share[i : i + 1]
+                stages[a][4][at : at + 32, 128 * q : 128 * q + 128] * share_bf[i : i + 1]
             )
     left = jnp.concatenate([stage[1][...] for stage in stages], axis=1)
     right_grad = mm(left, grad_scr[...])
@@ -375,18 +376,20 @@
             [part[8 * t : 8 * t + 8] for part in right_in], axis=0
         ).astype(BF)
 
-    bias = jnp.zeros((1, 128), F32)
-    ones = jnp.ones((128, 128), BF)
-    for p in range(8):
-        both_on = jnp.concatenate(
-            [mask_t[0:32] * mask_t[i : i + 1] for i in range(4 * p, 4 * p + 4)], axis=0
-        ).astype(BF)
-        counts = mm(both_on, ones)
-        pair = stages[p // 2][5][4 * (p % 2) : 4 * (p % 2) + 4]
-        scaled = pair.reshape(128, 128) / (counts + 0.001)
-        bias = bias + jnp.sum(scaled, axis=0, keepdims=True)
-        scaled_scr[128 * p : 128 * p + 128, :] = scaled.astype(BF)
-    bias_out[...] = bias
+    bias = jnp.zeros((32, 128), F32)
+    zero = jnp.zeros((32, 128), BF)
+    for k in range(16):
+        for half in range(2):
+            i = 4 * (k // 2) + k % 2 + 2 * half
+            scaled = stages[i // 8][5][i % 8] * jnp.broadcast_to(share[:, i : i + 1], (32, 128))
+            bias = bias + scaled
+            scaled = scaled.astype(BF)
+            at = 128 * k + 64 * half
+            scaled_scr[at : at + 32, 0:128] = scaled
+            scaled_scr[at : at + 32, 128:256] = zero
+            scaled_scr[at + 32 : at + 64, 0:128] = zero
+            scaled_scr[at + 32 : at + 64, 128:256] = scaled
+    bias_out[...] = jnp.sum(bias, axis=0, keepdims=True)
 
     left_t = jnp.concatenate([stage[2][...] for stage in stages], axis=0)
     for n in range(8):
@@ -395,15 +398,16 @@
         )
         outer = mm_nt(left_t, rights).astype(BF)
         for p in range(2):
-            for q in range(8):
-                rows = 64 * (2 * n + p)
-                block = outer[64 * q : 64 * q + 64, 128 * p : 128 * p + 128]
-                even, odd = interleave(block[:32], block[32:])
-                outer_scr[rows : rows + 32, 128 * q : 128 * q + 128] = even
-                outer_scr[rows + 32 : rows + 64, 128 * q : 128 * q + 128] = odd
-    wide_scr[...] = mm(outer_scr[...], scaled_scr[...])
-    for c in range(32):
-        final_out[32 * c : 32 * c + 32, :] = wide_scr[pl.ds(c, 32, stride=32), :]
+            rows = 32 * (2 * n + p)
+            for k in range(16):
+                outer_scr[rows : rows + 32, 128 * k : 128 * k + 128] = (
+                    outer[32 * k : 32 * k + 32, 128 * p : 128 * p + 128]
+                )
+    final = mm(outer_scr[...], scaled_scr[...])
+    for e in range(32):
+        final_out[pl.ds(e, 32, stride=32), :] = (
+            final[32 * (e // 2) : 32 * (e // 2) + 32, 128 * (e % 2) : 128 * (e % 2) + 128]
+        )
     final_send = pltpu.make_async_copy(final_out, final_hbm_out, out_sem)
     final_send.start()
 
@@ -567,10 +571,9 @@
         out_specs=(*vmem(1), hbm, *vmem(5)),
         scratch_shapes=[
             pltpu.VMEM((1024, 128), BF),
-            pltpu.VMEM((1024, 128), BF),
+            pltpu.VMEM((2048, 256), BF),
             pltpu.VMEM((1024, 1024), BF),
-            pltpu.VMEM((1024, 1024), BF),
-            pltpu.VMEM((1024, 128), F32),
+            pltpu.VMEM((512, 2048), BF),
             pltpu.VMEM((128, 2048), BF),
             pltpu.VMEM((1024, 128), F32),
             pltpu.SemaphoreType.DMA,

time: 24.1 us -> 24.3 us (level)
    pallas_call x1, Pallas kernels: 5.57 us -> 5.86 us  [gathered_body(): pl.pallas_call(functools.partial(part_kernel, n_row, n_col), out_shape=(s...]
where the time goes in v11:
time: 24.3 us; the launch traced here: 24.1 us
  Pallas kernels  10.7 us (44%)
  starting transfers between devices  9.32 us (38%)
  waiting for transfers between devices  3.27 us (13%)
  between operations  0.72 us (3%)
    ppermute x7, starting transfers between devices, over(): return lax.ppermute(array, axis, [(k, k ^ step) for k in range(size)])  9.32 us
    pallas_call x1, Pallas kernels, gathered_body(): pl.pallas_call(functools.partial(part_kernel, n_row, n_col), out_shape=(s...  5.86 us
    ppermute x7, waiting for transfers between devices, over(): return lax.ppermute(array, axis, [(k, k ^ step) for k in range(size)])  3.27 us
    pallas_call x3, Pallas kernels, stage(): pl.pallas_call(functools.partial(stage_kernel, n_col, a), out_shape=tuple...  2.44 us
    pallas_call x1, Pallas kernels, gathered_body(): pl.pallas_call(weights_kernel, out_shape=(held(8, 128), held_bf(256, 256)...  1.4 us
    pallas_call x1, Pallas kernels, gathered_body(): pl.pallas_call(pack_kernel, out_shape=held_bf(192, 128), in_specs=vmem(3)...  1.04 us
  transfers between devices with their start and end apart: 7, of which 3 were waited for; matrix products, arithmetic and copies ran while one was open for 0% of the time, Pallas kernels for 16%

profile of v11, /device:TPU:0, one launch (start us, length us, event | category | flops | bytes accessed | tf_op | source)
XLA Modules:
  0.0 24.1 jit_solution(16330486217876355944)
XLA Ops:
  0.6 1.0 %shard_map.135 = bf16[192,128]{1,0:T(8,128)(2,1)S(1)} custom-call(bf16[32,8,64]{2,1,0:T(8,128)(2,1)} %msa_ref.1, s32[8,32]{1,0:T(8,128)} %bitcast.23, bf16[8,8,128]{2,1,0:T(8,128)(2,1)} %pair_ref.1), custom_call_target="tpu_custom_call" | custom-call | tf_op jit(solution)/shard_map/pallas_call | solution.py:484
  1.7 5.1 %collective-permute-start = (bf16[192,128]{1,0:T(8,128)(2,1)S(1)}, bf16[192,128]{1,0:T(8,128)(2,1)S(1)}, u32[]{:S(2)}, u32[]{:S(2)}) collective-permute-start(bf16[192,128]{1,0:T(8,128)(2,1)S(1)} %shard_map.135), channel_id=1, source_target_pairs={{0,3},{1,2},{2,1},{3,0},{4,7},{5,6},{6,5},{7,4},{8,11},{9,10},{10,... | collective-permute-start | bytes 147464 | tf_op jit(solution)/shard_map/ppermute | solution.py:491
  6.8 0.0 collective-permute-start.3
  6.8 0.6 %collective-permute-start.2 = (bf16[192,128]{1,0:T(8,128)(2,1)S(1)}, bf16[192,128]{1,0:T(8,128)(2,1)S(1)}, u32[]{:S(2)}, u32[]{:S(2)}) collective-permute-start(bf16[192,128]{1,0:T(8,128)(2,1)S(1)} %shard_map.135), channel_id=1, source_target_pairs={{0,1},{1,0},{2,3},{3,2},{4,5},{5,4},{6,7},{7,6},{8,9},{9,8},{10,11... | collective-permute-start | bytes 147464 | tf_op jit(solution)/shard_map/ppermute | solution.py:491
  7.4 1.6 %collective-permute-done = bf16[192,128]{1,0:T(8,128)(2,1)S(1)} collective-permute-done((bf16[192,128]{1,0:T(8,128)(2,1)S(1)}, bf16[192,128]{1,0:T(8,128)(2,1)S(1)}, u32[]{:S(2)}, u32[]{:S(2)}) %collective-permute-start) | collective-permute-done | bytes 49184 | tf_op jit(solution)/shard_map/ppermute | solution.py:491
  9.0 1.9 %collective-permute-start.1 = (bf16[2,192,128]{2,1,0:T(8,128)(2,1)S(1)}, bf16[2,192,128]{2,1,0:T(8,128)(2,1)S(1)}, u32[]{:S(2)}, u32[]{:S(2)}) collective-permute-start(bf16[2,192,128]{2,1,0:T(8,128)(2,1)S(1)} %pad_maximum_fusion.2), channel_id=1, source_target_pairs={{0,8},{4,12},{8,0},{12,4},{1,9},{5,13},{9,1},{13,5},{2,10},{6,14},... | collective-permute-start | bytes 294920 | tf_op jit(solution)/shard_map/ppermute | solution.py:491
  10.9 0.9 %collective-permute-done.3 = bf16[192,128]{1,0:T(8,128)(2,1)S(1)} collective-permute-done((bf16[192,128]{1,0:T(8,128)(2,1)S(1)}, bf16[192,128]{1,0:T(8,128)(2,1)S(1)}, u32[]{:S(2)}, u32[]{:S(2)}) %collective-permute-start.3) | collective-permute-done | bytes 49184 | tf_op jit(solution)/shard_map/ppermute | solution.py:491
  11.8 0.0 collective-permute-done.2
  11.8 1.6 %collective-permute-start.4 = (bf16[2,192,128]{2,1,0:T(8,128)(2,1)S(1)}, bf16[2,192,128]{2,1,0:T(8,128)(2,1)S(1)}, u32[]{:S(2)}, u32[]{:S(2)}) collective-permute-start(bf16[2,192,128]{2,1,0:T(8,128)(2,1)S(1)} %pad_maximum_fusion.3), channel_id=1, source_target_pairs={{0,8},{4,12},{8,0},{12,4},{1,9},{5,13},{9,1},{13,5},{2,10},{6,14},... | collective-permute-start | bytes 294920 | tf_op jit(solution)/shard_map/ppermute | solution.py:491
  13.4 0.1 collective-permute-start.6
  13.5 1.4 %shard_map.136 = (f32[8,128]{1,0:T(8,128)S(1)}, bf16[256,256]{1,0:T(8,128)(2,1)S(1)}, bf16[512,256]{1,0:T(8,128)(2,1)S(1)}, f32[64,64]{1,0:T(8,128)S(1)}) custom-call(f32[1,64]{1,0:T(1,128)} %bitcast.24, f32[1,64]{1,0:T(1,128)} %bitcast.25, bf16[32,64]{1,0:T(8,128)(2,1)} %bitcast.21, bf16[32,64]{1,0:T(8,128)(2,1)} %bitcast.22, bf16[1024,128]{1,0:T(8,128)(2,1)} %refs_4_), custom_call_target="tpu_custom_call" | custom-call | tf_op jit(solution)/shard_map/pallas_call | solution.py:501
  14.9 0.8 %shard_map.137 = (bf16[512,256]{1,0:T(8,128)(2,1)S(1)}, bf16[128,256]{1,0:T(8,128)(2,1)S(1)}, bf16[128,256]{1,0:T(8,128)(2,1)S(1)}, f32[32,8,128]{2,1,0:T(8,128)...) custom-call(s32[1]{0:T(128)} %bitcast.place_ref, ...), custom_call_target="tpu_custom_call" | custom-call | flops 1000000000 | bytes 4000000 | tf_op jit(solution)/shard_map/pallas_call | solution.py:541
  15.7 0.8 %collective-permute-done.4 = bf16[2,192,128]{2,1,0:T(8,128)(2,1)S(1)} collective-permute-done((bf16[2,192,128]{2,1,0:T(8,128)(2,1)S(1)}, bf16[2,192,128]{2,1,0:T(8,128)(2,1)S(1)}, u32[]{:S(2)}, u32[]{:S(2)}) %collective-permute-start.4) | collective-permute-done | bytes 98336 | tf_op jit(solution)/shard_map/ppermute | solution.py:491
  16.5 0.0 collective-permute-done.1
  16.5 0.1 collective-permute-start.5
  16.6 0.8 %shard_map.139 = (bf16[512,256]{1,0:T(8,128)(2,1)S(1)}, bf16[128,256]{1,0:T(8,128)(2,1)S(1)}, bf16[128,256]{1,0:T(8,128)(2,1)S(1)}, f32[32,8,128]{2,1,0:T(8,128)...) custom-call(s32[1]{0:T(128)} %bitcast.place_ref, ...), custom_call_target="tpu_custom_call" | custom-call | flops 1000000000 | bytes 4000000 | tf_op jit(solution)/shard_map/pallas_call | solution.py:541
  17.4 0.0 collective-permute-done.6.set_ref
  17.4 0.8 %shard_map.138 = (bf16[512,256]{1,0:T(8,128)(2,1)S(1)}, bf16[128,256]{1,0:T(8,128)(2,1)S(1)}, bf16[128,256]{1,0:T(8,128)(2,1)S(1)}, f32[32,8,128]{2,1,0:T(8,128)...) custom-call(s32[1]{0:T(128)} %bitcast.place_ref, ...), custom_call_target="tpu_custom_call" | custom-call | flops 1000000000 | bytes 4000000 | tf_op jit(solution)/shard_map/pallas_call | solution.py:541
  18.2 0.0 collective-permute-done.5.last_ref
  18.3 5.9 %shard_map.140 = (f32[32,8,64]{2,1,0:T(8,128)}, f32[1024,128]{1,0:T(8,128)}, f32[32,64]{1,0:T(8,128)}, f32[32,64]{1,0:T(8,128)}, f32[1,64]{1,0:T(1,128)}, /*index=5*/f32[1,64]{1,0:T(1,128)}, f32[1,128]{1,0:T(1,128)}) custom-call(s32[1]{0:T(128)} %bitcast.place_ref, bf16[4,192,128]{2,1,0:T(8,128)(2,1)S(1)} %collective-permute-done.5.last_ref, ...), custom_call_target="tpu_custom_call" | custom-call | tf_op jit(solution)/shard_map/pallas_call | solution.py:559
  (4 shorter events, 0.1 us)
Async XLA Ops:
  1.7 7.3 %collective-permute-start = (bf16[192,128]{1,0:T(8,128)(2,1)S(1)}, bf16[192,128]{1,0:T(8,128)(2,1)S(1)}, u32[]{:S(2)}, u32[]{:S(2)}) collective-permute-start(bf16[192,128]{1,0:T(8,128)(2,1)S(1)} %shard_map.135), channel_id=1, source_target_pairs={{0,3},{1,2},{2,1},{3,0},{4,7},{5,6},{6,5},{7,4},{8,11},{9,10},{10,... | collective-permute-start | bytes 147464 | tf_op jit(solution)/shard_map/ppermute | solution.py:491
  6.8 5.0 %collective-permute-start.3 = (bf16[192,128]{1,0:T(8,128)(2,1)S(1)}, bf16[192,128]{1,0:T(8,128)(2,1)S(1)}, u32[]{:S(2)}, u32[]{:S(2)}) collective-permute-start(bf16[192,128]{1,0:T(8,128)(2,1)S(1)} %shard_map.135), channel_id=1, source_target_pairs={{0,2},{1,3},{2,0},{3,1},{4,6},{5,7},{6,4},{7,5},{8,10},{9,11},{10,... | collective-permute-start | bytes 147464 | tf_op jit(solution)/shard_map/ppermute | solution.py:491
  6.8 5.0 %collective-permute-start.2 = (bf16[192,128]{1,0:T(8,128)(2,1)S(1)}, bf16[192,128]{1,0:T(8,128)(2,1)S(1)}, u32[]{:S(2)}, u32[]{:S(2)}) collective-permute-start(bf16[192,128]{1,0:T(8,128)(2,1)S(1)} %shard_map.135), channel_id=1, source_target_pairs={{0,1},{1,0},{2,3},{3,2},{4,5},{5,4},{6,7},{7,6},{8,9},{9,8},{10,11... | collective-permute-start | bytes 147464 | tf_op jit(solution)/shard_map/ppermute | solution.py:491
  9.0 7.5 %collective-permute-start.1 = (bf16[2,192,128]{2,1,0:T(8,128)(2,1)S(1)}, bf16[2,192,128]{2,1,0:T(8,128)(2,1)S(1)}, u32[]{:S(2)}, u32[]{:S(2)}) collective-permute-start(bf16[2,192,128]{2,1,0:T(8,128)(2,1)S(1)} %pad_maximum_fusion.2), channel_id=1, source_target_pairs={{0,8},{4,12},{8,0},{12,4},{1,9},{5,13},{9,1},{13,5},{2,10},{6,14},... | collective-permute-start | bytes 294920 | tf_op jit(solution)/shard_map/ppermute | solution.py:491
  11.8 4.7 %collective-permute-start.4 = (bf16[2,192,128]{2,1,0:T(8,128)(2,1)S(1)}, bf16[2,192,128]{2,1,0:T(8,128)(2,1)S(1)}, u32[]{:S(2)}, u32[]{:S(2)}) collective-permute-start(bf16[2,192,128]{2,1,0:T(8,128)(2,1)S(1)} %pad_maximum_fusion.3), channel_id=1, source_target_pairs={{0,8},{4,12},{8,0},{12,4},{1,9},{5,13},{9,1},{13,5},{2,10},{6,14},... | collective-permute-start | bytes 294920 | tf_op jit(solution)/shard_map/ppermute | solution.py:491
  13.4 4.0 %collective-permute-start.6 = (bf16[4,192,128]{2,1,0:T(8,128)(2,1)S(1)}, bf16[4,192,128]{2,1,0:T(8,128)(2,1)S(1)}, u32[]{:S(2)}, u32[]{:S(2)}) collective-permute-start(bf16[4,192,128]{2,1,0:T(8,128)(2,1)S(1)} %pad_maximum_fusion.1.set_ref), channel_id=1, source_target_pairs={{0,4},{4,0},{8,12},{12,8},{1,5},{5,1},{9,13},{13,9},{2,6},{6,2},{1... | collective-permute-start | bytes 589832 | tf_op jit(solution)/shard_map/ppermute | solution.py:491
  16.5 1.7 %collective-permute-start.5 = (bf16[4,192,128]{2,1,0:T(8,128)(2,1)S(1)}, bf16[4,192,128]{2,1,0:T(8,128)(2,1)S(1)}, u32[]{:S(2)}, u32[]{:S(2)}) collective-permute-start(bf16[4,192,128]{2,1,0:T(8,128)(2,1)S(1)} %pad_maximum_fusion.set_ref), channel_id=1, source_target_pairs={{0,4},{4,0},{8,12},{12,8},{1,5},{5,1},{9,13},{13,9},{2,6},{6,2},{1... | collective-permute-start | bytes 589832 | tf_op jit(solution)/shard_map/ppermute | solution.py:491

commit v12 on v10

--- a/solution.py
+++ b/solution.py
@@ -252,7 +252,7 @@
     return spread(128, 128, lambda r, c: jnp.where(r // 64 == c // 64, 1.0 / 64, 0.0)).astype(BF)
 
 
-ORDER = (0, 3, 1, 2)
+ORDER = (0, 1, 2, 3)
 
 
 def stage_kernel(
@@ -486,12 +486,20 @@
     def over(axis, size, step, array):
         return lax.ppermute(array, axis, [(k, k ^ step) for k in range(size)])
 
-    far = over("col", n_col, 2, packed)
-    near = over("col", n_col, 1, packed)
-    last = over("col", n_col, 3, packed)
-    front = jnp.stack([packed, last])
+    def send(*pairs):
+        return lax.ppermute(packed, "col", pairs)
+
+    up = send((0, 2), (1, 3))
+    cross = send((2, 0), (3, 1), (0, 3))
+    around, down = lax.optimization_barrier((send((0, 1), (1, 2), (2, 3), (3, 0)), send((1, 0), (2, 1), (3, 2))))
+    here = lax.axis_index("col")
+    near = jnp.where(here % 2 == 0, down, around)
+    near, around, down = lax.optimization_barrier((near, around, down))
+    far = jnp.where(here >= 2, up, cross)
+    last = jnp.where(here == 1, down, jnp.where(here == 3, cross, around))
+    front = jnp.stack([packed, near])
     chip_front = over("row", n_row, 2, front)
-    rear = jnp.stack([near, far])
+    rear = jnp.stack([far, last])
     chip_rear = over("row", n_row, 2, rear)
     front, final_projection_matrix = lax.optimization_barrier((front, final_projection_matrix))
     weights = pl.pallas_call(

time: 24.1 us -> 28.2 us (1.17)
  the two profiles are of different devices: /device:TPU:0 before, /device:TPU:29 now
where the time goes in v12:
time: 28.2 us; the launch traced here: 27.9 us
  starting transfers between devices  13.1 us (46%)
  Pallas kernels  10.4 us (37%)
  waiting for transfers between devices  3.5 us (12%)
  between operations  0.8 us (3%)
    ppermute x4, starting transfers between devices, send(): return lax.ppermute(packed, 'col', pairs)  6.66 us
    ppermute x4, starting transfers between devices, over(): return lax.ppermute(array, axis, [(k, k ^ step) for k in range(size)])  6.41 us
    pallas_call x1, Pallas kernels, gathered_body(): pl.pallas_call(functools.partial(part_kernel, n_row, n_col), out_shape=(s...  5.57 us
    ppermute x4, waiting for transfers between devices, send(): return lax.ppermute(packed, 'col', pairs)  3.49 us
    pallas_call x3, Pallas kernels, stage(): pl.pallas_call(functools.partial(stage_kernel, n_col, a), out_shape=tuple...  2.44 us
    pallas_call x1, Pallas kernels, gathered_body(): pl.pallas_call(weights_kernel, out_shape=(held(8, 128), held_bf(256, 256)...  1.39 us
    pallas_call x1, Pallas kernels, gathered_body(): pl.pallas_call(pack_kernel, out_shape=held_bf(192, 128), in_specs=vmem(3)...  1.04 us
  transfers between devices with their start and end apart: 8, of which 2 were waited for; matrix products, arithmetic and copies ran while one was open for 0% of the time, Pallas kernels for 14%

profile of v12, /device:TPU:29, one launch (start us, length us, event | category | flops | bytes accessed | tf_op | source)
XLA Modules:
  0.0 27.9 jit_solution(442752863370501796)
XLA Ops:
  0.6 1.0 %shard_map.135 = bf16[192,128]{1,0:T(8,128)(2,1)S(1)} custom-call(bf16[32,8,64]{2,1,0:T(8,128)(2,1)} %msa_ref.1, s32[8,32]{1,0:T(8,128)} %bitcast.21, bf16[8,8,128]{2,1,0:T(8,128)(2,1)} %pair_ref.1), custom_call_target="tpu_custom_call" | custom-call | tf_op jit(solution)/shard_map/pallas_call | solution.py:480
  1.7 2.1 %collective-permute-start.1 = (bf16[192,128]{1,0:T(8,128)(2,1)S(1)}, bf16[192,128]{1,0:T(8,128)(2,1)S(1)}, u32[]{:S(2)}, u32[]{:S(2)}) collective-permute-start(bf16[192,128]{1,0:T(8,128)(2,1)S(1)} %shard_map.135), channel_id=1, source_target_pairs={{1,0},{2,1},{3,2},{5,4},{6,5},{7,6},{9,8},{10,9},{11,10},{13,12},{... | collective-permute-start | bytes 147464 | tf_op jit(solution)/shard_map/ppermute | solution.py:490
  3.8 0.1 collective-permute-start
  3.8 3.2 %collective-permute-start.4 = (bf16[192,128]{1,0:T(8,128)(2,1)S(1)}, bf16[192,128]{1,0:T(8,128)(2,1)S(1)}, u32[]{:S(2)}, u32[]{:S(2)}) collective-permute-start(bf16[192,128]{1,0:T(8,128)(2,1)S(1)} %shard_map.135), channel_id=1, source_target_pairs={{2,0},{3,1},{0,3},{6,4},{7,5},{4,7},{10,8},{11,9},{8,11},{14,12},{... | collective-permute-start | bytes 147464 | tf_op jit(solution)/shard_map/ppermute | solution.py:490
  7.1 1.3 %collective-permute-start.3 = (bf16[192,128]{1,0:T(8,128)(2,1)S(1)}, bf16[192,128]{1,0:T(8,128)(2,1)S(1)}, u32[]{:S(2)}, u32[]{:S(2)}) collective-permute-start(bf16[192,128]{1,0:T(8,128)(2,1)S(1)} %shard_map.135), channel_id=1, source_target_pairs={{0,2},{1,3},{4,6},{5,7},{8,10},{9,11},{12,14},{13,15},{16,18},{17,... | collective-permute-start | bytes 147464 | tf_op jit(solution)/shard_map/ppermute | solution.py:490
  8.4 0.0 collective-permute-done.1
  8.4 0.0 collective-permute-done
  8.4 1.3 %collective-permute-start.2 = (bf16[2,192,128]{2,1,0:T(8,128)(2,1)S(1)}, bf16[2,192,128]{2,1,0:T(8,128)(2,1)S(1)}, u32[]{:S(2)}, u32[]{:S(2)}) collective-permute-start(bf16[2,192,128]{2,1,0:T(8,128)(2,1)S(1)} %pad_maximum_fusion.2), channel_id=1, source_target_pairs={{0,8},{4,12},{8,0},{12,4},{1,9},{5,13},{9,1},{13,5},{2,10},{6,14},... | collective-permute-start | bytes 294920 | tf_op jit(solution)/shard_map/ppermute | solution.py:487
  9.7 0.7 %collective-permute-done.4 = bf16[192,128]{1,0:T(8,128)(2,1)S(1)} collective-permute-done((bf16[192,128]{1,0:T(8,128)(2,1)S(1)}, bf16[192,128]{1,0:T(8,128)(2,1)S(1)}, u32[]{:S(2)}, u32[]{:S(2)}) %collective-permute-start.4) | collective-permute-done | bytes 49184 | tf_op jit(solution)/shard_map/ppermute | solution.py:490
  10.5 2.8 %collective-permute-done.3 = bf16[192,128]{1,0:T(8,128)(2,1)S(1)} collective-permute-done((bf16[192,128]{1,0:T(8,128)(2,1)S(1)}, bf16[192,128]{1,0:T(8,128)(2,1)S(1)}, u32[]{:S(2)}, u32[]{:S(2)}) %collective-permute-start.3) | collective-permute-done | bytes 49184 | tf_op jit(solution)/shard_map/ppermute | solution.py:490
  13.3 1.3 %collective-permute-start.5 = (bf16[2,192,128]{2,1,0:T(8,128)(2,1)S(1)}, bf16[2,192,128]{2,1,0:T(8,128)(2,1)S(1)}, u32[]{:S(2)}, u32[]{:S(2)}) collective-permute-start(bf16[2,192,128]{2,1,0:T(8,128)(2,1)S(1)} %pad_maximum_fusion.3), channel_id=1, source_target_pairs={{0,8},{4,12},{8,0},{12,4},{1,9},{5,13},{9,1},{13,5},{2,10},{6,14},... | collective-permute-start | bytes 294920 | tf_op jit(solution)/shard_map/ppermute | solution.py:487
  14.6 3.0 %collective-permute-start.7 = (bf16[4,192,128]{2,1,0:T(8,128)(2,1)S(1)}, bf16[4,192,128]{2,1,0:T(8,128)(2,1)S(1)}, u32[]{:S(2)}, u32[]{:S(2)}) collective-permute-start(bf16[4,192,128]{2,1,0:T(8,128)(2,1)S(1)} %pad_maximum_fusion.1.set_ref), channel_id=1, source_target_pairs={{0,4},{4,0},{8,12},{12,8},{1,5},{5,1},{9,13},{13,9},{2,6},{6,2},{1... | collective-permute-start | bytes 589832 | tf_op jit(solution)/shard_map/ppermute | solution.py:487
  17.6 1.4 %shard_map.136 = (f32[8,128]{1,0:T(8,128)S(1)}, bf16[256,256]{1,0:T(8,128)(2,1)S(1)}, bf16[512,256]{1,0:T(8,128)(2,1)S(1)}, f32[64,64]{1,0:T(8,128)S(1)}) custom-call(f32[1,64]{1,0:T(1,128)} %bitcast.22, f32[1,64]{1,0:T(1,128)} %bitcast.23, bf16[32,64]{1,0:T(8,128)(2,1)} %bitcast.19, bf16[32,64]{1,0:T(8,128)(2,1)} %bitcast.20, bf16[1024,128]{1,0:T(8,128)(2,1)} %refs_4_), custom_call_target="tpu_custom_call" | custom-call | tf_op jit(solution)/shard_map/pallas_call | solution.py:505
  19.0 0.8 %shard_map.137 = (bf16[512,256]{1,0:T(8,128)(2,1)S(1)}, bf16[128,256]{1,0:T(8,128)(2,1)S(1)}, bf16[128,256]{1,0:T(8,128)(2,1)S(1)}, f32[32,8,128]{2,1,0:T(8,128)...) custom-call(s32[1]{0:T(128)} %bitcast.place_ref, ...), custom_call_target="tpu_custom_call" | custom-call | flops 1000000000 | bytes 4000000 | tf_op jit(solution)/shard_map/pallas_call | solution.py:545
  19.8 0.0 collective-permute-done.5
  19.8 0.0 collective-permute-done.2
  19.8 0.9 %collective-permute-start.6 = (bf16[4,192,128]{2,1,0:T(8,128)(2,1)S(1)}, bf16[4,192,128]{2,1,0:T(8,128)(2,1)S(1)}, u32[]{:S(2)}, u32[]{:S(2)}) collective-permute-start(bf16[4,192,128]{2,1,0:T(8,128)(2,1)S(1)} %pad_maximum_fusion.set_ref), channel_id=1, source_target_pairs={{0,4},{4,0},{8,12},{12,8},{1,5},{5,1},{9,13},{13,9},{2,6},{6,2},{1... | collective-permute-start | bytes 589832 | tf_op jit(solution)/shard_map/ppermute | solution.py:487
  20.7 0.8 %shard_map.139 = (bf16[512,256]{1,0:T(8,128)(2,1)S(1)}, bf16[128,256]{1,0:T(8,128)(2,1)S(1)}, bf16[128,256]{1,0:T(8,128)(2,1)S(1)}, f32[32,8,128]{2,1,0:T(8,128)...) custom-call(s32[1]{0:T(128)} %bitcast.place_ref, ...), custom_call_target="tpu_custom_call" | custom-call | flops 1000000000 | bytes 4000000 | tf_op jit(solution)/shard_map/pallas_call | solution.py:545
  21.5 0.0 collective-permute-done.7.set_ref
  21.5 0.8 %shard_map.138 = (bf16[512,256]{1,0:T(8,128)(2,1)S(1)}, bf16[128,256]{1,0:T(8,128)(2,1)S(1)}, bf16[128,256]{1,0:T(8,128)(2,1)S(1)}, f32[32,8,128]{2,1,0:T(8,128)...) custom-call(s32[1]{0:T(128)} %bitcast.place_ref, ...), custom_call_target="tpu_custom_call" | custom-call | flops 1000000000 | bytes 4000000 | tf_op jit(solution)/shard_map/pallas_call | solution.py:545
  22.3 0.0 collective-permute-done.6.last_ref
  22.3 5.6 %shard_map.140 = (f32[32,8,64]{2,1,0:T(8,128)}, f32[1024,128]{1,0:T(8,128)}, f32[32,64]{1,0:T(8,128)}, f32[32,64]{1,0:T(8,128)}, f32[1,64]{1,0:T(1,128)}, /*index=5*/f32[1,64]{1,0:T(1,128)}, f32[1,128]{1,0:T(1,128)}) custom-call(s32[1]{0:T(128)} %bitcast.place_ref, bf16[4,192,128]{2,1,0:T(8,128)(2,1)S(1)} %collective-permute-done.6.last_ref, ...), custom_call_target="tpu_custom_call" | custom-call | tf_op jit(solution)/shard_map/pallas_call | solution.py:563
  (6 shorter events, 0.1 us)
Async XLA Ops:
  1.7 6.7 %collective-permute-start.1 = (bf16[192,128]{1,0:T(8,128)(2,1)S(1)}, bf16[192,128]{1,0:T(8,128)(2,1)S(1)}, u32[]{:S(2)}, u32[]{:S(2)}) collective-permute-start(bf16[192,128]{1,0:T(8,128)(2,1)S(1)} %shard_map.135), channel_id=1, source_target_pairs={{1,0},{2,1},{3,2},{5,4},{6,5},{7,6},{9,8},{10,9},{11,10},{13,12},{... | collective-permute-start | bytes 147464 | tf_op jit(solution)/shard_map/ppermute | solution.py:490
  3.8 4.6 %collective-permute-start = (bf16[192,128]{1,0:T(8,128)(2,1)S(1)}, bf16[192,128]{1,0:T(8,128)(2,1)S(1)}, u32[]{:S(2)}, u32[]{:S(2)}) collective-permute-start(bf16[192,128]{1,0:T(8,128)(2,1)S(1)} %shard_map.135), channel_id=1, source_target_pairs={{0,1},{1,2},{2,3},{3,0},{4,5},{5,6},{6,7},{7,4},{8,9},{9,10},{10,1... | collective-permute-start | bytes 147464 | tf_op jit(solution)/shard_map/ppermute | solution.py:490
  3.8 6.6 %collective-permute-start.4 = (bf16[192,128]{1,0:T(8,128)(2,1)S(1)}, bf16[192,128]{1,0:T(8,128)(2,1)S(1)}, u32[]{:S(2)}, u32[]{:S(2)}) collective-permute-start(bf16[192,128]{1,0:T(8,128)(2,1)S(1)} %shard_map.135), channel_id=1, source_target_pairs={{2,0},{3,1},{0,3},{6,4},{7,5},{4,7},{10,8},{11,9},{8,11},{14,12},{... | collective-permute-start | bytes 147464 | tf_op jit(solution)/shard_map/ppermute | solution.py:490
  7.1 6.1 %collective-permute-start.3 = (bf16[192,128]{1,0:T(8,128)(2,1)S(1)}, bf16[192,128]{1,0:T(8,128)(2,1)S(1)}, u32[]{:S(2)}, u32[]{:S(2)}) collective-permute-start(bf16[192,128]{1,0:T(8,128)(2,1)S(1)} %shard_map.135), channel_id=1, source_target_pairs={{0,2},{1,3},{4,6},{5,7},{8,10},{9,11},{12,14},{13,15},{16,18},{17,... | collective-permute-start | bytes 147464 | tf_op jit(solution)/shard_map/ppermute | solution.py:490
  8.4 11.4 %collective-permute-start.2 = (bf16[2,192,128]{2,1,0:T(8,128)(2,1)S(1)}, bf16[2,192,128]{2,1,0:T(8,128)(2,1)S(1)}, u32[]{:S(2)}, u32[]{:S(2)}) collective-permute-start(bf16[2,192,128]{2,1,0:T(8,128)(2,1)S(1)} %pad_maximum_fusion.2), channel_id=1, source_target_pairs={{0,8},{4,12},{8,0},{12,4},{1,9},{5,13},{9,1},{13,5},{2,10},{6,14},... | collective-permute-start | bytes 294920 | tf_op jit(solution)/shard_map/ppermute | solution.py:487
  13.3 6.5 %collective-permute-start.5 = (bf16[2,192,128]{2,1,0:T(8,128)(2,1)S(1)}, bf16[2,192,128]{2,1,0:T(8,128)(2,1)S(1)}, u32[]{:S(2)}, u32[]{:S(2)}) collective-permute-start(bf16[2,192,128]{2,1,0:T(8,128)(2,1)S(1)} %pad_maximum_fusion.3), channel_id=1, source_target_pairs={{0,8},{4,12},{8,0},{12,4},{1,9},{5,13},{9,1},{13,5},{2,10},{6,14},... | collective-permute-start | bytes 294920 | tf_op jit(solution)/shard_map/ppermute | solution.py:487
  14.6 7.0 %collective-permute-start.7 = (bf16[4,192,128]{2,1,0:T(8,128)(2,1)S(1)}, bf16[4,192,128]{2,1,0:T(8,128)(2,1)S(1)}, u32[]{:S(2)}, u32[]{:S(2)}) collective-permute-start(bf16[4,192,128]{2,1,0:T(8,128)(2,1)S(1)} %pad_maximum_fusion.1.set_ref), channel_id=1, source_target_pairs={{0,4},{4,0},{8,12},{12,8},{1,5},{5,1},{9,13},{13,9},{2,6},{6,2},{1... | collective-permute-start | bytes 589832 | tf_op jit(solution)/shard_map/ppermute | solution.py:487
  19.8 2.5 %collective-permute-start.6 = (bf16[4,192,128]{2,1,0:T(8,128)(2,1)S(1)}, bf16[4,192,128]{2,1,0:T(8,128)(2,1)S(1)}, u32[]{:S(2)}, u32[]{:S(2)}) collective-permute-start(bf16[4,192,128]{2,1,0:T(8,128)(2,1)S(1)} %pad_maximum_fusion.set_ref), channel_id=1, source_target_pairs={{0,4},{4,0},{8,12},{12,8},{1,5},{5,1},{9,13},{13,9},{2,6},{6,2},{1... | collective-permute-start | bytes 589832 | tf_op jit(solution)/shard_map/ppermute | solution.py:487

commit v13 on v10

--- a/solution.py
+++ b/solution.py
@@ -324,7 +324,7 @@
     (
         normed_ref, inverse_ref, norm_ref, back_ref, final_ref, first_ref,
         emb_out, final_hbm_out, first_out, second_out, gain_out, offset_out, bias_out,
-        right_scr, scaled_scr, grad_scr, outer_scr, wide_scr, all_scr,
+        right_scr, scaled_scr, grad_scr, outer_scr, all_scr,
         final_out, out_sem, turn_scr,
     ) = refs[7 * (n_row - 1) : -7]
     stages.append(refs[-7:])
@@ -346,47 +346,47 @@
         ).astype(BF)
 
     mask_bf = mask.astype(BF)
-    share = (1.0 / (mm_tn(mask_bf, mask_bf)[0:32] + 0.001)).astype(BF)
+    share = 1.0 / (mm_tn(mask_bf, mask_bf)[0:32] + 0.001)
+    share_bf = share.astype(BF)
     for i in range(32):
         a, at = i // 8, 32 * (i % 8)
         for q in range(8):
             grad_scr[32 * i : 32 * i + 32, 128 * q : 128 * q + 128] = (
-                stages[a][4][at : at + 32, 128 * q : 128 * q + 128] * share[i : i + 1]
+                stages[a][4][at : at + 32, 128 * q : 128 * q + 128] * share_bf[i : i + 1]
             )
     left = jnp.concatenate([stage[1][...] for stage in stages], axis=1)
-    right_grad = mm(left, grad_scr[...])
-    left_grad = mm(grad_scr[...], right_scr[...])
 
     turn = spread(
         256, 256, lambda r, c: jnp.where((r // 8 == c % 32) & (r % 8 == c // 32), 1.0, 0.0)
     ).astype(BF)
     mask_two = jnp.concatenate([mask, mask], axis=1)
-    right_in = [
-        mm_nt(turn, (right_grad[:, 256 * q : 256 * q + 256] * mask_two).astype(BF))
-        for q in range(4)
-    ]
-    for t in range(32):
-        at = slice(128 * (t // 2), 128 * (t // 2) + 128)
-        row = 32 * (t % 2)
-        all_scr[row : row + 32, at] = (
-            left_grad[32 * t : 32 * t + 32] * mask_t[t : t + 1]
-        ).astype(BF)
-        all_scr[row + 64 : row + 96, at] = jnp.concatenate(
-            [part[8 * t : 8 * t + 8] for part in right_in], axis=0
-        ).astype(BF)
-
-    bias = jnp.zeros((1, 128), F32)
-    ones = jnp.ones((128, 128), BF)
-    for p in range(8):
-        both_on = jnp.concatenate(
-            [mask_t[0:32] * mask_t[i : i + 1] for i in range(4 * p, 4 * p + 4)], axis=0
-        ).astype(BF)
-        counts = mm(both_on, ones)
-        pair = stages[p // 2][5][4 * (p % 2) : 4 * (p % 2) + 4]
-        scaled = pair.reshape(128, 128) / (counts + 0.001)
-        bias = bias + jnp.sum(scaled, axis=0, keepdims=True)
-        scaled_scr[128 * p : 128 * p + 128, :] = scaled.astype(BF)
-    bias_out[...] = bias
+    for h in range(2):
+        parts = []
+        for q in (2 * h, 2 * h + 1):
+            right_grad = mm(left, grad_scr[:, 256 * q : 256 * q + 256])
+            parts.append(mm_nt(turn, (right_grad * mask_two).astype(BF)))
+        for t in range(32):
+            at = slice(128 * (t // 2), 128 * (t // 2) + 128)
+            row = 64 + 32 * (t % 2) + 16 * h
+            all_scr[row : row + 16, at] = jnp.concatenate(
+                [part[8 * t : 8 * t + 8] for part in parts], axis=0
+            ).astype(BF)
+    for h in range(4):
+        left_grad = mm(grad_scr[256 * h : 256 * h + 256, :], right_scr[...])
+        for k in range(8):
+            t = 8 * h + k
+            at = slice(128 * (t // 2), 128 * (t // 2) + 128)
+            row = 32 * (t % 2)
+            all_scr[row : row + 32, at] = (
+                left_grad[32 * k : 32 * k + 32] * mask_t[t : t + 1]
+            ).astype(BF)
+
+    bias = jnp.zeros((32, 128), F32)
+    for i in range(32):
+        scaled = stages[i // 8][5][i % 8] * jnp.broadcast_to(share[:, i : i + 1], (32, 128))
+        bias = bias + scaled
+        scaled_scr[32 * i : 32 * i + 32, :] = scaled.astype(BF)
+    bias_out[...] = jnp.sum(bias, axis=0, keepdims=True)
 
     left_t = jnp.concatenate([stage[2][...] for stage in stages], axis=0)
     for n in range(8):
@@ -401,9 +401,10 @@
                 even, odd = interleave(block[:32], block[32:])
                 outer_scr[rows : rows + 32, 128 * q : 128 * q + 128] = even
                 outer_scr[rows + 32 : rows + 64, 128 * q : 128 * q + 128] = odd
-    wide_scr[...] = mm(outer_scr[...], scaled_scr[...])
-    for c in range(32):
-        final_out[32 * c : 32 * c + 32, :] = wide_scr[pl.ds(c, 32, stride=32), :]
+    for h in range(4):
+        final = mm(outer_scr[256 * h : 256 * h + 256, :], scaled_scr[...])
+        for k in range(8):
+            final_out[pl.ds(8 * h + k, 32, stride=32), :] = final[32 * k : 32 * k + 32]
     final_send = pltpu.make_async_copy(final_out, final_hbm_out, out_sem)
     final_send.start()
 
@@ -570,7 +571,6 @@
             pltpu.VMEM((1024, 128), BF),
             pltpu.VMEM((1024, 1024), BF),
             pltpu.VMEM((1024, 1024), BF),
-            pltpu.VMEM((1024, 128), F32),
             pltpu.VMEM((128, 2048), BF),
             pltpu.VMEM((1024, 128), F32),
             pltpu.SemaphoreType.DMA,

time: 24.1 us -> 24.5 us (1.017)
  Pallas kernels: 10.5 us -> 10.9 us
    pallas_call x1, Pallas kernels: 5.57 us -> 6.01 us  [gathered_body(): pl.pallas_call(functools.partial(part_kernel, n_row, n_col), out_shape=(s...]
where the time goes in v13:
time: 24.5 us; the launch traced here: 24.3 us
  Pallas kernels  10.9 us (44%)
  starting transfers between devices  9.32 us (38%)
  waiting for transfers between devices  3.27 us (13%)
  between operations  0.72 us (3%)
    ppermute x7, starting transfers between devices, over(): return lax.ppermute(array, axis, [(k, k ^ step) for k in range(size)])  9.32 us
    pallas_call x1, Pallas kernels, gathered_body(): pl.pallas_call(functools.partial(part_kernel, n_row, n_col), out_shape=(s...  6.01 us
    ppermute x7, waiting for transfers between devices, over(): return lax.ppermute(array, axis, [(k, k ^ step) for k in range(size)])  3.27 us
    pallas_call x3, Pallas kernels, stage(): pl.pallas_call(functools.partial(stage_kernel, n_col, a), out_shape=tuple...  2.44 us
    pallas_call x1, Pallas kernels, gathered_body(): pl.pallas_call(weights_kernel, out_shape=(held(8, 128), held_bf(256, 256)...  1.4 us
    pallas_call x1, Pallas kernels, gathered_body(): pl.pallas_call(pack_kernel, out_shape=held_bf(192, 128), in_specs=vmem(3)...  1.04 us
  transfers between devices with their start and end apart: 7, of which 3 were waited for; matrix products, arithmetic and copies ran while one was open for 0% of the time, Pallas kernels for 16%

profile of v13, /device:TPU:0, one launch (start us, length us, event | category | flops | bytes accessed | tf_op | source)
XLA Modules:
  0.0 24.3 jit_solution(14078461156801845483)
XLA Ops:
  0.6 1.0 %shard_map.135 = bf16[192,128]{1,0:T(8,128)(2,1)S(1)} custom-call(bf16[32,8,64]{2,1,0:T(8,128)(2,1)} %msa_ref.1, s32[8,32]{1,0:T(8,128)} %bitcast.23, bf16[8,8,128]{2,1,0:T(8,128)(2,1)} %pair_ref.1), custom_call_target="tpu_custom_call" | custom-call | tf_op jit(solution)/shard_map/pallas_call | solution.py:481
  1.7 5.1 %collective-permute-start = (bf16[192,128]{1,0:T(8,128)(2,1)S(1)}, bf16[192,128]{1,0:T(8,128)(2,1)S(1)}, u32[]{:S(2)}, u32[]{:S(2)}) collective-permute-start(bf16[192,128]{1,0:T(8,128)(2,1)S(1)} %shard_map.135), channel_id=1, source_target_pairs={{0,3},{1,2},{2,1},{3,0},{4,7},{5,6},{6,5},{7,4},{8,11},{9,10},{10,... | collective-permute-start | bytes 147464 | tf_op jit(solution)/shard_map/ppermute | solution.py:488
  6.8 0.0 collective-permute-start.3
  6.8 0.6 %collective-permute-start.2 = (bf16[192,128]{1,0:T(8,128)(2,1)S(1)}, bf16[192,128]{1,0:T(8,128)(2,1)S(1)}, u32[]{:S(2)}, u32[]{:S(2)}) collective-permute-start(bf16[192,128]{1,0:T(8,128)(2,1)S(1)} %shard_map.135), channel_id=1, source_target_pairs={{0,1},{1,0},{2,3},{3,2},{4,5},{5,4},{6,7},{7,6},{8,9},{9,8},{10,11... | collective-permute-start | bytes 147464 | tf_op jit(solution)/shard_map/ppermute | solution.py:488
  7.4 1.6 %collective-permute-done = bf16[192,128]{1,0:T(8,128)(2,1)S(1)} collective-permute-done((bf16[192,128]{1,0:T(8,128)(2,1)S(1)}, bf16[192,128]{1,0:T(8,128)(2,1)S(1)}, u32[]{:S(2)}, u32[]{:S(2)}) %collective-permute-start) | collective-permute-done | bytes 49184 | tf_op jit(solution)/shard_map/ppermute | solution.py:488
  9.0 1.9 %collective-permute-start.1 = (bf16[2,192,128]{2,1,0:T(8,128)(2,1)S(1)}, bf16[2,192,128]{2,1,0:T(8,128)(2,1)S(1)}, u32[]{:S(2)}, u32[]{:S(2)}) collective-permute-start(bf16[2,192,128]{2,1,0:T(8,128)(2,1)S(1)} %pad_maximum_fusion.2), channel_id=1, source_target_pairs={{0,8},{4,12},{8,0},{12,4},{1,9},{5,13},{9,1},{13,5},{2,10},{6,14},... | collective-permute-start | bytes 294920 | tf_op jit(solution)/shard_map/ppermute | solution.py:488
  10.9 0.9 %collective-permute-done.3 = bf16[192,128]{1,0:T(8,128)(2,1)S(1)} collective-permute-done((bf16[192,128]{1,0:T(8,128)(2,1)S(1)}, bf16[192,128]{1,0:T(8,128)(2,1)S(1)}, u32[]{:S(2)}, u32[]{:S(2)}) %collective-permute-start.3) | collective-permute-done | bytes 49184 | tf_op jit(solution)/shard_map/ppermute | solution.py:488
  11.8 0.0 collective-permute-done.2
  11.8 1.6 %collective-permute-start.4 = (bf16[2,192,128]{2,1,0:T(8,128)(2,1)S(1)}, bf16[2,192,128]{2,1,0:T(8,128)(2,1)S(1)}, u32[]{:S(2)}, u32[]{:S(2)}) collective-permute-start(bf16[2,192,128]{2,1,0:T(8,128)(2,1)S(1)} %pad_maximum_fusion.3), channel_id=1, source_target_pairs={{0,8},{4,12},{8,0},{12,4},{1,9},{5,13},{9,1},{13,5},{2,10},{6,14},... | collective-permute-start | bytes 294920 | tf_op jit(solution)/shard_map/ppermute | solution.py:488
  13.4 0.1 collective-permute-start.6
  13.5 1.4 %shard_map.136 = (f32[8,128]{1,0:T(8,128)S(1)}, bf16[256,256]{1,0:T(8,128)(2,1)S(1)}, bf16[512,256]{1,0:T(8,128)(2,1)S(1)}, f32[64,64]{1,0:T(8,128)S(1)}) custom-call(f32[1,64]{1,0:T(1,128)} %bitcast.24, f32[1,64]{1,0:T(1,128)} %bitcast.25, bf16[32,64]{1,0:T(8,128)(2,1)} %bitcast.21, bf16[32,64]{1,0:T(8,128)(2,1)} %bitcast.22, bf16[1024,128]{1,0:T(8,128)(2,1)} %refs_4_), custom_call_target="tpu_custom_call" | custom-call | tf_op jit(solution)/shard_map/pallas_call | solution.py:498
  14.9 0.8 %shard_map.137 = (bf16[512,256]{1,0:T(8,128)(2,1)S(1)}, bf16[128,256]{1,0:T(8,128)(2,1)S(1)}, bf16[128,256]{1,0:T(8,128)(2,1)S(1)}, f32[32,8,128]{2,1,0:T(8,128)...) custom-call(s32[1]{0:T(128)} %bitcast.place_ref, ...), custom_call_target="tpu_custom_call" | custom-call | flops 1000000000 | bytes 4000000 | tf_op jit(solution)/shard_map/pallas_call | solution.py:538
  15.7 0.8 %collective-permute-done.4 = bf16[2,192,128]{2,1,0:T(8,128)(2,1)S(1)} collective-permute-done((bf16[2,192,128]{2,1,0:T(8,128)(2,1)S(1)}, bf16[2,192,128]{2,1,0:T(8,128)(2,1)S(1)}, u32[]{:S(2)}, u32[]{:S(2)}) %collective-permute-start.4) | collective-permute-done | bytes 98336 | tf_op jit(solution)/shard_map/ppermute | solution.py:488
  16.5 0.0 collective-permute-done.1
  16.5 0.1 collective-permute-start.5
  16.6 0.8 %shard_map.139 = (bf16[512,256]{1,0:T(8,128)(2,1)S(1)}, bf16[128,256]{1,0:T(8,128)(2,1)S(1)}, bf16[128,256]{1,0:T(8,128)(2,1)S(1)}, f32[32,8,128]{2,1,0:T(8,128)...) custom-call(s32[1]{0:T(128)} %bitcast.place_ref, ...), custom_call_target="tpu_custom_call" | custom-call | flops 1000000000 | bytes 4000000 | tf_op jit(solution)/shard_map/pallas_call | solution.py:538
  17.4 0.0 collective-permute-done.6.set_ref
  17.4 0.8 %shard_map.138 = (bf16[512,256]{1,0:T(8,128)(2,1)S(1)}, bf16[128,256]{1,0:T(8,128)(2,1)S(1)}, bf16[128,256]{1,0:T(8,128)(2,1)S(1)}, f32[32,8,128]{2,1,0:T(8,128)...) custom-call(s32[1]{0:T(128)} %bitcast.place_ref, ...), custom_call_target="tpu_custom_call" | custom-call | flops 1000000000 | bytes 4000000 | tf_op jit(solution)/shard_map/pallas_call | solution.py:538
  18.2 0.0 collective-permute-done.5.last_ref
  18.3 6.0 %shard_map.140 = (f32[32,8,64]{2,1,0:T(8,128)}, f32[1024,128]{1,0:T(8,128)}, f32[32,64]{1,0:T(8,128)}, f32[32,64]{1,0:T(8,128)}, f32[1,64]{1,0:T(1,128)}, /*index=5*/f32[1,64]{1,0:T(1,128)}, f32[1,128]{1,0:T(1,128)}) custom-call(s32[1]{0:T(128)} %bitcast.place_ref, bf16[4,192,128]{2,1,0:T(8,128)(2,1)S(1)} %collective-permute-done.5.last_ref, ...), custom_call_target="tpu_custom_call" | custom-call | tf_op jit(solution)/shard_map/pallas_call | solution.py:556
  (4 shorter events, 0.1 us)
Async XLA Ops:
  1.7 7.3 %collective-permute-start = (bf16[192,128]{1,0:T(8,128)(2,1)S(1)}, bf16[192,128]{1,0:T(8,128)(2,1)S(1)}, u32[]{:S(2)}, u32[]{:S(2)}) collective-permute-start(bf16[192,128]{1,0:T(8,128)(2,1)S(1)} %shard_map.135), channel_id=1, source_target_pairs={{0,3},{1,2},{2,1},{3,0},{4,7},{5,6},{6,5},{7,4},{8,11},{9,10},{10,... | collective-permute-start | bytes 147464 | tf_op jit(solution)/shard_map/ppermute | solution.py:488
  6.8 5.0 %collective-permute-start.3 = (bf16[192,128]{1,0:T(8,128)(2,1)S(1)}, bf16[192,128]{1,0:T(8,128)(2,1)S(1)}, u32[]{:S(2)}, u32[]{:S(2)}) collective-permute-start(bf16[192,128]{1,0:T(8,128)(2,1)S(1)} %shard_map.135), channel_id=1, source_target_pairs={{0,2},{1,3},{2,0},{3,1},{4,6},{5,7},{6,4},{7,5},{8,10},{9,11},{10,... | collective-permute-start | bytes 147464 | tf_op jit(solution)/shard_map/ppermute | solution.py:488
  6.8 5.0 %collective-permute-start.2 = (bf16[192,128]{1,0:T(8,128)(2,1)S(1)}, bf16[192,128]{1,0:T(8,128)(2,1)S(1)}, u32[]{:S(2)}, u32[]{:S(2)}) collective-permute-start(bf16[192,128]{1,0:T(8,128)(2,1)S(1)} %shard_map.135), channel_id=1, source_target_pairs={{0,1},{1,0},{2,3},{3,2},{4,5},{5,4},{6,7},{7,6},{8,9},{9,8},{10,11... | collective-permute-start | bytes 147464 | tf_op jit(solution)/shard_map/ppermute | solution.py:488
  9.0 7.5 %collective-permute-start.1 = (bf16[2,192,128]{2,1,0:T(8,128)(2,1)S(1)}, bf16[2,192,128]{2,1,0:T(8,128)(2,1)S(1)}, u32[]{:S(2)}, u32[]{:S(2)}) collective-permute-start(bf16[2,192,128]{2,1,0:T(8,128)(2,1)S(1)} %pad_maximum_fusion.2), channel_id=1, source_target_pairs={{0,8},{4,12},{8,0},{12,4},{1,9},{5,13},{9,1},{13,5},{2,10},{6,14},... | collective-permute-start | bytes 294920 | tf_op jit(solution)/shard_map/ppermute | solution.py:488
  11.8 4.7 %collective-permute-start.4 = (bf16[2,192,128]{2,1,0:T(8,128)(2,1)S(1)}, bf16[2,192,128]{2,1,0:T(8,128)(2,1)S(1)}, u32[]{:S(2)}, u32[]{:S(2)}) collective-permute-start(bf16[2,192,128]{2,1,0:T(8,128)(2,1)S(1)} %pad_maximum_fusion.3), channel_id=1, source_target_pairs={{0,8},{4,12},{8,0},{12,4},{1,9},{5,13},{9,1},{13,5},{2,10},{6,14},... | collective-permute-start | bytes 294920 | tf_op jit(solution)/shard_map/ppermute | solution.py:488
  13.4 4.0 %collective-permute-start.6 = (bf16[4,192,128]{2,1,0:T(8,128)(2,1)S(1)}, bf16[4,192,128]{2,1,0:T(8,128)(2,1)S(1)}, u32[]{:S(2)}, u32[]{:S(2)}) collective-permute-start(bf16[4,192,128]{2,1,0:T(8,128)(2,1)S(1)} %pad_maximum_fusion.1.set_ref), channel_id=1, source_target_pairs={{0,4},{4,0},{8,12},{12,8},{1,5},{5,1},{9,13},{13,9},{2,6},{6,2},{1... | collective-permute-start | bytes 589832 | tf_op jit(solution)/shard_map/ppermute | solution.py:488
  16.5 1.7 %collective-permute-start.5 = (bf16[4,192,128]{2,1,0:T(8,128)(2,1)S(1)}, bf16[4,192,128]{2,1,0:T(8,128)(2,1)S(1)}, u32[]{:S(2)}, u32[]{:S(2)}) collective-permute-start(bf16[4,192,128]{2,1,0:T(8,128)(2,1)S(1)} %pad_maximum_fusion.set_ref), channel_id=1, source_target_pairs={{0,4},{4,0},{8,12},{12,8},{1,5},{5,1},{9,13},{13,9},{2,6},{6,2},{1... | collective-permute-start | bytes 589832 | tf_op jit(solution)/shard_map/ppermute | solution.py:488

commit v14 on v10

--- a/solution.py
+++ b/solution.py
@@ -252,7 +252,7 @@
     return spread(128, 128, lambda r, c: jnp.where(r // 64 == c // 64, 1.0 / 64, 0.0)).astype(BF)
 
 
-ORDER = (0, 3, 1, 2)
+ORDER = (0, 2, 1, 3)
 
 
 def stage_kernel(
@@ -489,9 +489,9 @@
     far = over("col", n_col, 2, packed)
     near = over("col", n_col, 1, packed)
     last = over("col", n_col, 3, packed)
-    front = jnp.stack([packed, last])
+    front = jnp.stack([packed, far])
     chip_front = over("row", n_row, 2, front)
-    rear = jnp.stack([near, far])
+    rear = jnp.stack([near, last])
     chip_rear = over("row", n_row, 2, rear)
     front, final_projection_matrix = lax.optimization_barrier((front, final_projection_matrix))
     weights = pl.pallas_call(

time: 24.1 us -> 24 us (level)
  no operation moved by 1% of the time
where the time goes in v14:
time: 24 us; the launch traced here: 23.8 us
  Pallas kernels  10.4 us (43%)
  starting transfers between devices  9.14 us (38%)
  waiting for transfers between devices  3.41 us (14%)
  between operations  0.72 us (3%)
    ppermute x7, starting transfers between devices, over(): return lax.ppermute(array, axis, [(k, k ^ step) for k in range(size)])  9.14 us
    pallas_call x1, Pallas kernels, gathered_body(): pl.pallas_call(functools.partial(part_kernel, n_row, n_col), out_shape=(s...  5.57 us
    ppermute x7, waiting for transfers between devices, over(): return lax.ppermute(array, axis, [(k, k ^ step) for k in range(size)])  3.41 us
    pallas_call x3, Pallas kernels, stage(): pl.pallas_call(functools.partial(stage_kernel, n_col, a), out_shape=tuple...  2.44 us
    pallas_call x1, Pallas kernels, gathered_body(): pl.pallas_call(weights_kernel, out_shape=(held(8, 128), held_bf(256, 256)...  1.4 us
    pallas_call x1, Pallas kernels, gathered_body(): pl.pallas_call(pack_kernel, out_shape=held_bf(192, 128), in_specs=vmem(3)...  1.04 us
  transfers between devices with their start and end apart: 7, of which 3 were waited for; matrix products, arithmetic and copies ran while one was open for 0% of the time, Pallas kernels for 16%

profile of v14, /device:TPU:0, one launch (start us, length us, event | category | flops | bytes accessed | tf_op | source)
XLA Modules:
  0.0 23.8 jit_solution(10600435034730588990)
XLA Ops:
  0.6 1.0 %shard_map.135 = bf16[192,128]{1,0:T(8,128)(2,1)S(1)} custom-call(bf16[32,8,64]{2,1,0:T(8,128)(2,1)} %msa_ref.1, s32[8,32]{1,0:T(8,128)} %bitcast.23, bf16[8,8,128]{2,1,0:T(8,128)(2,1)} %pair_ref.1), custom_call_target="tpu_custom_call" | custom-call | tf_op jit(solution)/shard_map/pallas_call | solution.py:480
  1.7 4.1 %collective-permute-start = (bf16[192,128]{1,0:T(8,128)(2,1)S(1)}, bf16[192,128]{1,0:T(8,128)(2,1)S(1)}, u32[]{:S(2)}, u32[]{:S(2)}) collective-permute-start(bf16[192,128]{1,0:T(8,128)(2,1)S(1)} %shard_map.135), channel_id=1, source_target_pairs={{0,2},{1,3},{2,0},{3,1},{4,6},{5,7},{6,4},{7,5},{8,10},{9,11},{10,... | collective-permute-start | bytes 147464 | tf_op jit(solution)/shard_map/ppermute | solution.py:487
  5.8 1.3 %collective-permute-start.3 = (bf16[192,128]{1,0:T(8,128)(2,1)S(1)}, bf16[192,128]{1,0:T(8,128)(2,1)S(1)}, u32[]{:S(2)}, u32[]{:S(2)}) collective-permute-start(bf16[192,128]{1,0:T(8,128)(2,1)S(1)} %shard_map.135), channel_id=1, source_target_pairs={{0,3},{1,2},{2,1},{3,0},{4,7},{5,6},{6,5},{7,4},{8,11},{9,10},{10,... | collective-permute-start | bytes 147464 | tf_op jit(solution)/shard_map/ppermute | solution.py:487
  7.1 0.2 collective-permute-start.2
  7.4 1.0 %collective-permute-done = bf16[192,128]{1,0:T(8,128)(2,1)S(1)} collective-permute-done((bf16[192,128]{1,0:T(8,128)(2,1)S(1)}, bf16[192,128]{1,0:T(8,128)(2,1)S(1)}, u32[]{:S(2)}, u32[]{:S(2)}) %collective-permute-start) | collective-permute-done | bytes 49184 | tf_op jit(solution)/shard_map/ppermute | solution.py:487
  8.4 1.8 %collective-permute-start.1 = (bf16[2,192,128]{2,1,0:T(8,128)(2,1)S(1)}, bf16[2,192,128]{2,1,0:T(8,128)(2,1)S(1)}, u32[]{:S(2)}, u32[]{:S(2)}) collective-permute-start(bf16[2,192,128]{2,1,0:T(8,128)(2,1)S(1)} %pad_maximum_fusion.2), channel_id=1, source_target_pairs={{0,8},{4,12},{8,0},{12,4},{1,9},{5,13},{9,1},{13,5},{2,10},{6,14},... | collective-permute-start | bytes 294920 | tf_op jit(solution)/shard_map/ppermute | solution.py:487
  10.2 1.6 %collective-permute-done.3 = bf16[192,128]{1,0:T(8,128)(2,1)S(1)} collective-permute-done((bf16[192,128]{1,0:T(8,128)(2,1)S(1)}, bf16[192,128]{1,0:T(8,128)(2,1)S(1)}, u32[]{:S(2)}, u32[]{:S(2)}) %collective-permute-start.3) | collective-permute-done | bytes 49184 | tf_op jit(solution)/shard_map/ppermute | solution.py:487
  11.7 0.0 collective-permute-done.2
  11.8 1.6 %collective-permute-start.4 = (bf16[2,192,128]{2,1,0:T(8,128)(2,1)S(1)}, bf16[2,192,128]{2,1,0:T(8,128)(2,1)S(1)}, u32[]{:S(2)}, u32[]{:S(2)}) collective-permute-start(bf16[2,192,128]{2,1,0:T(8,128)(2,1)S(1)} %pad_maximum_fusion.3), channel_id=1, source_target_pairs={{0,8},{4,12},{8,0},{12,4},{1,9},{5,13},{9,1},{13,5},{2,10},{6,14},... | collective-permute-start | bytes 294920 | tf_op jit(solution)/shard_map/ppermute | solution.py:487
  13.3 0.1 collective-permute-start.6
  13.4 1.4 %shard_map.136 = (f32[8,128]{1,0:T(8,128)S(1)}, bf16[256,256]{1,0:T(8,128)(2,1)S(1)}, bf16[512,256]{1,0:T(8,128)(2,1)S(1)}, f32[64,64]{1,0:T(8,128)S(1)}) custom-call(f32[1,64]{1,0:T(1,128)} %bitcast.24, f32[1,64]{1,0:T(1,128)} %bitcast.25, bf16[32,64]{1,0:T(8,128)(2,1)} %bitcast.21, bf16[32,64]{1,0:T(8,128)(2,1)} %bitcast.22, bf16[1024,128]{1,0:T(8,128)(2,1)} %refs_4_), custom_call_target="tpu_custom_call" | custom-call | tf_op jit(solution)/shard_map/pallas_call | solution.py:497
  14.8 0.8 %shard_map.137 = (bf16[512,256]{1,0:T(8,128)(2,1)S(1)}, bf16[128,256]{1,0:T(8,128)(2,1)S(1)}, bf16[128,256]{1,0:T(8,128)(2,1)S(1)}, f32[32,8,128]{2,1,0:T(8,128)...) custom-call(s32[1]{0:T(128)} %bitcast.place_ref, ...), custom_call_target="tpu_custom_call" | custom-call | flops 1000000000 | bytes 4000000 | tf_op jit(solution)/shard_map/pallas_call | solution.py:537
  15.7 0.8 %collective-permute-done.4 = bf16[2,192,128]{2,1,0:T(8,128)(2,1)S(1)} collective-permute-done((bf16[2,192,128]{2,1,0:T(8,128)(2,1)S(1)}, bf16[2,192,128]{2,1,0:T(8,128)(2,1)S(1)}, u32[]{:S(2)}, u32[]{:S(2)}) %collective-permute-start.4) | collective-permute-done | bytes 98336 | tf_op jit(solution)/shard_map/ppermute | solution.py:487
  16.4 0.0 collective-permute-done.1
  16.5 0.1 collective-permute-start.5
  16.6 0.8 %shard_map.139 = (bf16[512,256]{1,0:T(8,128)(2,1)S(1)}, bf16[128,256]{1,0:T(8,128)(2,1)S(1)}, bf16[128,256]{1,0:T(8,128)(2,1)S(1)}, f32[32,8,128]{2,1,0:T(8,128)...) custom-call(s32[1]{0:T(128)} %bitcast.place_ref, ...), custom_call_target="tpu_custom_call" | custom-call | flops 1000000000 | bytes 4000000 | tf_op jit(solution)/shard_map/pallas_call | solution.py:537
  17.4 0.0 collective-permute-done.6.set_ref
  17.4 0.8 %shard_map.138 = (bf16[512,256]{1,0:T(8,128)(2,1)S(1)}, bf16[128,256]{1,0:T(8,128)(2,1)S(1)}, bf16[128,256]{1,0:T(8,128)(2,1)S(1)}, f32[32,8,128]{2,1,0:T(8,128)...) custom-call(s32[1]{0:T(128)} %bitcast.place_ref, ...), custom_call_target="tpu_custom_call" | custom-call | flops 1000000000 | bytes 4000000 | tf_op jit(solution)/shard_map/pallas_call | solution.py:537
  18.2 0.0 collective-permute-done.5.last_ref
  18.2 5.6 %shard_map.140 = (f32[32,8,64]{2,1,0:T(8,128)}, f32[1024,128]{1,0:T(8,128)}, f32[32,64]{1,0:T(8,128)}, f32[32,64]{1,0:T(8,128)}, f32[1,64]{1,0:T(1,128)}, /*index=5*/f32[1,64]{1,0:T(1,128)}, f32[1,128]{1,0:T(1,128)}) custom-call(s32[1]{0:T(128)} %bitcast.place_ref, bf16[4,192,128]{2,1,0:T(8,128)(2,1)S(1)} %collective-permute-done.5.last_ref, ...), custom_call_target="tpu_custom_call" | custom-call | tf_op jit(solution)/shard_map/pallas_call | solution.py:555
  (4 shorter events, 0.1 us)
Async XLA Ops:
  1.7 6.7 %collective-permute-start = (bf16[192,128]{1,0:T(8,128)(2,1)S(1)}, bf16[192,128]{1,0:T(8,128)(2,1)S(1)}, u32[]{:S(2)}, u32[]{:S(2)}) collective-permute-start(bf16[192,128]{1,0:T(8,128)(2,1)S(1)} %shard_map.135), channel_id=1, source_target_pairs={{0,2},{1,3},{2,0},{3,1},{4,6},{5,7},{6,4},{7,5},{8,10},{9,11},{10,... | collective-permute-start | bytes 147464 | tf_op jit(solution)/shard_map/ppermute | solution.py:487
  5.8 6.0 %collective-permute-start.3 = (bf16[192,128]{1,0:T(8,128)(2,1)S(1)}, bf16[192,128]{1,0:T(8,128)(2,1)S(1)}, u32[]{:S(2)}, u32[]{:S(2)}) collective-permute-start(bf16[192,128]{1,0:T(8,128)(2,1)S(1)} %shard_map.135), channel_id=1, source_target_pairs={{0,3},{1,2},{2,1},{3,0},{4,7},{5,6},{6,5},{7,4},{8,11},{9,10},{10,... | collective-permute-start | bytes 147464 | tf_op jit(solution)/shard_map/ppermute | solution.py:487
  7.1 4.6 %collective-permute-start.2 = (bf16[192,128]{1,0:T(8,128)(2,1)S(1)}, bf16[192,128]{1,0:T(8,128)(2,1)S(1)}, u32[]{:S(2)}, u32[]{:S(2)}) collective-permute-start(bf16[192,128]{1,0:T(8,128)(2,1)S(1)} %shard_map.135), channel_id=1, source_target_pairs={{0,1},{1,0},{2,3},{3,2},{4,5},{5,4},{6,7},{7,6},{8,9},{9,8},{10,11... | collective-permute-start | bytes 147464 | tf_op jit(solution)/shard_map/ppermute | solution.py:487
  8.4 8.1 %collective-permute-start.1 = (bf16[2,192,128]{2,1,0:T(8,128)(2,1)S(1)}, bf16[2,192,128]{2,1,0:T(8,128)(2,1)S(1)}, u32[]{:S(2)}, u32[]{:S(2)}) collective-permute-start(bf16[2,192,128]{2,1,0:T(8,128)(2,1)S(1)} %pad_maximum_fusion.2), channel_id=1, source_target_pairs={{0,8},{4,12},{8,0},{12,4},{1,9},{5,13},{9,1},{13,5},{2,10},{6,14},... | collective-permute-start | bytes 294920 | tf_op jit(solution)/shard_map/ppermute | solution.py:487
  11.8 4.7 %collective-permute-start.4 = (bf16[2,192,128]{2,1,0:T(8,128)(2,1)S(1)}, bf16[2,192,128]{2,1,0:T(8,128)(2,1)S(1)}, u32[]{:S(2)}, u32[]{:S(2)}) collective-permute-start(bf16[2,192,128]{2,1,0:T(8,128)(2,1)S(1)} %pad_maximum_fusion.3), channel_id=1, source_target_pairs={{0,8},{4,12},{8,0},{12,4},{1,9},{5,13},{9,1},{13,5},{2,10},{6,14},... | collective-permute-start | bytes 294920 | tf_op jit(solution)/shard_map/ppermute | solution.py:487
  13.3 4.0 %collective-permute-start.6 = (bf16[4,192,128]{2,1,0:T(8,128)(2,1)S(1)}, bf16[4,192,128]{2,1,0:T(8,128)(2,1)S(1)}, u32[]{:S(2)}, u32[]{:S(2)}) collective-permute-start(bf16[4,192,128]{2,1,0:T(8,128)(2,1)S(1)} %pad_maximum_fusion.1.set_ref), channel_id=1, source_target_pairs={{0,4},{4,0},{8,12},{12,8},{1,5},{5,1},{9,13},{13,9},{2,6},{6,2},{1... | collective-permute-start | bytes 589832 | tf_op jit(solution)/shard_map/ppermute | solution.py:487
  16.5 1.7 %collective-permute-start.5 = (bf16[4,192,128]{2,1,0:T(8,128)(2,1)S(1)}, bf16[4,192,128]{2,1,0:T(8,128)(2,1)S(1)}, u32[]{:S(2)}, u32[]{:S(2)}) collective-permute-start(bf16[4,192,128]{2,1,0:T(8,128)(2,1)S(1)} %pad_maximum_fusion.set_ref), channel_id=1, source_target_pairs={{0,4},{4,0},{8,12},{12,8},{1,5},{5,1},{9,13},{13,9},{2,6},{6,2},{1... | collective-permute-start | bytes 589832 | tf_op jit(solution)/shard_map/ppermute | solution.py:487

commit v15 on v14

--- a/solution.py
+++ b/solution.py
@@ -195,6 +195,14 @@
     )
 
 
+def swap_blocks(block):
+    upper = lax.broadcasted_iota(jnp.int16, (32, 128), 1) & 64 != 0
+    piece = [block[32 * a : 32 * a + 32] for a in range(4)]
+    low = [jnp.where(upper, pltpu.roll(piece[a + 2], 64, 1), piece[a]) for a in range(2)]
+    high = [jnp.where(upper, piece[a + 2], pltpu.roll(piece[a], 64, 1)) for a in range(2)]
+    return jnp.concatenate([*interleave(*low), *interleave(*high)], axis=0)
+
+
 def diagonal_pair(block):
     zero = jnp.zeros_like(block)
     return jnp.concatenate(
@@ -256,19 +264,20 @@
 
 
 def stage_kernel(
-    n_col, a, place_ref, set_ref, norm_ref, back_ref, final_ref,
+    n_col, a, place_ref, set_refs, norm_ref, back_ref, final_ref,
     rhs_out, left_out, leftt_out, rightt_out, grad_out, pair_out, found_out, *rest
 ):
     *own_out, turn_scr = rest
+    blocks = [ref.at[k] for ref in set_refs for k in range(ref.shape[0])]
     for b in range(n_col):
         at = pl.multiple_of(lax.bitwise_xor(place_ref[0], ORDER[b]) * 8, 8)
-        pair_out[:, pl.ds(at, 8), :] = set_ref[b, 128:192, :].astype(F32).reshape(8, 8, 128)
+        pair_out[:, pl.ds(at, 8), :] = blocks[b][128:192, :].astype(F32).reshape(8, 8, 128)
 
     gain = norm_ref[0:1, :]
     offset = norm_ref[1:2, :]
     averager = averager_of()
     x = jnp.concatenate(
-        [set_ref[b, 32 * g : 32 * g + 32, :] for g in range(4) for b in range(n_col)], axis=0
+        [blocks[b][32 * g : 32 * g + 32, :] for g in range(4) for b in range(n_col)], axis=0
     )
     mean = mm(x, averager)
     present = mean < ABSENT / 2
@@ -295,11 +304,8 @@
         at = slice(128 * h, 128 * h + 128)
         left_out[:, at] = mm_nt(masked, back_ref[:128, :]).astype(BF)
         both = mm_nt(back_ref[...], masked)
+        leftt_out[at, :] = both[:128].astype(BF)
         turn_scr[at, :] = both[128:]
-        for k in range(2):
-            leftt_out[64 * h + 32 * k : 64 * h + 32 * k + 32, :] = jnp.concatenate(
-                [both[32 * k : 32 * k + 32], both[32 * k + 64 : 32 * k + 96]], axis=1
-            ).astype(BF)
 
     for e in range(32):
         rightt_out[e] = turn_scr[pl.ds(e, 8, stride=32), :]
@@ -319,17 +325,28 @@
                 grad_out[rows + 32 : rows + 64, 128 * q : 128 * q + 128] = odd
 
 
-def part_kernel(n_row, n_col, place_ref, last_ref, *refs):
+def own_kernel(n_col, place_ref, front_ref, rear_ref, norm_ref, back_ref, final_ref, *rest):
+    stage_kernel(n_col, 0, place_ref, (front_ref, rear_ref), norm_ref, back_ref, final_ref, *rest)
+
+
+def pair_kernel(n_col, place_ref, core_ref, front_ref, rear_ref, norm_ref, back_ref, final_ref, *rest):
+    common = (norm_ref, back_ref, final_ref)
+    stage_kernel(n_col, 1, place_ref, (core_ref,), *common, *rest[:7], rest[14])
+    stage_kernel(n_col, 2, place_ref, (front_ref, rear_ref), *common, *rest[7:14], rest[15])
+
+
+def part_kernel(n_row, n_col, place_ref, front_ref, rear_ref, *refs):
     stages = [refs[7 * a : 7 * a + 7] for a in range(n_row - 1)]
     (
         normed_ref, inverse_ref, norm_ref, back_ref, final_ref, first_ref,
         emb_out, final_hbm_out, first_out, second_out, gain_out, offset_out, bias_out,
-        right_scr, scaled_scr, grad_scr, outer_scr, wide_scr, all_scr,
+        right_scr, rights_scr, scaled_scr, grad_scr, outer_scr, wide_scr, all_scr,
         final_out, out_sem, turn_scr,
     ) = refs[7 * (n_row - 1) : -7]
     stages.append(refs[-7:])
     stage_kernel(
-        n_col, n_row - 1, place_ref, last_ref, norm_ref, back_ref, final_ref, *stages[-1], turn_scr
+        n_col, n_row - 1, place_ref, (front_ref, rear_ref),
+        norm_ref, back_ref, final_ref, *stages[-1], turn_scr,
     )
     gain = norm_ref[0:1, :]
     averager = averager_of()
@@ -340,10 +357,13 @@
     mask = jnp.where((lane % 2 == 0) == (lane < 64), found, turned)
     mask_t = mask.T
 
-    for e in range(32):
-        right_scr[32 * e : 32 * e + 32, :] = jnp.concatenate(
-            [stage[3][e] for stage in stages], axis=0
-        ).astype(BF)
+    for q in range(8):
+        at = slice(128 * q, 128 * q + 128)
+        block = jnp.concatenate(
+            [stage[3][e] for e in range(4 * q, 4 * q + 4) for stage in stages], axis=0
+        )
+        right_scr[at, :] = block.astype(BF)
+        rights_scr[:, at] = block.T.astype(BF)
 
     mask_bf = mask.astype(BF)
     share = (1.0 / (mm_tn(mask_bf, mask_bf)[0:32] + 0.001)).astype(BF)
@@ -389,18 +409,14 @@
     bias_out[...] = bias
 
     left_t = jnp.concatenate([stage[2][...] for stage in stages], axis=0)
-    for n in range(8):
-        rights = jnp.concatenate(
-            [diagonal_pair(right_scr[64 * p : 64 * p + 64, :]) for p in (2 * n, 2 * n + 1)], axis=0
-        )
-        outer = mm_nt(left_t, rights).astype(BF)
-        for p in range(2):
-            for q in range(8):
-                rows = 64 * (2 * n + p)
-                block = outer[64 * q : 64 * q + 64, 128 * p : 128 * p + 128]
-                even, odd = interleave(block[:32], block[32:])
-                outer_scr[rows : rows + 32, 128 * q : 128 * q + 128] = even
-                outer_scr[rows + 32 : rows + 64, 128 * q : 128 * q + 128] = odd
+    for n in range(4):
+        outer = mm(left_t, rights_scr[:, 256 * n : 256 * n + 256]).astype(BF)
+        for p in range(8):
+            for q in range(2):
+                rows = 256 * n + 128 * q
+                outer_scr[rows : rows + 128, 128 * p : 128 * p + 128] = swap_blocks(
+                    outer[128 * p : 128 * p + 128, 128 * q : 128 * q + 128]
+                )
     wide_scr[...] = mm(outer_scr[...], scaled_scr[...])
     for c in range(32):
         final_out[32 * c : 32 * c + 32, :] = wide_scr[pl.ds(c, 32, stride=32), :]
@@ -525,33 +541,33 @@
     )
     norm, back, final_turned, first = weights
     own = jnp.concatenate([front, rear])
+    own, chip_front = lax.optimization_barrier((own, chip_front))
     core = over("row", n_row, 1, own)
     stage_outs = [
-        held_bf(512, 256), held_bf(128, 256), held_bf(128, 256), held(width, 8, 128),
+        held_bf(512, 256), held_bf(128, 256), held_bf(256, 128), held(width, 8, 128),
         held_bf(256, 1024), held(8, 32, 128), held(128, 128),
     ]
     scalar = pl.BlockSpec(memory_space=pltpu.SMEM)
 
-    def stage(a, block):
-        outs = stage_outs + [held(128, 128)] * 2 * (a == 0)
+    def stages_of(kernel, sets, outs, flops):
         return pl.pallas_call(
-            functools.partial(stage_kernel, n_col, a),
+            functools.partial(kernel, n_col),
             out_shape=tuple(outs),
-            in_specs=[scalar] + vmem(4),
+            in_specs=[scalar] + vmem(len(sets) + 3),
             out_specs=tuple(vmem(len(outs))),
-            scratch_shapes=[pltpu.VMEM((256, 128), F32)],
+            scratch_shapes=[pltpu.VMEM((256, 128), F32)] * (len(outs) // 7),
             compiler_params=LIMIT,
             cost_estimate=pl.CostEstimate(
-                flops=1_000_000_000, bytes_accessed=4_000_000, transcendentals=0
+                flops=flops, bytes_accessed=flops // 256, transcendentals=0
             ),
-        )(place, block, norm, back, final_turned)
-
-    own_stage = stage(0, own)
-    core_stage = stage(1, core)
-    chip = jnp.concatenate([chip_front, chip_rear])
-    chip, own_stage = lax.optimization_barrier((chip, own_stage))
-    both = over("row", n_row, 1, chip)
-    stages = [own_stage[:7], core_stage, stage(2, chip)]
+        )(place, *sets, norm, back, final_turned)
+
+    both_front = over("row", n_row, 1, chip_front)
+    own_stage = stages_of(own_kernel, (front, rear), stage_outs + [held(128, 128)] * 2, 1_000_000_000)
+    chip_rear, own_stage = lax.optimization_barrier((chip_rear, own_stage))
+    both_rear = over("row", n_row, 1, chip_rear)
+    pair_stages = stages_of(pair_kernel, (core, chip_front, chip_rear), stage_outs * 2, 1000000)
+    stages = [own_stage[:7], pair_stages]
     outs = pl.pallas_call(
         functools.partial(part_kernel, n_row, n_col),
         out_shape=(
@@ -563,10 +579,11 @@
             shape(1, features),
             shape(1, 128),
         ),
-        in_specs=[scalar] + vmem(7 * (n_row - 1) + 7),
+        in_specs=[scalar] + vmem(7 * (n_row - 1) + 8),
         out_specs=(*vmem(1), hbm, *vmem(5)),
         scratch_shapes=[
             pltpu.VMEM((1024, 128), BF),
+            pltpu.VMEM((128, 1024), BF),
             pltpu.VMEM((1024, 128), BF),
             pltpu.VMEM((1024, 1024), BF),
             pltpu.VMEM((1024, 1024), BF),
@@ -578,7 +595,7 @@
             *stage_outs,
         ],
         compiler_params=LIMIT,
-    )(place, both, *[x for s in stages for x in s], *own_stage[7:], norm, back, final_turned, first)
+    )(place, both_front, both_rear, *[x for s in stages for x in s], *own_stage[7:], norm, back, final_turned, first)
     emb, final, first, second, gain, offset, bias = outs
     return emb, final, first.T, second.T, gain.reshape(-1), offset.reshape(-1), bias.reshape(-1)
 

time: 24 us -> 25.6 us (1.067)
  the two profiles are of different devices: /device:TPU:0 before, /device:TPU:29 now
where the time goes in v15:
time: 25.6 us; the launch traced here: 25.4 us
  Pallas kernels  11.8 us (46%)
  starting transfers between devices  10.3 us (40%)
  waiting for transfers between devices  2.55 us (10%)
  between operations  0.7 us (3%)
    ppermute x8, starting transfers between devices, over(): return lax.ppermute(array, axis, [(k, k ^ step) for k in range(size)])  10.3 us
    pallas_call x1, Pallas kernels, gathered_body(): pl.pallas_call(functools.partial(part_kernel, n_row, n_col), out_shape=(s...  7.17 us
    ppermute x8, waiting for transfers between devices, over(): return lax.ppermute(array, axis, [(k, k ^ step) for k in range(size)])  2.55 us
    pallas_call x2, Pallas kernels, stages_of(): pl.pallas_call(functools.partial(kernel, n_col), out_shape=tuple(outs), i...  2.21 us
    pallas_call x1, Pallas kernels, gathered_body(): pl.pallas_call(weights_kernel, out_shape=(held(8, 128), held_bf(256, 256)...  1.39 us
    pallas_call x1, Pallas kernels, gathered_body(): pl.pallas_call(pack_kernel, out_shape=held_bf(192, 128), in_specs=vmem(3)...  1.04 us
  transfers between devices with their start and end apart: 8, of which 3 were waited for; matrix products, arithmetic and copies ran while one was open for 0% of the time, Pallas kernels for 14%

profile of v15, /device:TPU:29, one launch (start us, length us, event | category | flops | bytes accessed | tf_op | source)
XLA Modules:
  0.0 25.4 jit_solution(9690546242153660023)
XLA Ops:
  0.6 1.0 %shard_map.135 = bf16[192,128]{1,0:T(8,128)(2,1)S(1)} custom-call(bf16[32,8,64]{2,1,0:T(8,128)(2,1)} %msa_ref.1, s32[8,32]{1,0:T(8,128)} %bitcast.23, bf16[8,8,128]{2,1,0:T(8,128)(2,1)} %pair_ref.1), custom_call_target="tpu_custom_call" | custom-call | tf_op jit(solution)/shard_map/pallas_call | solution.py:496
  1.7 0.1 collective-permute-start
  1.8 2.2 %collective-permute-start.2 = (bf16[192,128]{1,0:T(8,128)(2,1)S(1)}, bf16[192,128]{1,0:T(8,128)(2,1)S(1)}, u32[]{:S(2)}, u32[]{:S(2)}) collective-permute-start(bf16[192,128]{1,0:T(8,128)(2,1)S(1)} %shard_map.135), channel_id=1, source_target_pairs={{0,3},{1,2},{2,1},{3,0},{4,7},{5,6},{6,5},{7,4},{8,11},{9,10},{10,... | collective-permute-start | bytes 147464 | tf_op jit(solution)/shard_map/ppermute | solution.py:503
  4.0 0.4 %collective-permute-start.1 = (bf16[192,128]{1,0:T(8,128)(2,1)S(1)}, bf16[192,128]{1,0:T(8,128)(2,1)S(1)}, u32[]{:S(2)}, u32[]{:S(2)}) collective-permute-start(bf16[192,128]{1,0:T(8,128)(2,1)S(1)} %shard_map.135), channel_id=1, source_target_pairs={{0,1},{1,0},{2,3},{3,2},{4,5},{5,4},{6,7},{7,6},{8,9},{9,8},{10,11... | collective-permute-start | bytes 147464 | tf_op jit(solution)/shard_map/ppermute | solution.py:503
  4.4 1.6 %collective-permute-done = bf16[192,128]{1,0:T(8,128)(2,1)S(1)} collective-permute-done((bf16[192,128]{1,0:T(8,128)(2,1)S(1)}, bf16[192,128]{1,0:T(8,128)(2,1)S(1)}, u32[]{:S(2)}, u32[]{:S(2)}) %collective-permute-start) | collective-permute-done | bytes 49184 | tf_op jit(solution)/shard_map/ppermute | solution.py:503
  6.0 1.3 %collective-permute-start.3 = (bf16[2,192,128]{2,1,0:T(8,128)(2,1)S(1)}, bf16[2,192,128]{2,1,0:T(8,128)(2,1)S(1)}, u32[]{:S(2)}, u32[]{:S(2)}) collective-permute-start(bf16[2,192,128]{2,1,0:T(8,128)(2,1)S(1)} %pad_maximum_fusion.1.front_ref), channel_id=1, source_target_pairs={{0,8},{4,12},{8,0},{12,4},{1,9},{5,13},{9,1},{13,5},{2,10},{6,14},... | collective-permute-start | bytes 294920 | tf_op jit(solution)/shard_map/ppermute | solution.py:503
  7.3 0.0 collective-permute-done.2
  7.3 0.4 %collective-permute-done.1 = bf16[192,128]{1,0:T(8,128)(2,1)S(1)} collective-permute-done((bf16[192,128]{1,0:T(8,128)(2,1)S(1)}, bf16[192,128]{1,0:T(8,128)(2,1)S(1)}, u32[]{:S(2)}, u32[]{:S(2)}) %collective-permute-start.1) | collective-permute-done | bytes 49184 | tf_op jit(solution)/shard_map/ppermute | solution.py:503
  7.7 1.3 %collective-permute-start.5 = (bf16[2,192,128]{2,1,0:T(8,128)(2,1)S(1)}, bf16[2,192,128]{2,1,0:T(8,128)(2,1)S(1)}, u32[]{:S(2)}, u32[]{:S(2)}) collective-permute-start(bf16[2,192,128]{2,1,0:T(8,128)(2,1)S(1)} %pad_maximum_fusion.2.rear_ref), channel_id=1, source_target_pairs={{0,8},{4,12},{8,0},{12,4},{1,9},{5,13},{9,1},{13,5},{2,10},{6,14},... | collective-permute-start | bytes 294920 | tf_op jit(solution)/shard_map/ppermute | solution.py:503
  9.0 0.5 %collective-permute-done.3.front_ref = bf16[2,192,128]{2,1,0:T(8,128)(2,1)S(1)} collective-permute-done((bf16[2,192,128]{2,1,0:T(8,128)(2,1)S(1)}, bf16[2,192,128]{2,1,0:T(8,128)(2,1)S(1)}, u32[]{:S(2)}, u32[]{:S(2)}) %collective-permute-start.3) | collective-permute-done | bytes 98336 | tf_op jit(solution)/shard_map/ppermute | solution.py:503
  9.5 4.5 %collective-permute-start.7 = (bf16[4,192,128]{2,1,0:T(8,128)(2,1)S(1)}, bf16[4,192,128]{2,1,0:T(8,128)(2,1)S(1)}, u32[]{:S(2)}, u32[]{:S(2)}) collective-permute-start(bf16[4,192,128]{2,1,0:T(8,128)(2,1)S(1)} %pad_maximum_fusion), channel_id=1, source_target_pairs={{0,4},{4,0},{8,12},{12,8},{1,5},{5,1},{9,13},{13,9},{2,6},{6,2},{1... | collective-permute-start | bytes 589832 | tf_op jit(solution)/shard_map/ppermute | solution.py:503
  14.0 1.4 %shard_map.136 = (f32[8,128]{1,0:T(8,128)S(1)}, bf16[256,256]{1,0:T(8,128)(2,1)S(1)}, bf16[512,256]{1,0:T(8,128)(2,1)S(1)}, f32[64,64]{1,0:T(8,128)S(1)}) custom-call(f32[1,64]{1,0:T(1,128)} %bitcast.24, f32[1,64]{1,0:T(1,128)} %bitcast.25, bf16[32,64]{1,0:T(8,128)(2,1)} %bitcast.21, bf16[32,64]{1,0:T(8,128)(2,1)} %bitcast.22, bf16[1024,128]{1,0:T(8,128)(2,1)} %refs_4_), custom_call_target="tpu_custom_call" | custom-call | tf_op jit(solution)/shard_map/pallas_call | solution.py:513
  15.4 0.8 %shard_map.137 = (bf16[512,256]{1,0:T(8,128)(2,1)S(1)}, bf16[128,256]{1,0:T(8,128)(2,1)S(1)}, bf16[256,128]{1,0:T(8,128)(2,1)S(1)}, f32[32,8,128]{2,1,0:T(8,128)...) custom-call(s32[1]{0:T(128)} %bitcast.place_ref, ...), custom_call_target="tpu_custom_call" | custom-call | flops 1000000000 | bytes 3906250 | tf_op jit(solution)/shard_map/pallas_call | solution.py:553
  16.3 0.1 collective-permute-start.4
  16.3 0.0 collective-permute-done.5.rear_ref
  16.3 0.5 %collective-permute-start.6 = (bf16[2,192,128]{2,1,0:T(8,128)(2,1)S(1)}, bf16[2,192,128]{2,1,0:T(8,128)(2,1)S(1)}, u32[]{:S(2)}, u32[]{:S(2)}) collective-permute-start(bf16[2,192,128]{2,1,0:T(8,128)(2,1)S(1)} %collective-permute-done.5.rear_ref), channel_id=1, source_target_pairs={{0,4},{4,0},{8,12},{12,8},{1,5},{5,1},{9,13},{13,9},{2,6},{6,2},{1... | collective-permute-start | bytes 294920 | tf_op jit(solution)/shard_map/ppermute | solution.py:503
  16.8 0.0 collective-permute-done.7.core_ref
  16.8 1.4 %shard_map.138 = (bf16[512,256]{1,0:T(8,128)(2,1)S(1)}, bf16[128,256]{1,0:T(8,128)(2,1)S(1)}, bf16[256,128]{1,0:T(8,128)(2,1)S(1)}, f32[32,8,128]{2,1,0:T(8,128)...) custom-call(s32[1]{0:T(128)} %bitcast.place_ref, ...), custom_call_target="tpu_custom_call" | custom-call | flops 1000000 | bytes 3906 | tf_op jit(solution)/shard_map/pallas_call | solution.py:553
  18.2 0.0 collective-permute-done.4.front_ref
  18.3 0.0 collective-permute-done.6.rear_ref
  18.3 7.2 %shard_map.139 = (f32[32,8,64]{2,1,0:T(8,128)}, f32[1024,128]{1,0:T(8,128)}, f32[32,64]{1,0:T(8,128)}, f32[32,64]{1,0:T(8,128)}, f32[1,64]{1,0:T(1,128)}, /*index=5*/f32[1,64]{1,0:T(1,128)}, f32[1,128]{1,0:T(1,128)}) custom-call(s32[1]{0:T(128)} %bitcast.place_ref, bf16[2,192,128]{2,1,0:T(8,128)(2,1)S(1)} %collective-permute-done.4.front_ref, ...), custom_call_target="tpu_custom_call" | custom-call | tf_op jit(solution)/shard_map/pallas_call | solution.py:571
  (3 shorter events, 0.0 us)
Async XLA Ops:
  1.7 4.3 %collective-permute-start = (bf16[192,128]{1,0:T(8,128)(2,1)S(1)}, bf16[192,128]{1,0:T(8,128)(2,1)S(1)}, u32[]{:S(2)}, u32[]{:S(2)}) collective-permute-start(bf16[192,128]{1,0:T(8,128)(2,1)S(1)} %shard_map.135), channel_id=1, source_target_pairs={{0,2},{1,3},{2,0},{3,1},{4,6},{5,7},{6,4},{7,5},{8,10},{9,11},{10,... | collective-permute-start | bytes 147464 | tf_op jit(solution)/shard_map/ppermute | solution.py:503
  1.8 5.5 %collective-permute-start.2 = (bf16[192,128]{1,0:T(8,128)(2,1)S(1)}, bf16[192,128]{1,0:T(8,128)(2,1)S(1)}, u32[]{:S(2)}, u32[]{:S(2)}) collective-permute-start(bf16[192,128]{1,0:T(8,128)(2,1)S(1)} %shard_map.135), channel_id=1, source_target_pairs={{0,3},{1,2},{2,1},{3,0},{4,7},{5,6},{6,5},{7,4},{8,11},{9,10},{10,... | collective-permute-start | bytes 147464 | tf_op jit(solution)/shard_map/ppermute | solution.py:503
  4.0 3.7 %collective-permute-start.1 = (bf16[192,128]{1,0:T(8,128)(2,1)S(1)}, bf16[192,128]{1,0:T(8,128)(2,1)S(1)}, u32[]{:S(2)}, u32[]{:S(2)}) collective-permute-start(bf16[192,128]{1,0:T(8,128)(2,1)S(1)} %shard_map.135), channel_id=1, source_target_pairs={{0,1},{1,0},{2,3},{3,2},{4,5},{5,4},{6,7},{7,6},{8,9},{9,8},{10,11... | collective-permute-start | bytes 147464 | tf_op jit(solution)/shard_map/ppermute | solution.py:503
  6.0 3.5 %collective-permute-start.3 = (bf16[2,192,128]{2,1,0:T(8,128)(2,1)S(1)}, bf16[2,192,128]{2,1,0:T(8,128)(2,1)S(1)}, u32[]{:S(2)}, u32[]{:S(2)}) collective-permute-start(bf16[2,192,128]{2,1,0:T(8,128)(2,1)S(1)} %pad_maximum_fusion.1.front_ref), channel_id=1, source_target_pairs={{0,8},{4,12},{8,0},{12,4},{1,9},{5,13},{9,1},{13,5},{2,10},{6,14},... | collective-permute-start | bytes 294920 | tf_op jit(solution)/shard_map/ppermute | solution.py:503
  7.7 8.6 %collective-permute-start.5 = (bf16[2,192,128]{2,1,0:T(8,128)(2,1)S(1)}, bf16[2,192,128]{2,1,0:T(8,128)(2,1)S(1)}, u32[]{:S(2)}, u32[]{:S(2)}) collective-permute-start(bf16[2,192,128]{2,1,0:T(8,128)(2,1)S(1)} %pad_maximum_fusion.2.rear_ref), channel_id=1, source_target_pairs={{0,8},{4,12},{8,0},{12,4},{1,9},{5,13},{9,1},{13,5},{2,10},{6,14},... | collective-permute-start | bytes 294920 | tf_op jit(solution)/shard_map/ppermute | solution.py:503
  9.5 7.3 %collective-permute-start.7 = (bf16[4,192,128]{2,1,0:T(8,128)(2,1)S(1)}, bf16[4,192,128]{2,1,0:T(8,128)(2,1)S(1)}, u32[]{:S(2)}, u32[]{:S(2)}) collective-permute-start(bf16[4,192,128]{2,1,0:T(8,128)(2,1)S(1)} %pad_maximum_fusion), channel_id=1, source_target_pairs={{0,4},{4,0},{8,12},{12,8},{1,5},{5,1},{9,13},{13,9},{2,6},{6,2},{1... | collective-permute-start | bytes 589832 | tf_op jit(solution)/shard_map/ppermute | solution.py:503
  16.3 2.0 %collective-permute-start.4 = (bf16[2,192,128]{2,1,0:T(8,128)(2,1)S(1)}, bf16[2,192,128]{2,1,0:T(8,128)(2,1)S(1)}, u32[]{:S(2)}, u32[]{:S(2)}) collective-permute-start(bf16[2,192,128]{2,1,0:T(8,128)(2,1)S(1)} %collective-permute-done.3.front_ref), channel_id=1, source_target_pairs={{0,4},{4,0},{8,12},{12,8},{1,5},{5,1},{9,13},{13,9},{2,6},{6,2},{1... | collective-permute-start | bytes 294920 | tf_op jit(solution)/shard_map/ppermute | solution.py:503
  16.3 1.9 %collective-permute-start.6 = (bf16[2,192,128]{2,1,0:T(8,128)(2,1)S(1)}, bf16[2,192,128]{2,1,0:T(8,128)(2,1)S(1)}, u32[]{:S(2)}, u32[]{:S(2)}) collective-permute-start(bf16[2,192,128]{2,1,0:T(8,128)(2,1)S(1)} %collective-permute-done.5.rear_ref), channel_id=1, source_target_pairs={{0,4},{4,0},{8,12},{12,8},{1,5},{5,1},{9,13},{13,9},{2,6},{6,2},{1... | collective-permute-start | bytes 294920 | tf_op jit(solution)/shard_map/ppermute | solution.py:503

commit v16 on v15

--- a/solution.py
+++ b/solution.py
@@ -187,26 +187,14 @@
     return lax.dot_general(a, b, (((0,), (0,)), ((), ())), preferred_element_type=F32)
 
 
-def interleave(first, second):
-    odd = lax.broadcasted_iota(jnp.int16, (32, 128), 1) & 32 != 0
-    return (
-        jnp.where(odd, pltpu.roll(second, 32, 1), first),
-        jnp.where(odd, second, pltpu.roll(first, 96, 1)),
-    )
-
-
-def swap_blocks(block):
-    upper = lax.broadcasted_iota(jnp.int16, (32, 128), 1) & 64 != 0
-    piece = [block[32 * a : 32 * a + 32] for a in range(4)]
-    low = [jnp.where(upper, pltpu.roll(piece[a + 2], 64, 1), piece[a]) for a in range(2)]
-    high = [jnp.where(upper, piece[a + 2], pltpu.roll(piece[a], 64, 1)) for a in range(2)]
-    return jnp.concatenate([*interleave(*low), *interleave(*high)], axis=0)
-
-
-def diagonal_pair(block):
+def diagonal(block, count):
     zero = jnp.zeros_like(block)
     return jnp.concatenate(
-        [jnp.concatenate([block, zero], axis=1), jnp.concatenate([zero, block], axis=1)], axis=0
+        [
+            jnp.concatenate([block if a == b else zero for b in range(count)], axis=1)
+            for a in range(count)
+        ],
+        axis=0,
     )
 
 
@@ -249,10 +237,9 @@
         own = spread(128, 256, lambda r, c: r // 32 == c // 64)
         back_out[128 * k : 128 * k + 128, :] = jnp.where(own, wide, 0.0).astype(BF)
     scr[...] = final_ref[...].astype(F32)
-    for k in range(16):
-        e = 4 * (k // 2) + k % 2
-        final_out[32 * k : 32 * k + 32, :] = jnp.concatenate(
-            [scr[pl.ds(e, 32, stride=32), :], scr[pl.ds(e + 2, 32, stride=32), :]], axis=1
+    for q in range(8):
+        final_out[32 * q : 32 * q + 32, :] = jnp.concatenate(
+            [scr[pl.ds(e, 32, stride=32), :] for e in range(4 * q, 4 * q + 4)], axis=1
         ).astype(BF)
 
 
@@ -304,25 +291,26 @@
         at = slice(128 * h, 128 * h + 128)
         left_out[:, at] = mm_nt(masked, back_ref[:128, :]).astype(BF)
         both = mm_nt(back_ref[...], masked)
-        leftt_out[at, :] = both[:128].astype(BF)
         turn_scr[at, :] = both[128:]
+        for k in range(2):
+            leftt_out[64 * h + 32 * k : 64 * h + 32 * k + 32, :] = jnp.concatenate(
+                [both[32 * k : 32 * k + 32], both[32 * k + 64 : 32 * k + 96]], axis=1
+            ).astype(BF)
 
     for e in range(32):
         rightt_out[e] = turn_scr[pl.ds(e, 8, stride=32), :]
 
-    pair = pair_out[...].reshape(256, 128).astype(BF)
-    for n in range(2):
+    for n in range(4):
         pairs = jnp.concatenate(
-            [diagonal_pair(pair[64 * p : 64 * p + 64]) for p in (2 * n, 2 * n + 1)], axis=0
+            [diagonal(pair_out[i].astype(BF), 4) for i in (2 * n, 2 * n + 1)], axis=0
         )
         grad = mm_nt(final_ref[...], pairs).astype(BF)
-        for p in range(2):
+        for i in range(2):
+            rows = 32 * (2 * n + i)
             for q in range(8):
-                rows = 64 * (2 * n + p)
-                block = grad[64 * q : 64 * q + 64, 128 * p : 128 * p + 128]
-                even, odd = interleave(block[:32], block[32:])
-                grad_out[rows : rows + 32, 128 * q : 128 * q + 128] = even
-                grad_out[rows + 32 : rows + 64, 128 * q : 128 * q + 128] = odd
+                grad_out[rows : rows + 32, 128 * q : 128 * q + 128] = (
+                    grad[32 * q : 32 * q + 32, 128 * i : 128 * i + 128]
+                )
 
 
 def own_kernel(n_col, place_ref, front_ref, rear_ref, norm_ref, back_ref, final_ref, *rest):
@@ -340,7 +328,7 @@
     (
         normed_ref, inverse_ref, norm_ref, back_ref, final_ref, first_ref,
         emb_out, final_hbm_out, first_out, second_out, gain_out, offset_out, bias_out,
-        right_scr, rights_scr, scaled_scr, grad_scr, outer_scr, wide_scr, all_scr,
+        right_scr, scaled_scr, grad_scr, outer_scr, wide_scr, all_scr,
         final_out, out_sem, turn_scr,
     ) = refs[7 * (n_row - 1) : -7]
     stages.append(refs[-7:])
@@ -357,13 +345,10 @@
     mask = jnp.where((lane % 2 == 0) == (lane < 64), found, turned)
     mask_t = mask.T
 
-    for q in range(8):
-        at = slice(128 * q, 128 * q + 128)
-        block = jnp.concatenate(
-            [stage[3][e] for e in range(4 * q, 4 * q + 4) for stage in stages], axis=0
-        )
-        right_scr[at, :] = block.astype(BF)
-        rights_scr[:, at] = block.T.astype(BF)
+    for e in range(32):
+        right_scr[32 * e : 32 * e + 32, :] = jnp.concatenate(
+            [stage[3][e] for stage in stages], axis=0
+        ).astype(BF)
 
     mask_bf = mask.astype(BF)
     share = (1.0 / (mm_tn(mask_bf, mask_bf)[0:32] + 0.001)).astype(BF)
@@ -397,6 +382,7 @@
 
     bias = jnp.zeros((1, 128), F32)
     ones = jnp.ones((128, 128), BF)
+    zero = jnp.zeros((32, 128), BF)
     for p in range(8):
         both_on = jnp.concatenate(
             [mask_t[0:32] * mask_t[i : i + 1] for i in range(4 * p, 4 * p + 4)], axis=0
@@ -405,19 +391,33 @@
         pair = stages[p // 2][5][4 * (p % 2) : 4 * (p % 2) + 4]
         scaled = pair.reshape(128, 128) / (counts + 0.001)
         bias = bias + jnp.sum(scaled, axis=0, keepdims=True)
-        scaled_scr[128 * p : 128 * p + 128, :] = scaled.astype(BF)
+        scaled = scaled.astype(BF)
+        for k in range(4):
+            at = 256 * p + 128 * (k % 2) + 64 * (k // 2)
+            part = scaled[32 * k : 32 * k + 32]
+            scaled_scr[at : at + 32, 0:128] = part
+            scaled_scr[at : at + 32, 128:256] = zero
+            scaled_scr[at + 32 : at + 64, 0:128] = zero
+            scaled_scr[at + 32 : at + 64, 128:256] = part
     bias_out[...] = bias
 
     left_t = jnp.concatenate([stage[2][...] for stage in stages], axis=0)
-    for n in range(4):
-        outer = mm(left_t, rights_scr[:, 256 * n : 256 * n + 256]).astype(BF)
-        for p in range(8):
-            for q in range(2):
-                rows = 256 * n + 128 * q
-                outer_scr[rows : rows + 128, 128 * p : 128 * p + 128] = swap_blocks(
-                    outer[128 * p : 128 * p + 128, 128 * q : 128 * q + 128]
+    for n in range(8):
+        rights = jnp.concatenate(
+            [diagonal(right_scr[64 * p : 64 * p + 64, :], 2) for p in (2 * n, 2 * n + 1)], axis=0
+        )
+        outer = mm_nt(left_t, rights).astype(BF)
+        for p in range(2):
+            rows = 32 * (2 * n + p)
+            for k in range(16):
+                outer_scr[rows : rows + 32, 128 * k : 128 * k + 128] = (
+                    outer[32 * k : 32 * k + 32, 128 * p : 128 * p + 128]
                 )
-    wide_scr[...] = mm(outer_scr[...], scaled_scr[...])
+    final = mm(outer_scr[...], scaled_scr[...])
+    for e in range(32):
+        wide_scr[32 * e : 32 * e + 32, :] = (
+            final[32 * (e // 2) : 32 * (e // 2) + 32, 128 * (e % 2) : 128 * (e % 2) + 128]
+        )
     for c in range(32):
         final_out[32 * c : 32 * c + 32, :] = wide_scr[pl.ds(c, 32, stride=32), :]
     final_send = pltpu.make_async_copy(final_out, final_hbm_out, out_sem)
@@ -513,7 +513,7 @@
     weights = pl.pallas_call(
         weights_kernel,
         out_shape=(
-            held(8, 128), held_bf(256, 256), held_bf(width * width // 2, 256), held(2 * width, features),
+            held(8, 128), held_bf(256, 256), held_bf(width * width // 4, 512), held(2 * width, features),
         ),
         in_specs=[hbm] * 5,
         out_specs=tuple(vmem(4)),
@@ -544,7 +544,7 @@
     own, chip_front = lax.optimization_barrier((own, chip_front))
     core = over("row", n_row, 1, own)
     stage_outs = [
-        held_bf(512, 256), held_bf(128, 256), held_bf(256, 128), held(width, 8, 128),
+        held_bf(512, 256), held_bf(128, 256), held_bf(128, 256), held(width, 8, 128),
         held_bf(256, 1024), held(8, 32, 128), held(128, 128),
     ]
     scalar = pl.BlockSpec(memory_space=pltpu.SMEM)
@@ -583,10 +583,9 @@
         out_specs=(*vmem(1), hbm, *vmem(5)),
         scratch_shapes=[
             pltpu.VMEM((1024, 128), BF),
-            pltpu.VMEM((128, 1024), BF),
-            pltpu.VMEM((1024, 128), BF),
+            pltpu.VMEM((2048, 256), BF),
             pltpu.VMEM((1024, 1024), BF),
-            pltpu.VMEM((1024, 1024), BF),
+            pltpu.VMEM((512, 2048), BF),
             pltpu.VMEM((1024, 128), F32),
             pltpu.VMEM((128, 2048), BF),
             pltpu.VMEM((1024, 128), F32),

time: 25.6 us -> 24.8 us (0.969)
  the two profiles are of different devices: /device:TPU:29 before, /device:TPU:25 now
where the time goes in v16:
time: 24.8 us; the launch traced here: 24.6 us
  Pallas kernels  11 us (44%)
  starting transfers between devices  10.3 us (42%)
  waiting for transfers between devices  2.55 us (10%)
  between operations  0.71 us (3%)
    ppermute x8, starting transfers between devices, over(): return lax.ppermute(array, axis, [(k, k ^ step) for k in range(size)])  10.3 us
    pallas_call x1, Pallas kernels, gathered_body(): pl.pallas_call(functools.partial(part_kernel, n_row, n_col), out_shape=(s...  6.03 us
    ppermute x8, waiting for transfers between devices, over(): return lax.ppermute(array, axis, [(k, k ^ step) for k in range(size)])  2.55 us
    pallas_call x2, Pallas kernels, stages_of(): pl.pallas_call(functools.partial(kernel, n_col), out_shape=tuple(outs), i...  2.5 us
    pallas_call x1, Pallas kernels, gathered_body(): pl.pallas_call(weights_kernel, out_shape=(held(8, 128), held_bf(256, 256)...  1.39 us
    pallas_call x1, Pallas kernels, gathered_body(): pl.pallas_call(pack_kernel, out_shape=held_bf(192, 128), in_specs=vmem(3)...  1.04 us
  transfers between devices with their start and end apart: 8, of which 3 were waited for; matrix products, arithmetic and copies ran while one was open for 0% of the time, Pallas kernels for 16%

profile of v16, /device:TPU:25, one launch (start us, length us, event | category | flops | bytes accessed | tf_op | source)
XLA Modules:
  0.0 24.6 jit_solution(17464511951905511712)
XLA Ops:
  0.6 1.0 %shard_map.135 = bf16[192,128]{1,0:T(8,128)(2,1)S(1)} custom-call(bf16[32,8,64]{2,1,0:T(8,128)(2,1)} %msa_ref.1, s32[8,32]{1,0:T(8,128)} %bitcast.23, bf16[8,8,128]{2,1,0:T(8,128)(2,1)} %pair_ref.1), custom_call_target="tpu_custom_call" | custom-call | tf_op jit(solution)/shard_map/pallas_call | solution.py:496
  1.7 0.1 collective-permute-start
  1.8 2.2 %collective-permute-start.2 = (bf16[192,128]{1,0:T(8,128)(2,1)S(1)}, bf16[192,128]{1,0:T(8,128)(2,1)S(1)}, u32[]{:S(2)}, u32[]{:S(2)}) collective-permute-start(bf16[192,128]{1,0:T(8,128)(2,1)S(1)} %shard_map.135), channel_id=1, source_target_pairs={{0,3},{1,2},{2,1},{3,0},{4,7},{5,6},{6,5},{7,4},{8,11},{9,10},{10,... | collective-permute-start | bytes 147464 | tf_op jit(solution)/shard_map/ppermute | solution.py:503
  4.0 0.4 %collective-permute-start.1 = (bf16[192,128]{1,0:T(8,128)(2,1)S(1)}, bf16[192,128]{1,0:T(8,128)(2,1)S(1)}, u32[]{:S(2)}, u32[]{:S(2)}) collective-permute-start(bf16[192,128]{1,0:T(8,128)(2,1)S(1)} %shard_map.135), channel_id=1, source_target_pairs={{0,1},{1,0},{2,3},{3,2},{4,5},{5,4},{6,7},{7,6},{8,9},{9,8},{10,11... | collective-permute-start | bytes 147464 | tf_op jit(solution)/shard_map/ppermute | solution.py:503
  4.4 1.6 %collective-permute-done = bf16[192,128]{1,0:T(8,128)(2,1)S(1)} collective-permute-done((bf16[192,128]{1,0:T(8,128)(2,1)S(1)}, bf16[192,128]{1,0:T(8,128)(2,1)S(1)}, u32[]{:S(2)}, u32[]{:S(2)}) %collective-permute-start) | collective-permute-done | bytes 49184 | tf_op jit(solution)/shard_map/ppermute | solution.py:503
  6.0 1.3 %collective-permute-start.3 = (bf16[2,192,128]{2,1,0:T(8,128)(2,1)S(1)}, bf16[2,192,128]{2,1,0:T(8,128)(2,1)S(1)}, u32[]{:S(2)}, u32[]{:S(2)}) collective-permute-start(bf16[2,192,128]{2,1,0:T(8,128)(2,1)S(1)} %pad_maximum_fusion.1.front_ref), channel_id=1, source_target_pairs={{0,8},{4,12},{8,0},{12,4},{1,9},{5,13},{9,1},{13,5},{2,10},{6,14},... | collective-permute-start | bytes 294920 | tf_op jit(solution)/shard_map/ppermute | solution.py:503
  7.3 0.0 collective-permute-done.2
  7.3 0.4 %collective-permute-done.1 = bf16[192,128]{1,0:T(8,128)(2,1)S(1)} collective-permute-done((bf16[192,128]{1,0:T(8,128)(2,1)S(1)}, bf16[192,128]{1,0:T(8,128)(2,1)S(1)}, u32[]{:S(2)}, u32[]{:S(2)}) %collective-permute-start.1) | collective-permute-done | bytes 49184 | tf_op jit(solution)/shard_map/ppermute | solution.py:503
  7.7 1.3 %collective-permute-start.5 = (bf16[2,192,128]{2,1,0:T(8,128)(2,1)S(1)}, bf16[2,192,128]{2,1,0:T(8,128)(2,1)S(1)}, u32[]{:S(2)}, u32[]{:S(2)}) collective-permute-start(bf16[2,192,128]{2,1,0:T(8,128)(2,1)S(1)} %pad_maximum_fusion.2.rear_ref), channel_id=1, source_target_pairs={{0,8},{4,12},{8,0},{12,4},{1,9},{5,13},{9,1},{13,5},{2,10},{6,14},... | collective-permute-start | bytes 294920 | tf_op jit(solution)/shard_map/ppermute | solution.py:503
  9.0 0.5 %collective-permute-done.3.front_ref = bf16[2,192,128]{2,1,0:T(8,128)(2,1)S(1)} collective-permute-done((bf16[2,192,128]{2,1,0:T(8,128)(2,1)S(1)}, bf16[2,192,128]{2,1,0:T(8,128)(2,1)S(1)}, u32[]{:S(2)}, u32[]{:S(2)}) %collective-permute-start.3) | collective-permute-done | bytes 98336 | tf_op jit(solution)/shard_map/ppermute | solution.py:503
  9.5 4.5 %collective-permute-start.7 = (bf16[4,192,128]{2,1,0:T(8,128)(2,1)S(1)}, bf16[4,192,128]{2,1,0:T(8,128)(2,1)S(1)}, u32[]{:S(2)}, u32[]{:S(2)}) collective-permute-start(bf16[4,192,128]{2,1,0:T(8,128)(2,1)S(1)} %pad_maximum_fusion), channel_id=1, source_target_pairs={{0,4},{4,0},{8,12},{12,8},{1,5},{5,1},{9,13},{13,9},{2,6},{6,2},{1... | collective-permute-start | bytes 589832 | tf_op jit(solution)/shard_map/ppermute | solution.py:503
  14.0 1.4 %shard_map.136 = (f32[8,128]{1,0:T(8,128)S(1)}, bf16[256,256]{1,0:T(8,128)(2,1)S(1)}, bf16[256,512]{1,0:T(8,128)(2,1)S(1)}, f32[64,64]{1,0:T(8,128)S(1)}) custom-call(f32[1,64]{1,0:T(1,128)} %bitcast.24, f32[1,64]{1,0:T(1,128)} %bitcast.25, bf16[32,64]{1,0:T(8,128)(2,1)} %bitcast.21, bf16[32,64]{1,0:T(8,128)(2,1)} %bitcast.22, bf16[1024,128]{1,0:T(8,128)(2,1)} %refs_4_), custom_call_target="tpu_custom_call" | custom-call | tf_op jit(solution)/shard_map/pallas_call | solution.py:513
  15.4 0.9 %shard_map.137 = (bf16[512,256]{1,0:T(8,128)(2,1)S(1)}, bf16[128,256]{1,0:T(8,128)(2,1)S(1)}, bf16[128,256]{1,0:T(8,128)(2,1)S(1)}, f32[32,8,128]{2,1,0:T(8,128)...) custom-call(s32[1]{0:T(128)} %bitcast.place_ref, ...), custom_call_target="tpu_custom_call" | custom-call | flops 1000000000 | bytes 3906250 | tf_op jit(solution)/shard_map/pallas_call | solution.py:553
  16.3 0.1 collective-permute-start.4
  16.4 0.0 collective-permute-done.5.rear_ref
  16.4 0.5 %collective-permute-start.6 = (bf16[2,192,128]{2,1,0:T(8,128)(2,1)S(1)}, bf16[2,192,128]{2,1,0:T(8,128)(2,1)S(1)}, u32[]{:S(2)}, u32[]{:S(2)}) collective-permute-start(bf16[2,192,128]{2,1,0:T(8,128)(2,1)S(1)} %collective-permute-done.5.rear_ref), channel_id=1, source_target_pairs={{0,4},{4,0},{8,12},{12,8},{1,5},{5,1},{9,13},{13,9},{2,6},{6,2},{1... | collective-permute-start | bytes 294920 | tf_op jit(solution)/shard_map/ppermute | solution.py:503
  16.9 0.0 collective-permute-done.7.core_ref
  16.9 1.6 %shard_map.138 = (bf16[512,256]{1,0:T(8,128)(2,1)S(1)}, bf16[128,256]{1,0:T(8,128)(2,1)S(1)}, bf16[128,256]{1,0:T(8,128)(2,1)S(1)}, f32[32,8,128]{2,1,0:T(8,128)...) custom-call(s32[1]{0:T(128)} %bitcast.place_ref, ...), custom_call_target="tpu_custom_call" | custom-call | flops 1000000 | bytes 3906 | tf_op jit(solution)/shard_map/pallas_call | solution.py:553
  18.5 0.0 collective-permute-done.4.front_ref
  18.5 0.0 collective-permute-done.6.rear_ref
  18.5 6.0 %shard_map.139 = (f32[32,8,64]{2,1,0:T(8,128)}, f32[1024,128]{1,0:T(8,128)}, f32[32,64]{1,0:T(8,128)}, f32[32,64]{1,0:T(8,128)}, f32[1,64]{1,0:T(1,128)}, /*index=5*/f32[1,64]{1,0:T(1,128)}, f32[1,128]{1,0:T(1,128)}) custom-call(s32[1]{0:T(128)} %bitcast.place_ref, bf16[2,192,128]{2,1,0:T(8,128)(2,1)S(1)} %collective-permute-done.4.front_ref, ...), custom_call_target="tpu_custom_call" | custom-call | tf_op jit(solution)/shard_map/pallas_call | solution.py:571
  (3 shorter events, 0.0 us)
Async XLA Ops:
  1.7 4.3 %collective-permute-start = (bf16[192,128]{1,0:T(8,128)(2,1)S(1)}, bf16[192,128]{1,0:T(8,128)(2,1)S(1)}, u32[]{:S(2)}, u32[]{:S(2)}) collective-permute-start(bf16[192,128]{1,0:T(8,128)(2,1)S(1)} %shard_map.135), channel_id=1, source_target_pairs={{0,2},{1,3},{2,0},{3,1},{4,6},{5,7},{6,4},{7,5},{8,10},{9,11},{10,... | collective-permute-start | bytes 147464 | tf_op jit(solution)/shard_map/ppermute | solution.py:503
  1.8 5.5 %collective-permute-start.2 = (bf16[192,128]{1,0:T(8,128)(2,1)S(1)}, bf16[192,128]{1,0:T(8,128)(2,1)S(1)}, u32[]{:S(2)}, u32[]{:S(2)}) collective-permute-start(bf16[192,128]{1,0:T(8,128)(2,1)S(1)} %shard_map.135), channel_id=1, source_target_pairs={{0,3},{1,2},{2,1},{3,0},{4,7},{5,6},{6,5},{7,4},{8,11},{9,10},{10,... | collective-permute-start | bytes 147464 | tf_op jit(solution)/shard_map/ppermute | solution.py:503
  4.0 3.7 %collective-permute-start.1 = (bf16[192,128]{1,0:T(8,128)(2,1)S(1)}, bf16[192,128]{1,0:T(8,128)(2,1)S(1)}, u32[]{:S(2)}, u32[]{:S(2)}) collective-permute-start(bf16[192,128]{1,0:T(8,128)(2,1)S(1)} %shard_map.135), channel_id=1, source_target_pairs={{0,1},{1,0},{2,3},{3,2},{4,5},{5,4},{6,7},{7,6},{8,9},{9,8},{10,11... | collective-permute-start | bytes 147464 | tf_op jit(solution)/shard_map/ppermute | solution.py:503
  6.0 3.5 %collective-permute-start.3 = (bf16[2,192,128]{2,1,0:T(8,128)(2,1)S(1)}, bf16[2,192,128]{2,1,0:T(8,128)(2,1)S(1)}, u32[]{:S(2)}, u32[]{:S(2)}) collective-permute-start(bf16[2,192,128]{2,1,0:T(8,128)(2,1)S(1)} %pad_maximum_fusion.1.front_ref), channel_id=1, source_target_pairs={{0,8},{4,12},{8,0},{12,4},{1,9},{5,13},{9,1},{13,5},{2,10},{6,14},... | collective-permute-start | bytes 294920 | tf_op jit(solution)/shard_map/ppermute | solution.py:503
  7.7 8.7 %collective-permute-start.5 = (bf16[2,192,128]{2,1,0:T(8,128)(2,1)S(1)}, bf16[2,192,128]{2,1,0:T(8,128)(2,1)S(1)}, u32[]{:S(2)}, u32[]{:S(2)}) collective-permute-start(bf16[2,192,128]{2,1,0:T(8,128)(2,1)S(1)} %pad_maximum_fusion.2.rear_ref), channel_id=1, source_target_pairs={{0,8},{4,12},{8,0},{12,4},{1,9},{5,13},{9,1},{13,5},{2,10},{6,14},... | collective-permute-start | bytes 294920 | tf_op jit(solution)/shard_map/ppermute | solution.py:503
  9.5 7.4 %collective-permute-start.7 = (bf16[4,192,128]{2,1,0:T(8,128)(2,1)S(1)}, bf16[4,192,128]{2,1,0:T(8,128)(2,1)S(1)}, u32[]{:S(2)}, u32[]{:S(2)}) collective-permute-start(bf16[4,192,128]{2,1,0:T(8,128)(2,1)S(1)} %pad_maximum_fusion), channel_id=1, source_target_pairs={{0,4},{4,0},{8,12},{12,8},{1,5},{5,1},{9,13},{13,9},{2,6},{6,2},{1... | collective-permute-start | bytes 589832 | tf_op jit(solution)/shard_map/ppermute | solution.py:503
  16.3 2.2 %collective-permute-start.4 = (bf16[2,192,128]{2,1,0:T(8,128)(2,1)S(1)}, bf16[2,192,128]{2,1,0:T(8,128)(2,1)S(1)}, u32[]{:S(2)}, u32[]{:S(2)}) collective-permute-start(bf16[2,192,128]{2,1,0:T(8,128)(2,1)S(1)} %collective-permute-done.3.front_ref), channel_id=1, source_target_pairs={{0,4},{4,0},{8,12},{12,8},{1,5},{5,1},{9,13},{13,9},{2,6},{6,2},{1... | collective-permute-start | bytes 294920 | tf_op jit(solution)/shard_map/ppermute | solution.py:503
  16.4 2.1 %collective-permute-start.6 = (bf16[2,192,128]{2,1,0:T(8,128)(2,1)S(1)}, bf16[2,192,128]{2,1,0:T(8,128)(2,1)S(1)}, u32[]{:S(2)}, u32[]{:S(2)}) collective-permute-start(bf16[2,192,128]{2,1,0:T(8,128)(2,1)S(1)} %collective-permute-done.5.rear_ref), channel_id=1, source_target_pairs={{0,4},{4,0},{8,12},{12,8},{1,5},{5,1},{9,13},{13,9},{2,6},{6,2},{1... | collective-permute-start | bytes 294920 | tf_op jit(solution)/shard_map/ppermute | solution.py:503

commit v17 on v15

--- a/solution.py
+++ b/solution.py
@@ -193,14 +193,6 @@
         jnp.where(odd, pltpu.roll(second, 32, 1), first),
         jnp.where(odd, second, pltpu.roll(first, 96, 1)),
     )
-
-
-def swap_blocks(block):
-    upper = lax.broadcasted_iota(jnp.int16, (32, 128), 1) & 64 != 0
-    piece = [block[32 * a : 32 * a + 32] for a in range(4)]
-    low = [jnp.where(upper, pltpu.roll(piece[a + 2], 64, 1), piece[a]) for a in range(2)]
-    high = [jnp.where(upper, piece[a + 2], pltpu.roll(piece[a], 64, 1)) for a in range(2)]
-    return jnp.concatenate([*interleave(*low), *interleave(*high)], axis=0)
 
 
 def diagonal_pair(block):
@@ -304,8 +296,11 @@
         at = slice(128 * h, 128 * h + 128)
         left_out[:, at] = mm_nt(masked, back_ref[:128, :]).astype(BF)
         both = mm_nt(back_ref[...], masked)
-        leftt_out[at, :] = both[:128].astype(BF)
         turn_scr[at, :] = both[128:]
+        for k in range(2):
+            leftt_out[64 * h + 32 * k : 64 * h + 32 * k + 32, :] = jnp.concatenate(
+                [both[32 * k : 32 * k + 32], both[32 * k + 64 : 32 * k + 96]], axis=1
+            ).astype(BF)
 
     for e in range(32):
         rightt_out[e] = turn_scr[pl.ds(e, 8, stride=32), :]
@@ -340,7 +335,7 @@
     (
         normed_ref, inverse_ref, norm_ref, back_ref, final_ref, first_ref,
         emb_out, final_hbm_out, first_out, second_out, gain_out, offset_out, bias_out,
-        right_scr, rights_scr, scaled_scr, grad_scr, outer_scr, wide_scr, all_scr,
+        right_scr, scaled_scr, grad_scr, outer_scr, wide_scr, all_scr,
         final_out, out_sem, turn_scr,
     ) = refs[7 * (n_row - 1) : -7]
     stages.append(refs[-7:])
@@ -357,13 +352,10 @@
     mask = jnp.where((lane % 2 == 0) == (lane < 64), found, turned)
     mask_t = mask.T
 
-    for q in range(8):
-        at = slice(128 * q, 128 * q + 128)
-        block = jnp.concatenate(
-            [stage[3][e] for e in range(4 * q, 4 * q + 4) for stage in stages], axis=0
-        )
-        right_scr[at, :] = block.astype(BF)
-        rights_scr[:, at] = block.T.astype(BF)
+    for e in range(32):
+        right_scr[32 * e : 32 * e + 32, :] = jnp.concatenate(
+            [stage[3][e] for stage in stages], axis=0
+        ).astype(BF)
 
     mask_bf = mask.astype(BF)
     share = (1.0 / (mm_tn(mask_bf, mask_bf)[0:32] + 0.001)).astype(BF)
@@ -409,14 +401,18 @@
     bias_out[...] = bias
 
     left_t = jnp.concatenate([stage[2][...] for stage in stages], axis=0)
-    for n in range(4):
-        outer = mm(left_t, rights_scr[:, 256 * n : 256 * n + 256]).astype(BF)
-        for p in range(8):
-            for q in range(2):
-                rows = 256 * n + 128 * q
-                outer_scr[rows : rows + 128, 128 * p : 128 * p + 128] = swap_blocks(
-                    outer[128 * p : 128 * p + 128, 128 * q : 128 * q + 128]
-                )
+    for n in range(8):
+        rights = jnp.concatenate(
+            [diagonal_pair(right_scr[64 * p : 64 * p + 64, :]) for p in (2 * n, 2 * n + 1)], axis=0
+        )
+        outer = mm_nt(left_t, rights).astype(BF)
+        for p in range(2):
+            for q in range(8):
+                rows = 64 * (2 * n + p)
+                block = outer[64 * q : 64 * q + 64, 128 * p : 128 * p + 128]
+                even, odd = interleave(block[:32], block[32:])
+                outer_scr[rows : rows + 32, 128 * q : 128 * q + 128] = even
+                outer_scr[rows + 32 : rows + 64, 128 * q : 128 * q + 128] = odd
     wide_scr[...] = mm(outer_scr[...], scaled_scr[...])
     for c in range(32):
         final_out[32 * c : 32 * c + 32, :] = wide_scr[pl.ds(c, 32, stride=32), :]
@@ -544,7 +540,7 @@
     own, chip_front = lax.optimization_barrier((own, chip_front))
     core = over("row", n_row, 1, own)
     stage_outs = [
-        held_bf(512, 256), held_bf(128, 256), held_bf(256, 128), held(width, 8, 128),
+        held_bf(512, 256), held_bf(128, 256), held_bf(128, 256), held(width, 8, 128),
         held_bf(256, 1024), held(8, 32, 128), held(128, 128),
     ]
     scalar = pl.BlockSpec(memory_space=pltpu.SMEM)
@@ -583,7 +579,6 @@
         out_specs=(*vmem(1), hbm, *vmem(5)),
         scratch_shapes=[
             pltpu.VMEM((1024, 128), BF),
-            pltpu.VMEM((128, 1024), BF),
             pltpu.VMEM((1024, 128), BF),
             pltpu.VMEM((1024, 1024), BF),
             pltpu.VMEM((1024, 1024), BF),

time: 25.6 us -> 24 us (0.938)
  the two profiles are of different devices: /device:TPU:29 before, /device:TPU:31 now
where the time goes in v17:
time: 24 us; the launch traced here: 23.8 us
  Pallas kernels  10.2 us (42%)
  starting transfers between devices  8.4 us (35%)
  waiting for transfers between devices  4.46 us (19%)
  between operations  0.71 us (3%)
    ppermute x8, starting transfers between devices, over(): return lax.ppermute(array, axis, [(k, k ^ step) for k in range(size)])  8.4 us
    pallas_call x1, Pallas kernels, gathered_body(): pl.pallas_call(functools.partial(part_kernel, n_row, n_col), out_shape=(s...  5.57 us
    ppermute x8, waiting for transfers between devices, over(): return lax.ppermute(array, axis, [(k, k ^ step) for k in range(size)])  4.46 us
    pallas_call x2, Pallas kernels, stages_of(): pl.pallas_call(functools.partial(kernel, n_col), out_shape=tuple(outs), i...  2.21 us
    pallas_call x1, Pallas kernels, gathered_body(): pl.pallas_call(weights_kernel, out_shape=(held(8, 128), held_bf(256, 256)...  1.39 us
    pallas_call x1, Pallas kernels, gathered_body(): pl.pallas_call(pack_kernel, out_shape=held_bf(192, 128), in_specs=vmem(3)...  1.04 us
  transfers between devices with their start and end apart: 8, of which 4 were waited for; matrix products, arithmetic and copies ran while one was open for 0% of the time, Pallas kernels for 15%

profile of v17, /device:TPU:31, one launch (start us, length us, event | category | flops | bytes accessed | tf_op | source)
XLA Modules:
  0.0 23.8 jit_solution(11665066819135014454)
XLA Ops:
  0.6 1.0 %shard_map.135 = bf16[192,128]{1,0:T(8,128)(2,1)S(1)} custom-call(bf16[32,8,64]{2,1,0:T(8,128)(2,1)} %msa_ref.1, s32[8,32]{1,0:T(8,128)} %bitcast.23, bf16[8,8,128]{2,1,0:T(8,128)(2,1)} %pair_ref.1), custom_call_target="tpu_custom_call" | custom-call | tf_op jit(solution)/shard_map/pallas_call | solution.py:492
  1.7 0.1 collective-permute-start
  1.8 2.2 %collective-permute-start.2 = (bf16[192,128]{1,0:T(8,128)(2,1)S(1)}, bf16[192,128]{1,0:T(8,128)(2,1)S(1)}, u32[]{:S(2)}, u32[]{:S(2)}) collective-permute-start(bf16[192,128]{1,0:T(8,128)(2,1)S(1)} %shard_map.135), channel_id=1, source_target_pairs={{0,3},{1,2},{2,1},{3,0},{4,7},{5,6},{6,5},{7,4},{8,11},{9,10},{10,... | collective-permute-start | bytes 147464 | tf_op jit(solution)/shard_map/ppermute | solution.py:499
  4.0 0.4 %collective-permute-start.1 = (bf16[192,128]{1,0:T(8,128)(2,1)S(1)}, bf16[192,128]{1,0:T(8,128)(2,1)S(1)}, u32[]{:S(2)}, u32[]{:S(2)}) collective-permute-start(bf16[192,128]{1,0:T(8,128)(2,1)S(1)} %shard_map.135), channel_id=1, source_target_pairs={{0,1},{1,0},{2,3},{3,2},{4,5},{5,4},{6,7},{7,6},{8,9},{9,8},{10,11... | collective-permute-start | bytes 147464 | tf_op jit(solution)/shard_map/ppermute | solution.py:499
  4.4 1.6 %collective-permute-done = bf16[192,128]{1,0:T(8,128)(2,1)S(1)} collective-permute-done((bf16[192,128]{1,0:T(8,128)(2,1)S(1)}, bf16[192,128]{1,0:T(8,128)(2,1)S(1)}, u32[]{:S(2)}, u32[]{:S(2)}) %collective-permute-start) | collective-permute-done | bytes 49184 | tf_op jit(solution)/shard_map/ppermute | solution.py:499
  6.0 0.3 %collective-permute-start.3 = (bf16[2,192,128]{2,1,0:T(8,128)(2,1)S(1)}, bf16[2,192,128]{2,1,0:T(8,128)(2,1)S(1)}, u32[]{:S(2)}, u32[]{:S(2)}) collective-permute-start(bf16[2,192,128]{2,1,0:T(8,128)(2,1)S(1)} %pad_maximum_fusion.1.front_ref), channel_id=1, source_target_pairs={{0,8},{4,12},{8,0},{12,4},{1,9},{5,13},{9,1},{13,5},{2,10},{6,14},... | collective-permute-start | bytes 294920 | tf_op jit(solution)/shard_map/ppermute | solution.py:499
  6.3 0.8 %collective-permute-done.2 = bf16[192,128]{1,0:T(8,128)(2,1)S(1)} collective-permute-done((bf16[192,128]{1,0:T(8,128)(2,1)S(1)}, bf16[192,128]{1,0:T(8,128)(2,1)S(1)}, u32[]{:S(2)}, u32[]{:S(2)}) %collective-permute-start.2) | collective-permute-done | bytes 49184 | tf_op jit(solution)/shard_map/ppermute | solution.py:499
  7.1 0.6 %collective-permute-done.1 = bf16[192,128]{1,0:T(8,128)(2,1)S(1)} collective-permute-done((bf16[192,128]{1,0:T(8,128)(2,1)S(1)}, bf16[192,128]{1,0:T(8,128)(2,1)S(1)}, u32[]{:S(2)}, u32[]{:S(2)}) %collective-permute-start.1) | collective-permute-done | bytes 49184 | tf_op jit(solution)/shard_map/ppermute | solution.py:499
  7.7 0.3 %collective-permute-start.5 = (bf16[2,192,128]{2,1,0:T(8,128)(2,1)S(1)}, bf16[2,192,128]{2,1,0:T(8,128)(2,1)S(1)}, u32[]{:S(2)}, u32[]{:S(2)}) collective-permute-start(bf16[2,192,128]{2,1,0:T(8,128)(2,1)S(1)} %pad_maximum_fusion.2.rear_ref), channel_id=1, source_target_pairs={{0,8},{4,12},{8,0},{12,4},{1,9},{5,13},{9,1},{13,5},{2,10},{6,14},... | collective-permute-start | bytes 294920 | tf_op jit(solution)/shard_map/ppermute | solution.py:499
  8.1 1.5 %collective-permute-done.3.front_ref = bf16[2,192,128]{2,1,0:T(8,128)(2,1)S(1)} collective-permute-done((bf16[2,192,128]{2,1,0:T(8,128)(2,1)S(1)}, bf16[2,192,128]{2,1,0:T(8,128)(2,1)S(1)}, u32[]{:S(2)}, u32[]{:S(2)}) %collective-permute-start.3) | collective-permute-done | bytes 98336 | tf_op jit(solution)/shard_map/ppermute | solution.py:499
  9.5 4.5 %collective-permute-start.7 = (bf16[4,192,128]{2,1,0:T(8,128)(2,1)S(1)}, bf16[4,192,128]{2,1,0:T(8,128)(2,1)S(1)}, u32[]{:S(2)}, u32[]{:S(2)}) collective-permute-start(bf16[4,192,128]{2,1,0:T(8,128)(2,1)S(1)} %pad_maximum_fusion), channel_id=1, source_target_pairs={{0,4},{4,0},{8,12},{12,8},{1,5},{5,1},{9,13},{13,9},{2,6},{6,2},{1... | collective-permute-start | bytes 589832 | tf_op jit(solution)/shard_map/ppermute | solution.py:499
  14.0 1.4 %shard_map.136 = (f32[8,128]{1,0:T(8,128)S(1)}, bf16[256,256]{1,0:T(8,128)(2,1)S(1)}, bf16[512,256]{1,0:T(8,128)(2,1)S(1)}, f32[64,64]{1,0:T(8,128)S(1)}) custom-call(f32[1,64]{1,0:T(1,128)} %bitcast.24, f32[1,64]{1,0:T(1,128)} %bitcast.25, bf16[32,64]{1,0:T(8,128)(2,1)} %bitcast.21, bf16[32,64]{1,0:T(8,128)(2,1)} %bitcast.22, bf16[1024,128]{1,0:T(8,128)(2,1)} %refs_4_), custom_call_target="tpu_custom_call" | custom-call | tf_op jit(solution)/shard_map/pallas_call | solution.py:509
  15.4 0.8 %shard_map.137 = (bf16[512,256]{1,0:T(8,128)(2,1)S(1)}, bf16[128,256]{1,0:T(8,128)(2,1)S(1)}, bf16[128,256]{1,0:T(8,128)(2,1)S(1)}, f32[32,8,128]{2,1,0:T(8,128)...) custom-call(s32[1]{0:T(128)} %bitcast.place_ref, ...), custom_call_target="tpu_custom_call" | custom-call | flops 1000000000 | bytes 3906250 | tf_op jit(solution)/shard_map/pallas_call | solution.py:549
  16.3 0.1 collective-permute-start.4
  16.3 0.0 collective-permute-done.5.rear_ref
  16.3 0.5 %collective-permute-start.6 = (bf16[2,192,128]{2,1,0:T(8,128)(2,1)S(1)}, bf16[2,192,128]{2,1,0:T(8,128)(2,1)S(1)}, u32[]{:S(2)}, u32[]{:S(2)}) collective-permute-start(bf16[2,192,128]{2,1,0:T(8,128)(2,1)S(1)} %collective-permute-done.5.rear_ref), channel_id=1, source_target_pairs={{0,4},{4,0},{8,12},{12,8},{1,5},{5,1},{9,13},{13,9},{2,6},{6,2},{1... | collective-permute-start | bytes 294920 | tf_op jit(solution)/shard_map/ppermute | solution.py:499
  16.8 0.0 collective-permute-done.7.core_ref
  16.8 1.4 %shard_map.138 = (bf16[512,256]{1,0:T(8,128)(2,1)S(1)}, bf16[128,256]{1,0:T(8,128)(2,1)S(1)}, bf16[128,256]{1,0:T(8,128)(2,1)S(1)}, f32[32,8,128]{2,1,0:T(8,128)...) custom-call(s32[1]{0:T(128)} %bitcast.place_ref, ...), custom_call_target="tpu_custom_call" | custom-call | flops 1000000 | bytes 3906 | tf_op jit(solution)/shard_map/pallas_call | solution.py:549
  18.2 0.0 collective-permute-done.4.front_ref
  18.2 0.0 collective-permute-done.6.rear_ref
  18.3 5.6 %shard_map.139 = (f32[32,8,64]{2,1,0:T(8,128)}, f32[1024,128]{1,0:T(8,128)}, f32[32,64]{1,0:T(8,128)}, f32[32,64]{1,0:T(8,128)}, f32[1,64]{1,0:T(1,128)}, /*index=5*/f32[1,64]{1,0:T(1,128)}, f32[1,128]{1,0:T(1,128)}) custom-call(s32[1]{0:T(128)} %bitcast.place_ref, bf16[2,192,128]{2,1,0:T(8,128)(2,1)S(1)} %collective-permute-done.4.front_ref, ...), custom_call_target="tpu_custom_call" | custom-call | tf_op jit(solution)/shard_map/pallas_call | solution.py:567
  (3 shorter events, 0.0 us)
Async XLA Ops:
  1.7 4.3 %collective-permute-start = (bf16[192,128]{1,0:T(8,128)(2,1)S(1)}, bf16[192,128]{1,0:T(8,128)(2,1)S(1)}, u32[]{:S(2)}, u32[]{:S(2)}) collective-permute-start(bf16[192,128]{1,0:T(8,128)(2,1)S(1)} %shard_map.135), channel_id=1, source_target_pairs={{0,2},{1,3},{2,0},{3,1},{4,6},{5,7},{6,4},{7,5},{8,10},{9,11},{10,... | collective-permute-start | bytes 147464 | tf_op jit(solution)/shard_map/ppermute | solution.py:499
  1.8 5.3 %collective-permute-start.2 = (bf16[192,128]{1,0:T(8,128)(2,1)S(1)}, bf16[192,128]{1,0:T(8,128)(2,1)S(1)}, u32[]{:S(2)}, u32[]{:S(2)}) collective-permute-start(bf16[192,128]{1,0:T(8,128)(2,1)S(1)} %shard_map.135), channel_id=1, source_target_pairs={{0,3},{1,2},{2,1},{3,0},{4,7},{5,6},{6,5},{7,4},{8,11},{9,10},{10,... | collective-permute-start | bytes 147464 | tf_op jit(solution)/shard_map/ppermute | solution.py:499
  4.0 3.7 %collective-permute-start.1 = (bf16[192,128]{1,0:T(8,128)(2,1)S(1)}, bf16[192,128]{1,0:T(8,128)(2,1)S(1)}, u32[]{:S(2)}, u32[]{:S(2)}) collective-permute-start(bf16[192,128]{1,0:T(8,128)(2,1)S(1)} %shard_map.135), channel_id=1, source_target_pairs={{0,1},{1,0},{2,3},{3,2},{4,5},{5,4},{6,7},{7,6},{8,9},{9,8},{10,11... | collective-permute-start | bytes 147464 | tf_op jit(solution)/shard_map/ppermute | solution.py:499
  6.0 3.5 %collective-permute-start.3 = (bf16[2,192,128]{2,1,0:T(8,128)(2,1)S(1)}, bf16[2,192,128]{2,1,0:T(8,128)(2,1)S(1)}, u32[]{:S(2)}, u32[]{:S(2)}) collective-permute-start(bf16[2,192,128]{2,1,0:T(8,128)(2,1)S(1)} %pad_maximum_fusion.1.front_ref), channel_id=1, source_target_pairs={{0,8},{4,12},{8,0},{12,4},{1,9},{5,13},{9,1},{13,5},{2,10},{6,14},... | collective-permute-start | bytes 294920 | tf_op jit(solution)/shard_map/ppermute | solution.py:499
  7.7 8.6 %collective-permute-start.5 = (bf16[2,192,128]{2,1,0:T(8,128)(2,1)S(1)}, bf16[2,192,128]{2,1,0:T(8,128)(2,1)S(1)}, u32[]{:S(2)}, u32[]{:S(2)}) collective-permute-start(bf16[2,192,128]{2,1,0:T(8,128)(2,1)S(1)} %pad_maximum_fusion.2.rear_ref), channel_id=1, source_target_pairs={{0,8},{4,12},{8,0},{12,4},{1,9},{5,13},{9,1},{13,5},{2,10},{6,14},... | collective-permute-start | bytes 294920 | tf_op jit(solution)/shard_map/ppermute | solution.py:499
  9.5 7.3 %collective-permute-start.7 = (bf16[4,192,128]{2,1,0:T(8,128)(2,1)S(1)}, bf16[4,192,128]{2,1,0:T(8,128)(2,1)S(1)}, u32[]{:S(2)}, u32[]{:S(2)}) collective-permute-start(bf16[4,192,128]{2,1,0:T(8,128)(2,1)S(1)} %pad_maximum_fusion), channel_id=1, source_target_pairs={{0,4},{4,0},{8,12},{12,8},{1,5},{5,1},{9,13},{13,9},{2,6},{6,2},{1... | collective-permute-start | bytes 589832 | tf_op jit(solution)/shard_map/ppermute | solution.py:499
  16.3 2.0 %collective-permute-start.4 = (bf16[2,192,128]{2,1,0:T(8,128)(2,1)S(1)}, bf16[2,192,128]{2,1,0:T(8,128)(2,1)S(1)}, u32[]{:S(2)}, u32[]{:S(2)}) collective-permute-start(bf16[2,192,128]{2,1,0:T(8,128)(2,1)S(1)} %collective-permute-done.3.front_ref), channel_id=1, source_target_pairs={{0,4},{4,0},{8,12},{12,8},{1,5},{5,1},{9,13},{13,9},{2,6},{6,2},{1... | collective-permute-start | bytes 294920 | tf_op jit(solution)/shard_map/ppermute | solution.py:499
  16.3 1.9 %collective-permute-start.6 = (bf16[2,192,128]{2,1,0:T(8,128)(2,1)S(1)}, bf16[2,192,128]{2,1,0:T(8,128)(2,1)S(1)}, u32[]{:S(2)}, u32[]{:S(2)}) collective-permute-start(bf16[2,192,128]{2,1,0:T(8,128)(2,1)S(1)} %collective-permute-done.5.rear_ref), channel_id=1, source_target_pairs={{0,4},{4,0},{8,12},{12,8},{1,5},{5,1},{9,13},{13,9},{2,6},{6,2},{1... | collective-permute-start | bytes 294920 | tf_op jit(solution)/shard_map/ppermute | solution.py:499

commit v18 on v17

--- a/solution.py
+++ b/solution.py
@@ -537,7 +537,7 @@
     )
     norm, back, final_turned, first = weights
     own = jnp.concatenate([front, rear])
-    own, chip_front = lax.optimization_barrier((own, chip_front))
+    own, chip_front, norm = lax.optimization_barrier((own, chip_front, norm))
     core = over("row", n_row, 1, own)
     stage_outs = [
         held_bf(512, 256), held_bf(128, 256), held_bf(128, 256), held(width, 8, 128),

time: 24 us -> 23.7 us (0.987)
  the two profiles are of different devices: /device:TPU:31 before, /device:TPU:0 now
where the time goes in v18:
time: 23.7 us; the launch traced here: 23.4 us
  Pallas kernels  10.2 us (43%)
  starting transfers between devices  9.57 us (40%)
  waiting for transfers between devices  2.91 us (12%)
  between operations  0.71 us (3%)
    ppermute x8, starting transfers between devices, over(): return lax.ppermute(array, axis, [(k, k ^ step) for k in range(size)])  9.57 us
    pallas_call x1, Pallas kernels, gathered_body(): pl.pallas_call(functools.partial(part_kernel, n_row, n_col), out_shape=(s...  5.57 us
    ppermute x8, waiting for transfers between devices, over(): return lax.ppermute(array, axis, [(k, k ^ step) for k in range(size)])  2.91 us
    pallas_call x2, Pallas kernels, stages_of(): pl.pallas_call(functools.partial(kernel, n_col), out_shape=tuple(outs), i...  2.2 us
    pallas_call x1, Pallas kernels, gathered_body(): pl.pallas_call(weights_kernel, out_shape=(held(8, 128), held_bf(256, 256)...  1.4 us
    pallas_call x1, Pallas kernels, gathered_body(): pl.pallas_call(pack_kernel, out_shape=held_bf(192, 128), in_specs=vmem(3)...  1.04 us
  transfers between devices with their start and end apart: 8, of which 3 were waited for; matrix products, arithmetic and copies ran while one was open for 0% of the time, Pallas kernels for 15%

profile of v18, /device:TPU:0, one launch (start us, length us, event | category | flops | bytes accessed | tf_op | source)
XLA Modules:
  0.0 23.4 jit_solution(4364813012993065217)
XLA Ops:
  0.6 1.0 %shard_map.135 = bf16[192,128]{1,0:T(8,128)(2,1)S(1)} custom-call(bf16[32,8,64]{2,1,0:T(8,128)(2,1)} %msa_ref.1, s32[8,32]{1,0:T(8,128)} %bitcast.23, bf16[8,8,128]{2,1,0:T(8,128)(2,1)} %pair_ref.1), custom_call_target="tpu_custom_call" | custom-call | tf_op jit(solution)/shard_map/pallas_call | solution.py:492
  1.7 4.1 %collective-permute-start = (bf16[192,128]{1,0:T(8,128)(2,1)S(1)}, bf16[192,128]{1,0:T(8,128)(2,1)S(1)}, u32[]{:S(2)}, u32[]{:S(2)}) collective-permute-start(bf16[192,128]{1,0:T(8,128)(2,1)S(1)} %shard_map.135), channel_id=1, source_target_pairs={{0,2},{1,3},{2,0},{3,1},{4,6},{5,7},{6,4},{7,5},{8,10},{9,11},{10,... | collective-permute-start | bytes 147464 | tf_op jit(solution)/shard_map/ppermute | solution.py:499
  5.8 1.3 %collective-permute-start.2 = (bf16[192,128]{1,0:T(8,128)(2,1)S(1)}, bf16[192,128]{1,0:T(8,128)(2,1)S(1)}, u32[]{:S(2)}, u32[]{:S(2)}) collective-permute-start(bf16[192,128]{1,0:T(8,128)(2,1)S(1)} %shard_map.135), channel_id=1, source_target_pairs={{0,3},{1,2},{2,1},{3,0},{4,7},{5,6},{6,5},{7,4},{8,11},{9,10},{10,... | collective-permute-start | bytes 147464 | tf_op jit(solution)/shard_map/ppermute | solution.py:499
  7.1 0.2 collective-permute-start.1
  7.4 1.0 %collective-permute-done = bf16[192,128]{1,0:T(8,128)(2,1)S(1)} collective-permute-done((bf16[192,128]{1,0:T(8,128)(2,1)S(1)}, bf16[192,128]{1,0:T(8,128)(2,1)S(1)}, u32[]{:S(2)}, u32[]{:S(2)}) %collective-permute-start) | collective-permute-done | bytes 49184 | tf_op jit(solution)/shard_map/ppermute | solution.py:499
  8.4 1.8 %collective-permute-start.3 = (bf16[2,192,128]{2,1,0:T(8,128)(2,1)S(1)}, bf16[2,192,128]{2,1,0:T(8,128)(2,1)S(1)}, u32[]{:S(2)}, u32[]{:S(2)}) collective-permute-start(bf16[2,192,128]{2,1,0:T(8,128)(2,1)S(1)} %pad_maximum_fusion.1.front_ref), channel_id=1, source_target_pairs={{0,8},{4,12},{8,0},{12,4},{1,9},{5,13},{9,1},{13,5},{2,10},{6,14},... | collective-permute-start | bytes 294920 | tf_op jit(solution)/shard_map/ppermute | solution.py:499
  10.2 1.6 %collective-permute-done.2 = bf16[192,128]{1,0:T(8,128)(2,1)S(1)} collective-permute-done((bf16[192,128]{1,0:T(8,128)(2,1)S(1)}, bf16[192,128]{1,0:T(8,128)(2,1)S(1)}, u32[]{:S(2)}, u32[]{:S(2)}) %collective-permute-start.2) | collective-permute-done | bytes 49184 | tf_op jit(solution)/shard_map/ppermute | solution.py:499
  11.7 0.0 collective-permute-done.1
  11.8 1.6 %collective-permute-start.5 = (bf16[2,192,128]{2,1,0:T(8,128)(2,1)S(1)}, bf16[2,192,128]{2,1,0:T(8,128)(2,1)S(1)}, u32[]{:S(2)}, u32[]{:S(2)}) collective-permute-start(bf16[2,192,128]{2,1,0:T(8,128)(2,1)S(1)} %pad_maximum_fusion.2.rear_ref), channel_id=1, source_target_pairs={{0,8},{4,12},{8,0},{12,4},{1,9},{5,13},{9,1},{13,5},{2,10},{6,14},... | collective-permute-start | bytes 294920 | tf_op jit(solution)/shard_map/ppermute | solution.py:499
  13.3 1.4 %shard_map.136 = (f32[8,128]{1,0:T(8,128)S(1)}, bf16[256,256]{1,0:T(8,128)(2,1)S(1)}, bf16[512,256]{1,0:T(8,128)(2,1)S(1)}, f32[64,64]{1,0:T(8,128)S(1)}) custom-call(f32[1,64]{1,0:T(1,128)} %bitcast.24, f32[1,64]{1,0:T(1,128)} %bitcast.25, bf16[32,64]{1,0:T(8,128)(2,1)} %bitcast.21, bf16[32,64]{1,0:T(8,128)(2,1)} %bitcast.22, bf16[1024,128]{1,0:T(8,128)(2,1)} %refs_4_), custom_call_target="tpu_custom_call" | custom-call | tf_op jit(solution)/shard_map/pallas_call | solution.py:509
  14.8 0.0 collective-permute-done.3.front_ref
  14.8 0.1 collective-permute-start.7
  14.9 0.5 %collective-permute-start.4 = (bf16[2,192,128]{2,1,0:T(8,128)(2,1)S(1)}, bf16[2,192,128]{2,1,0:T(8,128)(2,1)S(1)}, u32[]{:S(2)}, u32[]{:S(2)}) collective-permute-start(bf16[2,192,128]{2,1,0:T(8,128)(2,1)S(1)} %collective-permute-done.3.front_ref), channel_id=1, source_target_pairs={{0,4},{4,0},{8,12},{12,8},{1,5},{5,1},{9,13},{13,9},{2,6},{6,2},{1... | collective-permute-start | bytes 294920 | tf_op jit(solution)/shard_map/ppermute | solution.py:499
  15.3 0.8 %shard_map.137 = (bf16[512,256]{1,0:T(8,128)(2,1)S(1)}, bf16[128,256]{1,0:T(8,128)(2,1)S(1)}, bf16[128,256]{1,0:T(8,128)(2,1)S(1)}, f32[32,8,128]{2,1,0:T(8,128)...) custom-call(s32[1]{0:T(128)} %bitcast.place_ref, ...), custom_call_target="tpu_custom_call" | custom-call | flops 1000000000 | bytes 3906250 | tf_op jit(solution)/shard_map/pallas_call | solution.py:549
  16.2 0.3 %collective-permute-done.5.rear_ref = bf16[2,192,128]{2,1,0:T(8,128)(2,1)S(1)} collective-permute-done((bf16[2,192,128]{2,1,0:T(8,128)(2,1)S(1)}, bf16[2,192,128]{2,1,0:T(8,128)(2,1)S(1)}, u32[]{:S(2)}, u32[]{:S(2)}) %collective-permute-start.5) | collective-permute-done | bytes 98336 | tf_op jit(solution)/shard_map/ppermute | solution.py:499
  16.4 0.0 collective-permute-start.6
  16.4 0.0 collective-permute-done.7.core_ref
  16.5 1.4 %shard_map.138 = (bf16[512,256]{1,0:T(8,128)(2,1)S(1)}, bf16[128,256]{1,0:T(8,128)(2,1)S(1)}, bf16[128,256]{1,0:T(8,128)(2,1)S(1)}, f32[32,8,128]{2,1,0:T(8,128)...) custom-call(s32[1]{0:T(128)} %bitcast.place_ref, ...), custom_call_target="tpu_custom_call" | custom-call | flops 1000000 | bytes 3906 | tf_op jit(solution)/shard_map/pallas_call | solution.py:549
  17.9 0.0 collective-permute-done.4.front_ref
  17.9 0.0 collective-permute-done.6.rear_ref
  17.9 5.6 %shard_map.139 = (f32[32,8,64]{2,1,0:T(8,128)}, f32[1024,128]{1,0:T(8,128)}, f32[32,64]{1,0:T(8,128)}, f32[32,64]{1,0:T(8,128)}, f32[1,64]{1,0:T(1,128)}, /*index=5*/f32[1,64]{1,0:T(1,128)}, f32[1,128]{1,0:T(1,128)}) custom-call(s32[1]{0:T(128)} %bitcast.place_ref, bf16[2,192,128]{2,1,0:T(8,128)(2,1)S(1)} %collective-permute-done.4.front_ref, ...), custom_call_target="tpu_custom_call" | custom-call | tf_op jit(solution)/shard_map/pallas_call | solution.py:567
  (3 shorter events, 0.0 us)
Async XLA Ops:
  1.7 6.7 %collective-permute-start = (bf16[192,128]{1,0:T(8,128)(2,1)S(1)}, bf16[192,128]{1,0:T(8,128)(2,1)S(1)}, u32[]{:S(2)}, u32[]{:S(2)}) collective-permute-start(bf16[192,128]{1,0:T(8,128)(2,1)S(1)} %shard_map.135), channel_id=1, source_target_pairs={{0,2},{1,3},{2,0},{3,1},{4,6},{5,7},{6,4},{7,5},{8,10},{9,11},{10,... | collective-permute-start | bytes 147464 | tf_op jit(solution)/shard_map/ppermute | solution.py:499
  5.8 6.0 %collective-permute-start.2 = (bf16[192,128]{1,0:T(8,128)(2,1)S(1)}, bf16[192,128]{1,0:T(8,128)(2,1)S(1)}, u32[]{:S(2)}, u32[]{:S(2)}) collective-permute-start(bf16[192,128]{1,0:T(8,128)(2,1)S(1)} %shard_map.135), channel_id=1, source_target_pairs={{0,3},{1,2},{2,1},{3,0},{4,7},{5,6},{6,5},{7,4},{8,11},{9,10},{10,... | collective-permute-start | bytes 147464 | tf_op jit(solution)/shard_map/ppermute | solution.py:499
  7.1 4.6 %collective-permute-start.1 = (bf16[192,128]{1,0:T(8,128)(2,1)S(1)}, bf16[192,128]{1,0:T(8,128)(2,1)S(1)}, u32[]{:S(2)}, u32[]{:S(2)}) collective-permute-start(bf16[192,128]{1,0:T(8,128)(2,1)S(1)} %shard_map.135), channel_id=1, source_target_pairs={{0,1},{1,0},{2,3},{3,2},{4,5},{5,4},{6,7},{7,6},{8,9},{9,8},{10,11... | collective-permute-start | bytes 147464 | tf_op jit(solution)/shard_map/ppermute | solution.py:499
  8.4 6.4 %collective-permute-start.3 = (bf16[2,192,128]{2,1,0:T(8,128)(2,1)S(1)}, bf16[2,192,128]{2,1,0:T(8,128)(2,1)S(1)}, u32[]{:S(2)}, u32[]{:S(2)}) collective-permute-start(bf16[2,192,128]{2,1,0:T(8,128)(2,1)S(1)} %pad_maximum_fusion.1.front_ref), channel_id=1, source_target_pairs={{0,8},{4,12},{8,0},{12,4},{1,9},{5,13},{9,1},{13,5},{2,10},{6,14},... | collective-permute-start | bytes 294920 | tf_op jit(solution)/shard_map/ppermute | solution.py:499
  11.8 4.7 %collective-permute-start.5 = (bf16[2,192,128]{2,1,0:T(8,128)(2,1)S(1)}, bf16[2,192,128]{2,1,0:T(8,128)(2,1)S(1)}, u32[]{:S(2)}, u32[]{:S(2)}) collective-permute-start(bf16[2,192,128]{2,1,0:T(8,128)(2,1)S(1)} %pad_maximum_fusion.2.rear_ref), channel_id=1, source_target_pairs={{0,8},{4,12},{8,0},{12,4},{1,9},{5,13},{9,1},{13,5},{2,10},{6,14},... | collective-permute-start | bytes 294920 | tf_op jit(solution)/shard_map/ppermute | solution.py:499
  14.8 1.7 %collective-permute-start.7 = (bf16[4,192,128]{2,1,0:T(8,128)(2,1)S(1)}, bf16[4,192,128]{2,1,0:T(8,128)(2,1)S(1)}, u32[]{:S(2)}, u32[]{:S(2)}) collective-permute-start(bf16[4,192,128]{2,1,0:T(8,128)(2,1)S(1)} %pad_maximum_fusion), channel_id=1, source_target_pairs={{0,4},{4,0},{8,12},{12,8},{1,5},{5,1},{9,13},{13,9},{2,6},{6,2},{1... | collective-permute-start | bytes 589832 | tf_op jit(solution)/shard_map/ppermute | solution.py:499
  14.9 3.0 %collective-permute-start.4 = (bf16[2,192,128]{2,1,0:T(8,128)(2,1)S(1)}, bf16[2,192,128]{2,1,0:T(8,128)(2,1)S(1)}, u32[]{:S(2)}, u32[]{:S(2)}) collective-permute-start(bf16[2,192,128]{2,1,0:T(8,128)(2,1)S(1)} %collective-permute-done.3.front_ref), channel_id=1, source_target_pairs={{0,4},{4,0},{8,12},{12,8},{1,5},{5,1},{9,13},{13,9},{2,6},{6,2},{1... | collective-permute-start | bytes 294920 | tf_op jit(solution)/shard_map/ppermute | solution.py:499
  16.4 1.4 %collective-permute-start.6 = (bf16[2,192,128]{2,1,0:T(8,128)(2,1)S(1)}, bf16[2,192,128]{2,1,0:T(8,128)(2,1)S(1)}, u32[]{:S(2)}, u32[]{:S(2)}) collective-permute-start(bf16[2,192,128]{2,1,0:T(8,128)(2,1)S(1)} %collective-permute-done.5.rear_ref), channel_id=1, source_target_pairs={{0,4},{4,0},{8,12},{12,8},{1,5},{5,1},{9,13},{13,9},{2,6},{6,2},{1... | collective-permute-start | bytes 294920 | tf_op jit(solution)/shard_map/ppermute | solution.py:499

commit v19 on v18

--- a/solution.py
+++ b/solution.py
@@ -188,10 +188,10 @@
 
 
 def interleave(first, second):
-    odd = lax.broadcasted_iota(jnp.int16, (32, 128), 1) & 32 != 0
+    odd = lax.broadcasted_iota(jnp.int32, (32, 128), 1) & 32 != 0
     return (
-        jnp.where(odd, pltpu.roll(second, 32, 1), first),
-        jnp.where(odd, second, pltpu.roll(first, 96, 1)),
+        jnp.where(odd, pltpu.roll(second, 32, 1), first).astype(BF),
+        jnp.where(odd, second, pltpu.roll(first, 96, 1)).astype(BF),
     )
 
 
@@ -310,7 +310,7 @@
         pairs = jnp.concatenate(
             [diagonal_pair(pair[64 * p : 64 * p + 64]) for p in (2 * n, 2 * n + 1)], axis=0
         )
-        grad = mm_nt(final_ref[...], pairs).astype(BF)
+        grad = mm_nt(final_ref[...], pairs)
         for p in range(2):
             for q in range(8):
                 rows = 64 * (2 * n + p)
@@ -405,7 +405,7 @@
         rights = jnp.concatenate(
             [diagonal_pair(right_scr[64 * p : 64 * p + 64, :]) for p in (2 * n, 2 * n + 1)], axis=0
         )
-        outer = mm_nt(left_t, rights).astype(BF)
+        outer = mm_nt(left_t, rights)
         for p in range(2):
             for q in range(8):
                 rows = 64 * (2 * n + p)

time: 23.7 us -> 23.8 us (level)
  transfers between devices with their start and end apart: 8 -> 8, of which waited for: 3 -> 3; matrix products, arithmetic and copies ran while one was open for 0% -> 0% of each run, Pallas kernels for 15% -> 16%
where the time goes in v19:
time: 23.8 us; the launch traced here: 23.5 us
  Pallas kernels  10.3 us (43%)
  starting transfers between devices  9.57 us (40%)
  waiting for transfers between devices  2.9 us (12%)
  between operations  0.72 us (3%)
    ppermute x8, starting transfers between devices, over(): return lax.ppermute(array, axis, [(k, k ^ step) for k in range(size)])  9.57 us
    pallas_call x1, Pallas kernels, gathered_body(): pl.pallas_call(functools.partial(part_kernel, n_row, n_col), out_shape=(s...  5.6 us
    ppermute x8, waiting for transfers between devices, over(): return lax.ppermute(array, axis, [(k, k ^ step) for k in range(size)])  2.9 us
    pallas_call x2, Pallas kernels, stages_of(): pl.pallas_call(functools.partial(kernel, n_col), out_shape=tuple(outs), i...  2.26 us
    pallas_call x1, Pallas kernels, gathered_body(): pl.pallas_call(weights_kernel, out_shape=(held(8, 128), held_bf(256, 256)...  1.4 us
    pallas_call x1, Pallas kernels, gathered_body(): pl.pallas_call(pack_kernel, out_shape=held_bf(192, 128), in_specs=vmem(3)...  1.04 us
  transfers between devices with their start and end apart: 8, of which 3 were waited for; matrix products, arithmetic and copies ran while one was open for 0% of the time, Pallas kernels for 16%

profile of v19, /device:TPU:0, one launch (start us, length us, event | category | flops | bytes accessed | tf_op | source)
XLA Modules:
  0.0 23.5 jit_solution(11859572437244752877)
XLA Ops:
  0.6 1.0 %shard_map.135 = bf16[192,128]{1,0:T(8,128)(2,1)S(1)} custom-call(bf16[32,8,64]{2,1,0:T(8,128)(2,1)} %msa_ref.1, s32[8,32]{1,0:T(8,128)} %bitcast.23, bf16[8,8,128]{2,1,0:T(8,128)(2,1)} %pair_ref.1), custom_call_target="tpu_custom_call" | custom-call | tf_op jit(solution)/shard_map/pallas_call | solution.py:492
  1.7 4.1 %collective-permute-start = (bf16[192,128]{1,0:T(8,128)(2,1)S(1)}, bf16[192,128]{1,0:T(8,128)(2,1)S(1)}, u32[]{:S(2)}, u32[]{:S(2)}) collective-permute-start(bf16[192,128]{1,0:T(8,128)(2,1)S(1)} %shard_map.135), channel_id=1, source_target_pairs={{0,2},{1,3},{2,0},{3,1},{4,6},{5,7},{6,4},{7,5},{8,10},{9,11},{10,... | collective-permute-start | bytes 147464 | tf_op jit(solution)/shard_map/ppermute | solution.py:499
  5.8 1.3 %collective-permute-start.2 = (bf16[192,128]{1,0:T(8,128)(2,1)S(1)}, bf16[192,128]{1,0:T(8,128)(2,1)S(1)}, u32[]{:S(2)}, u32[]{:S(2)}) collective-permute-start(bf16[192,128]{1,0:T(8,128)(2,1)S(1)} %shard_map.135), channel_id=1, source_target_pairs={{0,3},{1,2},{2,1},{3,0},{4,7},{5,6},{6,5},{7,4},{8,11},{9,10},{10,... | collective-permute-start | bytes 147464 | tf_op jit(solution)/shard_map/ppermute | solution.py:499
  7.1 0.2 collective-permute-start.1
  7.4 1.0 %collective-permute-done = bf16[192,128]{1,0:T(8,128)(2,1)S(1)} collective-permute-done((bf16[192,128]{1,0:T(8,128)(2,1)S(1)}, bf16[192,128]{1,0:T(8,128)(2,1)S(1)}, u32[]{:S(2)}, u32[]{:S(2)}) %collective-permute-start) | collective-permute-done | bytes 49184 | tf_op jit(solution)/shard_map/ppermute | solution.py:499
  8.4 1.8 %collective-permute-start.3 = (bf16[2,192,128]{2,1,0:T(8,128)(2,1)S(1)}, bf16[2,192,128]{2,1,0:T(8,128)(2,1)S(1)}, u32[]{:S(2)}, u32[]{:S(2)}) collective-permute-start(bf16[2,192,128]{2,1,0:T(8,128)(2,1)S(1)} %pad_maximum_fusion.1.front_ref), channel_id=1, source_target_pairs={{0,8},{4,12},{8,0},{12,4},{1,9},{5,13},{9,1},{13,5},{2,10},{6,14},... | collective-permute-start | bytes 294920 | tf_op jit(solution)/shard_map/ppermute | solution.py:499
  10.2 1.6 %collective-permute-done.2 = bf16[192,128]{1,0:T(8,128)(2,1)S(1)} collective-permute-done((bf16[192,128]{1,0:T(8,128)(2,1)S(1)}, bf16[192,128]{1,0:T(8,128)(2,1)S(1)}, u32[]{:S(2)}, u32[]{:S(2)}) %collective-permute-start.2) | collective-permute-done | bytes 49184 | tf_op jit(solution)/shard_map/ppermute | solution.py:499
  11.7 0.0 collective-permute-done.1
  11.8 1.6 %collective-permute-start.5 = (bf16[2,192,128]{2,1,0:T(8,128)(2,1)S(1)}, bf16[2,192,128]{2,1,0:T(8,128)(2,1)S(1)}, u32[]{:S(2)}, u32[]{:S(2)}) collective-permute-start(bf16[2,192,128]{2,1,0:T(8,128)(2,1)S(1)} %pad_maximum_fusion.2.rear_ref), channel_id=1, source_target_pairs={{0,8},{4,12},{8,0},{12,4},{1,9},{5,13},{9,1},{13,5},{2,10},{6,14},... | collective-permute-start | bytes 294920 | tf_op jit(solution)/shard_map/ppermute | solution.py:499
  13.3 1.4 %shard_map.136 = (f32[8,128]{1,0:T(8,128)S(1)}, bf16[256,256]{1,0:T(8,128)(2,1)S(1)}, bf16[512,256]{1,0:T(8,128)(2,1)S(1)}, f32[64,64]{1,0:T(8,128)S(1)}) custom-call(f32[1,64]{1,0:T(1,128)} %bitcast.24, f32[1,64]{1,0:T(1,128)} %bitcast.25, bf16[32,64]{1,0:T(8,128)(2,1)} %bitcast.21, bf16[32,64]{1,0:T(8,128)(2,1)} %bitcast.22, bf16[1024,128]{1,0:T(8,128)(2,1)} %refs_4_), custom_call_target="tpu_custom_call" | custom-call | tf_op jit(solution)/shard_map/pallas_call | solution.py:509
  14.8 0.0 collective-permute-done.3.front_ref
  14.8 0.1 collective-permute-start.7
  14.9 0.5 %collective-permute-start.4 = (bf16[2,192,128]{2,1,0:T(8,128)(2,1)S(1)}, bf16[2,192,128]{2,1,0:T(8,128)(2,1)S(1)}, u32[]{:S(2)}, u32[]{:S(2)}) collective-permute-start(bf16[2,192,128]{2,1,0:T(8,128)(2,1)S(1)} %collective-permute-done.3.front_ref), channel_id=1, source_target_pairs={{0,4},{4,0},{8,12},{12,8},{1,5},{5,1},{9,13},{13,9},{2,6},{6,2},{1... | collective-permute-start | bytes 294920 | tf_op jit(solution)/shard_map/ppermute | solution.py:499
  15.3 0.8 %shard_map.137 = (bf16[512,256]{1,0:T(8,128)(2,1)S(1)}, bf16[128,256]{1,0:T(8,128)(2,1)S(1)}, bf16[128,256]{1,0:T(8,128)(2,1)S(1)}, f32[32,8,128]{2,1,0:T(8,128)...) custom-call(s32[1]{0:T(128)} %bitcast.place_ref, ...), custom_call_target="tpu_custom_call" | custom-call | flops 1000000000 | bytes 3906250 | tf_op jit(solution)/shard_map/pallas_call | solution.py:549
  16.2 0.3 %collective-permute-done.5.rear_ref = bf16[2,192,128]{2,1,0:T(8,128)(2,1)S(1)} collective-permute-done((bf16[2,192,128]{2,1,0:T(8,128)(2,1)S(1)}, bf16[2,192,128]{2,1,0:T(8,128)(2,1)S(1)}, u32[]{:S(2)}, u32[]{:S(2)}) %collective-permute-start.5) | collective-permute-done | bytes 98336 | tf_op jit(solution)/shard_map/ppermute | solution.py:499
  16.4 0.0 collective-permute-start.6
  16.4 0.0 collective-permute-done.7.core_ref
  16.5 1.4 %shard_map.138 = (bf16[512,256]{1,0:T(8,128)(2,1)S(1)}, bf16[128,256]{1,0:T(8,128)(2,1)S(1)}, bf16[128,256]{1,0:T(8,128)(2,1)S(1)}, f32[32,8,128]{2,1,0:T(8,128)...) custom-call(s32[1]{0:T(128)} %bitcast.place_ref, ...), custom_call_target="tpu_custom_call" | custom-call | flops 1000000 | bytes 3906 | tf_op jit(solution)/shard_map/pallas_call | solution.py:549
  17.9 0.0 collective-permute-done.4.front_ref
  17.9 0.0 collective-permute-done.6.rear_ref
  17.9 5.6 %shard_map.139 = (f32[32,8,64]{2,1,0:T(8,128)}, f32[1024,128]{1,0:T(8,128)}, f32[32,64]{1,0:T(8,128)}, f32[32,64]{1,0:T(8,128)}, f32[1,64]{1,0:T(1,128)}, /*index=5*/f32[1,64]{1,0:T(1,128)}, f32[1,128]{1,0:T(1,128)}) custom-call(s32[1]{0:T(128)} %bitcast.place_ref, bf16[2,192,128]{2,1,0:T(8,128)(2,1)S(1)} %collective-permute-done.4.front_ref, ...), custom_call_target="tpu_custom_call" | custom-call | tf_op jit(solution)/shard_map/pallas_call | solution.py:567
  (3 shorter events, 0.0 us)
Async XLA Ops:
  1.7 6.7 %collective-permute-start = (bf16[192,128]{1,0:T(8,128)(2,1)S(1)}, bf16[192,128]{1,0:T(8,128)(2,1)S(1)}, u32[]{:S(2)}, u32[]{:S(2)}) collective-permute-start(bf16[192,128]{1,0:T(8,128)(2,1)S(1)} %shard_map.135), channel_id=1, source_target_pairs={{0,2},{1,3},{2,0},{3,1},{4,6},{5,7},{6,4},{7,5},{8,10},{9,11},{10,... | collective-permute-start | bytes 147464 | tf_op jit(solution)/shard_map/ppermute | solution.py:499
  5.8 6.0 %collective-permute-start.2 = (bf16[192,128]{1,0:T(8,128)(2,1)S(1)}, bf16[192,128]{1,0:T(8,128)(2,1)S(1)}, u32[]{:S(2)}, u32[]{:S(2)}) collective-permute-start(bf16[192,128]{1,0:T(8,128)(2,1)S(1)} %shard_map.135), channel_id=1, source_target_pairs={{0,3},{1,2},{2,1},{3,0},{4,7},{5,6},{6,5},{7,4},{8,11},{9,10},{10,... | collective-permute-start | bytes 147464 | tf_op jit(solution)/shard_map/ppermute | solution.py:499
  7.1 4.6 %collective-permute-start.1 = (bf16[192,128]{1,0:T(8,128)(2,1)S(1)}, bf16[192,128]{1,0:T(8,128)(2,1)S(1)}, u32[]{:S(2)}, u32[]{:S(2)}) collective-permute-start(bf16[192,128]{1,0:T(8,128)(2,1)S(1)} %shard_map.135), channel_id=1, source_target_pairs={{0,1},{1,0},{2,3},{3,2},{4,5},{5,4},{6,7},{7,6},{8,9},{9,8},{10,11... | collective-permute-start | bytes 147464 | tf_op jit(solution)/shard_map/ppermute | solution.py:499
  8.4 6.4 %collective-permute-start.3 = (bf16[2,192,128]{2,1,0:T(8,128)(2,1)S(1)}, bf16[2,192,128]{2,1,0:T(8,128)(2,1)S(1)}, u32[]{:S(2)}, u32[]{:S(2)}) collective-permute-start(bf16[2,192,128]{2,1,0:T(8,128)(2,1)S(1)} %pad_maximum_fusion.1.front_ref), channel_id=1, source_target_pairs={{0,8},{4,12},{8,0},{12,4},{1,9},{5,13},{9,1},{13,5},{2,10},{6,14},... | collective-permute-start | bytes 294920 | tf_op jit(solution)/shard_map/ppermute | solution.py:499
  11.8 4.7 %collective-permute-start.5 = (bf16[2,192,128]{2,1,0:T(8,128)(2,1)S(1)}, bf16[2,192,128]{2,1,0:T(8,128)(2,1)S(1)}, u32[]{:S(2)}, u32[]{:S(2)}) collective-permute-start(bf16[2,192,128]{2,1,0:T(8,128)(2,1)S(1)} %pad_maximum_fusion.2.rear_ref), channel_id=1, source_target_pairs={{0,8},{4,12},{8,0},{12,4},{1,9},{5,13},{9,1},{13,5},{2,10},{6,14},... | collective-permute-start | bytes 294920 | tf_op jit(solution)/shard_map/ppermute | solution.py:499
  14.8 1.7 %collective-permute-start.7 = (bf16[4,192,128]{2,1,0:T(8,128)(2,1)S(1)}, bf16[4,192,128]{2,1,0:T(8,128)(2,1)S(1)}, u32[]{:S(2)}, u32[]{:S(2)}) collective-permute-start(bf16[4,192,128]{2,1,0:T(8,128)(2,1)S(1)} %pad_maximum_fusion), channel_id=1, source_target_pairs={{0,4},{4,0},{8,12},{12,8},{1,5},{5,1},{9,13},{13,9},{2,6},{6,2},{1... | collective-permute-start | bytes 589832 | tf_op jit(solution)/shard_map/ppermute | solution.py:499
  14.9 3.1 %collective-permute-start.4 = (bf16[2,192,128]{2,1,0:T(8,128)(2,1)S(1)}, bf16[2,192,128]{2,1,0:T(8,128)(2,1)S(1)}, u32[]{:S(2)}, u32[]{:S(2)}) collective-permute-start(bf16[2,192,128]{2,1,0:T(8,128)(2,1)S(1)} %collective-permute-done.3.front_ref), channel_id=1, source_target_pairs={{0,4},{4,0},{8,12},{12,8},{1,5},{5,1},{9,13},{13,9},{2,6},{6,2},{1... | collective-permute-start | bytes 294920 | tf_op jit(solution)/shard_map/ppermute | solution.py:499
  16.4 1.5 %collective-permute-start.6 = (bf16[2,192,128]{2,1,0:T(8,128)(2,1)S(1)}, bf16[2,192,128]{2,1,0:T(8,128)(2,1)S(1)}, u32[]{:S(2)}, u32[]{:S(2)}) collective-permute-start(bf16[2,192,128]{2,1,0:T(8,128)(2,1)S(1)} %collective-permute-done.5.rear_ref), channel_id=1, source_target_pairs={{0,4},{4,0},{8,12},{12,8},{1,5},{5,1},{9,13},{13,9},{2,6},{6,2},{1... | collective-permute-start | bytes 294920 | tf_op jit(solution)/shard_map/ppermute | solution.py:499

commit v20 on v18

--- a/solution.py
+++ b/solution.py
@@ -205,12 +205,14 @@
 ABSENT = 1024.0
 
 
-def pack_kernel(msa_ref, mask_ref, pair_ref, out_ref):
-    msa = msa_ref[...].astype(F32)
+def pack_kernel(msa_ref, mask_ref, pair_ref, out_ref, scr):
+    scr[...] = msa_ref[...].astype(F32).reshape(256, 64)
     pick = spread(8, 512, lambda r, c: jnp.where(c // 64 == r, 1.0, 0.0)).astype(BF)
     present = mm_tn(mask_ref[...].astype(F32).astype(BF), pick) > 0.5
     for g in range(4):
-        rows = jnp.concatenate([msa[:, 2 * g, :], msa[:, 2 * g + 1, :]], axis=1)
+        rows = jnp.concatenate(
+            [scr[pl.ds(t, 32, stride=8), :] for t in (2 * g, 2 * g + 1)], axis=1
+        )
         out_ref[32 * g : 32 * g + 32, :] = jnp.where(
             present[:, 128 * g : 128 * g + 128], rows, ABSENT
         ).astype(BF)
@@ -387,38 +389,6 @@
             [part[8 * t : 8 * t + 8] for part in right_in], axis=0
         ).astype(BF)
 
-    bias = jnp.zeros((1, 128), F32)
-    ones = jnp.ones((128, 128), BF)
-    for p in range(8):
-        both_on = jnp.concatenate(
-            [mask_t[0:32] * mask_t[i : i + 1] for i in range(4 * p, 4 * p + 4)], axis=0
-        ).astype(BF)
-        counts = mm(both_on, ones)
-        pair = stages[p // 2][5][4 * (p % 2) : 4 * (p % 2) + 4]
-        scaled = pair.reshape(128, 128) / (counts + 0.001)
-        bias = bias + jnp.sum(scaled, axis=0, keepdims=True)
-        scaled_scr[128 * p : 128 * p + 128, :] = scaled.astype(BF)
-    bias_out[...] = bias
-
-    left_t = jnp.concatenate([stage[2][...] for stage in stages], axis=0)
-    for n in range(8):
-        rights = jnp.concatenate(
-            [diagonal_pair(right_scr[64 * p : 64 * p + 64, :]) for p in (2 * n, 2 * n + 1)], axis=0
-        )
-        outer = mm_nt(left_t, rights).astype(BF)
-        for p in range(2):
-            for q in range(8):
-                rows = 64 * (2 * n + p)
-                block = outer[64 * q : 64 * q + 64, 128 * p : 128 * p + 128]
-                even, odd = interleave(block[:32], block[32:])
-                outer_scr[rows : rows + 32, 128 * q : 128 * q + 128] = even
-                outer_scr[rows + 32 : rows + 64, 128 * q : 128 * q + 128] = odd
-    wide_scr[...] = mm(outer_scr[...], scaled_scr[...])
-    for c in range(32):
-        final_out[32 * c : 32 * c + 32, :] = wide_scr[pl.ds(c, 32, stride=32), :]
-    final_send = pltpu.make_async_copy(final_out, final_hbm_out, out_sem)
-    final_send.start()
-
     total = mm(
         all_scr[...], jnp.concatenate([stage[0][...] for stage in stages], axis=0)
     )
@@ -458,7 +428,44 @@
     for g in range(4):
         emb_out[:, 2 * g, :] = result[32 * g : 32 * g + 32, 0:64]
         emb_out[:, 2 * g + 1, :] = result[32 * g : 32 * g + 32, 64:128]
-    final_send.wait()
+    bias = jnp.zeros((1, 128), F32)
+    ones = jnp.ones((128, 128), BF)
+    for p in range(8):
+        both_on = jnp.concatenate(
+            [mask_t[0:32] * mask_t[i : i + 1] for i in range(4 * p, 4 * p + 4)], axis=0
+        ).astype(BF)
+        counts = mm(both_on, ones)
+        pair = stages[p // 2][5][4 * (p % 2) : 4 * (p % 2) + 4]
+        scaled = pair.reshape(128, 128) / (counts + 0.001)
+        bias = bias + jnp.sum(scaled, axis=0, keepdims=True)
+        scaled_scr[128 * p : 128 * p + 128, :] = scaled.astype(BF)
+    bias_out[...] = bias
+
+    left_t = jnp.concatenate([stage[2][...] for stage in stages], axis=0)
+    for n in range(8):
+        rights = jnp.concatenate(
+            [diagonal_pair(right_scr[64 * p : 64 * p + 64, :]) for p in (2 * n, 2 * n + 1)], axis=0
+        )
+        outer = mm_nt(left_t, rights).astype(BF)
+        for p in range(2):
+            for q in range(8):
+                rows = 64 * (2 * n + p)
+                block = outer[64 * q : 64 * q + 64, 128 * p : 128 * p + 128]
+                even, odd = interleave(block[:32], block[32:])
+                outer_scr[rows : rows + 32, 128 * q : 128 * q + 128] = even
+                outer_scr[rows + 32 : rows + 64, 128 * q : 128 * q + 128] = odd
+    wide_scr[...] = mm(outer_scr[...], scaled_scr[...])
+    sends = []
+    for h in range(4):
+        for c in range(8 * h, 8 * h + 8):
+            final_out[32 * c : 32 * c + 32, :] = wide_scr[pl.ds(c, 32, stride=32), :]
+        at = pl.ds(256 * h, 256)
+        sends.append(
+            pltpu.make_async_copy(final_out.at[at], final_hbm_out.at[at], out_sem.at[h])
+        )
+        sends[-1].start()
+    for send in sends:
+        send.wait()
 
 
 def vmem(count):
@@ -494,6 +501,7 @@
         out_shape=held_bf(192, 128),
         in_specs=vmem(3),
         out_specs=vmem(1)[0],
+        scratch_shapes=[pltpu.VMEM((256, 64), F32)],
     )(homolog_embedding, presence_indicator.T, coupling_change_derivative)
     def over(axis, size, step, array):
         return lax.ppermute(array, axis, [(k, k ^ step) for k in range(size)])
@@ -585,7 +593,7 @@
             pltpu.VMEM((1024, 128), F32),
             pltpu.VMEM((128, 2048), BF),
             pltpu.VMEM((1024, 128), F32),
-            pltpu.SemaphoreType.DMA,
+            pltpu.SemaphoreType.DMA((4,)),
             pltpu.VMEM((256, 128), F32),
             *stage_outs,
         ],

time: 23.7 us -> 24.4 us (1.030)
  Pallas kernels: 10.2 us -> 10.9 us
    pallas_call x1, Pallas kernels: 5.57 us -> 6.29 us  [gathered_body(): pl.pallas_call(functools.partial(part_kernel, n_row, n_col), out_shape=(s...]
where the time goes in v20:
time: 24.4 us; the launch traced here: 24.2 us
  Pallas kernels  10.9 us (45%)
  starting transfers between devices  9.57 us (39%)
  waiting for transfers between devices  2.91 us (12%)
  between operations  0.71 us (3%)
    ppermute x8, starting transfers between devices, over(): return lax.ppermute(array, axis, [(k, k ^ step) for k in range(size)])  9.57 us
    pallas_call x1, Pallas kernels, gathered_body(): pl.pallas_call(functools.partial(part_kernel, n_row, n_col), out_shape=(s...  6.29 us
    ppermute x8, waiting for transfers between devices, over(): return lax.ppermute(array, axis, [(k, k ^ step) for k in range(size)])  2.91 us
    pallas_call x2, Pallas kernels, stages_of(): pl.pallas_call(functools.partial(kernel, n_col), out_shape=tuple(outs), i...  2.2 us
    pallas_call x1, Pallas kernels, gathered_body(): pl.pallas_call(weights_kernel, out_shape=(held(8, 128), held_bf(256, 256)...  1.4 us
    pallas_call x1, Pallas kernels, gathered_body(): pl.pallas_call(pack_kernel, out_shape=held_bf(192, 128), in_specs=vmem(3)...  1.04 us
  transfers between devices with their start and end apart: 8, of which 3 were waited for; matrix products, arithmetic and copies ran while one was open for 0% of the time, Pallas kernels for 15%

profile of v20, /device:TPU:0, one launch (start us, length us, event | category | flops | bytes accessed | tf_op | source)
XLA Modules:
  0.0 24.2 jit_solution(16717561828896293434)
XLA Ops:
  0.6 1.0 %shard_map.135 = bf16[192,128]{1,0:T(8,128)(2,1)S(1)} custom-call(bf16[32,8,64]{2,1,0:T(8,128)(2,1)} %msa_ref.1, s32[8,32]{1,0:T(8,128)} %bitcast.23, bf16[8,8,128]{2,1,0:T(8,128)(2,1)} %pair_ref.1), custom_call_target="tpu_custom_call" | custom-call | tf_op jit(solution)/shard_map/pallas_call | solution.py:499
  1.7 4.1 %collective-permute-start = (bf16[192,128]{1,0:T(8,128)(2,1)S(1)}, bf16[192,128]{1,0:T(8,128)(2,1)S(1)}, u32[]{:S(2)}, u32[]{:S(2)}) collective-permute-start(bf16[192,128]{1,0:T(8,128)(2,1)S(1)} %shard_map.135), channel_id=1, source_target_pairs={{0,2},{1,3},{2,0},{3,1},{4,6},{5,7},{6,4},{7,5},{8,10},{9,11},{10,... | collective-permute-start | bytes 147464 | tf_op jit(solution)/shard_map/ppermute | solution.py:507
  5.8 1.3 %collective-permute-start.2 = (bf16[192,128]{1,0:T(8,128)(2,1)S(1)}, bf16[192,128]{1,0:T(8,128)(2,1)S(1)}, u32[]{:S(2)}, u32[]{:S(2)}) collective-permute-start(bf16[192,128]{1,0:T(8,128)(2,1)S(1)} %shard_map.135), channel_id=1, source_target_pairs={{0,3},{1,2},{2,1},{3,0},{4,7},{5,6},{6,5},{7,4},{8,11},{9,10},{10,... | collective-permute-start | bytes 147464 | tf_op jit(solution)/shard_map/ppermute | solution.py:507
  7.1 0.2 collective-permute-start.1
  7.4 1.0 %collective-permute-done = bf16[192,128]{1,0:T(8,128)(2,1)S(1)} collective-permute-done((bf16[192,128]{1,0:T(8,128)(2,1)S(1)}, bf16[192,128]{1,0:T(8,128)(2,1)S(1)}, u32[]{:S(2)}, u32[]{:S(2)}) %collective-permute-start) | collective-permute-done | bytes 49184 | tf_op jit(solution)/shard_map/ppermute | solution.py:507
  8.4 1.8 %collective-permute-start.3 = (bf16[2,192,128]{2,1,0:T(8,128)(2,1)S(1)}, bf16[2,192,128]{2,1,0:T(8,128)(2,1)S(1)}, u32[]{:S(2)}, u32[]{:S(2)}) collective-permute-start(bf16[2,192,128]{2,1,0:T(8,128)(2,1)S(1)} %pad_maximum_fusion.1.front_ref), channel_id=1, source_target_pairs={{0,8},{4,12},{8,0},{12,4},{1,9},{5,13},{9,1},{13,5},{2,10},{6,14},... | collective-permute-start | bytes 294920 | tf_op jit(solution)/shard_map/ppermute | solution.py:507
  10.2 1.6 %collective-permute-done.2 = bf16[192,128]{1,0:T(8,128)(2,1)S(1)} collective-permute-done((bf16[192,128]{1,0:T(8,128)(2,1)S(1)}, bf16[192,128]{1,0:T(8,128)(2,1)S(1)}, u32[]{:S(2)}, u32[]{:S(2)}) %collective-permute-start.2) | collective-permute-done | bytes 49184 | tf_op jit(solution)/shard_map/ppermute | solution.py:507
  11.7 0.0 collective-permute-done.1
  11.8 1.6 %collective-permute-start.5 = (bf16[2,192,128]{2,1,0:T(8,128)(2,1)S(1)}, bf16[2,192,128]{2,1,0:T(8,128)(2,1)S(1)}, u32[]{:S(2)}, u32[]{:S(2)}) collective-permute-start(bf16[2,192,128]{2,1,0:T(8,128)(2,1)S(1)} %pad_maximum_fusion.2.rear_ref), channel_id=1, source_target_pairs={{0,8},{4,12},{8,0},{12,4},{1,9},{5,13},{9,1},{13,5},{2,10},{6,14},... | collective-permute-start | bytes 294920 | tf_op jit(solution)/shard_map/ppermute | solution.py:507
  13.3 1.4 %shard_map.136 = (f32[8,128]{1,0:T(8,128)S(1)}, bf16[256,256]{1,0:T(8,128)(2,1)S(1)}, bf16[512,256]{1,0:T(8,128)(2,1)S(1)}, f32[64,64]{1,0:T(8,128)S(1)}) custom-call(f32[1,64]{1,0:T(1,128)} %bitcast.24, f32[1,64]{1,0:T(1,128)} %bitcast.25, bf16[32,64]{1,0:T(8,128)(2,1)} %bitcast.21, bf16[32,64]{1,0:T(8,128)(2,1)} %bitcast.22, bf16[1024,128]{1,0:T(8,128)(2,1)} %refs_4_), custom_call_target="tpu_custom_call" | custom-call | tf_op jit(solution)/shard_map/pallas_call | solution.py:517
  14.8 0.0 collective-permute-done.3.front_ref
  14.8 0.1 collective-permute-start.7
  14.8 0.5 %collective-permute-start.4 = (bf16[2,192,128]{2,1,0:T(8,128)(2,1)S(1)}, bf16[2,192,128]{2,1,0:T(8,128)(2,1)S(1)}, u32[]{:S(2)}, u32[]{:S(2)}) collective-permute-start(bf16[2,192,128]{2,1,0:T(8,128)(2,1)S(1)} %collective-permute-done.3.front_ref), channel_id=1, source_target_pairs={{0,4},{4,0},{8,12},{12,8},{1,5},{5,1},{9,13},{13,9},{2,6},{6,2},{1... | collective-permute-start | bytes 294920 | tf_op jit(solution)/shard_map/ppermute | solution.py:507
  15.3 0.8 %shard_map.137 = (bf16[512,256]{1,0:T(8,128)(2,1)S(1)}, bf16[128,256]{1,0:T(8,128)(2,1)S(1)}, bf16[128,256]{1,0:T(8,128)(2,1)S(1)}, f32[32,8,128]{2,1,0:T(8,128)...) custom-call(s32[1]{0:T(128)} %bitcast.place_ref, ...), custom_call_target="tpu_custom_call" | custom-call | flops 1000000000 | bytes 3906250 | tf_op jit(solution)/shard_map/pallas_call | solution.py:557
  16.2 0.3 %collective-permute-done.5.rear_ref = bf16[2,192,128]{2,1,0:T(8,128)(2,1)S(1)} collective-permute-done((bf16[2,192,128]{2,1,0:T(8,128)(2,1)S(1)}, bf16[2,192,128]{2,1,0:T(8,128)(2,1)S(1)}, u32[]{:S(2)}, u32[]{:S(2)}) %collective-permute-start.5) | collective-permute-done | bytes 98336 | tf_op jit(solution)/shard_map/ppermute | solution.py:507
  16.4 0.0 collective-permute-start.6
  16.4 0.0 collective-permute-done.7.core_ref
  16.4 1.4 %shard_map.138 = (bf16[512,256]{1,0:T(8,128)(2,1)S(1)}, bf16[128,256]{1,0:T(8,128)(2,1)S(1)}, bf16[128,256]{1,0:T(8,128)(2,1)S(1)}, f32[32,8,128]{2,1,0:T(8,128)...) custom-call(s32[1]{0:T(128)} %bitcast.place_ref, ...), custom_call_target="tpu_custom_call" | custom-call | flops 1000000 | bytes 3906 | tf_op jit(solution)/shard_map/pallas_call | solution.py:557
  17.8 0.0 collective-permute-done.4.front_ref
  17.9 0.0 collective-permute-done.6.rear_ref
  17.9 6.3 %shard_map.139 = (f32[32,8,64]{2,1,0:T(8,128)}, f32[1024,128]{1,0:T(8,128)}, f32[32,64]{1,0:T(8,128)}, f32[32,64]{1,0:T(8,128)}, f32[1,64]{1,0:T(1,128)}, /*index=5*/f32[1,64]{1,0:T(1,128)}, f32[1,128]{1,0:T(1,128)}) custom-call(s32[1]{0:T(128)} %bitcast.place_ref, bf16[2,192,128]{2,1,0:T(8,128)(2,1)S(1)} %collective-permute-done.4.front_ref, ...), custom_call_target="tpu_custom_call" | custom-call | tf_op jit(solution)/shard_map/pallas_call | solution.py:575
  (3 shorter events, 0.0 us)
Async XLA Ops:
  1.7 6.7 %collective-permute-start = (bf16[192,128]{1,0:T(8,128)(2,1)S(1)}, bf16[192,128]{1,0:T(8,128)(2,1)S(1)}, u32[]{:S(2)}, u32[]{:S(2)}) collective-permute-start(bf16[192,128]{1,0:T(8,128)(2,1)S(1)} %shard_map.135), channel_id=1, source_target_pairs={{0,2},{1,3},{2,0},{3,1},{4,6},{5,7},{6,4},{7,5},{8,10},{9,11},{10,... | collective-permute-start | bytes 147464 | tf_op jit(solution)/shard_map/ppermute | solution.py:507
  5.8 6.0 %collective-permute-start.2 = (bf16[192,128]{1,0:T(8,128)(2,1)S(1)}, bf16[192,128]{1,0:T(8,128)(2,1)S(1)}, u32[]{:S(2)}, u32[]{:S(2)}) collective-permute-start(bf16[192,128]{1,0:T(8,128)(2,1)S(1)} %shard_map.135), channel_id=1, source_target_pairs={{0,3},{1,2},{2,1},{3,0},{4,7},{5,6},{6,5},{7,4},{8,11},{9,10},{10,... | collective-permute-start | bytes 147464 | tf_op jit(solution)/shard_map/ppermute | solution.py:507
  7.1 4.6 %collective-permute-start.1 = (bf16[192,128]{1,0:T(8,128)(2,1)S(1)}, bf16[192,128]{1,0:T(8,128)(2,1)S(1)}, u32[]{:S(2)}, u32[]{:S(2)}) collective-permute-start(bf16[192,128]{1,0:T(8,128)(2,1)S(1)} %shard_map.135), channel_id=1, source_target_pairs={{0,1},{1,0},{2,3},{3,2},{4,5},{5,4},{6,7},{7,6},{8,9},{9,8},{10,11... | collective-permute-start | bytes 147464 | tf_op jit(solution)/shard_map/ppermute | solution.py:507
  8.4 6.4 %collective-permute-start.3 = (bf16[2,192,128]{2,1,0:T(8,128)(2,1)S(1)}, bf16[2,192,128]{2,1,0:T(8,128)(2,1)S(1)}, u32[]{:S(2)}, u32[]{:S(2)}) collective-permute-start(bf16[2,192,128]{2,1,0:T(8,128)(2,1)S(1)} %pad_maximum_fusion.1.front_ref), channel_id=1, source_target_pairs={{0,8},{4,12},{8,0},{12,4},{1,9},{5,13},{9,1},{13,5},{2,10},{6,14},... | collective-permute-start | bytes 294920 | tf_op jit(solution)/shard_map/ppermute | solution.py:507
  11.8 4.7 %collective-permute-start.5 = (bf16[2,192,128]{2,1,0:T(8,128)(2,1)S(1)}, bf16[2,192,128]{2,1,0:T(8,128)(2,1)S(1)}, u32[]{:S(2)}, u32[]{:S(2)}) collective-permute-start(bf16[2,192,128]{2,1,0:T(8,128)(2,1)S(1)} %pad_maximum_fusion.2.rear_ref), channel_id=1, source_target_pairs={{0,8},{4,12},{8,0},{12,4},{1,9},{5,13},{9,1},{13,5},{2,10},{6,14},... | collective-permute-start | bytes 294920 | tf_op jit(solution)/shard_map/ppermute | solution.py:507
  14.8 1.7 %collective-permute-start.7 = (bf16[4,192,128]{2,1,0:T(8,128)(2,1)S(1)}, bf16[4,192,128]{2,1,0:T(8,128)(2,1)S(1)}, u32[]{:S(2)}, u32[]{:S(2)}) collective-permute-start(bf16[4,192,128]{2,1,0:T(8,128)(2,1)S(1)} %pad_maximum_fusion), channel_id=1, source_target_pairs={{0,4},{4,0},{8,12},{12,8},{1,5},{5,1},{9,13},{13,9},{2,6},{6,2},{1... | collective-permute-start | bytes 589832 | tf_op jit(solution)/shard_map/ppermute | solution.py:507
  14.8 3.0 %collective-permute-start.4 = (bf16[2,192,128]{2,1,0:T(8,128)(2,1)S(1)}, bf16[2,192,128]{2,1,0:T(8,128)(2,1)S(1)}, u32[]{:S(2)}, u32[]{:S(2)}) collective-permute-start(bf16[2,192,128]{2,1,0:T(8,128)(2,1)S(1)} %collective-permute-done.3.front_ref), channel_id=1, source_target_pairs={{0,4},{4,0},{8,12},{12,8},{1,5},{5,1},{9,13},{13,9},{2,6},{6,2},{1... | collective-permute-start | bytes 294920 | tf_op jit(solution)/shard_map/ppermute | solution.py:507
  16.4 1.4 %collective-permute-start.6 = (bf16[2,192,128]{2,1,0:T(8,128)(2,1)S(1)}, bf16[2,192,128]{2,1,0:T(8,128)(2,1)S(1)}, u32[]{:S(2)}, u32[]{:S(2)}) collective-permute-start(bf16[2,192,128]{2,1,0:T(8,128)(2,1)S(1)} %collective-permute-done.5.rear_ref), channel_id=1, source_target_pairs={{0,4},{4,0},{8,12},{12,8},{1,5},{5,1},{9,13},{13,9},{2,6},{6,2},{1... | collective-permute-start | bytes 294920 | tf_op jit(solution)/shard_map/ppermute | solution.py:507

commit v21 on v18

--- a/solution.py
+++ b/solution.py
@@ -1,4 +1,5 @@
 import functools
+from itertools import zip_longest
 
 import jax
 import jax.numpy as jnp
@@ -255,15 +256,12 @@
 ORDER = (0, 2, 1, 3)
 
 
-def stage_kernel(
+def stage_steps(
     n_col, a, place_ref, set_refs, norm_ref, back_ref, final_ref,
     rhs_out, left_out, leftt_out, rightt_out, grad_out, pair_out, found_out, *rest
 ):
     *own_out, turn_scr = rest
     blocks = [ref.at[k] for ref in set_refs for k in range(ref.shape[0])]
-    for b in range(n_col):
-        at = pl.multiple_of(lax.bitwise_xor(place_ref[0], ORDER[b]) * 8, 8)
-        pair_out[:, pl.ds(at, 8), :] = blocks[b][128:192, :].astype(F32).reshape(8, 8, 128)
 
     gain = norm_ref[0:1, :]
     offset = norm_ref[1:2, :]
@@ -273,6 +271,16 @@
     )
     mean = mm(x, averager)
     present = mean < ABSENT / 2
+    here = jnp.where(present, 1.0, 0.0)
+    lane = lax.broadcasted_iota(jnp.int32, (128, 128), 1)
+    found = jnp.zeros((128, 128), F32)
+    for g in range(4):
+        found = jnp.where(lane % 32 // 2 == 4 * a + g, here[128 * g : 128 * g + 128], found)
+    found_out[...] = found
+    for b in range(n_col):
+        at = pl.multiple_of(lax.bitwise_xor(place_ref[0], ORDER[b]) * 8, 8)
+        pair_out[:, pl.ds(at, 8), :] = blocks[b][128:192, :].astype(F32).reshape(8, 8, 128)
+    yield
     varied = x.astype(F32) - mean
     inverse = lax.rsqrt(mm((varied * varied).astype(BF), averager) + 1e-05)
     normed = varied * inverse
@@ -280,15 +288,26 @@
         for g in range(4):
             own_out[0][32 * g : 32 * g + 32, :] = normed[128 * g : 128 * g + 32]
             own_out[1][32 * g : 32 * g + 32, :] = inverse[128 * g : 128 * g + 32]
+    yield
+
+    def grad_piece(n):
+        pair = pair_out[4 * n : 4 * n + 4].reshape(128, 128).astype(BF)
+        pairs = jnp.concatenate([diagonal_pair(pair[:64]), diagonal_pair(pair[64:])], axis=0)
+        grad = mm_nt(final_ref[...], pairs).astype(BF)
+        for p in range(2):
+            for q in range(8):
+                rows = 64 * (2 * n + p)
+                block = grad[64 * q : 64 * q + 64, 128 * p : 128 * p + 128]
+                even, odd = interleave(block[:32], block[32:])
+                grad_out[rows : rows + 32, 128 * q : 128 * q + 128] = even
+                grad_out[rows + 32 : rows + 64, 128 * q : 128 * q + 128] = odd
+
+    grad_piece(0)
+    yield
+
     normal = jnp.where(present, normed * gain + offset, 0.0).astype(BF)
     rhs_out[:, 0:128] = normal
     rhs_out[:, 128:256] = normed.astype(BF)
-    here = jnp.where(present, 1.0, 0.0)
-    lane = lax.broadcasted_iota(jnp.int32, (128, 128), 1)
-    found = jnp.zeros((128, 128), F32)
-    for g in range(4):
-        found = jnp.where(lane % 32 // 2 == 4 * a + g, here[128 * g : 128 * g + 128], found)
-    found_out[...] = found
     for h in range(2):
         masked = jnp.concatenate(
             [normal[128 * g : 128 * g + 128] for g in (2 * h, 2 * h + 1)], axis=1
@@ -301,23 +320,16 @@
             leftt_out[64 * h + 32 * k : 64 * h + 32 * k + 32, :] = jnp.concatenate(
                 [both[32 * k : 32 * k + 32], both[32 * k + 64 : 32 * k + 96]], axis=1
             ).astype(BF)
-
+    yield
+    grad_piece(1)
+    yield
     for e in range(32):
         rightt_out[e] = turn_scr[pl.ds(e, 8, stride=32), :]
 
-    pair = pair_out[...].reshape(256, 128).astype(BF)
-    for n in range(2):
-        pairs = jnp.concatenate(
-            [diagonal_pair(pair[64 * p : 64 * p + 64]) for p in (2 * n, 2 * n + 1)], axis=0
-        )
-        grad = mm_nt(final_ref[...], pairs).astype(BF)
-        for p in range(2):
-            for q in range(8):
-                rows = 64 * (2 * n + p)
-                block = grad[64 * q : 64 * q + 64, 128 * p : 128 * p + 128]
-                even, odd = interleave(block[:32], block[32:])
-                grad_out[rows : rows + 32, 128 * q : 128 * q + 128] = even
-                grad_out[rows + 32 : rows + 64, 128 * q : 128 * q + 128] = odd
+
+def stage_kernel(*arguments):
+    for _ in stage_steps(*arguments):
+        pass
 
 
 def own_kernel(n_col, place_ref, front_ref, rear_ref, norm_ref, back_ref, final_ref, *rest):
@@ -326,8 +338,12 @@
 
 def pair_kernel(n_col, place_ref, core_ref, front_ref, rear_ref, norm_ref, back_ref, final_ref, *rest):
     common = (norm_ref, back_ref, final_ref)
-    stage_kernel(n_col, 1, place_ref, (core_ref,), *common, *rest[:7], rest[14])
-    stage_kernel(n_col, 2, place_ref, (front_ref, rear_ref), *common, *rest[7:14], rest[15])
+    both = (
+        stage_steps(n_col, 1, place_ref, (core_ref,), *common, *rest[:7], rest[14]),
+        stage_steps(n_col, 2, place_ref, (front_ref, rear_ref), *common, *rest[7:14], rest[15]),
+    )
+    for _ in zip_longest(*both):
+        pass
 
 
 def part_kernel(n_row, n_col, place_ref, front_ref, rear_ref, *refs):
@@ -339,10 +355,11 @@
         final_out, out_sem, turn_scr,
     ) = refs[7 * (n_row - 1) : -7]
     stages.append(refs[-7:])
-    stage_kernel(
+    last = stage_steps(
         n_col, n_row - 1, place_ref, (front_ref, rear_ref),
         norm_ref, back_ref, final_ref, *stages[-1], turn_scr,
     )
+    next(last)
     gain = norm_ref[0:1, :]
     averager = averager_of()
     lane = lax.broadcasted_iota(jnp.int32, (128, 128), 1)
@@ -351,61 +368,109 @@
     turned = pltpu.roll(found, 64, 1)
     mask = jnp.where((lane % 2 == 0) == (lane < 64), found, turned)
     mask_t = mask.T
-
-    for e in range(32):
-        right_scr[32 * e : 32 * e + 32, :] = jnp.concatenate(
-            [stage[3][e] for stage in stages], axis=0
-        ).astype(BF)
-
     mask_bf = mask.astype(BF)
     share = (1.0 / (mm_tn(mask_bf, mask_bf)[0:32] + 0.001)).astype(BF)
-    for i in range(32):
-        a, at = i // 8, 32 * (i % 8)
-        for q in range(8):
-            grad_scr[32 * i : 32 * i + 32, 128 * q : 128 * q + 128] = (
-                stages[a][4][at : at + 32, 128 * q : 128 * q + 128] * share[i : i + 1]
-            )
-    left = jnp.concatenate([stage[1][...] for stage in stages], axis=1)
-    right_grad = mm(left, grad_scr[...])
-    left_grad = mm(grad_scr[...], right_scr[...])
-
-    turn = spread(
-        256, 256, lambda r, c: jnp.where((r // 8 == c % 32) & (r % 8 == c // 32), 1.0, 0.0)
-    ).astype(BF)
-    mask_two = jnp.concatenate([mask, mask], axis=1)
-    right_in = [
-        mm_nt(turn, (right_grad[:, 256 * q : 256 * q + 256] * mask_two).astype(BF))
-        for q in range(4)
-    ]
-    for t in range(32):
-        at = slice(128 * (t // 2), 128 * (t // 2) + 128)
-        row = 32 * (t % 2)
-        all_scr[row : row + 32, at] = (
-            left_grad[32 * t : 32 * t + 32] * mask_t[t : t + 1]
-        ).astype(BF)
-        all_scr[row + 64 : row + 96, at] = jnp.concatenate(
-            [part[8 * t : 8 * t + 8] for part in right_in], axis=0
-        ).astype(BF)
-
-    bias = jnp.zeros((1, 128), F32)
+
+    def scale(a):
+        for i in range(8 * a, 8 * a + 8):
+            at = 32 * (i % 8)
+            for q in range(8):
+                grad_scr[32 * i : 32 * i + 32, 128 * q : 128 * q + 128] = (
+                    stages[a][4][at : at + 32, 128 * q : 128 * q + 128] * share[i : i + 1]
+                )
+
     ones = jnp.ones((128, 128), BF)
-    for p in range(8):
+
+    def scaled_piece(p):
         both_on = jnp.concatenate(
             [mask_t[0:32] * mask_t[i : i + 1] for i in range(4 * p, 4 * p + 4)], axis=0
         ).astype(BF)
         counts = mm(both_on, ones)
         pair = stages[p // 2][5][4 * (p % 2) : 4 * (p % 2) + 4]
         scaled = pair.reshape(128, 128) / (counts + 0.001)
-        bias = bias + jnp.sum(scaled, axis=0, keepdims=True)
         scaled_scr[128 * p : 128 * p + 128, :] = scaled.astype(BF)
+        return jnp.sum(scaled, axis=0, keepdims=True)
+
+    next(last)
+    bias = scaled_piece(0)
+    scale(0)
+    next(last)
+    bias = bias + scaled_piece(1)
+    scale(1)
+    next(last)
+    bias = bias + scaled_piece(2)
+    scale(2)
+    next(last)
+    bias = bias + scaled_piece(3)
+    for _ in last:
+        pass
+    scale(3)
+
+    for e in range(32):
+        right_scr[32 * e : 32 * e + 32, :] = jnp.concatenate(
+            [stage[3][e] for stage in stages], axis=0
+        ).astype(BF)
+
+    left = jnp.concatenate([stage[1][...] for stage in stages], axis=1)
+    right_grad = mm(left, grad_scr[...])
+    bias = bias + scaled_piece(4) + scaled_piece(5)
+    left_grad = mm(grad_scr[...], right_scr[...])
+    bias = bias + scaled_piece(6) + scaled_piece(7)
     bias_out[...] = bias
 
+    def finish():
+        turn = spread(
+            256, 256, lambda r, c: jnp.where((r // 8 == c % 32) & (r % 8 == c // 32), 1.0, 0.0)
+        ).astype(BF)
+        mask_two = jnp.concatenate([mask, mask], axis=1)
+        right_in = []
+        for q in range(4):
+            right_in.append(
+                mm_nt(turn, (right_grad[:, 256 * q : 256 * q + 256] * mask_two).astype(BF))
+            )
+            if q % 2:
+                yield
+        for t in range(32):
+            at = slice(128 * (t // 2), 128 * (t // 2) + 128)
+            row = 32 * (t % 2)
+            all_scr[row : row + 32, at] = (
+                left_grad[32 * t : 32 * t + 32] * mask_t[t : t + 1]
+            ).astype(BF)
+            all_scr[row + 64 : row + 96, at] = jnp.concatenate(
+                [part[8 * t : 8 * t + 8] for part in right_in], axis=0
+            ).astype(BF)
+            if t % 16 == 15:
+                yield
+
+        d_hat = []
+        for h in range(2):
+            sides = [
+                jnp.concatenate(
+                    [all_scr[row : row + 64, 128 * g : 128 * g + 128] for g in (2 * h, 2 * h + 1)],
+                    axis=0,
+                )
+                for row in (0, 64)
+            ]
+            d_normal = mm_tn(jnp.concatenate(sides, axis=0), back_ref[...])
+            d_hat += [d_normal[0:32, 0:128] * gain, d_normal[0:32, 128:256] * gain]
+        d_hat = jnp.concatenate(d_hat, axis=0)
+        yield
+        normed = normed_ref[...]
+        means = mm(jnp.concatenate([d_hat, d_hat * normed], axis=0).astype(BF), averager)
+        yield
+        result = inverse_ref[...] * (d_hat - means[:128] - normed * means[128:])
+        for g in range(4):
+            emb_out[:, 2 * g, :] = result[32 * g : 32 * g + 32, 0:64]
+            emb_out[:, 2 * g + 1, :] = result[32 * g : 32 * g + 32, 64:128]
+
+    finishing = finish()
     left_t = jnp.concatenate([stage[2][...] for stage in stages], axis=0)
     for n in range(8):
         rights = jnp.concatenate(
             [diagonal_pair(right_scr[64 * p : 64 * p + 64, :]) for p in (2 * n, 2 * n + 1)], axis=0
         )
         outer = mm_nt(left_t, rights).astype(BF)
+        next(finishing, None)
         for p in range(2):
             for q in range(8):
                 rows = 64 * (2 * n + p)
@@ -413,6 +478,8 @@
                 even, odd = interleave(block[:32], block[32:])
                 outer_scr[rows : rows + 32, 128 * q : 128 * q + 128] = even
                 outer_scr[rows + 32 : rows + 64, 128 * q : 128 * q + 128] = odd
+    for _ in finishing:
+        pass
     wide_scr[...] = mm(outer_scr[...], scaled_scr[...])
     for c in range(32):
         final_out[32 * c : 32 * c + 32, :] = wide_scr[pl.ds(c, 32, stride=32), :]
@@ -441,23 +508,6 @@
     )
     offset_out[...] = jnp.sum(first * left_sum + second * right_sum, axis=0, keepdims=True)
 
-    d_hat = []
-    for h in range(2):
-        sides = [
-            jnp.concatenate(
-                [all_scr[row : row + 64, 128 * g : 128 * g + 128] for g in (2 * h, 2 * h + 1)], axis=0
-            )
-            for row in (0, 64)
-        ]
-        d_normal = mm_tn(jnp.concatenate(sides, axis=0), back_ref[...])
-        d_hat += [d_normal[0:32, 0:128] * gain, d_normal[0:32, 128:256] * gain]
-    d_hat = jnp.concatenate(d_hat, axis=0)
-    normed = normed_ref[...]
-    means = mm(jnp.concatenate([d_hat, d_hat * normed], axis=0).astype(BF), averager)
-    result = inverse_ref[...] * (d_hat - means[:128] - normed * means[128:])
-    for g in range(4):
-        emb_out[:, 2 * g, :] = result[32 * g : 32 * g + 32, 0:64]
-        emb_out[:, 2 * g + 1, :] = result[32 * g : 32 * g + 32, 64:128]
     final_send.wait()
 
 

time: 23.7 us -> 23.8 us (level)
    pallas_call x2, Pallas kernels: 2.2 us -> 1.85 us  [stages_of(): pl.pallas_call(functools.partial(kernel, n_col), out_shape=tuple(outs), i...]
    pallas_call x1, Pallas kernels: 5.57 us -> 5.88 us  [gathered_body(): pl.pallas_call(functools.partial(part_kernel, n_row, n_col), out_shape=(s...]
  transfers between devices with their start and end apart: 8 -> 8, of which waited for: 3 -> 4; matrix products, arithmetic and copies ran while one was open for 0% -> 0% of each run, Pallas kernels for 15% -> 14%
where the time goes in v21:
time: 23.8 us; the launch traced here: 23.6 us
  Pallas kernels  10.2 us (43%)
  starting transfers between devices  9.57 us (40%)
  waiting for transfers between devices  3.14 us (13%)
  between operations  0.71 us (3%)
    ppermute x8, starting transfers between devices, over(): return lax.ppermute(array, axis, [(k, k ^ step) for k in range(size)])  9.57 us
    pallas_call x1, Pallas kernels, gathered_body(): pl.pallas_call(functools.partial(part_kernel, n_row, n_col), out_shape=(s...  5.88 us
    ppermute x8, waiting for transfers between devices, over(): return lax.ppermute(array, axis, [(k, k ^ step) for k in range(size)])  3.14 us
    pallas_call x2, Pallas kernels, stages_of(): pl.pallas_call(functools.partial(kernel, n_col), out_shape=tuple(outs), i...  1.85 us
    pallas_call x1, Pallas kernels, gathered_body(): pl.pallas_call(weights_kernel, out_shape=(held(8, 128), held_bf(256, 256)...  1.4 us
    pallas_call x1, Pallas kernels, gathered_body(): pl.pallas_call(pack_kernel, out_shape=held_bf(192, 128), in_specs=vmem(3)...  1.04 us
  transfers between devices with their start and end apart: 8, of which 4 were waited for; matrix products, arithmetic and copies ran while one was open for 0% of the time, Pallas kernels for 14%

profile of v21, /device:TPU:0, one launch (start us, length us, event | category | flops | bytes accessed | tf_op | source)
XLA Modules:
  0.0 23.6 jit_solution(4518874196635376441)
XLA Ops:
  0.6 1.0 %shard_map.135 = bf16[192,128]{1,0:T(8,128)(2,1)S(1)} custom-call(bf16[32,8,64]{2,1,0:T(8,128)(2,1)} %msa_ref.1, s32[8,32]{1,0:T(8,128)} %bitcast.23, bf16[8,8,128]{2,1,0:T(8,128)(2,1)} %pair_ref.1), custom_call_target="tpu_custom_call" | custom-call | tf_op jit(solution)/shard_map/pallas_call | solution.py:542
  1.7 4.1 %collective-permute-start = (bf16[192,128]{1,0:T(8,128)(2,1)S(1)}, bf16[192,128]{1,0:T(8,128)(2,1)S(1)}, u32[]{:S(2)}, u32[]{:S(2)}) collective-permute-start(bf16[192,128]{1,0:T(8,128)(2,1)S(1)} %shard_map.135), channel_id=1, source_target_pairs={{0,2},{1,3},{2,0},{3,1},{4,6},{5,7},{6,4},{7,5},{8,10},{9,11},{10,... | collective-permute-start | bytes 147464 | tf_op jit(solution)/shard_map/ppermute | solution.py:549
  5.8 1.3 %collective-permute-start.2 = (bf16[192,128]{1,0:T(8,128)(2,1)S(1)}, bf16[192,128]{1,0:T(8,128)(2,1)S(1)}, u32[]{:S(2)}, u32[]{:S(2)}) collective-permute-start(bf16[192,128]{1,0:T(8,128)(2,1)S(1)} %shard_map.135), channel_id=1, source_target_pairs={{0,3},{1,2},{2,1},{3,0},{4,7},{5,6},{6,5},{7,4},{8,11},{9,10},{10,... | collective-permute-start | bytes 147464 | tf_op jit(solution)/shard_map/ppermute | solution.py:549
  7.1 0.2 collective-permute-start.1
  7.4 1.0 %collective-permute-done = bf16[192,128]{1,0:T(8,128)(2,1)S(1)} collective-permute-done((bf16[192,128]{1,0:T(8,128)(2,1)S(1)}, bf16[192,128]{1,0:T(8,128)(2,1)S(1)}, u32[]{:S(2)}, u32[]{:S(2)}) %collective-permute-start) | collective-permute-done | bytes 49184 | tf_op jit(solution)/shard_map/ppermute | solution.py:549
  8.4 1.8 %collective-permute-start.3 = (bf16[2,192,128]{2,1,0:T(8,128)(2,1)S(1)}, bf16[2,192,128]{2,1,0:T(8,128)(2,1)S(1)}, u32[]{:S(2)}, u32[]{:S(2)}) collective-permute-start(bf16[2,192,128]{2,1,0:T(8,128)(2,1)S(1)} %pad_maximum_fusion.1.front_ref), channel_id=1, source_target_pairs={{0,8},{4,12},{8,0},{12,4},{1,9},{5,13},{9,1},{13,5},{2,10},{6,14},... | collective-permute-start | bytes 294920 | tf_op jit(solution)/shard_map/ppermute | solution.py:549
  10.2 1.6 %collective-permute-done.2 = bf16[192,128]{1,0:T(8,128)(2,1)S(1)} collective-permute-done((bf16[192,128]{1,0:T(8,128)(2,1)S(1)}, bf16[192,128]{1,0:T(8,128)(2,1)S(1)}, u32[]{:S(2)}, u32[]{:S(2)}) %collective-permute-start.2) | collective-permute-done | bytes 49184 | tf_op jit(solution)/shard_map/ppermute | solution.py:549
  11.7 0.0 collective-permute-done.1
  11.8 1.6 %collective-permute-start.5 = (bf16[2,192,128]{2,1,0:T(8,128)(2,1)S(1)}, bf16[2,192,128]{2,1,0:T(8,128)(2,1)S(1)}, u32[]{:S(2)}, u32[]{:S(2)}) collective-permute-start(bf16[2,192,128]{2,1,0:T(8,128)(2,1)S(1)} %pad_maximum_fusion.2.rear_ref), channel_id=1, source_target_pairs={{0,8},{4,12},{8,0},{12,4},{1,9},{5,13},{9,1},{13,5},{2,10},{6,14},... | collective-permute-start | bytes 294920 | tf_op jit(solution)/shard_map/ppermute | solution.py:549
  13.3 1.4 %shard_map.136 = (f32[8,128]{1,0:T(8,128)S(1)}, bf16[256,256]{1,0:T(8,128)(2,1)S(1)}, bf16[512,256]{1,0:T(8,128)(2,1)S(1)}, f32[64,64]{1,0:T(8,128)S(1)}) custom-call(f32[1,64]{1,0:T(1,128)} %bitcast.24, f32[1,64]{1,0:T(1,128)} %bitcast.25, bf16[32,64]{1,0:T(8,128)(2,1)} %bitcast.21, bf16[32,64]{1,0:T(8,128)(2,1)} %bitcast.22, bf16[1024,128]{1,0:T(8,128)(2,1)} %refs_4_), custom_call_target="tpu_custom_call" | custom-call | tf_op jit(solution)/shard_map/pallas_call | solution.py:559
  14.8 0.0 collective-permute-done.3.front_ref
  14.8 0.1 collective-permute-start.7
  14.9 0.5 %collective-permute-start.4 = (bf16[2,192,128]{2,1,0:T(8,128)(2,1)S(1)}, bf16[2,192,128]{2,1,0:T(8,128)(2,1)S(1)}, u32[]{:S(2)}, u32[]{:S(2)}) collective-permute-start(bf16[2,192,128]{2,1,0:T(8,128)(2,1)S(1)} %collective-permute-done.3.front_ref), channel_id=1, source_target_pairs={{0,4},{4,0},{8,12},{12,8},{1,5},{5,1},{9,13},{13,9},{2,6},{6,2},{1... | collective-permute-start | bytes 294920 | tf_op jit(solution)/shard_map/ppermute | solution.py:549
  15.3 0.8 %shard_map.137 = (bf16[512,256]{1,0:T(8,128)(2,1)S(1)}, bf16[128,256]{1,0:T(8,128)(2,1)S(1)}, bf16[128,256]{1,0:T(8,128)(2,1)S(1)}, f32[32,8,128]{2,1,0:T(8,128)...) custom-call(s32[1]{0:T(128)} %bitcast.place_ref, ...), custom_call_target="tpu_custom_call" | custom-call | flops 1000000000 | bytes 3906250 | tf_op jit(solution)/shard_map/pallas_call | solution.py:599
  16.1 0.3 %collective-permute-done.5.rear_ref = bf16[2,192,128]{2,1,0:T(8,128)(2,1)S(1)} collective-permute-done((bf16[2,192,128]{2,1,0:T(8,128)(2,1)S(1)}, bf16[2,192,128]{2,1,0:T(8,128)(2,1)S(1)}, u32[]{:S(2)}, u32[]{:S(2)}) %collective-permute-start.5) | collective-permute-done | bytes 98336 | tf_op jit(solution)/shard_map/ppermute | solution.py:549
  16.4 0.0 collective-permute-start.6
  16.4 0.0 collective-permute-done.7.core_ref
  16.5 1.1 %shard_map.138 = (bf16[512,256]{1,0:T(8,128)(2,1)S(1)}, bf16[128,256]{1,0:T(8,128)(2,1)S(1)}, bf16[128,256]{1,0:T(8,128)(2,1)S(1)}, f32[32,8,128]{2,1,0:T(8,128)...) custom-call(s32[1]{0:T(128)} %bitcast.place_ref, ...), custom_call_target="tpu_custom_call" | custom-call | flops 1000000 | bytes 3906 | tf_op jit(solution)/shard_map/pallas_call | solution.py:599
  17.5 0.0 collective-permute-done.4.front_ref
  17.6 0.2 collective-permute-done.6.rear_ref
  17.7 5.9 %shard_map.139 = (f32[32,8,64]{2,1,0:T(8,128)}, f32[1024,128]{1,0:T(8,128)}, f32[32,64]{1,0:T(8,128)}, f32[32,64]{1,0:T(8,128)}, f32[1,64]{1,0:T(1,128)}, /*index=5*/f32[1,64]{1,0:T(1,128)}, f32[1,128]{1,0:T(1,128)}) custom-call(s32[1]{0:T(128)} %bitcast.place_ref, bf16[2,192,128]{2,1,0:T(8,128)(2,1)S(1)} %collective-permute-done.4.front_ref, ...), custom_call_target="tpu_custom_call" | custom-call | tf_op jit(solution)/shard_map/pallas_call | solution.py:617
  (3 shorter events, 0.0 us)
Async XLA Ops:
  1.7 6.7 %collective-permute-start = (bf16[192,128]{1,0:T(8,128)(2,1)S(1)}, bf16[192,128]{1,0:T(8,128)(2,1)S(1)}, u32[]{:S(2)}, u32[]{:S(2)}) collective-permute-start(bf16[192,128]{1,0:T(8,128)(2,1)S(1)} %shard_map.135), channel_id=1, source_target_pairs={{0,2},{1,3},{2,0},{3,1},{4,6},{5,7},{6,4},{7,5},{8,10},{9,11},{10,... | collective-permute-start | bytes 147464 | tf_op jit(solution)/shard_map/ppermute | solution.py:549
  5.8 6.0 %collective-permute-start.2 = (bf16[192,128]{1,0:T(8,128)(2,1)S(1)}, bf16[192,128]{1,0:T(8,128)(2,1)S(1)}, u32[]{:S(2)}, u32[]{:S(2)}) collective-permute-start(bf16[192,128]{1,0:T(8,128)(2,1)S(1)} %shard_map.135), channel_id=1, source_target_pairs={{0,3},{1,2},{2,1},{3,0},{4,7},{5,6},{6,5},{7,4},{8,11},{9,10},{10,... | collective-permute-start | bytes 147464 | tf_op jit(solution)/shard_map/ppermute | solution.py:549
  7.1 4.6 %collective-permute-start.1 = (bf16[192,128]{1,0:T(8,128)(2,1)S(1)}, bf16[192,128]{1,0:T(8,128)(2,1)S(1)}, u32[]{:S(2)}, u32[]{:S(2)}) collective-permute-start(bf16[192,128]{1,0:T(8,128)(2,1)S(1)} %shard_map.135), channel_id=1, source_target_pairs={{0,1},{1,0},{2,3},{3,2},{4,5},{5,4},{6,7},{7,6},{8,9},{9,8},{10,11... | collective-permute-start | bytes 147464 | tf_op jit(solution)/shard_map/ppermute | solution.py:549
  8.4 6.4 %collective-permute-start.3 = (bf16[2,192,128]{2,1,0:T(8,128)(2,1)S(1)}, bf16[2,192,128]{2,1,0:T(8,128)(2,1)S(1)}, u32[]{:S(2)}, u32[]{:S(2)}) collective-permute-start(bf16[2,192,128]{2,1,0:T(8,128)(2,1)S(1)} %pad_maximum_fusion.1.front_ref), channel_id=1, source_target_pairs={{0,8},{4,12},{8,0},{12,4},{1,9},{5,13},{9,1},{13,5},{2,10},{6,14},... | collective-permute-start | bytes 294920 | tf_op jit(solution)/shard_map/ppermute | solution.py:549
  11.8 4.7 %collective-permute-start.5 = (bf16[2,192,128]{2,1,0:T(8,128)(2,1)S(1)}, bf16[2,192,128]{2,1,0:T(8,128)(2,1)S(1)}, u32[]{:S(2)}, u32[]{:S(2)}) collective-permute-start(bf16[2,192,128]{2,1,0:T(8,128)(2,1)S(1)} %pad_maximum_fusion.2.rear_ref), channel_id=1, source_target_pairs={{0,8},{4,12},{8,0},{12,4},{1,9},{5,13},{9,1},{13,5},{2,10},{6,14},... | collective-permute-start | bytes 294920 | tf_op jit(solution)/shard_map/ppermute | solution.py:549
  14.8 1.7 %collective-permute-start.7 = (bf16[4,192,128]{2,1,0:T(8,128)(2,1)S(1)}, bf16[4,192,128]{2,1,0:T(8,128)(2,1)S(1)}, u32[]{:S(2)}, u32[]{:S(2)}) collective-permute-start(bf16[4,192,128]{2,1,0:T(8,128)(2,1)S(1)} %pad_maximum_fusion), channel_id=1, source_target_pairs={{0,4},{4,0},{8,12},{12,8},{1,5},{5,1},{9,13},{13,9},{2,6},{6,2},{1... | collective-permute-start | bytes 589832 | tf_op jit(solution)/shard_map/ppermute | solution.py:549
  14.9 2.7 %collective-permute-start.4 = (bf16[2,192,128]{2,1,0:T(8,128)(2,1)S(1)}, bf16[2,192,128]{2,1,0:T(8,128)(2,1)S(1)}, u32[]{:S(2)}, u32[]{:S(2)}) collective-permute-start(bf16[2,192,128]{2,1,0:T(8,128)(2,1)S(1)} %collective-permute-done.3.front_ref), channel_id=1, source_target_pairs={{0,4},{4,0},{8,12},{12,8},{1,5},{5,1},{9,13},{13,9},{2,6},{6,2},{1... | collective-permute-start | bytes 294920 | tf_op jit(solution)/shard_map/ppermute | solution.py:549
  16.4 1.3 %collective-permute-start.6 = (bf16[2,192,128]{2,1,0:T(8,128)(2,1)S(1)}, bf16[2,192,128]{2,1,0:T(8,128)(2,1)S(1)}, u32[]{:S(2)}, u32[]{:S(2)}) collective-permute-start(bf16[2,192,128]{2,1,0:T(8,128)(2,1)S(1)} %collective-permute-done.5.rear_ref), channel_id=1, source_target_pairs={{0,4},{4,0},{8,12},{12,8},{1,5},{5,1},{9,13},{13,9},{2,6},{6,2},{1... | collective-permute-start | bytes 294920 | tf_op jit(solution)/shard_map/ppermute | solution.py:549

commit v22 on v18

--- a/solution.py
+++ b/solution.py
@@ -1,4 +1,5 @@
 import functools
+from itertools import zip_longest
 
 import jax
 import jax.numpy as jnp
@@ -255,15 +256,12 @@
 ORDER = (0, 2, 1, 3)
 
 
-def stage_kernel(
+def stage_steps(
     n_col, a, place_ref, set_refs, norm_ref, back_ref, final_ref,
     rhs_out, left_out, leftt_out, rightt_out, grad_out, pair_out, found_out, *rest
 ):
     *own_out, turn_scr = rest
     blocks = [ref.at[k] for ref in set_refs for k in range(ref.shape[0])]
-    for b in range(n_col):
-        at = pl.multiple_of(lax.bitwise_xor(place_ref[0], ORDER[b]) * 8, 8)
-        pair_out[:, pl.ds(at, 8), :] = blocks[b][128:192, :].astype(F32).reshape(8, 8, 128)
 
     gain = norm_ref[0:1, :]
     offset = norm_ref[1:2, :]
@@ -273,6 +271,16 @@
     )
     mean = mm(x, averager)
     present = mean < ABSENT / 2
+    here = jnp.where(present, 1.0, 0.0)
+    lane = lax.broadcasted_iota(jnp.int32, (128, 128), 1)
+    found = jnp.zeros((128, 128), F32)
+    for g in range(4):
+        found = jnp.where(lane % 32 // 2 == 4 * a + g, here[128 * g : 128 * g + 128], found)
+    found_out[...] = found
+    for b in range(n_col):
+        at = pl.multiple_of(lax.bitwise_xor(place_ref[0], ORDER[b]) * 8, 8)
+        pair_out[:, pl.ds(at, 8), :] = blocks[b][128:192, :].astype(F32).reshape(8, 8, 128)
+    yield
     varied = x.astype(F32) - mean
     inverse = lax.rsqrt(mm((varied * varied).astype(BF), averager) + 1e-05)
     normed = varied * inverse
@@ -280,15 +288,26 @@
         for g in range(4):
             own_out[0][32 * g : 32 * g + 32, :] = normed[128 * g : 128 * g + 32]
             own_out[1][32 * g : 32 * g + 32, :] = inverse[128 * g : 128 * g + 32]
+    yield
+
+    def grad_piece(n):
+        pair = pair_out[4 * n : 4 * n + 4].reshape(128, 128).astype(BF)
+        pairs = jnp.concatenate([diagonal_pair(pair[:64]), diagonal_pair(pair[64:])], axis=0)
+        grad = mm_nt(final_ref[...], pairs).astype(BF)
+        for p in range(2):
+            for q in range(8):
+                rows = 64 * (2 * n + p)
+                block = grad[64 * q : 64 * q + 64, 128 * p : 128 * p + 128]
+                even, odd = interleave(block[:32], block[32:])
+                grad_out[rows : rows + 32, 128 * q : 128 * q + 128] = even
+                grad_out[rows + 32 : rows + 64, 128 * q : 128 * q + 128] = odd
+
+    grad_piece(0)
+    yield
+
     normal = jnp.where(present, normed * gain + offset, 0.0).astype(BF)
     rhs_out[:, 0:128] = normal
     rhs_out[:, 128:256] = normed.astype(BF)
-    here = jnp.where(present, 1.0, 0.0)
-    lane = lax.broadcasted_iota(jnp.int32, (128, 128), 1)
-    found = jnp.zeros((128, 128), F32)
-    for g in range(4):
-        found = jnp.where(lane % 32 // 2 == 4 * a + g, here[128 * g : 128 * g + 128], found)
-    found_out[...] = found
     for h in range(2):
         masked = jnp.concatenate(
             [normal[128 * g : 128 * g + 128] for g in (2 * h, 2 * h + 1)], axis=1
@@ -301,23 +320,16 @@
             leftt_out[64 * h + 32 * k : 64 * h + 32 * k + 32, :] = jnp.concatenate(
                 [both[32 * k : 32 * k + 32], both[32 * k + 64 : 32 * k + 96]], axis=1
             ).astype(BF)
-
+    yield
+    grad_piece(1)
+    yield
     for e in range(32):
         rightt_out[e] = turn_scr[pl.ds(e, 8, stride=32), :]
 
-    pair = pair_out[...].reshape(256, 128).astype(BF)
-    for n in range(2):
-        pairs = jnp.concatenate(
-            [diagonal_pair(pair[64 * p : 64 * p + 64]) for p in (2 * n, 2 * n + 1)], axis=0
-        )
-        grad = mm_nt(final_ref[...], pairs).astype(BF)
-        for p in range(2):
-            for q in range(8):
-                rows = 64 * (2 * n + p)
-                block = grad[64 * q : 64 * q + 64, 128 * p : 128 * p + 128]
-                even, odd = interleave(block[:32], block[32:])
-                grad_out[rows : rows + 32, 128 * q : 128 * q + 128] = even
-                grad_out[rows + 32 : rows + 64, 128 * q : 128 * q + 128] = odd
+
+def stage_kernel(*arguments):
+    for _ in stage_steps(*arguments):
+        pass
 
 
 def own_kernel(n_col, place_ref, front_ref, rear_ref, norm_ref, back_ref, final_ref, *rest):
@@ -326,8 +338,12 @@
 
 def pair_kernel(n_col, place_ref, core_ref, front_ref, rear_ref, norm_ref, back_ref, final_ref, *rest):
     common = (norm_ref, back_ref, final_ref)
-    stage_kernel(n_col, 1, place_ref, (core_ref,), *common, *rest[:7], rest[14])
-    stage_kernel(n_col, 2, place_ref, (front_ref, rear_ref), *common, *rest[7:14], rest[15])
+    both = (
+        stage_steps(n_col, 1, place_ref, (core_ref,), *common, *rest[:7], rest[14]),
+        stage_steps(n_col, 2, place_ref, (front_ref, rear_ref), *common, *rest[7:14], rest[15]),
+    )
+    for _ in zip_longest(*both):
+        pass
 
 
 def part_kernel(n_row, n_col, place_ref, front_ref, rear_ref, *refs):
@@ -339,10 +355,11 @@
         final_out, out_sem, turn_scr,
     ) = refs[7 * (n_row - 1) : -7]
     stages.append(refs[-7:])
-    stage_kernel(
+    last = stage_steps(
         n_col, n_row - 1, place_ref, (front_ref, rear_ref),
         norm_ref, back_ref, final_ref, *stages[-1], turn_scr,
     )
+    next(last)
     gain = norm_ref[0:1, :]
     averager = averager_of()
     lane = lax.broadcasted_iota(jnp.int32, (128, 128), 1)
@@ -352,19 +369,26 @@
     mask = jnp.where((lane % 2 == 0) == (lane < 64), found, turned)
     mask_t = mask.T
 
+    mask_bf = mask.astype(BF)
+    share = (1.0 / (mm_tn(mask_bf, mask_bf)[0:32] + 0.001)).astype(BF)
+    for a in range(n_row):
+        if a < n_row - 1:
+            next(last)
+        else:
+            for _ in last:
+                pass
+        for i in range(8 * a, 8 * a + 8):
+            at = 32 * (i % 8)
+            for q in range(8):
+                grad_scr[32 * i : 32 * i + 32, 128 * q : 128 * q + 128] = (
+                    stages[a][4][at : at + 32, 128 * q : 128 * q + 128] * share[i : i + 1]
+                )
+
     for e in range(32):
         right_scr[32 * e : 32 * e + 32, :] = jnp.concatenate(
             [stage[3][e] for stage in stages], axis=0
         ).astype(BF)
 
-    mask_bf = mask.astype(BF)
-    share = (1.0 / (mm_tn(mask_bf, mask_bf)[0:32] + 0.001)).astype(BF)
-    for i in range(32):
-        a, at = i // 8, 32 * (i % 8)
-        for q in range(8):
-            grad_scr[32 * i : 32 * i + 32, 128 * q : 128 * q + 128] = (
-                stages[a][4][at : at + 32, 128 * q : 128 * q + 128] * share[i : i + 1]
-            )
     left = jnp.concatenate([stage[1][...] for stage in stages], axis=1)
     right_grad = mm(left, grad_scr[...])
     left_grad = mm(grad_scr[...], right_scr[...])

time: 23.7 us -> 23.8 us (level)
    pallas_call x2, Pallas kernels: 2.2 us -> 1.85 us  [stages_of(): pl.pallas_call(functools.partial(kernel, n_col), out_shape=tuple(outs), i...]
    pallas_call x1, Pallas kernels: 5.57 us -> 5.84 us  [gathered_body(): pl.pallas_call(functools.partial(part_kernel, n_row, n_col), out_shape=(s...]
  transfers between devices with their start and end apart: 8 -> 8, of which waited for: 3 -> 4; matrix products, arithmetic and copies ran while one was open for 0% -> 0% of each run, Pallas kernels for 15% -> 14%
where the time goes in v22:
time: 23.8 us; the launch traced here: 23.6 us
  Pallas kernels  10.1 us (42%)
  starting transfers between devices  9.57 us (40%)
  waiting for transfers between devices  3.14 us (13%)
  between operations  0.71 us (3%)
    ppermute x8, starting transfers between devices, over(): return lax.ppermute(array, axis, [(k, k ^ step) for k in range(size)])  9.57 us
    pallas_call x1, Pallas kernels, gathered_body(): pl.pallas_call(functools.partial(part_kernel, n_row, n_col), out_shape=(s...  5.84 us
    ppermute x8, waiting for transfers between devices, over(): return lax.ppermute(array, axis, [(k, k ^ step) for k in range(size)])  3.14 us
    pallas_call x2, Pallas kernels, stages_of(): pl.pallas_call(functools.partial(kernel, n_col), out_shape=tuple(outs), i...  1.85 us
    pallas_call x1, Pallas kernels, gathered_body(): pl.pallas_call(weights_kernel, out_shape=(held(8, 128), held_bf(256, 256)...  1.4 us
    pallas_call x1, Pallas kernels, gathered_body(): pl.pallas_call(pack_kernel, out_shape=held_bf(192, 128), in_specs=vmem(3)...  1.04 us
  transfers between devices with their start and end apart: 8, of which 4 were waited for; matrix products, arithmetic and copies ran while one was open for 0% of the time, Pallas kernels for 14%

profile of v22, /device:TPU:0, one launch (start us, length us, event | category | flops | bytes accessed | tf_op | source)
XLA Modules:
  0.0 23.6 jit_solution(6766546732503537917)
XLA Ops:
  0.6 1.0 %shard_map.135 = bf16[192,128]{1,0:T(8,128)(2,1)S(1)} custom-call(bf16[32,8,64]{2,1,0:T(8,128)(2,1)} %msa_ref.1, s32[8,32]{1,0:T(8,128)} %bitcast.23, bf16[8,8,128]{2,1,0:T(8,128)(2,1)} %pair_ref.1), custom_call_target="tpu_custom_call" | custom-call | tf_op jit(solution)/shard_map/pallas_call | solution.py:516
  1.7 4.1 %collective-permute-start = (bf16[192,128]{1,0:T(8,128)(2,1)S(1)}, bf16[192,128]{1,0:T(8,128)(2,1)S(1)}, u32[]{:S(2)}, u32[]{:S(2)}) collective-permute-start(bf16[192,128]{1,0:T(8,128)(2,1)S(1)} %shard_map.135), channel_id=1, source_target_pairs={{0,2},{1,3},{2,0},{3,1},{4,6},{5,7},{6,4},{7,5},{8,10},{9,11},{10,... | collective-permute-start | bytes 147464 | tf_op jit(solution)/shard_map/ppermute | solution.py:523
  5.8 1.3 %collective-permute-start.2 = (bf16[192,128]{1,0:T(8,128)(2,1)S(1)}, bf16[192,128]{1,0:T(8,128)(2,1)S(1)}, u32[]{:S(2)}, u32[]{:S(2)}) collective-permute-start(bf16[192,128]{1,0:T(8,128)(2,1)S(1)} %shard_map.135), channel_id=1, source_target_pairs={{0,3},{1,2},{2,1},{3,0},{4,7},{5,6},{6,5},{7,4},{8,11},{9,10},{10,... | collective-permute-start | bytes 147464 | tf_op jit(solution)/shard_map/ppermute | solution.py:523
  7.1 0.2 collective-permute-start.1
  7.4 1.0 %collective-permute-done = bf16[192,128]{1,0:T(8,128)(2,1)S(1)} collective-permute-done((bf16[192,128]{1,0:T(8,128)(2,1)S(1)}, bf16[192,128]{1,0:T(8,128)(2,1)S(1)}, u32[]{:S(2)}, u32[]{:S(2)}) %collective-permute-start) | collective-permute-done | bytes 49184 | tf_op jit(solution)/shard_map/ppermute | solution.py:523
  8.4 1.8 %collective-permute-start.3 = (bf16[2,192,128]{2,1,0:T(8,128)(2,1)S(1)}, bf16[2,192,128]{2,1,0:T(8,128)(2,1)S(1)}, u32[]{:S(2)}, u32[]{:S(2)}) collective-permute-start(bf16[2,192,128]{2,1,0:T(8,128)(2,1)S(1)} %pad_maximum_fusion.1.front_ref), channel_id=1, source_target_pairs={{0,8},{4,12},{8,0},{12,4},{1,9},{5,13},{9,1},{13,5},{2,10},{6,14},... | collective-permute-start | bytes 294920 | tf_op jit(solution)/shard_map/ppermute | solution.py:523
  10.2 1.6 %collective-permute-done.2 = bf16[192,128]{1,0:T(8,128)(2,1)S(1)} collective-permute-done((bf16[192,128]{1,0:T(8,128)(2,1)S(1)}, bf16[192,128]{1,0:T(8,128)(2,1)S(1)}, u32[]{:S(2)}, u32[]{:S(2)}) %collective-permute-start.2) | collective-permute-done | bytes 49184 | tf_op jit(solution)/shard_map/ppermute | solution.py:523
  11.7 0.0 collective-permute-done.1
  11.8 1.6 %collective-permute-start.5 = (bf16[2,192,128]{2,1,0:T(8,128)(2,1)S(1)}, bf16[2,192,128]{2,1,0:T(8,128)(2,1)S(1)}, u32[]{:S(2)}, u32[]{:S(2)}) collective-permute-start(bf16[2,192,128]{2,1,0:T(8,128)(2,1)S(1)} %pad_maximum_fusion.2.rear_ref), channel_id=1, source_target_pairs={{0,8},{4,12},{8,0},{12,4},{1,9},{5,13},{9,1},{13,5},{2,10},{6,14},... | collective-permute-start | bytes 294920 | tf_op jit(solution)/shard_map/ppermute | solution.py:523
  13.3 1.4 %shard_map.136 = (f32[8,128]{1,0:T(8,128)S(1)}, bf16[256,256]{1,0:T(8,128)(2,1)S(1)}, bf16[512,256]{1,0:T(8,128)(2,1)S(1)}, f32[64,64]{1,0:T(8,128)S(1)}) custom-call(f32[1,64]{1,0:T(1,128)} %bitcast.24, f32[1,64]{1,0:T(1,128)} %bitcast.25, bf16[32,64]{1,0:T(8,128)(2,1)} %bitcast.21, bf16[32,64]{1,0:T(8,128)(2,1)} %bitcast.22, bf16[1024,128]{1,0:T(8,128)(2,1)} %refs_4_), custom_call_target="tpu_custom_call" | custom-call | tf_op jit(solution)/shard_map/pallas_call | solution.py:533
  14.8 0.0 collective-permute-done.3.front_ref
  14.8 0.1 collective-permute-start.7
  14.9 0.5 %collective-permute-start.4 = (bf16[2,192,128]{2,1,0:T(8,128)(2,1)S(1)}, bf16[2,192,128]{2,1,0:T(8,128)(2,1)S(1)}, u32[]{:S(2)}, u32[]{:S(2)}) collective-permute-start(bf16[2,192,128]{2,1,0:T(8,128)(2,1)S(1)} %collective-permute-done.3.front_ref), channel_id=1, source_target_pairs={{0,4},{4,0},{8,12},{12,8},{1,5},{5,1},{9,13},{13,9},{2,6},{6,2},{1... | collective-permute-start | bytes 294920 | tf_op jit(solution)/shard_map/ppermute | solution.py:523
  15.3 0.8 %shard_map.137 = (bf16[512,256]{1,0:T(8,128)(2,1)S(1)}, bf16[128,256]{1,0:T(8,128)(2,1)S(1)}, bf16[128,256]{1,0:T(8,128)(2,1)S(1)}, f32[32,8,128]{2,1,0:T(8,128)...) custom-call(s32[1]{0:T(128)} %bitcast.place_ref, ...), custom_call_target="tpu_custom_call" | custom-call | flops 1000000000 | bytes 3906250 | tf_op jit(solution)/shard_map/pallas_call | solution.py:573
  16.1 0.3 %collective-permute-done.5.rear_ref = bf16[2,192,128]{2,1,0:T(8,128)(2,1)S(1)} collective-permute-done((bf16[2,192,128]{2,1,0:T(8,128)(2,1)S(1)}, bf16[2,192,128]{2,1,0:T(8,128)(2,1)S(1)}, u32[]{:S(2)}, u32[]{:S(2)}) %collective-permute-start.5) | collective-permute-done | bytes 98336 | tf_op jit(solution)/shard_map/ppermute | solution.py:523
  16.4 0.0 collective-permute-start.6
  16.4 0.0 collective-permute-done.7.core_ref
  16.5 1.1 %shard_map.138 = (bf16[512,256]{1,0:T(8,128)(2,1)S(1)}, bf16[128,256]{1,0:T(8,128)(2,1)S(1)}, bf16[128,256]{1,0:T(8,128)(2,1)S(1)}, f32[32,8,128]{2,1,0:T(8,128)...) custom-call(s32[1]{0:T(128)} %bitcast.place_ref, ...), custom_call_target="tpu_custom_call" | custom-call | flops 1000000 | bytes 3906 | tf_op jit(solution)/shard_map/pallas_call | solution.py:573
  17.5 0.0 collective-permute-done.4.front_ref
  17.6 0.2 collective-permute-done.6.rear_ref
  17.7 5.8 %shard_map.139 = (f32[32,8,64]{2,1,0:T(8,128)}, f32[1024,128]{1,0:T(8,128)}, f32[32,64]{1,0:T(8,128)}, f32[32,64]{1,0:T(8,128)}, f32[1,64]{1,0:T(1,128)}, /*index=5*/f32[1,64]{1,0:T(1,128)}, f32[1,128]{1,0:T(1,128)}) custom-call(s32[1]{0:T(128)} %bitcast.place_ref, bf16[2,192,128]{2,1,0:T(8,128)(2,1)S(1)} %collective-permute-done.4.front_ref, ...), custom_call_target="tpu_custom_call" | custom-call | tf_op jit(solution)/shard_map/pallas_call | solution.py:591
  (3 shorter events, 0.0 us)
Async XLA Ops:
  1.7 6.7 %collective-permute-start = (bf16[192,128]{1,0:T(8,128)(2,1)S(1)}, bf16[192,128]{1,0:T(8,128)(2,1)S(1)}, u32[]{:S(2)}, u32[]{:S(2)}) collective-permute-start(bf16[192,128]{1,0:T(8,128)(2,1)S(1)} %shard_map.135), channel_id=1, source_target_pairs={{0,2},{1,3},{2,0},{3,1},{4,6},{5,7},{6,4},{7,5},{8,10},{9,11},{10,... | collective-permute-start | bytes 147464 | tf_op jit(solution)/shard_map/ppermute | solution.py:523
  5.8 6.0 %collective-permute-start.2 = (bf16[192,128]{1,0:T(8,128)(2,1)S(1)}, bf16[192,128]{1,0:T(8,128)(2,1)S(1)}, u32[]{:S(2)}, u32[]{:S(2)}) collective-permute-start(bf16[192,128]{1,0:T(8,128)(2,1)S(1)} %shard_map.135), channel_id=1, source_target_pairs={{0,3},{1,2},{2,1},{3,0},{4,7},{5,6},{6,5},{7,4},{8,11},{9,10},{10,... | collective-permute-start | bytes 147464 | tf_op jit(solution)/shard_map/ppermute | solution.py:523
  7.1 4.6 %collective-permute-start.1 = (bf16[192,128]{1,0:T(8,128)(2,1)S(1)}, bf16[192,128]{1,0:T(8,128)(2,1)S(1)}, u32[]{:S(2)}, u32[]{:S(2)}) collective-permute-start(bf16[192,128]{1,0:T(8,128)(2,1)S(1)} %shard_map.135), channel_id=1, source_target_pairs={{0,1},{1,0},{2,3},{3,2},{4,5},{5,4},{6,7},{7,6},{8,9},{9,8},{10,11... | collective-permute-start | bytes 147464 | tf_op jit(solution)/shard_map/ppermute | solution.py:523
  8.4 6.4 %collective-permute-start.3 = (bf16[2,192,128]{2,1,0:T(8,128)(2,1)S(1)}, bf16[2,192,128]{2,1,0:T(8,128)(2,1)S(1)}, u32[]{:S(2)}, u32[]{:S(2)}) collective-permute-start(bf16[2,192,128]{2,1,0:T(8,128)(2,1)S(1)} %pad_maximum_fusion.1.front_ref), channel_id=1, source_target_pairs={{0,8},{4,12},{8,0},{12,4},{1,9},{5,13},{9,1},{13,5},{2,10},{6,14},... | collective-permute-start | bytes 294920 | tf_op jit(solution)/shard_map/ppermute | solution.py:523
  11.8 4.7 %collective-permute-start.5 = (bf16[2,192,128]{2,1,0:T(8,128)(2,1)S(1)}, bf16[2,192,128]{2,1,0:T(8,128)(2,1)S(1)}, u32[]{:S(2)}, u32[]{:S(2)}) collective-permute-start(bf16[2,192,128]{2,1,0:T(8,128)(2,1)S(1)} %pad_maximum_fusion.2.rear_ref), channel_id=1, source_target_pairs={{0,8},{4,12},{8,0},{12,4},{1,9},{5,13},{9,1},{13,5},{2,10},{6,14},... | collective-permute-start | bytes 294920 | tf_op jit(solution)/shard_map/ppermute | solution.py:523
  14.8 1.7 %collective-permute-start.7 = (bf16[4,192,128]{2,1,0:T(8,128)(2,1)S(1)}, bf16[4,192,128]{2,1,0:T(8,128)(2,1)S(1)}, u32[]{:S(2)}, u32[]{:S(2)}) collective-permute-start(bf16[4,192,128]{2,1,0:T(8,128)(2,1)S(1)} %pad_maximum_fusion), channel_id=1, source_target_pairs={{0,4},{4,0},{8,12},{12,8},{1,5},{5,1},{9,13},{13,9},{2,6},{6,2},{1... | collective-permute-start | bytes 589832 | tf_op jit(solution)/shard_map/ppermute | solution.py:523
  14.9 2.7 %collective-permute-start.4 = (bf16[2,192,128]{2,1,0:T(8,128)(2,1)S(1)}, bf16[2,192,128]{2,1,0:T(8,128)(2,1)S(1)}, u32[]{:S(2)}, u32[]{:S(2)}) collective-permute-start(bf16[2,192,128]{2,1,0:T(8,128)(2,1)S(1)} %collective-permute-done.3.front_ref), channel_id=1, source_target_pairs={{0,4},{4,0},{8,12},{12,8},{1,5},{5,1},{9,13},{13,9},{2,6},{6,2},{1... | collective-permute-start | bytes 294920 | tf_op jit(solution)/shard_map/ppermute | solution.py:523
  16.4 1.3 %collective-permute-start.6 = (bf16[2,192,128]{2,1,0:T(8,128)(2,1)S(1)}, bf16[2,192,128]{2,1,0:T(8,128)(2,1)S(1)}, u32[]{:S(2)}, u32[]{:S(2)}) collective-permute-start(bf16[2,192,128]{2,1,0:T(8,128)(2,1)S(1)} %collective-permute-done.5.rear_ref), channel_id=1, source_target_pairs={{0,4},{4,0},{8,12},{12,8},{1,5},{5,1},{9,13},{13,9},{2,6},{6,2},{1... | collective-permute-start | bytes 294920 | tf_op jit(solution)/shard_map/ppermute | solution.py:523

commit v23 on v22

--- a/solution.py
+++ b/solution.py
@@ -257,7 +257,7 @@
 
 
 def stage_steps(
-    n_col, a, place_ref, set_refs, norm_ref, back_ref, final_ref,
+    n_col, a, last, place_ref, set_refs, norm_ref, back_ref, final_ref,
     rhs_out, left_out, leftt_out, rightt_out, grad_out, pair_out, found_out, *rest
 ):
     *own_out, turn_scr = rest
@@ -302,7 +302,8 @@
                 grad_out[rows : rows + 32, 128 * q : 128 * q + 128] = even
                 grad_out[rows + 32 : rows + 64, 128 * q : 128 * q + 128] = odd
 
-    grad_piece(0)
+    if not last:
+        grad_piece(0)
     yield
 
     normal = jnp.where(present, normed * gain + offset, 0.0).astype(BF)
@@ -321,10 +322,14 @@
                 [both[32 * k : 32 * k + 32], both[32 * k + 64 : 32 * k + 96]], axis=1
             ).astype(BF)
     yield
-    grad_piece(1)
+    if not last:
+        grad_piece(1)
     yield
     for e in range(32):
         rightt_out[e] = turn_scr[pl.ds(e, 8, stride=32), :]
+    if last:
+        grad_piece(0)
+        grad_piece(1)
 
 
 def stage_kernel(*arguments):
@@ -333,14 +338,14 @@
 
 
 def own_kernel(n_col, place_ref, front_ref, rear_ref, norm_ref, back_ref, final_ref, *rest):
-    stage_kernel(n_col, 0, place_ref, (front_ref, rear_ref), norm_ref, back_ref, final_ref, *rest)
+    stage_kernel(n_col, 0, False, place_ref, (front_ref, rear_ref), norm_ref, back_ref, final_ref, *rest)
 
 
 def pair_kernel(n_col, place_ref, core_ref, front_ref, rear_ref, norm_ref, back_ref, final_ref, *rest):
     common = (norm_ref, back_ref, final_ref)
     both = (
-        stage_steps(n_col, 1, place_ref, (core_ref,), *common, *rest[:7], rest[14]),
-        stage_steps(n_col, 2, place_ref, (front_ref, rear_ref), *common, *rest[7:14], rest[15]),
+        stage_steps(n_col, 1, False, place_ref, (core_ref,), *common, *rest[:7], rest[14]),
+        stage_steps(n_col, 2, False, place_ref, (front_ref, rear_ref), *common, *rest[7:14], rest[15]),
     )
     for _ in zip_longest(*both):
         pass
@@ -355,11 +360,10 @@
         final_out, out_sem, turn_scr,
     ) = refs[7 * (n_row - 1) : -7]
     stages.append(refs[-7:])
-    last = stage_steps(
-        n_col, n_row - 1, place_ref, (front_ref, rear_ref),
+    stage_kernel(
+        n_col, n_row - 1, True, place_ref, (front_ref, rear_ref),
         norm_ref, back_ref, final_ref, *stages[-1], turn_scr,
     )
-    next(last)
     gain = norm_ref[0:1, :]
     averager = averager_of()
     lane = lax.broadcasted_iota(jnp.int32, (128, 128), 1)
@@ -369,26 +373,19 @@
     mask = jnp.where((lane % 2 == 0) == (lane < 64), found, turned)
     mask_t = mask.T
 
-    mask_bf = mask.astype(BF)
-    share = (1.0 / (mm_tn(mask_bf, mask_bf)[0:32] + 0.001)).astype(BF)
-    for a in range(n_row):
-        if a < n_row - 1:
-            next(last)
-        else:
-            for _ in last:
-                pass
-        for i in range(8 * a, 8 * a + 8):
-            at = 32 * (i % 8)
-            for q in range(8):
-                grad_scr[32 * i : 32 * i + 32, 128 * q : 128 * q + 128] = (
-                    stages[a][4][at : at + 32, 128 * q : 128 * q + 128] * share[i : i + 1]
-                )
-
     for e in range(32):
         right_scr[32 * e : 32 * e + 32, :] = jnp.concatenate(
             [stage[3][e] for stage in stages], axis=0
         ).astype(BF)
 
+    mask_bf = mask.astype(BF)
+    share = (1.0 / (mm_tn(mask_bf, mask_bf)[0:32] + 0.001)).astype(BF)
+    for i in range(32):
+        a, at = i // 8, 32 * (i % 8)
+        for q in range(8):
+            grad_scr[32 * i : 32 * i + 32, 128 * q : 128 * q + 128] = (
+                stages[a][4][at : at + 32, 128 * q : 128 * q + 128] * share[i : i + 1]
+            )
     left = jnp.concatenate([stage[1][...] for stage in stages], axis=1)
     right_grad = mm(left, grad_scr[...])
     left_grad = mm(grad_scr[...], right_scr[...])

time: 23.8 us -> 23.5 us (0.987)
  Pallas kernels: 10.1 us -> 9.79 us
    pallas_call x1, Pallas kernels: 5.84 us -> 5.51 us  [gathered_body(): pl.pallas_call(functools.partial(part_kernel, n_row, n_col), out_shape=(s...]
where the time goes in v23:
time: 23.5 us; the launch traced here: 23.3 us
  Pallas kernels  9.79 us (42%)
  starting transfers between devices  9.57 us (41%)
  waiting for transfers between devices  3.14 us (13%)
  between operations  0.71 us (3%)
    ppermute x8, starting transfers between devices, over(): return lax.ppermute(array, axis, [(k, k ^ step) for k in range(size)])  9.57 us
    pallas_call x1, Pallas kernels, gathered_body(): pl.pallas_call(functools.partial(part_kernel, n_row, n_col), out_shape=(s...  5.51 us
    ppermute x8, waiting for transfers between devices, over(): return lax.ppermute(array, axis, [(k, k ^ step) for k in range(size)])  3.14 us
    pallas_call x2, Pallas kernels, stages_of(): pl.pallas_call(functools.partial(kernel, n_col), out_shape=tuple(outs), i...  1.85 us
    pallas_call x1, Pallas kernels, gathered_body(): pl.pallas_call(weights_kernel, out_shape=(held(8, 128), held_bf(256, 256)...  1.4 us
    pallas_call x1, Pallas kernels, gathered_body(): pl.pallas_call(pack_kernel, out_shape=held_bf(192, 128), in_specs=vmem(3)...  1.04 us
  transfers between devices with their start and end apart: 8, of which 4 were waited for; matrix products, arithmetic and copies ran while one was open for 0% of the time, Pallas kernels for 14%

profile of v23, /device:TPU:0, one launch (start us, length us, event | category | flops | bytes accessed | tf_op | source)
XLA Modules:
  0.0 23.3 jit_solution(17535256053746955367)
XLA Ops:
  0.6 1.0 %shard_map.135 = bf16[192,128]{1,0:T(8,128)(2,1)S(1)} custom-call(bf16[32,8,64]{2,1,0:T(8,128)(2,1)} %msa_ref.1, s32[8,32]{1,0:T(8,128)} %bitcast.23, bf16[8,8,128]{2,1,0:T(8,128)(2,1)} %pair_ref.1), custom_call_target="tpu_custom_call" | custom-call | tf_op jit(solution)/shard_map/pallas_call | solution.py:513
  1.7 4.1 %collective-permute-start = (bf16[192,128]{1,0:T(8,128)(2,1)S(1)}, bf16[192,128]{1,0:T(8,128)(2,1)S(1)}, u32[]{:S(2)}, u32[]{:S(2)}) collective-permute-start(bf16[192,128]{1,0:T(8,128)(2,1)S(1)} %shard_map.135), channel_id=1, source_target_pairs={{0,2},{1,3},{2,0},{3,1},{4,6},{5,7},{6,4},{7,5},{8,10},{9,11},{10,... | collective-permute-start | bytes 147464 | tf_op jit(solution)/shard_map/ppermute | solution.py:520
  5.8 1.3 %collective-permute-start.2 = (bf16[192,128]{1,0:T(8,128)(2,1)S(1)}, bf16[192,128]{1,0:T(8,128)(2,1)S(1)}, u32[]{:S(2)}, u32[]{:S(2)}) collective-permute-start(bf16[192,128]{1,0:T(8,128)(2,1)S(1)} %shard_map.135), channel_id=1, source_target_pairs={{0,3},{1,2},{2,1},{3,0},{4,7},{5,6},{6,5},{7,4},{8,11},{9,10},{10,... | collective-permute-start | bytes 147464 | tf_op jit(solution)/shard_map/ppermute | solution.py:520
  7.1 0.2 collective-permute-start.1
  7.4 1.0 %collective-permute-done = bf16[192,128]{1,0:T(8,128)(2,1)S(1)} collective-permute-done((bf16[192,128]{1,0:T(8,128)(2,1)S(1)}, bf16[192,128]{1,0:T(8,128)(2,1)S(1)}, u32[]{:S(2)}, u32[]{:S(2)}) %collective-permute-start) | collective-permute-done | bytes 49184 | tf_op jit(solution)/shard_map/ppermute | solution.py:520
  8.4 1.8 %collective-permute-start.3 = (bf16[2,192,128]{2,1,0:T(8,128)(2,1)S(1)}, bf16[2,192,128]{2,1,0:T(8,128)(2,1)S(1)}, u32[]{:S(2)}, u32[]{:S(2)}) collective-permute-start(bf16[2,192,128]{2,1,0:T(8,128)(2,1)S(1)} %pad_maximum_fusion.1.front_ref), channel_id=1, source_target_pairs={{0,8},{4,12},{8,0},{12,4},{1,9},{5,13},{9,1},{13,5},{2,10},{6,14},... | collective-permute-start | bytes 294920 | tf_op jit(solution)/shard_map/ppermute | solution.py:520
  10.2 1.6 %collective-permute-done.2 = bf16[192,128]{1,0:T(8,128)(2,1)S(1)} collective-permute-done((bf16[192,128]{1,0:T(8,128)(2,1)S(1)}, bf16[192,128]{1,0:T(8,128)(2,1)S(1)}, u32[]{:S(2)}, u32[]{:S(2)}) %collective-permute-start.2) | collective-permute-done | bytes 49184 | tf_op jit(solution)/shard_map/ppermute | solution.py:520
  11.7 0.0 collective-permute-done.1
  11.8 1.6 %collective-permute-start.5 = (bf16[2,192,128]{2,1,0:T(8,128)(2,1)S(1)}, bf16[2,192,128]{2,1,0:T(8,128)(2,1)S(1)}, u32[]{:S(2)}, u32[]{:S(2)}) collective-permute-start(bf16[2,192,128]{2,1,0:T(8,128)(2,1)S(1)} %pad_maximum_fusion.2.rear_ref), channel_id=1, source_target_pairs={{0,8},{4,12},{8,0},{12,4},{1,9},{5,13},{9,1},{13,5},{2,10},{6,14},... | collective-permute-start | bytes 294920 | tf_op jit(solution)/shard_map/ppermute | solution.py:520
  13.3 1.4 %shard_map.136 = (f32[8,128]{1,0:T(8,128)S(1)}, bf16[256,256]{1,0:T(8,128)(2,1)S(1)}, bf16[512,256]{1,0:T(8,128)(2,1)S(1)}, f32[64,64]{1,0:T(8,128)S(1)}) custom-call(f32[1,64]{1,0:T(1,128)} %bitcast.24, f32[1,64]{1,0:T(1,128)} %bitcast.25, bf16[32,64]{1,0:T(8,128)(2,1)} %bitcast.21, bf16[32,64]{1,0:T(8,128)(2,1)} %bitcast.22, bf16[1024,128]{1,0:T(8,128)(2,1)} %refs_4_), custom_call_target="tpu_custom_call" | custom-call | tf_op jit(solution)/shard_map/pallas_call | solution.py:530
  14.8 0.0 collective-permute-done.3.front_ref
  14.8 0.1 collective-permute-start.7
  14.9 0.5 %collective-permute-start.4 = (bf16[2,192,128]{2,1,0:T(8,128)(2,1)S(1)}, bf16[2,192,128]{2,1,0:T(8,128)(2,1)S(1)}, u32[]{:S(2)}, u32[]{:S(2)}) collective-permute-start(bf16[2,192,128]{2,1,0:T(8,128)(2,1)S(1)} %collective-permute-done.3.front_ref), channel_id=1, source_target_pairs={{0,4},{4,0},{8,12},{12,8},{1,5},{5,1},{9,13},{13,9},{2,6},{6,2},{1... | collective-permute-start | bytes 294920 | tf_op jit(solution)/shard_map/ppermute | solution.py:520
  15.3 0.8 %shard_map.137 = (bf16[512,256]{1,0:T(8,128)(2,1)S(1)}, bf16[128,256]{1,0:T(8,128)(2,1)S(1)}, bf16[128,256]{1,0:T(8,128)(2,1)S(1)}, f32[32,8,128]{2,1,0:T(8,128)...) custom-call(s32[1]{0:T(128)} %bitcast.place_ref, ...), custom_call_target="tpu_custom_call" | custom-call | flops 1000000000 | bytes 3906250 | tf_op jit(solution)/shard_map/pallas_call | solution.py:570
  16.1 0.3 %collective-permute-done.5.rear_ref = bf16[2,192,128]{2,1,0:T(8,128)(2,1)S(1)} collective-permute-done((bf16[2,192,128]{2,1,0:T(8,128)(2,1)S(1)}, bf16[2,192,128]{2,1,0:T(8,128)(2,1)S(1)}, u32[]{:S(2)}, u32[]{:S(2)}) %collective-permute-start.5) | collective-permute-done | bytes 98336 | tf_op jit(solution)/shard_map/ppermute | solution.py:520
  16.4 0.0 collective-permute-start.6
  16.4 0.0 collective-permute-done.7.core_ref
  16.5 1.1 %shard_map.138 = (bf16[512,256]{1,0:T(8,128)(2,1)S(1)}, bf16[128,256]{1,0:T(8,128)(2,1)S(1)}, bf16[128,256]{1,0:T(8,128)(2,1)S(1)}, f32[32,8,128]{2,1,0:T(8,128)...) custom-call(s32[1]{0:T(128)} %bitcast.place_ref, ...), custom_call_target="tpu_custom_call" | custom-call | flops 1000000 | bytes 3906 | tf_op jit(solution)/shard_map/pallas_call | solution.py:570
  17.5 0.0 collective-permute-done.4.front_ref
  17.6 0.2 collective-permute-done.6.rear_ref
  17.7 5.5 %shard_map.139 = (f32[32,8,64]{2,1,0:T(8,128)}, f32[1024,128]{1,0:T(8,128)}, f32[32,64]{1,0:T(8,128)}, f32[32,64]{1,0:T(8,128)}, f32[1,64]{1,0:T(1,128)}, /*index=5*/f32[1,64]{1,0:T(1,128)}, f32[1,128]{1,0:T(1,128)}) custom-call(s32[1]{0:T(128)} %bitcast.place_ref, bf16[2,192,128]{2,1,0:T(8,128)(2,1)S(1)} %collective-permute-done.4.front_ref, ...), custom_call_target="tpu_custom_call" | custom-call | tf_op jit(solution)/shard_map/pallas_call | solution.py:588
  (3 shorter events, 0.0 us)
Async XLA Ops:
  1.7 6.7 %collective-permute-start = (bf16[192,128]{1,0:T(8,128)(2,1)S(1)}, bf16[192,128]{1,0:T(8,128)(2,1)S(1)}, u32[]{:S(2)}, u32[]{:S(2)}) collective-permute-start(bf16[192,128]{1,0:T(8,128)(2,1)S(1)} %shard_map.135), channel_id=1, source_target_pairs={{0,2},{1,3},{2,0},{3,1},{4,6},{5,7},{6,4},{7,5},{8,10},{9,11},{10,... | collective-permute-start | bytes 147464 | tf_op jit(solution)/shard_map/ppermute | solution.py:520
  5.8 6.0 %collective-permute-start.2 = (bf16[192,128]{1,0:T(8,128)(2,1)S(1)}, bf16[192,128]{1,0:T(8,128)(2,1)S(1)}, u32[]{:S(2)}, u32[]{:S(2)}) collective-permute-start(bf16[192,128]{1,0:T(8,128)(2,1)S(1)} %shard_map.135), channel_id=1, source_target_pairs={{0,3},{1,2},{2,1},{3,0},{4,7},{5,6},{6,5},{7,4},{8,11},{9,10},{10,... | collective-permute-start | bytes 147464 | tf_op jit(solution)/shard_map/ppermute | solution.py:520
  7.1 4.6 %collective-permute-start.1 = (bf16[192,128]{1,0:T(8,128)(2,1)S(1)}, bf16[192,128]{1,0:T(8,128)(2,1)S(1)}, u32[]{:S(2)}, u32[]{:S(2)}) collective-permute-start(bf16[192,128]{1,0:T(8,128)(2,1)S(1)} %shard_map.135), channel_id=1, source_target_pairs={{0,1},{1,0},{2,3},{3,2},{4,5},{5,4},{6,7},{7,6},{8,9},{9,8},{10,11... | collective-permute-start | bytes 147464 | tf_op jit(solution)/shard_map/ppermute | solution.py:520
  8.4 6.4 %collective-permute-start.3 = (bf16[2,192,128]{2,1,0:T(8,128)(2,1)S(1)}, bf16[2,192,128]{2,1,0:T(8,128)(2,1)S(1)}, u32[]{:S(2)}, u32[]{:S(2)}) collective-permute-start(bf16[2,192,128]{2,1,0:T(8,128)(2,1)S(1)} %pad_maximum_fusion.1.front_ref), channel_id=1, source_target_pairs={{0,8},{4,12},{8,0},{12,4},{1,9},{5,13},{9,1},{13,5},{2,10},{6,14},... | collective-permute-start | bytes 294920 | tf_op jit(solution)/shard_map/ppermute | solution.py:520
  11.8 4.7 %collective-permute-start.5 = (bf16[2,192,128]{2,1,0:T(8,128)(2,1)S(1)}, bf16[2,192,128]{2,1,0:T(8,128)(2,1)S(1)}, u32[]{:S(2)}, u32[]{:S(2)}) collective-permute-start(bf16[2,192,128]{2,1,0:T(8,128)(2,1)S(1)} %pad_maximum_fusion.2.rear_ref), channel_id=1, source_target_pairs={{0,8},{4,12},{8,0},{12,4},{1,9},{5,13},{9,1},{13,5},{2,10},{6,14},... | collective-permute-start | bytes 294920 | tf_op jit(solution)/shard_map/ppermute | solution.py:520
  14.8 1.7 %collective-permute-start.7 = (bf16[4,192,128]{2,1,0:T(8,128)(2,1)S(1)}, bf16[4,192,128]{2,1,0:T(8,128)(2,1)S(1)}, u32[]{:S(2)}, u32[]{:S(2)}) collective-permute-start(bf16[4,192,128]{2,1,0:T(8,128)(2,1)S(1)} %pad_maximum_fusion), channel_id=1, source_target_pairs={{0,4},{4,0},{8,12},{12,8},{1,5},{5,1},{9,13},{13,9},{2,6},{6,2},{1... | collective-permute-start | bytes 589832 | tf_op jit(solution)/shard_map/ppermute | solution.py:520
  14.9 2.7 %collective-permute-start.4 = (bf16[2,192,128]{2,1,0:T(8,128)(2,1)S(1)}, bf16[2,192,128]{2,1,0:T(8,128)(2,1)S(1)}, u32[]{:S(2)}, u32[]{:S(2)}) collective-permute-start(bf16[2,192,128]{2,1,0:T(8,128)(2,1)S(1)} %collective-permute-done.3.front_ref), channel_id=1, source_target_pairs={{0,4},{4,0},{8,12},{12,8},{1,5},{5,1},{9,13},{13,9},{2,6},{6,2},{1... | collective-permute-start | bytes 294920 | tf_op jit(solution)/shard_map/ppermute | solution.py:520
  16.4 1.3 %collective-permute-start.6 = (bf16[2,192,128]{2,1,0:T(8,128)(2,1)S(1)}, bf16[2,192,128]{2,1,0:T(8,128)(2,1)S(1)}, u32[]{:S(2)}, u32[]{:S(2)}) collective-permute-start(bf16[2,192,128]{2,1,0:T(8,128)(2,1)S(1)} %collective-permute-done.5.rear_ref), channel_id=1, source_target_pairs={{0,4},{4,0},{8,12},{12,8},{1,5},{5,1},{9,13},{13,9},{2,6},{6,2},{1... | collective-permute-start | bytes 294920 | tf_op jit(solution)/shard_map/ppermute | solution.py:520

commit v24 on v23

--- a/solution.py
+++ b/solution.py
@@ -309,13 +309,19 @@
     normal = jnp.where(present, normed * gain + offset, 0.0).astype(BF)
     rhs_out[:, 0:128] = normal
     rhs_out[:, 128:256] = normed.astype(BF)
+    masked = jnp.concatenate(
+        [
+            jnp.concatenate([normal[128 * g : 128 * g + 128] for g in (2 * h, 2 * h + 1)], axis=1)
+            for h in range(2)
+        ],
+        axis=0,
+    )
+    lefts = mm_nt(masked, back_ref[:128, :]).astype(BF)
+    sides = mm_nt(back_ref[...], masked)
     for h in range(2):
-        masked = jnp.concatenate(
-            [normal[128 * g : 128 * g + 128] for g in (2 * h, 2 * h + 1)], axis=1
-        )
         at = slice(128 * h, 128 * h + 128)
-        left_out[:, at] = mm_nt(masked, back_ref[:128, :]).astype(BF)
-        both = mm_nt(back_ref[...], masked)
+        left_out[:, at] = lefts[at]
+        both = sides[:, at]
         turn_scr[at, :] = both[128:]
         for k in range(2):
             leftt_out[64 * h + 32 * k : 64 * h + 32 * k + 32, :] = jnp.concatenate(
@@ -408,18 +414,14 @@
             [part[8 * t : 8 * t + 8] for part in right_in], axis=0
         ).astype(BF)
 
-    bias = jnp.zeros((1, 128), F32)
-    ones = jnp.ones((128, 128), BF)
-    for p in range(8):
-        both_on = jnp.concatenate(
-            [mask_t[0:32] * mask_t[i : i + 1] for i in range(4 * p, 4 * p + 4)], axis=0
-        ).astype(BF)
-        counts = mm(both_on, ones)
-        pair = stages[p // 2][5][4 * (p % 2) : 4 * (p % 2) + 4]
-        scaled = pair.reshape(128, 128) / (counts + 0.001)
-        bias = bias + jnp.sum(scaled, axis=0, keepdims=True)
-        scaled_scr[128 * p : 128 * p + 128, :] = scaled.astype(BF)
-    bias_out[...] = bias
+    both_on = jnp.concatenate(
+        [mask_t[0:32] * mask_t[i : i + 1] for i in range(32)], axis=0
+    ).astype(BF)
+    counts = mm(both_on, jnp.ones((128, 128), BF))
+    pair = jnp.concatenate([stage[5][...].reshape(256, 128) for stage in stages], axis=0)
+    scaled = pair / (counts + 0.001)
+    scaled_scr[...] = scaled.astype(BF)
+    bias_out[...] = jnp.sum(scaled, axis=0, keepdims=True)
 
     left_t = jnp.concatenate([stage[2][...] for stage in stages], axis=0)
     for n in range(8):
@@ -462,17 +464,29 @@
     )
     offset_out[...] = jnp.sum(first * left_sum + second * right_sum, axis=0, keepdims=True)
 
-    d_hat = []
-    for h in range(2):
-        sides = [
+    grads = jnp.concatenate(
+        [
             jnp.concatenate(
-                [all_scr[row : row + 64, 128 * g : 128 * g + 128] for g in (2 * h, 2 * h + 1)], axis=0
+                [
+                    all_scr[row : row + 64, 128 * g : 128 * g + 128]
+                    for row in (0, 64)
+                    for g in (2 * h, 2 * h + 1)
+                ],
+                axis=0,
             )
-            for row in (0, 64)
-        ]
-        d_normal = mm_tn(jnp.concatenate(sides, axis=0), back_ref[...])
-        d_hat += [d_normal[0:32, 0:128] * gain, d_normal[0:32, 128:256] * gain]
-    d_hat = jnp.concatenate(d_hat, axis=0)
+            for h in range(2)
+        ],
+        axis=1,
+    )
+    d_normal = mm_tn(grads, back_ref[...])
+    d_hat = jnp.concatenate(
+        [
+            d_normal[128 * h : 128 * h + 32, 128 * half : 128 * half + 128] * gain
+            for h in range(2)
+            for half in range(2)
+        ],
+        axis=0,
+    )
     normed = normed_ref[...]
     means = mm(jnp.concatenate([d_hat, d_hat * normed], axis=0).astype(BF), averager)
     result = inverse_ref[...] * (d_hat - means[:128] - normed * means[128:])

time: 23.5 us -> 23.4 us (level)
  transfers between devices with their start and end apart: 8 -> 8, of which waited for: 4 -> 4; matrix products, arithmetic and copies ran while one was open for 0% -> 0% of each run, Pallas kernels for 14% -> 13%
where the time goes in v24:
time: 23.4 us; the launch traced here: 23.2 us
  Pallas kernels  9.57 us (41%)
  starting transfers between devices  9.57 us (41%)
  waiting for transfers between devices  3.3 us (14%)
  between operations  0.71 us (3%)
    ppermute x8, starting transfers between devices, over(): return lax.ppermute(array, axis, [(k, k ^ step) for k in range(size)])  9.57 us
    pallas_call x1, Pallas kernels, gathered_body(): pl.pallas_call(functools.partial(part_kernel, n_row, n_col), out_shape=(s...  5.45 us
    ppermute x8, waiting for transfers between devices, over(): return lax.ppermute(array, axis, [(k, k ^ step) for k in range(size)])  3.3 us
    pallas_call x2, Pallas kernels, stages_of(): pl.pallas_call(functools.partial(kernel, n_col), out_shape=tuple(outs), i...  1.68 us
    pallas_call x1, Pallas kernels, gathered_body(): pl.pallas_call(weights_kernel, out_shape=(held(8, 128), held_bf(256, 256)...  1.4 us
    pallas_call x1, Pallas kernels, gathered_body(): pl.pallas_call(pack_kernel, out_shape=held_bf(192, 128), in_specs=vmem(3)...  1.04 us
  transfers between devices with their start and end apart: 8, of which 4 were waited for; matrix products, arithmetic and copies ran while one was open for 0% of the time, Pallas kernels for 13%

profile of v24, /device:TPU:0, one launch (start us, length us, event | category | flops | bytes accessed | tf_op | source)
XLA Modules:
  0.0 23.2 jit_solution(11791587660748598395)
XLA Ops:
  0.6 1.0 %shard_map.135 = bf16[192,128]{1,0:T(8,128)(2,1)S(1)} custom-call(bf16[32,8,64]{2,1,0:T(8,128)(2,1)} %msa_ref.1, s32[8,32]{1,0:T(8,128)} %bitcast.23, bf16[8,8,128]{2,1,0:T(8,128)(2,1)} %pair_ref.1), custom_call_target="tpu_custom_call" | custom-call | tf_op jit(solution)/shard_map/pallas_call | solution.py:527
  1.7 4.1 %collective-permute-start = (bf16[192,128]{1,0:T(8,128)(2,1)S(1)}, bf16[192,128]{1,0:T(8,128)(2,1)S(1)}, u32[]{:S(2)}, u32[]{:S(2)}) collective-permute-start(bf16[192,128]{1,0:T(8,128)(2,1)S(1)} %shard_map.135), channel_id=1, source_target_pairs={{0,2},{1,3},{2,0},{3,1},{4,6},{5,7},{6,4},{7,5},{8,10},{9,11},{10,... | collective-permute-start | bytes 147464 | tf_op jit(solution)/shard_map/ppermute | solution.py:534
  5.8 1.3 %collective-permute-start.2 = (bf16[192,128]{1,0:T(8,128)(2,1)S(1)}, bf16[192,128]{1,0:T(8,128)(2,1)S(1)}, u32[]{:S(2)}, u32[]{:S(2)}) collective-permute-start(bf16[192,128]{1,0:T(8,128)(2,1)S(1)} %shard_map.135), channel_id=1, source_target_pairs={{0,3},{1,2},{2,1},{3,0},{4,7},{5,6},{6,5},{7,4},{8,11},{9,10},{10,... | collective-permute-start | bytes 147464 | tf_op jit(solution)/shard_map/ppermute | solution.py:534
  7.1 0.2 collective-permute-start.1
  7.4 1.0 %collective-permute-done = bf16[192,128]{1,0:T(8,128)(2,1)S(1)} collective-permute-done((bf16[192,128]{1,0:T(8,128)(2,1)S(1)}, bf16[192,128]{1,0:T(8,128)(2,1)S(1)}, u32[]{:S(2)}, u32[]{:S(2)}) %collective-permute-start) | collective-permute-done | bytes 49184 | tf_op jit(solution)/shard_map/ppermute | solution.py:534
  8.4 1.8 %collective-permute-start.3 = (bf16[2,192,128]{2,1,0:T(8,128)(2,1)S(1)}, bf16[2,192,128]{2,1,0:T(8,128)(2,1)S(1)}, u32[]{:S(2)}, u32[]{:S(2)}) collective-permute-start(bf16[2,192,128]{2,1,0:T(8,128)(2,1)S(1)} %pad_maximum_fusion.1.front_ref), channel_id=1, source_target_pairs={{0,8},{4,12},{8,0},{12,4},{1,9},{5,13},{9,1},{13,5},{2,10},{6,14},... | collective-permute-start | bytes 294920 | tf_op jit(solution)/shard_map/ppermute | solution.py:534
  10.2 1.6 %collective-permute-done.2 = bf16[192,128]{1,0:T(8,128)(2,1)S(1)} collective-permute-done((bf16[192,128]{1,0:T(8,128)(2,1)S(1)}, bf16[192,128]{1,0:T(8,128)(2,1)S(1)}, u32[]{:S(2)}, u32[]{:S(2)}) %collective-permute-start.2) | collective-permute-done | bytes 49184 | tf_op jit(solution)/shard_map/ppermute | solution.py:534
  11.7 0.0 collective-permute-done.1
  11.8 1.6 %collective-permute-start.5 = (bf16[2,192,128]{2,1,0:T(8,128)(2,1)S(1)}, bf16[2,192,128]{2,1,0:T(8,128)(2,1)S(1)}, u32[]{:S(2)}, u32[]{:S(2)}) collective-permute-start(bf16[2,192,128]{2,1,0:T(8,128)(2,1)S(1)} %pad_maximum_fusion.2.rear_ref), channel_id=1, source_target_pairs={{0,8},{4,12},{8,0},{12,4},{1,9},{5,13},{9,1},{13,5},{2,10},{6,14},... | collective-permute-start | bytes 294920 | tf_op jit(solution)/shard_map/ppermute | solution.py:534
  13.3 1.4 %shard_map.136 = (f32[8,128]{1,0:T(8,128)S(1)}, bf16[256,256]{1,0:T(8,128)(2,1)S(1)}, bf16[512,256]{1,0:T(8,128)(2,1)S(1)}, f32[64,64]{1,0:T(8,128)S(1)}) custom-call(f32[1,64]{1,0:T(1,128)} %bitcast.24, f32[1,64]{1,0:T(1,128)} %bitcast.25, bf16[32,64]{1,0:T(8,128)(2,1)} %bitcast.21, bf16[32,64]{1,0:T(8,128)(2,1)} %bitcast.22, bf16[1024,128]{1,0:T(8,128)(2,1)} %refs_4_), custom_call_target="tpu_custom_call" | custom-call | tf_op jit(solution)/shard_map/pallas_call | solution.py:544
  14.8 0.0 collective-permute-done.3.front_ref
  14.8 0.1 collective-permute-start.7
  14.9 0.5 %collective-permute-start.4 = (bf16[2,192,128]{2,1,0:T(8,128)(2,1)S(1)}, bf16[2,192,128]{2,1,0:T(8,128)(2,1)S(1)}, u32[]{:S(2)}, u32[]{:S(2)}) collective-permute-start(bf16[2,192,128]{2,1,0:T(8,128)(2,1)S(1)} %collective-permute-done.3.front_ref), channel_id=1, source_target_pairs={{0,4},{4,0},{8,12},{12,8},{1,5},{5,1},{9,13},{13,9},{2,6},{6,2},{1... | collective-permute-start | bytes 294920 | tf_op jit(solution)/shard_map/ppermute | solution.py:534
  15.3 0.6 %shard_map.137 = (bf16[512,256]{1,0:T(8,128)(2,1)S(1)}, bf16[128,256]{1,0:T(8,128)(2,1)S(1)}, bf16[128,256]{1,0:T(8,128)(2,1)S(1)}, f32[32,8,128]{2,1,0:T(8,128)...) custom-call(s32[1]{0:T(128)} %bitcast.place_ref, ...), custom_call_target="tpu_custom_call" | custom-call | flops 1000000000 | bytes 3906250 | tf_op jit(solution)/shard_map/pallas_call | solution.py:584
  16.0 0.5 %collective-permute-done.5.rear_ref = bf16[2,192,128]{2,1,0:T(8,128)(2,1)S(1)} collective-permute-done((bf16[2,192,128]{2,1,0:T(8,128)(2,1)S(1)}, bf16[2,192,128]{2,1,0:T(8,128)(2,1)S(1)}, u32[]{:S(2)}, u32[]{:S(2)}) %collective-permute-start.5) | collective-permute-done | bytes 98336 | tf_op jit(solution)/shard_map/ppermute | solution.py:534
  16.4 0.0 collective-permute-start.6
  16.4 0.0 collective-permute-done.7.core_ref
  16.5 1.1 %shard_map.138 = (bf16[512,256]{1,0:T(8,128)(2,1)S(1)}, bf16[128,256]{1,0:T(8,128)(2,1)S(1)}, bf16[128,256]{1,0:T(8,128)(2,1)S(1)}, f32[32,8,128]{2,1,0:T(8,128)...) custom-call(s32[1]{0:T(128)} %bitcast.place_ref, ...), custom_call_target="tpu_custom_call" | custom-call | flops 1000000 | bytes 3906 | tf_op jit(solution)/shard_map/pallas_call | solution.py:584
  17.5 0.0 collective-permute-done.4.front_ref
  17.5 0.2 collective-permute-done.6.rear_ref
  17.7 5.4 %shard_map.139 = (f32[32,8,64]{2,1,0:T(8,128)}, f32[1024,128]{1,0:T(8,128)}, f32[32,64]{1,0:T(8,128)}, f32[32,64]{1,0:T(8,128)}, f32[1,64]{1,0:T(1,128)}, /*index=5*/f32[1,64]{1,0:T(1,128)}, f32[1,128]{1,0:T(1,128)}) custom-call(s32[1]{0:T(128)} %bitcast.place_ref, bf16[2,192,128]{2,1,0:T(8,128)(2,1)S(1)} %collective-permute-done.4.front_ref, ...), custom_call_target="tpu_custom_call" | custom-call | tf_op jit(solution)/shard_map/pallas_call | solution.py:602
  (3 shorter events, 0.0 us)
Async XLA Ops:
  1.7 6.7 %collective-permute-start = (bf16[192,128]{1,0:T(8,128)(2,1)S(1)}, bf16[192,128]{1,0:T(8,128)(2,1)S(1)}, u32[]{:S(2)}, u32[]{:S(2)}) collective-permute-start(bf16[192,128]{1,0:T(8,128)(2,1)S(1)} %shard_map.135), channel_id=1, source_target_pairs={{0,2},{1,3},{2,0},{3,1},{4,6},{5,7},{6,4},{7,5},{8,10},{9,11},{10,... | collective-permute-start | bytes 147464 | tf_op jit(solution)/shard_map/ppermute | solution.py:534
  5.8 6.0 %collective-permute-start.2 = (bf16[192,128]{1,0:T(8,128)(2,1)S(1)}, bf16[192,128]{1,0:T(8,128)(2,1)S(1)}, u32[]{:S(2)}, u32[]{:S(2)}) collective-permute-start(bf16[192,128]{1,0:T(8,128)(2,1)S(1)} %shard_map.135), channel_id=1, source_target_pairs={{0,3},{1,2},{2,1},{3,0},{4,7},{5,6},{6,5},{7,4},{8,11},{9,10},{10,... | collective-permute-start | bytes 147464 | tf_op jit(solution)/shard_map/ppermute | solution.py:534
  7.1 4.6 %collective-permute-start.1 = (bf16[192,128]{1,0:T(8,128)(2,1)S(1)}, bf16[192,128]{1,0:T(8,128)(2,1)S(1)}, u32[]{:S(2)}, u32[]{:S(2)}) collective-permute-start(bf16[192,128]{1,0:T(8,128)(2,1)S(1)} %shard_map.135), channel_id=1, source_target_pairs={{0,1},{1,0},{2,3},{3,2},{4,5},{5,4},{6,7},{7,6},{8,9},{9,8},{10,11... | collective-permute-start | bytes 147464 | tf_op jit(solution)/shard_map/ppermute | solution.py:534
  8.4 6.4 %collective-permute-start.3 = (bf16[2,192,128]{2,1,0:T(8,128)(2,1)S(1)}, bf16[2,192,128]{2,1,0:T(8,128)(2,1)S(1)}, u32[]{:S(2)}, u32[]{:S(2)}) collective-permute-start(bf16[2,192,128]{2,1,0:T(8,128)(2,1)S(1)} %pad_maximum_fusion.1.front_ref), channel_id=1, source_target_pairs={{0,8},{4,12},{8,0},{12,4},{1,9},{5,13},{9,1},{13,5},{2,10},{6,14},... | collective-permute-start | bytes 294920 | tf_op jit(solution)/shard_map/ppermute | solution.py:534
  11.8 4.7 %collective-permute-start.5 = (bf16[2,192,128]{2,1,0:T(8,128)(2,1)S(1)}, bf16[2,192,128]{2,1,0:T(8,128)(2,1)S(1)}, u32[]{:S(2)}, u32[]{:S(2)}) collective-permute-start(bf16[2,192,128]{2,1,0:T(8,128)(2,1)S(1)} %pad_maximum_fusion.2.rear_ref), channel_id=1, source_target_pairs={{0,8},{4,12},{8,0},{12,4},{1,9},{5,13},{9,1},{13,5},{2,10},{6,14},... | collective-permute-start | bytes 294920 | tf_op jit(solution)/shard_map/ppermute | solution.py:534
  14.8 1.7 %collective-permute-start.7 = (bf16[4,192,128]{2,1,0:T(8,128)(2,1)S(1)}, bf16[4,192,128]{2,1,0:T(8,128)(2,1)S(1)}, u32[]{:S(2)}, u32[]{:S(2)}) collective-permute-start(bf16[4,192,128]{2,1,0:T(8,128)(2,1)S(1)} %pad_maximum_fusion), channel_id=1, source_target_pairs={{0,4},{4,0},{8,12},{12,8},{1,5},{5,1},{9,13},{13,9},{2,6},{6,2},{1... | collective-permute-start | bytes 589832 | tf_op jit(solution)/shard_map/ppermute | solution.py:534
  14.9 2.7 %collective-permute-start.4 = (bf16[2,192,128]{2,1,0:T(8,128)(2,1)S(1)}, bf16[2,192,128]{2,1,0:T(8,128)(2,1)S(1)}, u32[]{:S(2)}, u32[]{:S(2)}) collective-permute-start(bf16[2,192,128]{2,1,0:T(8,128)(2,1)S(1)} %collective-permute-done.3.front_ref), channel_id=1, source_target_pairs={{0,4},{4,0},{8,12},{12,8},{1,5},{5,1},{9,13},{13,9},{2,6},{6,2},{1... | collective-permute-start | bytes 294920 | tf_op jit(solution)/shard_map/ppermute | solution.py:534
  16.4 1.3 %collective-permute-start.6 = (bf16[2,192,128]{2,1,0:T(8,128)(2,1)S(1)}, bf16[2,192,128]{2,1,0:T(8,128)(2,1)S(1)}, u32[]{:S(2)}, u32[]{:S(2)}) collective-permute-start(bf16[2,192,128]{2,1,0:T(8,128)(2,1)S(1)} %collective-permute-done.5.rear_ref), channel_id=1, source_target_pairs={{0,4},{4,0},{8,12},{12,8},{1,5},{5,1},{9,13},{13,9},{2,6},{6,2},{1... | collective-permute-start | bytes 294920 | tf_op jit(solution)/shard_map/ppermute | solution.py:534

commit v25 on v24

--- a/solution.py
+++ b/solution.py
@@ -414,14 +414,18 @@
             [part[8 * t : 8 * t + 8] for part in right_in], axis=0
         ).astype(BF)
 
-    both_on = jnp.concatenate(
-        [mask_t[0:32] * mask_t[i : i + 1] for i in range(32)], axis=0
-    ).astype(BF)
-    counts = mm(both_on, jnp.ones((128, 128), BF))
-    pair = jnp.concatenate([stage[5][...].reshape(256, 128) for stage in stages], axis=0)
-    scaled = pair / (counts + 0.001)
-    scaled_scr[...] = scaled.astype(BF)
-    bias_out[...] = jnp.sum(scaled, axis=0, keepdims=True)
+    bias = jnp.zeros((1, 128), F32)
+    ones = jnp.ones((128, 128), BF)
+    for p in range(8):
+        both_on = jnp.concatenate(
+            [mask_t[0:32] * mask_t[i : i + 1] for i in range(4 * p, 4 * p + 4)], axis=0
+        ).astype(BF)
+        counts = mm(both_on, ones)
+        pair = stages[p // 2][5][4 * (p % 2) : 4 * (p % 2) + 4]
+        scaled = pair.reshape(128, 128) / (counts + 0.001)
+        bias = bias + jnp.sum(scaled, axis=0, keepdims=True)
+        scaled_scr[128 * p : 128 * p + 128, :] = scaled.astype(BF)
+    bias_out[...] = bias
 
     left_t = jnp.concatenate([stage[2][...] for stage in stages], axis=0)
     for n in range(8):

time: 23.4 us -> 23.3 us (level)
  no operation moved by 1% of the time
where the time goes in v25:
time: 23.3 us; the launch traced here: 23.1 us
  starting transfers between devices  9.57 us (41%)
  Pallas kernels  9.46 us (41%)
  waiting for transfers between devices  3.3 us (14%)
  between operations  0.71 us (3%)
    ppermute x8, starting transfers between devices, over(): return lax.ppermute(array, axis, [(k, k ^ step) for k in range(size)])  9.57 us
    pallas_call x1, Pallas kernels, gathered_body(): pl.pallas_call(functools.partial(part_kernel, n_row, n_col), out_shape=(s...  5.34 us
    ppermute x8, waiting for transfers between devices, over(): return lax.ppermute(array, axis, [(k, k ^ step) for k in range(size)])  3.3 us
    pallas_call x2, Pallas kernels, stages_of(): pl.pallas_call(functools.partial(kernel, n_col), out_shape=tuple(outs), i...  1.68 us
    pallas_call x1, Pallas kernels, gathered_body(): pl.pallas_call(weights_kernel, out_shape=(held(8, 128), held_bf(256, 256)...  1.4 us
    pallas_call x1, Pallas kernels, gathered_body(): pl.pallas_call(pack_kernel, out_shape=held_bf(192, 128), in_specs=vmem(3)...  1.04 us
  transfers between devices with their start and end apart: 8, of which 4 were waited for; matrix products, arithmetic and copies ran while one was open for 0% of the time, Pallas kernels for 13%

profile of v25, /device:TPU:0, one launch (start us, length us, event | category | flops | bytes accessed | tf_op | source)
XLA Modules:
  0.0 23.1 jit_solution(9436122438663972216)
XLA Ops:
  0.6 1.0 %shard_map.135 = bf16[192,128]{1,0:T(8,128)(2,1)S(1)} custom-call(bf16[32,8,64]{2,1,0:T(8,128)(2,1)} %msa_ref.1, s32[8,32]{1,0:T(8,128)} %bitcast.23, bf16[8,8,128]{2,1,0:T(8,128)(2,1)} %pair_ref.1), custom_call_target="tpu_custom_call" | custom-call | tf_op jit(solution)/shard_map/pallas_call | solution.py:531
  1.7 4.1 %collective-permute-start = (bf16[192,128]{1,0:T(8,128)(2,1)S(1)}, bf16[192,128]{1,0:T(8,128)(2,1)S(1)}, u32[]{:S(2)}, u32[]{:S(2)}) collective-permute-start(bf16[192,128]{1,0:T(8,128)(2,1)S(1)} %shard_map.135), channel_id=1, source_target_pairs={{0,2},{1,3},{2,0},{3,1},{4,6},{5,7},{6,4},{7,5},{8,10},{9,11},{10,... | collective-permute-start | bytes 147464 | tf_op jit(solution)/shard_map/ppermute | solution.py:538
  5.8 1.3 %collective-permute-start.2 = (bf16[192,128]{1,0:T(8,128)(2,1)S(1)}, bf16[192,128]{1,0:T(8,128)(2,1)S(1)}, u32[]{:S(2)}, u32[]{:S(2)}) collective-permute-start(bf16[192,128]{1,0:T(8,128)(2,1)S(1)} %shard_map.135), channel_id=1, source_target_pairs={{0,3},{1,2},{2,1},{3,0},{4,7},{5,6},{6,5},{7,4},{8,11},{9,10},{10,... | collective-permute-start | bytes 147464 | tf_op jit(solution)/shard_map/ppermute | solution.py:538
  7.1 0.2 collective-permute-start.1
  7.4 1.0 %collective-permute-done = bf16[192,128]{1,0:T(8,128)(2,1)S(1)} collective-permute-done((bf16[192,128]{1,0:T(8,128)(2,1)S(1)}, bf16[192,128]{1,0:T(8,128)(2,1)S(1)}, u32[]{:S(2)}, u32[]{:S(2)}) %collective-permute-start) | collective-permute-done | bytes 49184 | tf_op jit(solution)/shard_map/ppermute | solution.py:538
  8.4 1.8 %collective-permute-start.3 = (bf16[2,192,128]{2,1,0:T(8,128)(2,1)S(1)}, bf16[2,192,128]{2,1,0:T(8,128)(2,1)S(1)}, u32[]{:S(2)}, u32[]{:S(2)}) collective-permute-start(bf16[2,192,128]{2,1,0:T(8,128)(2,1)S(1)} %pad_maximum_fusion.1.front_ref), channel_id=1, source_target_pairs={{0,8},{4,12},{8,0},{12,4},{1,9},{5,13},{9,1},{13,5},{2,10},{6,14},... | collective-permute-start | bytes 294920 | tf_op jit(solution)/shard_map/ppermute | solution.py:538
  10.2 1.6 %collective-permute-done.2 = bf16[192,128]{1,0:T(8,128)(2,1)S(1)} collective-permute-done((bf16[192,128]{1,0:T(8,128)(2,1)S(1)}, bf16[192,128]{1,0:T(8,128)(2,1)S(1)}, u32[]{:S(2)}, u32[]{:S(2)}) %collective-permute-start.2) | collective-permute-done | bytes 49184 | tf_op jit(solution)/shard_map/ppermute | solution.py:538
  11.7 0.0 collective-permute-done.1
  11.8 1.6 %collective-permute-start.5 = (bf16[2,192,128]{2,1,0:T(8,128)(2,1)S(1)}, bf16[2,192,128]{2,1,0:T(8,128)(2,1)S(1)}, u32[]{:S(2)}, u32[]{:S(2)}) collective-permute-start(bf16[2,192,128]{2,1,0:T(8,128)(2,1)S(1)} %pad_maximum_fusion.2.rear_ref), channel_id=1, source_target_pairs={{0,8},{4,12},{8,0},{12,4},{1,9},{5,13},{9,1},{13,5},{2,10},{6,14},... | collective-permute-start | bytes 294920 | tf_op jit(solution)/shard_map/ppermute | solution.py:538
  13.3 1.4 %shard_map.136 = (f32[8,128]{1,0:T(8,128)S(1)}, bf16[256,256]{1,0:T(8,128)(2,1)S(1)}, bf16[512,256]{1,0:T(8,128)(2,1)S(1)}, f32[64,64]{1,0:T(8,128)S(1)}) custom-call(f32[1,64]{1,0:T(1,128)} %bitcast.24, f32[1,64]{1,0:T(1,128)} %bitcast.25, bf16[32,64]{1,0:T(8,128)(2,1)} %bitcast.21, bf16[32,64]{1,0:T(8,128)(2,1)} %bitcast.22, bf16[1024,128]{1,0:T(8,128)(2,1)} %refs_4_), custom_call_target="tpu_custom_call" | custom-call | tf_op jit(solution)/shard_map/pallas_call | solution.py:548
  14.8 0.0 collective-permute-done.3.front_ref
  14.8 0.1 collective-permute-start.7
  14.9 0.5 %collective-permute-start.4 = (bf16[2,192,128]{2,1,0:T(8,128)(2,1)S(1)}, bf16[2,192,128]{2,1,0:T(8,128)(2,1)S(1)}, u32[]{:S(2)}, u32[]{:S(2)}) collective-permute-start(bf16[2,192,128]{2,1,0:T(8,128)(2,1)S(1)} %collective-permute-done.3.front_ref), channel_id=1, source_target_pairs={{0,4},{4,0},{8,12},{12,8},{1,5},{5,1},{9,13},{13,9},{2,6},{6,2},{1... | collective-permute-start | bytes 294920 | tf_op jit(solution)/shard_map/ppermute | solution.py:538
  15.3 0.6 %shard_map.137 = (bf16[512,256]{1,0:T(8,128)(2,1)S(1)}, bf16[128,256]{1,0:T(8,128)(2,1)S(1)}, bf16[128,256]{1,0:T(8,128)(2,1)S(1)}, f32[32,8,128]{2,1,0:T(8,128)...) custom-call(s32[1]{0:T(128)} %bitcast.place_ref, ...), custom_call_target="tpu_custom_call" | custom-call | flops 1000000000 | bytes 3906250 | tf_op jit(solution)/shard_map/pallas_call | solution.py:588
  16.0 0.5 %collective-permute-done.5.rear_ref = bf16[2,192,128]{2,1,0:T(8,128)(2,1)S(1)} collective-permute-done((bf16[2,192,128]{2,1,0:T(8,128)(2,1)S(1)}, bf16[2,192,128]{2,1,0:T(8,128)(2,1)S(1)}, u32[]{:S(2)}, u32[]{:S(2)}) %collective-permute-start.5) | collective-permute-done | bytes 98336 | tf_op jit(solution)/shard_map/ppermute | solution.py:538
  16.4 0.0 collective-permute-start.6
  16.4 0.0 collective-permute-done.7.core_ref
  16.5 1.1 %shard_map.138 = (bf16[512,256]{1,0:T(8,128)(2,1)S(1)}, bf16[128,256]{1,0:T(8,128)(2,1)S(1)}, bf16[128,256]{1,0:T(8,128)(2,1)S(1)}, f32[32,8,128]{2,1,0:T(8,128)...) custom-call(s32[1]{0:T(128)} %bitcast.place_ref, ...), custom_call_target="tpu_custom_call" | custom-call | flops 1000000 | bytes 3906 | tf_op jit(solution)/shard_map/pallas_call | solution.py:588
  17.5 0.0 collective-permute-done.4.front_ref
  17.5 0.2 collective-permute-done.6.rear_ref
  17.7 5.3 %shard_map.139 = (f32[32,8,64]{2,1,0:T(8,128)}, f32[1024,128]{1,0:T(8,128)}, f32[32,64]{1,0:T(8,128)}, f32[32,64]{1,0:T(8,128)}, f32[1,64]{1,0:T(1,128)}, /*index=5*/f32[1,64]{1,0:T(1,128)}, f32[1,128]{1,0:T(1,128)}) custom-call(s32[1]{0:T(128)} %bitcast.place_ref, bf16[2,192,128]{2,1,0:T(8,128)(2,1)S(1)} %collective-permute-done.4.front_ref, ...), custom_call_target="tpu_custom_call" | custom-call | tf_op jit(solution)/shard_map/pallas_call | solution.py:606
  (3 shorter events, 0.0 us)
Async XLA Ops:
  1.7 6.7 %collective-permute-start = (bf16[192,128]{1,0:T(8,128)(2,1)S(1)}, bf16[192,128]{1,0:T(8,128)(2,1)S(1)}, u32[]{:S(2)}, u32[]{:S(2)}) collective-permute-start(bf16[192,128]{1,0:T(8,128)(2,1)S(1)} %shard_map.135), channel_id=1, source_target_pairs={{0,2},{1,3},{2,0},{3,1},{4,6},{5,7},{6,4},{7,5},{8,10},{9,11},{10,... | collective-permute-start | bytes 147464 | tf_op jit(solution)/shard_map/ppermute | solution.py:538
  5.8 6.0 %collective-permute-start.2 = (bf16[192,128]{1,0:T(8,128)(2,1)S(1)}, bf16[192,128]{1,0:T(8,128)(2,1)S(1)}, u32[]{:S(2)}, u32[]{:S(2)}) collective-permute-start(bf16[192,128]{1,0:T(8,128)(2,1)S(1)} %shard_map.135), channel_id=1, source_target_pairs={{0,3},{1,2},{2,1},{3,0},{4,7},{5,6},{6,5},{7,4},{8,11},{9,10},{10,... | collective-permute-start | bytes 147464 | tf_op jit(solution)/shard_map/ppermute | solution.py:538
  7.1 4.6 %collective-permute-start.1 = (bf16[192,128]{1,0:T(8,128)(2,1)S(1)}, bf16[192,128]{1,0:T(8,128)(2,1)S(1)}, u32[]{:S(2)}, u32[]{:S(2)}) collective-permute-start(bf16[192,128]{1,0:T(8,128)(2,1)S(1)} %shard_map.135), channel_id=1, source_target_pairs={{0,1},{1,0},{2,3},{3,2},{4,5},{5,4},{6,7},{7,6},{8,9},{9,8},{10,11... | collective-permute-start | bytes 147464 | tf_op jit(solution)/shard_map/ppermute | solution.py:538
  8.4 6.4 %collective-permute-start.3 = (bf16[2,192,128]{2,1,0:T(8,128)(2,1)S(1)}, bf16[2,192,128]{2,1,0:T(8,128)(2,1)S(1)}, u32[]{:S(2)}, u32[]{:S(2)}) collective-permute-start(bf16[2,192,128]{2,1,0:T(8,128)(2,1)S(1)} %pad_maximum_fusion.1.front_ref), channel_id=1, source_target_pairs={{0,8},{4,12},{8,0},{12,4},{1,9},{5,13},{9,1},{13,5},{2,10},{6,14},... | collective-permute-start | bytes 294920 | tf_op jit(solution)/shard_map/ppermute | solution.py:538
  11.8 4.7 %collective-permute-start.5 = (bf16[2,192,128]{2,1,0:T(8,128)(2,1)S(1)}, bf16[2,192,128]{2,1,0:T(8,128)(2,1)S(1)}, u32[]{:S(2)}, u32[]{:S(2)}) collective-permute-start(bf16[2,192,128]{2,1,0:T(8,128)(2,1)S(1)} %pad_maximum_fusion.2.rear_ref), channel_id=1, source_target_pairs={{0,8},{4,12},{8,0},{12,4},{1,9},{5,13},{9,1},{13,5},{2,10},{6,14},... | collective-permute-start | bytes 294920 | tf_op jit(solution)/shard_map/ppermute | solution.py:538
  14.8 1.7 %collective-permute-start.7 = (bf16[4,192,128]{2,1,0:T(8,128)(2,1)S(1)}, bf16[4,192,128]{2,1,0:T(8,128)(2,1)S(1)}, u32[]{:S(2)}, u32[]{:S(2)}) collective-permute-start(bf16[4,192,128]{2,1,0:T(8,128)(2,1)S(1)} %pad_maximum_fusion), channel_id=1, source_target_pairs={{0,4},{4,0},{8,12},{12,8},{1,5},{5,1},{9,13},{13,9},{2,6},{6,2},{1... | collective-permute-start | bytes 589832 | tf_op jit(solution)/shard_map/ppermute | solution.py:538
  14.9 2.7 %collective-permute-start.4 = (bf16[2,192,128]{2,1,0:T(8,128)(2,1)S(1)}, bf16[2,192,128]{2,1,0:T(8,128)(2,1)S(1)}, u32[]{:S(2)}, u32[]{:S(2)}) collective-permute-start(bf16[2,192,128]{2,1,0:T(8,128)(2,1)S(1)} %collective-permute-done.3.front_ref), channel_id=1, source_target_pairs={{0,4},{4,0},{8,12},{12,8},{1,5},{5,1},{9,13},{13,9},{2,6},{6,2},{1... | collective-permute-start | bytes 294920 | tf_op jit(solution)/shard_map/ppermute | solution.py:538
  16.4 1.3 %collective-permute-start.6 = (bf16[2,192,128]{2,1,0:T(8,128)(2,1)S(1)}, bf16[2,192,128]{2,1,0:T(8,128)(2,1)S(1)}, u32[]{:S(2)}, u32[]{:S(2)}) collective-permute-start(bf16[2,192,128]{2,1,0:T(8,128)(2,1)S(1)} %collective-permute-done.5.rear_ref), channel_id=1, source_target_pairs={{0,4},{4,0},{8,12},{12,8},{1,5},{5,1},{9,13},{13,9},{2,6},{6,2},{1... | collective-permute-start | bytes 294920 | tf_op jit(solution)/shard_map/ppermute | solution.py:538

commit v26 on v25

--- a/solution.py
+++ b/solution.py
@@ -400,10 +400,14 @@
         256, 256, lambda r, c: jnp.where((r // 8 == c % 32) & (r % 8 == c // 32), 1.0, 0.0)
     ).astype(BF)
     mask_two = jnp.concatenate([mask, mask], axis=1)
-    right_in = [
-        mm_nt(turn, (right_grad[:, 256 * q : 256 * q + 256] * mask_two).astype(BF))
-        for q in range(4)
-    ]
+    right_in = []
+    for h in range(2):
+        pieces = [
+            (right_grad[:, 256 * q : 256 * q + 256] * mask_two).astype(BF)
+            for q in (2 * h, 2 * h + 1)
+        ]
+        turned = mm_nt(turn, jnp.concatenate(pieces, axis=0))
+        right_in += [turned[:, :128], turned[:, 128:]]
     for t in range(32):
         at = slice(128 * (t // 2), 128 * (t // 2) + 128)
         row = 32 * (t % 2)

time: 23.3 us -> 23.8 us (1.021)
  Pallas kernels: 9.46 us -> 9.95 us
    pallas_call x1, Pallas kernels: 5.34 us -> 5.83 us  [gathered_body(): pl.pallas_call(functools.partial(part_kernel, n_row, n_col), out_shape=(s...]
where the time goes in v26:
time: 23.8 us; the launch traced here: 23.6 us
  Pallas kernels  9.95 us (42%)
  starting transfers between devices  9.57 us (40%)
  waiting for transfers between devices  3.3 us (14%)
  between operations  0.71 us (3%)
    ppermute x8, starting transfers between devices, over(): return lax.ppermute(array, axis, [(k, k ^ step) for k in range(size)])  9.57 us
    pallas_call x1, Pallas kernels, gathered_body(): pl.pallas_call(functools.partial(part_kernel, n_row, n_col), out_shape=(s...  5.83 us
    ppermute x8, waiting for transfers between devices, over(): return lax.ppermute(array, axis, [(k, k ^ step) for k in range(size)])  3.3 us
    pallas_call x2, Pallas kernels, stages_of(): pl.pallas_call(functools.partial(kernel, n_col), out_shape=tuple(outs), i...  1.68 us
    pallas_call x1, Pallas kernels, gathered_body(): pl.pallas_call(weights_kernel, out_shape=(held(8, 128), held_bf(256, 256)...  1.4 us
    pallas_call x1, Pallas kernels, gathered_body(): pl.pallas_call(pack_kernel, out_shape=held_bf(192, 128), in_specs=vmem(3)...  1.04 us
  transfers between devices with their start and end apart: 8, of which 4 were waited for; matrix products, arithmetic and copies ran while one was open for 0% of the time, Pallas kernels for 13%

profile of v26, /device:TPU:0, one launch (start us, length us, event | category | flops | bytes accessed | tf_op | source)
XLA Modules:
  0.0 23.6 jit_solution(800792874578951232)
XLA Ops:
  0.6 1.0 %shard_map.135 = bf16[192,128]{1,0:T(8,128)(2,1)S(1)} custom-call(bf16[32,8,64]{2,1,0:T(8,128)(2,1)} %msa_ref.1, s32[8,32]{1,0:T(8,128)} %bitcast.23, bf16[8,8,128]{2,1,0:T(8,128)(2,1)} %pair_ref.1), custom_call_target="tpu_custom_call" | custom-call | tf_op jit(solution)/shard_map/pallas_call | solution.py:535
  1.7 4.1 %collective-permute-start = (bf16[192,128]{1,0:T(8,128)(2,1)S(1)}, bf16[192,128]{1,0:T(8,128)(2,1)S(1)}, u32[]{:S(2)}, u32[]{:S(2)}) collective-permute-start(bf16[192,128]{1,0:T(8,128)(2,1)S(1)} %shard_map.135), channel_id=1, source_target_pairs={{0,2},{1,3},{2,0},{3,1},{4,6},{5,7},{6,4},{7,5},{8,10},{9,11},{10,... | collective-permute-start | bytes 147464 | tf_op jit(solution)/shard_map/ppermute | solution.py:542
  5.8 1.3 %collective-permute-start.2 = (bf16[192,128]{1,0:T(8,128)(2,1)S(1)}, bf16[192,128]{1,0:T(8,128)(2,1)S(1)}, u32[]{:S(2)}, u32[]{:S(2)}) collective-permute-start(bf16[192,128]{1,0:T(8,128)(2,1)S(1)} %shard_map.135), channel_id=1, source_target_pairs={{0,3},{1,2},{2,1},{3,0},{4,7},{5,6},{6,5},{7,4},{8,11},{9,10},{10,... | collective-permute-start | bytes 147464 | tf_op jit(solution)/shard_map/ppermute | solution.py:542
  7.1 0.2 collective-permute-start.1
  7.4 1.0 %collective-permute-done = bf16[192,128]{1,0:T(8,128)(2,1)S(1)} collective-permute-done((bf16[192,128]{1,0:T(8,128)(2,1)S(1)}, bf16[192,128]{1,0:T(8,128)(2,1)S(1)}, u32[]{:S(2)}, u32[]{:S(2)}) %collective-permute-start) | collective-permute-done | bytes 49184 | tf_op jit(solution)/shard_map/ppermute | solution.py:542
  8.4 1.8 %collective-permute-start.3 = (bf16[2,192,128]{2,1,0:T(8,128)(2,1)S(1)}, bf16[2,192,128]{2,1,0:T(8,128)(2,1)S(1)}, u32[]{:S(2)}, u32[]{:S(2)}) collective-permute-start(bf16[2,192,128]{2,1,0:T(8,128)(2,1)S(1)} %pad_maximum_fusion.1.front_ref), channel_id=1, source_target_pairs={{0,8},{4,12},{8,0},{12,4},{1,9},{5,13},{9,1},{13,5},{2,10},{6,14},... | collective-permute-start | bytes 294920 | tf_op jit(solution)/shard_map/ppermute | solution.py:542
  10.2 1.6 %collective-permute-done.2 = bf16[192,128]{1,0:T(8,128)(2,1)S(1)} collective-permute-done((bf16[192,128]{1,0:T(8,128)(2,1)S(1)}, bf16[192,128]{1,0:T(8,128)(2,1)S(1)}, u32[]{:S(2)}, u32[]{:S(2)}) %collective-permute-start.2) | collective-permute-done | bytes 49184 | tf_op jit(solution)/shard_map/ppermute | solution.py:542
  11.7 0.0 collective-permute-done.1
  11.8 1.6 %collective-permute-start.5 = (bf16[2,192,128]{2,1,0:T(8,128)(2,1)S(1)}, bf16[2,192,128]{2,1,0:T(8,128)(2,1)S(1)}, u32[]{:S(2)}, u32[]{:S(2)}) collective-permute-start(bf16[2,192,128]{2,1,0:T(8,128)(2,1)S(1)} %pad_maximum_fusion.2.rear_ref), channel_id=1, source_target_pairs={{0,8},{4,12},{8,0},{12,4},{1,9},{5,13},{9,1},{13,5},{2,10},{6,14},... | collective-permute-start | bytes 294920 | tf_op jit(solution)/shard_map/ppermute | solution.py:542
  13.3 1.4 %shard_map.136 = (f32[8,128]{1,0:T(8,128)S(1)}, bf16[256,256]{1,0:T(8,128)(2,1)S(1)}, bf16[512,256]{1,0:T(8,128)(2,1)S(1)}, f32[64,64]{1,0:T(8,128)S(1)}) custom-call(f32[1,64]{1,0:T(1,128)} %bitcast.24, f32[1,64]{1,0:T(1,128)} %bitcast.25, bf16[32,64]{1,0:T(8,128)(2,1)} %bitcast.21, bf16[32,64]{1,0:T(8,128)(2,1)} %bitcast.22, bf16[1024,128]{1,0:T(8,128)(2,1)} %refs_4_), custom_call_target="tpu_custom_call" | custom-call | tf_op jit(solution)/shard_map/pallas_call | solution.py:552
  14.8 0.0 collective-permute-done.3.front_ref
  14.8 0.1 collective-permute-start.7
  14.9 0.5 %collective-permute-start.4 = (bf16[2,192,128]{2,1,0:T(8,128)(2,1)S(1)}, bf16[2,192,128]{2,1,0:T(8,128)(2,1)S(1)}, u32[]{:S(2)}, u32[]{:S(2)}) collective-permute-start(bf16[2,192,128]{2,1,0:T(8,128)(2,1)S(1)} %collective-permute-done.3.front_ref), channel_id=1, source_target_pairs={{0,4},{4,0},{8,12},{12,8},{1,5},{5,1},{9,13},{13,9},{2,6},{6,2},{1... | collective-permute-start | bytes 294920 | tf_op jit(solution)/shard_map/ppermute | solution.py:542
  15.3 0.6 %shard_map.137 = (bf16[512,256]{1,0:T(8,128)(2,1)S(1)}, bf16[128,256]{1,0:T(8,128)(2,1)S(1)}, bf16[128,256]{1,0:T(8,128)(2,1)S(1)}, f32[32,8,128]{2,1,0:T(8,128)...) custom-call(s32[1]{0:T(128)} %bitcast.place_ref, ...), custom_call_target="tpu_custom_call" | custom-call | flops 1000000000 | bytes 3906250 | tf_op jit(solution)/shard_map/pallas_call | solution.py:592
  16.0 0.5 %collective-permute-done.5.rear_ref = bf16[2,192,128]{2,1,0:T(8,128)(2,1)S(1)} collective-permute-done((bf16[2,192,128]{2,1,0:T(8,128)(2,1)S(1)}, bf16[2,192,128]{2,1,0:T(8,128)(2,1)S(1)}, u32[]{:S(2)}, u32[]{:S(2)}) %collective-permute-start.5) | collective-permute-done | bytes 98336 | tf_op jit(solution)/shard_map/ppermute | solution.py:542
  16.4 0.0 collective-permute-start.6
  16.4 0.0 collective-permute-done.7.core_ref
  16.5 1.1 %shard_map.138 = (bf16[512,256]{1,0:T(8,128)(2,1)S(1)}, bf16[128,256]{1,0:T(8,128)(2,1)S(1)}, bf16[128,256]{1,0:T(8,128)(2,1)S(1)}, f32[32,8,128]{2,1,0:T(8,128)...) custom-call(s32[1]{0:T(128)} %bitcast.place_ref, ...), custom_call_target="tpu_custom_call" | custom-call | flops 1000000 | bytes 3906 | tf_op jit(solution)/shard_map/pallas_call | solution.py:592
  17.5 0.0 collective-permute-done.4.front_ref
  17.5 0.2 collective-permute-done.6.rear_ref
  17.7 5.8 %shard_map.139 = (f32[32,8,64]{2,1,0:T(8,128)}, f32[1024,128]{1,0:T(8,128)}, f32[32,64]{1,0:T(8,128)}, f32[32,64]{1,0:T(8,128)}, f32[1,64]{1,0:T(1,128)}, /*index=5*/f32[1,64]{1,0:T(1,128)}, f32[1,128]{1,0:T(1,128)}) custom-call(s32[1]{0:T(128)} %bitcast.place_ref, bf16[2,192,128]{2,1,0:T(8,128)(2,1)S(1)} %collective-permute-done.4.front_ref, ...), custom_call_target="tpu_custom_call" | custom-call | tf_op jit(solution)/shard_map/pallas_call | solution.py:610
  (3 shorter events, 0.0 us)
Async XLA Ops:
  1.7 6.7 %collective-permute-start = (bf16[192,128]{1,0:T(8,128)(2,1)S(1)}, bf16[192,128]{1,0:T(8,128)(2,1)S(1)}, u32[]{:S(2)}, u32[]{:S(2)}) collective-permute-start(bf16[192,128]{1,0:T(8,128)(2,1)S(1)} %shard_map.135), channel_id=1, source_target_pairs={{0,2},{1,3},{2,0},{3,1},{4,6},{5,7},{6,4},{7,5},{8,10},{9,11},{10,... | collective-permute-start | bytes 147464 | tf_op jit(solution)/shard_map/ppermute | solution.py:542
  5.8 6.0 %collective-permute-start.2 = (bf16[192,128]{1,0:T(8,128)(2,1)S(1)}, bf16[192,128]{1,0:T(8,128)(2,1)S(1)}, u32[]{:S(2)}, u32[]{:S(2)}) collective-permute-start(bf16[192,128]{1,0:T(8,128)(2,1)S(1)} %shard_map.135), channel_id=1, source_target_pairs={{0,3},{1,2},{2,1},{3,0},{4,7},{5,6},{6,5},{7,4},{8,11},{9,10},{10,... | collective-permute-start | bytes 147464 | tf_op jit(solution)/shard_map/ppermute | solution.py:542
  7.1 4.6 %collective-permute-start.1 = (bf16[192,128]{1,0:T(8,128)(2,1)S(1)}, bf16[192,128]{1,0:T(8,128)(2,1)S(1)}, u32[]{:S(2)}, u32[]{:S(2)}) collective-permute-start(bf16[192,128]{1,0:T(8,128)(2,1)S(1)} %shard_map.135), channel_id=1, source_target_pairs={{0,1},{1,0},{2,3},{3,2},{4,5},{5,4},{6,7},{7,6},{8,9},{9,8},{10,11... | collective-permute-start | bytes 147464 | tf_op jit(solution)/shard_map/ppermute | solution.py:542
  8.4 6.4 %collective-permute-start.3 = (bf16[2,192,128]{2,1,0:T(8,128)(2,1)S(1)}, bf16[2,192,128]{2,1,0:T(8,128)(2,1)S(1)}, u32[]{:S(2)}, u32[]{:S(2)}) collective-permute-start(bf16[2,192,128]{2,1,0:T(8,128)(2,1)S(1)} %pad_maximum_fusion.1.front_ref), channel_id=1, source_target_pairs={{0,8},{4,12},{8,0},{12,4},{1,9},{5,13},{9,1},{13,5},{2,10},{6,14},... | collective-permute-start | bytes 294920 | tf_op jit(solution)/shard_map/ppermute | solution.py:542
  11.8 4.7 %collective-permute-start.5 = (bf16[2,192,128]{2,1,0:T(8,128)(2,1)S(1)}, bf16[2,192,128]{2,1,0:T(8,128)(2,1)S(1)}, u32[]{:S(2)}, u32[]{:S(2)}) collective-permute-start(bf16[2,192,128]{2,1,0:T(8,128)(2,1)S(1)} %pad_maximum_fusion.2.rear_ref), channel_id=1, source_target_pairs={{0,8},{4,12},{8,0},{12,4},{1,9},{5,13},{9,1},{13,5},{2,10},{6,14},... | collective-permute-start | bytes 294920 | tf_op jit(solution)/shard_map/ppermute | solution.py:542
  14.8 1.7 %collective-permute-start.7 = (bf16[4,192,128]{2,1,0:T(8,128)(2,1)S(1)}, bf16[4,192,128]{2,1,0:T(8,128)(2,1)S(1)}, u32[]{:S(2)}, u32[]{:S(2)}) collective-permute-start(bf16[4,192,128]{2,1,0:T(8,128)(2,1)S(1)} %pad_maximum_fusion), channel_id=1, source_target_pairs={{0,4},{4,0},{8,12},{12,8},{1,5},{5,1},{9,13},{13,9},{2,6},{6,2},{1... | collective-permute-start | bytes 589832 | tf_op jit(solution)/shard_map/ppermute | solution.py:542
  14.9 2.7 %collective-permute-start.4 = (bf16[2,192,128]{2,1,0:T(8,128)(2,1)S(1)}, bf16[2,192,128]{2,1,0:T(8,128)(2,1)S(1)}, u32[]{:S(2)}, u32[]{:S(2)}) collective-permute-start(bf16[2,192,128]{2,1,0:T(8,128)(2,1)S(1)} %collective-permute-done.3.front_ref), channel_id=1, source_target_pairs={{0,4},{4,0},{8,12},{12,8},{1,5},{5,1},{9,13},{13,9},{2,6},{6,2},{1... | collective-permute-start | bytes 294920 | tf_op jit(solution)/shard_map/ppermute | solution.py:542
  16.4 1.3 %collective-permute-start.6 = (bf16[2,192,128]{2,1,0:T(8,128)(2,1)S(1)}, bf16[2,192,128]{2,1,0:T(8,128)(2,1)S(1)}, u32[]{:S(2)}, u32[]{:S(2)}) collective-permute-start(bf16[2,192,128]{2,1,0:T(8,128)(2,1)S(1)} %collective-permute-done.5.rear_ref), channel_id=1, source_target_pairs={{0,4},{4,0},{8,12},{12,8},{1,5},{5,1},{9,13},{13,9},{2,6},{6,2},{1... | collective-permute-start | bytes 294920 | tf_op jit(solution)/shard_map/ppermute | solution.py:542

commit v27 on v25

--- a/solution.py
+++ b/solution.py
@@ -362,7 +362,7 @@
     (
         normed_ref, inverse_ref, norm_ref, back_ref, final_ref, first_ref,
         emb_out, final_hbm_out, first_out, second_out, gain_out, offset_out, bias_out,
-        right_scr, scaled_scr, grad_scr, outer_scr, wide_scr, all_scr,
+        right_scr, scaled_scr, grad_scr, outer_scr, all_scr,
         final_out, out_sem, turn_scr,
     ) = refs[7 * (n_row - 1) : -7]
     stages.append(refs[-7:])
@@ -440,9 +440,9 @@
                 even, odd = interleave(block[:32], block[32:])
                 outer_scr[rows : rows + 32, 128 * q : 128 * q + 128] = even
                 outer_scr[rows + 32 : rows + 64, 128 * q : 128 * q + 128] = odd
-    wide_scr[...] = mm(outer_scr[...], scaled_scr[...])
-    for c in range(32):
-        final_out[32 * c : 32 * c + 32, :] = wide_scr[pl.ds(c, 32, stride=32), :]
+    final = mm(outer_scr[...], scaled_scr[...])
+    for e in range(32):
+        final_out[pl.ds(e, 32, stride=32), :] = final[32 * e : 32 * e + 32]
     final_send = pltpu.make_async_copy(final_out, final_hbm_out, out_sem)
     final_send.start()
 
@@ -621,7 +621,6 @@
             pltpu.VMEM((1024, 128), BF),
             pltpu.VMEM((1024, 1024), BF),
             pltpu.VMEM((1024, 1024), BF),
-            pltpu.VMEM((1024, 128), F32),
             pltpu.VMEM((128, 2048), BF),
             pltpu.VMEM((1024, 128), F32),
             pltpu.SemaphoreType.DMA,

time: 23.3 us -> 23.4 us (level)
  no operation moved by 1% of the time
where the time goes in v27:
time: 23.4 us; the launch traced here: 23.2 us
  starting transfers between devices  9.57 us (41%)
  Pallas kernels  9.55 us (41%)
  waiting for transfers between devices  3.3 us (14%)
  between operations  0.71 us (3%)
    ppermute x8, starting transfers between devices, over(): return lax.ppermute(array, axis, [(k, k ^ step) for k in range(size)])  9.57 us
    pallas_call x1, Pallas kernels, gathered_body(): pl.pallas_call(functools.partial(part_kernel, n_row, n_col), out_shape=(s...  5.43 us
    ppermute x8, waiting for transfers between devices, over(): return lax.ppermute(array, axis, [(k, k ^ step) for k in range(size)])  3.3 us
    pallas_call x2, Pallas kernels, stages_of(): pl.pallas_call(functools.partial(kernel, n_col), out_shape=tuple(outs), i...  1.68 us
    pallas_call x1, Pallas kernels, gathered_body(): pl.pallas_call(weights_kernel, out_shape=(held(8, 128), held_bf(256, 256)...  1.4 us
    pallas_call x1, Pallas kernels, gathered_body(): pl.pallas_call(pack_kernel, out_shape=held_bf(192, 128), in_specs=vmem(3)...  1.04 us
  transfers between devices with their start and end apart: 8, of which 4 were waited for; matrix products, arithmetic and copies ran while one was open for 0% of the time, Pallas kernels for 13%

profile of v27, /device:TPU:0, one launch (start us, length us, event | category | flops | bytes accessed | tf_op | source)
XLA Modules:
  0.0 23.2 jit_solution(14332476143210620249)
XLA Ops:
  0.6 1.0 %shard_map.135 = bf16[192,128]{1,0:T(8,128)(2,1)S(1)} custom-call(bf16[32,8,64]{2,1,0:T(8,128)(2,1)} %msa_ref.1, s32[8,32]{1,0:T(8,128)} %bitcast.23, bf16[8,8,128]{2,1,0:T(8,128)(2,1)} %pair_ref.1), custom_call_target="tpu_custom_call" | custom-call | tf_op jit(solution)/shard_map/pallas_call | solution.py:531
  1.7 4.1 %collective-permute-start = (bf16[192,128]{1,0:T(8,128)(2,1)S(1)}, bf16[192,128]{1,0:T(8,128)(2,1)S(1)}, u32[]{:S(2)}, u32[]{:S(2)}) collective-permute-start(bf16[192,128]{1,0:T(8,128)(2,1)S(1)} %shard_map.135), channel_id=1, source_target_pairs={{0,2},{1,3},{2,0},{3,1},{4,6},{5,7},{6,4},{7,5},{8,10},{9,11},{10,... | collective-permute-start | bytes 147464 | tf_op jit(solution)/shard_map/ppermute | solution.py:538
  5.8 1.3 %collective-permute-start.2 = (bf16[192,128]{1,0:T(8,128)(2,1)S(1)}, bf16[192,128]{1,0:T(8,128)(2,1)S(1)}, u32[]{:S(2)}, u32[]{:S(2)}) collective-permute-start(bf16[192,128]{1,0:T(8,128)(2,1)S(1)} %shard_map.135), channel_id=1, source_target_pairs={{0,3},{1,2},{2,1},{3,0},{4,7},{5,6},{6,5},{7,4},{8,11},{9,10},{10,... | collective-permute-start | bytes 147464 | tf_op jit(solution)/shard_map/ppermute | solution.py:538
  7.1 0.2 collective-permute-start.1
  7.4 1.0 %collective-permute-done = bf16[192,128]{1,0:T(8,128)(2,1)S(1)} collective-permute-done((bf16[192,128]{1,0:T(8,128)(2,1)S(1)}, bf16[192,128]{1,0:T(8,128)(2,1)S(1)}, u32[]{:S(2)}, u32[]{:S(2)}) %collective-permute-start) | collective-permute-done | bytes 49184 | tf_op jit(solution)/shard_map/ppermute | solution.py:538
  8.4 1.8 %collective-permute-start.3 = (bf16[2,192,128]{2,1,0:T(8,128)(2,1)S(1)}, bf16[2,192,128]{2,1,0:T(8,128)(2,1)S(1)}, u32[]{:S(2)}, u32[]{:S(2)}) collective-permute-start(bf16[2,192,128]{2,1,0:T(8,128)(2,1)S(1)} %pad_maximum_fusion.1.front_ref), channel_id=1, source_target_pairs={{0,8},{4,12},{8,0},{12,4},{1,9},{5,13},{9,1},{13,5},{2,10},{6,14},... | collective-permute-start | bytes 294920 | tf_op jit(solution)/shard_map/ppermute | solution.py:538
  10.2 1.6 %collective-permute-done.2 = bf16[192,128]{1,0:T(8,128)(2,1)S(1)} collective-permute-done((bf16[192,128]{1,0:T(8,128)(2,1)S(1)}, bf16[192,128]{1,0:T(8,128)(2,1)S(1)}, u32[]{:S(2)}, u32[]{:S(2)}) %collective-permute-start.2) | collective-permute-done | bytes 49184 | tf_op jit(solution)/shard_map/ppermute | solution.py:538
  11.7 0.0 collective-permute-done.1
  11.8 1.6 %collective-permute-start.5 = (bf16[2,192,128]{2,1,0:T(8,128)(2,1)S(1)}, bf16[2,192,128]{2,1,0:T(8,128)(2,1)S(1)}, u32[]{:S(2)}, u32[]{:S(2)}) collective-permute-start(bf16[2,192,128]{2,1,0:T(8,128)(2,1)S(1)} %pad_maximum_fusion.2.rear_ref), channel_id=1, source_target_pairs={{0,8},{4,12},{8,0},{12,4},{1,9},{5,13},{9,1},{13,5},{2,10},{6,14},... | collective-permute-start | bytes 294920 | tf_op jit(solution)/shard_map/ppermute | solution.py:538
  13.3 1.4 %shard_map.136 = (f32[8,128]{1,0:T(8,128)S(1)}, bf16[256,256]{1,0:T(8,128)(2,1)S(1)}, bf16[512,256]{1,0:T(8,128)(2,1)S(1)}, f32[64,64]{1,0:T(8,128)S(1)}) custom-call(f32[1,64]{1,0:T(1,128)} %bitcast.24, f32[1,64]{1,0:T(1,128)} %bitcast.25, bf16[32,64]{1,0:T(8,128)(2,1)} %bitcast.21, bf16[32,64]{1,0:T(8,128)(2,1)} %bitcast.22, bf16[1024,128]{1,0:T(8,128)(2,1)} %refs_4_), custom_call_target="tpu_custom_call" | custom-call | tf_op jit(solution)/shard_map/pallas_call | solution.py:548
  14.8 0.0 collective-permute-done.3.front_ref
  14.8 0.1 collective-permute-start.7
  14.9 0.5 %collective-permute-start.4 = (bf16[2,192,128]{2,1,0:T(8,128)(2,1)S(1)}, bf16[2,192,128]{2,1,0:T(8,128)(2,1)S(1)}, u32[]{:S(2)}, u32[]{:S(2)}) collective-permute-start(bf16[2,192,128]{2,1,0:T(8,128)(2,1)S(1)} %collective-permute-done.3.front_ref), channel_id=1, source_target_pairs={{0,4},{4,0},{8,12},{12,8},{1,5},{5,1},{9,13},{13,9},{2,6},{6,2},{1... | collective-permute-start | bytes 294920 | tf_op jit(solution)/shard_map/ppermute | solution.py:538
  15.3 0.6 %shard_map.137 = (bf16[512,256]{1,0:T(8,128)(2,1)S(1)}, bf16[128,256]{1,0:T(8,128)(2,1)S(1)}, bf16[128,256]{1,0:T(8,128)(2,1)S(1)}, f32[32,8,128]{2,1,0:T(8,128)...) custom-call(s32[1]{0:T(128)} %bitcast.place_ref, ...), custom_call_target="tpu_custom_call" | custom-call | flops 1000000000 | bytes 3906250 | tf_op jit(solution)/shard_map/pallas_call | solution.py:588
  16.0 0.5 %collective-permute-done.5.rear_ref = bf16[2,192,128]{2,1,0:T(8,128)(2,1)S(1)} collective-permute-done((bf16[2,192,128]{2,1,0:T(8,128)(2,1)S(1)}, bf16[2,192,128]{2,1,0:T(8,128)(2,1)S(1)}, u32[]{:S(2)}, u32[]{:S(2)}) %collective-permute-start.5) | collective-permute-done | bytes 98336 | tf_op jit(solution)/shard_map/ppermute | solution.py:538
  16.4 0.0 collective-permute-start.6
  16.4 0.0 collective-permute-done.7.core_ref
  16.5 1.1 %shard_map.138 = (bf16[512,256]{1,0:T(8,128)(2,1)S(1)}, bf16[128,256]{1,0:T(8,128)(2,1)S(1)}, bf16[128,256]{1,0:T(8,128)(2,1)S(1)}, f32[32,8,128]{2,1,0:T(8,128)...) custom-call(s32[1]{0:T(128)} %bitcast.place_ref, ...), custom_call_target="tpu_custom_call" | custom-call | flops 1000000 | bytes 3906 | tf_op jit(solution)/shard_map/pallas_call | solution.py:588
  17.5 0.0 collective-permute-done.4.front_ref
  17.5 0.2 collective-permute-done.6.rear_ref
  17.7 5.4 %shard_map.139 = (f32[32,8,64]{2,1,0:T(8,128)}, f32[1024,128]{1,0:T(8,128)}, f32[32,64]{1,0:T(8,128)}, f32[32,64]{1,0:T(8,128)}, f32[1,64]{1,0:T(1,128)}, /*index=5*/f32[1,64]{1,0:T(1,128)}, f32[1,128]{1,0:T(1,128)}) custom-call(s32[1]{0:T(128)} %bitcast.place_ref, bf16[2,192,128]{2,1,0:T(8,128)(2,1)S(1)} %collective-permute-done.4.front_ref, ...), custom_call_target="tpu_custom_call" | custom-call | tf_op jit(solution)/shard_map/pallas_call | solution.py:606
  (3 shorter events, 0.0 us)
Async XLA Ops:
  1.7 6.7 %collective-permute-start = (bf16[192,128]{1,0:T(8,128)(2,1)S(1)}, bf16[192,128]{1,0:T(8,128)(2,1)S(1)}, u32[]{:S(2)}, u32[]{:S(2)}) collective-permute-start(bf16[192,128]{1,0:T(8,128)(2,1)S(1)} %shard_map.135), channel_id=1, source_target_pairs={{0,2},{1,3},{2,0},{3,1},{4,6},{5,7},{6,4},{7,5},{8,10},{9,11},{10,... | collective-permute-start | bytes 147464 | tf_op jit(solution)/shard_map/ppermute | solution.py:538
  5.8 6.0 %collective-permute-start.2 = (bf16[192,128]{1,0:T(8,128)(2,1)S(1)}, bf16[192,128]{1,0:T(8,128)(2,1)S(1)}, u32[]{:S(2)}, u32[]{:S(2)}) collective-permute-start(bf16[192,128]{1,0:T(8,128)(2,1)S(1)} %shard_map.135), channel_id=1, source_target_pairs={{0,3},{1,2},{2,1},{3,0},{4,7},{5,6},{6,5},{7,4},{8,11},{9,10},{10,... | collective-permute-start | bytes 147464 | tf_op jit(solution)/shard_map/ppermute | solution.py:538
  7.1 4.6 %collective-permute-start.1 = (bf16[192,128]{1,0:T(8,128)(2,1)S(1)}, bf16[192,128]{1,0:T(8,128)(2,1)S(1)}, u32[]{:S(2)}, u32[]{:S(2)}) collective-permute-start(bf16[192,128]{1,0:T(8,128)(2,1)S(1)} %shard_map.135), channel_id=1, source_target_pairs={{0,1},{1,0},{2,3},{3,2},{4,5},{5,4},{6,7},{7,6},{8,9},{9,8},{10,11... | collective-permute-start | bytes 147464 | tf_op jit(solution)/shard_map/ppermute | solution.py:538
  8.4 6.4 %collective-permute-start.3 = (bf16[2,192,128]{2,1,0:T(8,128)(2,1)S(1)}, bf16[2,192,128]{2,1,0:T(8,128)(2,1)S(1)}, u32[]{:S(2)}, u32[]{:S(2)}) collective-permute-start(bf16[2,192,128]{2,1,0:T(8,128)(2,1)S(1)} %pad_maximum_fusion.1.front_ref), channel_id=1, source_target_pairs={{0,8},{4,12},{8,0},{12,4},{1,9},{5,13},{9,1},{13,5},{2,10},{6,14},... | collective-permute-start | bytes 294920 | tf_op jit(solution)/shard_map/ppermute | solution.py:538
  11.8 4.7 %collective-permute-start.5 = (bf16[2,192,128]{2,1,0:T(8,128)(2,1)S(1)}, bf16[2,192,128]{2,1,0:T(8,128)(2,1)S(1)}, u32[]{:S(2)}, u32[]{:S(2)}) collective-permute-start(bf16[2,192,128]{2,1,0:T(8,128)(2,1)S(1)} %pad_maximum_fusion.2.rear_ref), channel_id=1, source_target_pairs={{0,8},{4,12},{8,0},{12,4},{1,9},{5,13},{9,1},{13,5},{2,10},{6,14},... | collective-permute-start | bytes 294920 | tf_op jit(solution)/shard_map/ppermute | solution.py:538
  14.8 1.7 %collective-permute-start.7 = (bf16[4,192,128]{2,1,0:T(8,128)(2,1)S(1)}, bf16[4,192,128]{2,1,0:T(8,128)(2,1)S(1)}, u32[]{:S(2)}, u32[]{:S(2)}) collective-permute-start(bf16[4,192,128]{2,1,0:T(8,128)(2,1)S(1)} %pad_maximum_fusion), channel_id=1, source_target_pairs={{0,4},{4,0},{8,12},{12,8},{1,5},{5,1},{9,13},{13,9},{2,6},{6,2},{1... | collective-permute-start | bytes 589832 | tf_op jit(solution)/shard_map/ppermute | solution.py:538
  14.9 2.7 %collective-permute-start.4 = (bf16[2,192,128]{2,1,0:T(8,128)(2,1)S(1)}, bf16[2,192,128]{2,1,0:T(8,128)(2,1)S(1)}, u32[]{:S(2)}, u32[]{:S(2)}) collective-permute-start(bf16[2,192,128]{2,1,0:T(8,128)(2,1)S(1)} %collective-permute-done.3.front_ref), channel_id=1, source_target_pairs={{0,4},{4,0},{8,12},{12,8},{1,5},{5,1},{9,13},{13,9},{2,6},{6,2},{1... | collective-permute-start | bytes 294920 | tf_op jit(solution)/shard_map/ppermute | solution.py:538
  16.4 1.3 %collective-permute-start.6 = (bf16[2,192,128]{2,1,0:T(8,128)(2,1)S(1)}, bf16[2,192,128]{2,1,0:T(8,128)(2,1)S(1)}, u32[]{:S(2)}, u32[]{:S(2)}) collective-permute-start(bf16[2,192,128]{2,1,0:T(8,128)(2,1)S(1)} %collective-permute-done.5.rear_ref), channel_id=1, source_target_pairs={{0,4},{4,0},{8,12},{12,8},{1,5},{5,1},{9,13},{13,9},{2,6},{6,2},{1... | collective-permute-start | bytes 294920 | tf_op jit(solution)/shard_map/ppermute | solution.py:538
